TPU v7x, 32 devices: a whole 2x2x4 slice. The times are simulated.
32 devices in a mesh: dp: 8 (over y, x, core), mp: 4 (over z).
Axes of the slice: x: 2, y: 2, z: 4, core: 2. Of those that a mesh axis runs over, the one named last changes fastest.
Arguments:
- queries: bfloat16 [16, 128, 8192], P('dp', None, 'mp'), may hold values from -6 to 6
- out_grad: bfloat16 [16, 128, 8192], P('dp', None, 'mp'), may hold values from -12 to 12
- images: bfloat16 [16, 128, 7680], P('dp', 'mp'), may hold values from -6 to 6
- key_weight: bfloat16 [7680, 1024], P('dp', 'mp'), may hold values from -0.0625 to 0.0625
- value_weight: bfloat16 [7680, 1024], P('dp', 'mp'), may hold values from -0.0625 to 0.0625
- query_gain: float32 [128], replicated, may hold values from 0.1 to 1.9
- key_gain: float32 [128], replicated, may hold values from 0.1 to 1.9
- assignment: int32 [16], P('dp'), may hold values from 0 to 1
- tile_counts: int32 [16], P('dp'), may hold values from 1 to 4
- lengths: int32 [16], P('dp'), may hold values from 1 to 128
Outputs:
- query_grad: bfloat16 [16, 128, 8192], P('dp', None, 'mp')
- image_grad: bfloat16 [16, 128, 7680], P('dp', 'mp')
- key_weight_grad: float32 [7680, 1024], P('dp', 'mp')
- value_weight_grad: float32 [7680, 1024], P('dp', 'mp')
Inputs may be any that keep to these rules, and one draw needn't show every extreme that they name: assignment[s] picks one of the 2 images of the same block: sequence s attends to image (s // 2) * 2 + assignment[s]. Image i has tile_counts[i] * 32 rows in use, the first ones; the others are padding. Sequence s has its first lengths[s] tokens in use.
All inputs are finite; a program needn't handle non-finite values.
Results may differ from a plain program's by a relative error of at most 0.012.
Values may be sent and summed in bfloat16 or wider, within the bound.
No kernel may reach another device: no remote copies, remote signals or barrier semaphores. Data moves between devices by JAX's collectives and lax.ppermute only.
A program may use at most 128 MiB of HBM per device.

v0:
```python
import math

import jax
import jax.numpy as jnp
from jax import lax
from jax.sharding import PartitionSpec as P

TILE_ROWS = 32


EPSILON = 1e-05


def rms_scale(source):
    return lax.rsqrt(jnp.mean(source * source, axis=-1, keepdims=True) + EPSILON)


def rms_back(source, factor, gain_vector, upstream):
    weighted = gain_vector * upstream
    return factor * weighted - source * (factor * factor * factor) * jnp.mean(
        source * weighted, axis=-1, keepdims=True
    )


def attend(query_normed, masked_grad, key_normed, value_heads, key_live):
    inv_root = 1.0 / math.sqrt(query_normed.shape[-1])
    scores = (
        jnp.einsum(
            "btgjd,brgd->bgjtr", query_normed, key_normed, preferred_element_type=jnp.float32
        )
        * inv_root
    )
    raised = jnp.exp(scores) * key_live[:, None, None, None, :]
    prob_full = raised / jnp.sum(raised, axis=-1, keepdims=True)
    prob_half = prob_full.astype(jnp.bfloat16)
    value_part = jnp.einsum(
        "bgjtr,btgjd->brgd", prob_half, masked_grad, preferred_element_type=jnp.float32
    )
    prob_grad = jnp.einsum(
        "btgjd,brgd->bgjtr", masked_grad, value_heads, preferred_element_type=jnp.float32
    )
    score_grad = (
        prob_full * (prob_grad - jnp.sum(prob_full * prob_grad, axis=-1, keepdims=True))
    ).astype(jnp.bfloat16)
    query_part = (
        jnp.einsum("bgjtr,brgd->btgjd", score_grad, key_normed, preferred_element_type=jnp.float32)
        * inv_root
    )
    key_part = (
        jnp.einsum(
            "bgjtr,btgjd->brgd", score_grad, query_normed, preferred_element_type=jnp.float32
        )
        * inv_root
    )
    return (query_part, key_part, value_part)


def per_device(
    queries,
    out_grad,
    images,
    key_weight,
    value_weight,
    query_gain,
    key_gain,
    assignment,
    tile_counts,
    lengths,
):
    seq_count, text_len, query_cols = queries.shape
    img_count, own_rows, vis_width = images.shape
    head_dim = query_gain.shape[0]
    key_cols = key_weight.shape[1]
    key_heads = key_cols // head_dim
    group_size = query_cols // head_dim // key_heads
    stacked = jnp.stack((key_weight, value_weight))
    gathered = lax.all_gather(images, "mp", axis=1, tiled=True)
    img_rows = gathered.shape[1]
    image_flat = gathered.reshape(img_count * img_rows, vis_width)
    shard_piece = lax.all_gather(stacked, "dp", axis=1, tiled=True)
    col_slice = image_flat
    key_pre = jnp.dot(col_slice, shard_piece[0], preferred_element_type=jnp.float32)
    value_acc = jnp.dot(col_slice, shard_piece[1], preferred_element_type=jnp.float32)
    value_heads = value_acc.astype(jnp.bfloat16).reshape(img_count, img_rows, key_heads, head_dim)
    key_pre = key_pre.reshape(img_count, img_rows, key_heads, head_dim)
    key_scale = rms_scale(key_pre)
    key_normed = (key_pre * key_scale * key_gain).astype(jnp.bfloat16)
    picker = assignment[:, None] == jnp.arange(img_count, dtype=jnp.int32)[None, :]
    pick_half = picker.astype(jnp.bfloat16)
    seq_keys = jnp.einsum(
        "bi,irgd->brgd", pick_half, key_normed, preferred_element_type=jnp.float32
    ).astype(jnp.bfloat16)
    seq_values = jnp.einsum(
        "bi,irgd->brgd", pick_half, value_heads, preferred_element_type=jnp.float32
    ).astype(jnp.bfloat16)
    seq_tiles = jnp.sum(picker.astype(jnp.int32) * tile_counts[None, :], axis=1)
    key_live = (
        jnp.arange(img_rows, dtype=jnp.int32)[None, :] < (seq_tiles * TILE_ROWS)[:, None]
    ).astype(jnp.float32)
    row_live = (jnp.arange(text_len, dtype=jnp.int32)[None, :] < lengths[:, None]).astype(
        jnp.bfloat16
    )
    query_float = queries.astype(jnp.float32).reshape(
        seq_count, text_len, key_heads, group_size, head_dim
    )
    query_scale = rms_scale(query_float)
    query_normed = (query_float * query_scale * query_gain).astype(jnp.bfloat16)
    masked_grad = (out_grad * row_live[:, :, None]).reshape(
        seq_count, text_len, key_heads, group_size, head_dim
    )
    query_part, key_part, value_part = attend(
        query_normed, masked_grad, seq_keys, seq_values, key_live
    )
    pick_float = picker.astype(jnp.float32)[:, :, None, None, None]
    image_value = jnp.sum(pick_float * value_part[:, None], axis=0)
    value_rows = image_value.astype(jnp.bfloat16).reshape(img_count * img_rows, key_cols)
    image_key = jnp.sum(pick_float * key_part[:, None], axis=0)
    key_rows = (
        rms_back(key_pre, key_scale, key_gain, image_key)
        .astype(jnp.bfloat16)
        .reshape(img_count * img_rows, key_cols)
    )
    query_grad = (
        rms_back(query_float, query_scale, query_gain, query_part)
        .astype(jnp.bfloat16)
        .reshape(seq_count, text_len, query_cols)
    )
    both_grads = jnp.concatenate((key_rows, value_rows), axis=1)
    col_slice = image_flat
    summed = lax.psum_scatter(
        lax.dot_general(
            col_slice, both_grads, (((0,), (0,)), ((), ())), preferred_element_type=jnp.float32
        ),
        "dp",
        scatter_dimension=0,
        tiled=True,
    )
    key_weight_grad = summed[:, :key_cols]
    value_weight_grad = summed[:, key_cols:]
    col_dims = (((1,), (1,)), ((), ()))
    shard_piece = lax.all_gather(stacked, "dp", axis=1, tiled=True)
    result = lax.dot_general(key_rows, shard_piece[0], col_dims, preferred_element_type=jnp.float32)
    partial_value = result + lax.dot_general(
        value_rows, shard_piece[1], col_dims, preferred_element_type=jnp.float32
    )
    partial_value = partial_value.reshape(img_count, img_rows, vis_width)
    image_grad = lax.psum_scatter(
        partial_value.astype(jnp.bfloat16), "mp", scatter_dimension=1, tiled=True
    )
    return (query_grad, image_grad, key_weight_grad, value_weight_grad)


def solution(mesh):
    placed = (
        P("dp", None, "mp"),
        P("dp", None, "mp"),
        P("dp", "mp", None),
        P("dp", "mp"),
        P("dp", "mp"),
        P(),
        P(),
        P("dp"),
        P("dp"),
        P("dp"),
    )
    return jax.shard_map(
        per_device,
        mesh=mesh,
        in_specs=placed,
        out_specs=(P("dp", None, "mp"), P("dp", "mp", None), P("dp", "mp"), P("dp", "mp")),
        check_vma=False,
    )
```

profile of v0, /device:TPU:0, one launch (start us, length us, event | category | flops | bytes accessed | tf_op | source)
XLA Modules:
  0.0 396.2 jit_solution(18187108283683124221)
XLA Ops:
  7.2 0.7 all-gather.5.cloned.1.call-update
  8.0 2.2 pad_maximum_fusion
  10.5 1.2 copy.116
  11.7 0.5 copy.72
  12.3 0.2 select_reduce_fusion
  12.4 0.2 multiply_reduce_fusion
  12.6 0.6 fusion.30
  13.3 0.6 broadcast_bitcast_fusion
  13.9 0.6 multiply_multiply_fusion
  14.5 74.3 %all-gather.5.cloned.1.call-done = bf16[2,128,7680]{2,1,0:T(8,128)(2,1)} async-done(((bf16[2,32,7680]{2,1,0:T(8,128)(2,1)}), bf16[2,128,7680]{2,1,0:T(8,128)(2,1)}) %all-gather.5.cloned.1.call-update) | async-done | bytes 3932176 | tf_op jit(solution)/shard_map/all_gather | solution.py:77
  88.8 53.3 %all-gather.3.cloned.1.call-done = bf16[2,7680,256]{2,1,0:T(8,128)(2,1)} async-done(((bf16[2,960,256]{2,1,0:T(8,128)(2,1)}), bf16[2,7680,256]{2,1,0:T(8,128)(2,1)}) %all-gather.3.cloned.1.call-update) | async-done | bytes 7864336 | tf_op jit(solution)/shard_map/all_gather | solution.py:80
  142.0 4.5 %fusion.10 = f32[256,256]{0,1:T(8,128)S(1)} fusion(bf16[256,7680]{1,0:T(8,128)(2,1)} %bitcast.153, bf16[2,7680,256]{2,1,0:T(8,128)(2,1)} %all-gather.3.cloned.1.call-done), kind=kOutput, calls=%fused_computation.23 | convolution fusion | flops 1006632960 | bytes 8126464 | tf_op jit(solution)/shard_map/dot_general | solution.py:82
  147.0 4.5 %fusion.16 = bf16[256,256]{0,1:T(8,128)(2,1)S(1)} fusion(bf16[256,7680]{1,0:T(8,128)(2,1)} %bitcast.154, bf16[2,7680,256]{2,1,0:T(8,128)(2,1)} %all-gather.3.cloned.1.call-done), kind=kOutput, calls=%fused_computation.33 | convolution fusion | flops 1006698496 | bytes 7995392 | tf_op jit(solution)/shard_map/dot_general | solution.py:83
  151.8 0.4 fusion.15
  152.2 0.6 multiply_multiply_fusion.1
  152.8 0.6 copy-done.6
  153.5 0.4 fusion.14
  154.0 0.7 bitcast_reduce_fusion
  154.7 0.5 copy-done.4
  155.2 0.8 fusion.7
  156.0 2.7 fusion.35
  158.7 2.4 copy.90
  161.1 2.7 convolution_bitcast_fusion.1
  163.8 1.8 copy.91
  165.6 1.8 fusion.12
  167.4 1.8 copy.85
  169.2 1.9 multiply_reduce_fusion.1
  171.1 0.7 copy-done
  171.8 1.4 multiply_reduce_fusion.3
  173.2 1.8 copy.86
  175.0 1.0 copy.92
  176.0 0.7 copy_multiply_fusion
  176.7 0.7 mul.244.clone
  177.5 0.8 mul.290
  178.3 1.1 fusion.21
  179.5 9.8 %convolution_bitcast_fusion = f32[7680,512]{0,1:T(8,128)} fusion(bf16[256,7680]{1,0:T(8,128)(2,1)} %bitcast.155, bf16[256,256]{0,1:T(8,128)(2,1)S(1)} %bitcast.164, bf16[256,256]{0,1:T(8,128)(2,1)S(1)} %fusion.21), kind=kOutput, calls=%fused_computation | convolution fusion | flops 2013790208 | bytes 19922944 | tf_op jit(solution)/shard_map/dot_general | solution.py:131
  189.3 15.6 %copy.111 = f32[7680,512]{1,0:T(8,128)} copy(f32[7680,512]{0,1:T(8,128)} %convolution_bitcast_fusion) | data formatting | bytes 31457280
  204.9 0.2 reduce-scatter.5.cloned.1.call-start
  205.2 3.4 fusion.1
  208.5 5.6 %fusion = bf16[256,7680]{1,0:T(8,128)(2,1)} fusion(f32[256,7680]{1,0:T(8,128)S(1)} %fusion.1, bf16[2,7680,256]{2,1,0:T(8,128)(2,1)} %all-gather.3.cloned.1.call-done, bf16[32,8,2,128]{3,2,1,0:T(2,128)(2,1)S(1)} %bitcast.157), kind=kOutput, calls=%fused_computation.2 | convolution fusion | flops 1010565120 | bytes 15859712 | tf_op jit(solution)/shard_map/dot_general | solution.py:143
  214.2 0.7 copy-done.11
  214.8 0.4 fusion.6
  215.3 0.3 copy-done.5
  215.5 0.7 fusion.5
  216.2 1.3 copy.93
  217.5 96.7 %reduce-scatter.7.cloned.1.call-done = f32[960,512]{1,0:T(8,128)} async-done(((f32[7680,512]{1,0:T(8,128)}), f32[960,512]{1,0:T(8,128)}) %reduce-scatter.7.cloned.1.call-update) | async-done | bytes 1966096
  314.3 2.9 fusion.36
  317.2 72.5 %reduce-scatter.5.cloned.1.call-done = bf16[2,32,7680]{2,1,0:T(8,128)(2,1)} async-done(((bf16[2,128,7680]{2,1,0:T(8,128)(2,1)}), bf16[2,32,7680]{2,1,0:T(8,128)(2,1)}) %reduce-scatter.5.cloned.1.call-update) | async-done | bytes 983056 | tf_op jit(solution)/shard_map/reduce_scatter | solution.py:147
  (49 shorter events, 1.5 us)
Async XLA Ops:
  7.2 3.1 copy-start.12
  7.2 3.2 copy-start.2
  7.2 81.6 %all-gather.5.cloned.1.call-start = ((), (), s32[]{:S(2)}) async-start(), calls=%async_computation.3 | async-start | bytes 4915200 | tf_op jit(solution)/shard_map/all_gather | solution.py:77
  7.9 134.1 %all-gather.3.cloned.1.call-start = ((), (), s32[]{:S(2)}) async-start(), calls=%async_computation.2 | async-start | bytes 8847360 | tf_op jit(solution)/shard_map/all_gather | solution.py:80
  10.2 304.1 %reduce-scatter.7.cloned.1.call-start = ((), (), s32[]{:S(2)}) async-start(), calls=%async_computation.5 | async-start | bytes 17694720
  10.3 1.4 copy-start.1
  10.5 1.8 copy-start.13
  10.5 1.8 copy-start.14
  11.7 1.6 copy-start.8
  13.3 141.4 %copy-start.7 = (f32[2,128]{1,0:T(2,128)}, f32[2,128]{1,0:T(2,128)S(1)}, u32[]{:S(2)}) copy-start(f32[2,128]{1,0:T(2,128)S(1)} %compare_convert_fusion.1) | copy-start | bytes 3076
  146.6 5.0 %copy-start.3 = (f32[256,256]{0,1:T(8,128)}, f32[256,256]{0,1:T(8,128)S(1)}, u32[]{:S(2)}) copy-start(f32[256,256]{0,1:T(8,128)S(1)} %fusion.10) | copy-start | bytes 786436
  147.0 4.8 %copy-start.15 = (s32[2]{0:T(128)S(1)}, s32[2]{0:T(128)}, u32[]{:S(2)}) copy-start(s32[2]{0:T(128)} %param.17) | copy-start | bytes 28
  147.0 6.3 %copy-start.9 = (f32[128]{0:T(128)S(1)}, f32[128]{0:T(128)}, u32[]{:S(2)}) copy-start(f32[128]{0:T(128)} %param.16) | copy-start | bytes 1540
  151.6 2.4 copy-start.10
  152.8 0.6 copy-start.6
  154.0 1.2 copy-start.4
  171.1 0.7 copy-start
  204.9 184.8 %reduce-scatter.5.cloned.1.call-start = ((), (), s32[]{:S(2)}) async-start(), calls=%async_computation.4 | async-start | bytes 4915200 | tf_op jit(solution)/shard_map/reduce_scatter | solution.py:147
  214.1 0.7 copy-start.11
  214.8 0.7 copy-start.5
Sparse Core Ops, SparseCore 0:
  9.6 79.1 all-gather.4
  91.2 50.7 all-gather.2
  205.1 109.1 reduce-scatter.6
  317.0 72.6 reduce-scatter.4
where the time goes:
time: 397 us; the launch traced here: 396 us
  waiting for transfers between devices  298 us (75%)
  local copies, waits for them, and re-layouts  35.8 us (9%)
  matrix products  35.1 us (9%)
  between operations  14.1 us (4%)
  other arithmetic  13.4 us (3%)
    unnamed x5, waiting for transfers between devices  97.5 us
    all_gather x1, waiting for transfers between devices, per_device(): gathered = lax.all_gather(images, 'mp', axis=1, tiled=True)  74.3 us
    reduce_scatter x1, waiting for transfers between devices, per_device(): lax.psum_scatter(partial_value.astype(jnp.bfloat16), 'mp', scatter_dimens...  72.5 us
    all_gather x1, waiting for transfers between devices, per_device(): shard_piece = lax.all_gather(stacked, 'dp', axis=1, tiled=True)  53.3 us
    unnamed x36, local copies, waits for them, and re-layouts  20.9 us
    dot_general x1, matrix products, per_device(): lax.dot_general(col_slice, both_grads, (((0,), (0,)), ((), ())), preferre...  9.84 us
  transfers between devices with their start and end apart: 4, of which 4 were waited for; matrix products, arithmetic and copies ran while one was open for 5% of the time, Pallas kernels for 0%

commit v1 on v0

--- a/solution.py
+++ b/solution.py
@@ -56,6 +56,7 @@
 
 
 def per_device(
+    dp_size,
     queries,
     out_grad,
     images,
@@ -70,19 +71,47 @@
     seq_count, text_len, query_cols = queries.shape
     img_count, own_rows, vis_width = images.shape
     head_dim = query_gain.shape[0]
-    key_cols = key_weight.shape[1]
+    own_width, key_cols = key_weight.shape
     key_heads = key_cols // head_dim
     group_size = query_cols // head_dim // key_heads
-    stacked = jnp.stack((key_weight, value_weight))
-    gathered = lax.all_gather(images, "mp", axis=1, tiled=True)
-    img_rows = gathered.shape[1]
-    image_flat = gathered.reshape(img_count * img_rows, vis_width)
-    shard_piece = lax.all_gather(stacked, "dp", axis=1, tiled=True)
-    col_slice = image_flat
-    key_pre = jnp.dot(col_slice, shard_piece[0], preferred_element_type=jnp.float32)
-    value_acc = jnp.dot(col_slice, shard_piece[1], preferred_element_type=jnp.float32)
-    value_heads = value_acc.astype(jnp.bfloat16).reshape(img_count, img_rows, key_heads, head_dim)
-    key_pre = key_pre.reshape(img_count, img_rows, key_heads, head_dim)
+    pairs = dp_size // 2
+    width = 2 * own_width
+    place = lax.axis_index("dp")
+    pair, core = place // 2, place % 2
+
+    def swap(value, mask):
+        return lax.ppermute(value, "dp", [(i, i ^ mask) for i in range(dp_size)])
+
+    own_weight = jnp.concatenate((key_weight, value_weight), axis=1)
+    mate_weight = swap(own_weight, 1)
+    weight = jnp.where(
+        core == 0,
+        jnp.concatenate((own_weight, mate_weight), axis=0),
+        jnp.concatenate((mate_weight, own_weight), axis=0),
+    )
+
+    chunks = []
+    for r in range(pairs):
+        piece = lax.dynamic_slice_in_dim(images, (pair ^ r) * width, width, axis=2)
+        chunks.append(swap(piece, 2 * r) if r else piece)
+    mine = jnp.stack(chunks)
+    features = lax.all_gather(mine, "mp", axis=0)
+    mp_size = features.shape[0]
+    img_rows = mp_size * own_rows
+    flat = features.reshape(-1, width)
+    partial = jnp.dot(flat, weight, preferred_element_type=jnp.float32).astype(jnp.bfloat16)
+    partial = partial.reshape(mp_size, pairs, img_count, own_rows, 2 * key_cols)
+    total = 0.0
+    for r in range(pairs):
+        piece = partial[:, r]
+        total = total + (swap(piece, 2 * r) if r else piece).astype(jnp.float32)
+    total = total.transpose(1, 0, 2, 3).reshape(img_count, img_rows, 2 * key_cols)
+    key_pre = total[..., :key_cols].reshape(img_count, img_rows, key_heads, head_dim)
+    value_heads = (
+        total[..., key_cols:]
+        .astype(jnp.bfloat16)
+        .reshape(img_count, img_rows, key_heads, head_dim)
+    )
     key_scale = rms_scale(key_pre)
     key_normed = (key_pre * key_scale * key_gain).astype(jnp.bfloat16)
     picker = assignment[:, None] == jnp.arange(img_count, dtype=jnp.int32)[None, :]
@@ -113,41 +142,42 @@
     )
     pick_float = picker.astype(jnp.float32)[:, :, None, None, None]
     image_value = jnp.sum(pick_float * value_part[:, None], axis=0)
-    value_rows = image_value.astype(jnp.bfloat16).reshape(img_count * img_rows, key_cols)
+    value_rows = image_value.astype(jnp.bfloat16).reshape(img_count, img_rows, key_cols)
     image_key = jnp.sum(pick_float * key_part[:, None], axis=0)
     key_rows = (
         rms_back(key_pre, key_scale, key_gain, image_key)
         .astype(jnp.bfloat16)
-        .reshape(img_count * img_rows, key_cols)
+        .reshape(img_count, img_rows, key_cols)
     )
     query_grad = (
         rms_back(query_float, query_scale, query_gain, query_part)
         .astype(jnp.bfloat16)
         .reshape(seq_count, text_len, query_cols)
     )
-    both_grads = jnp.concatenate((key_rows, value_rows), axis=1)
-    col_slice = image_flat
-    summed = lax.psum_scatter(
-        lax.dot_general(
-            col_slice, both_grads, (((0,), (0,)), ((), ())), preferred_element_type=jnp.float32
-        ),
-        "dp",
-        scatter_dimension=0,
-        tiled=True,
-    )
-    key_weight_grad = summed[:, :key_cols]
-    value_weight_grad = summed[:, key_cols:]
-    col_dims = (((1,), (1,)), ((), ()))
-    shard_piece = lax.all_gather(stacked, "dp", axis=1, tiled=True)
-    result = lax.dot_general(key_rows, shard_piece[0], col_dims, preferred_element_type=jnp.float32)
-    partial_value = result + lax.dot_general(
-        value_rows, shard_piece[1], col_dims, preferred_element_type=jnp.float32
-    )
-    partial_value = partial_value.reshape(img_count, img_rows, vis_width)
-    image_grad = lax.psum_scatter(
-        partial_value.astype(jnp.bfloat16), "mp", scatter_dimension=1, tiled=True
-    )
-    return (query_grad, image_grad, key_weight_grad, value_weight_grad)
+    rows = jnp.concatenate((key_rows, value_rows), axis=2)
+    rows = rows.reshape(img_count, mp_size, own_rows, 2 * key_cols).transpose(1, 0, 2, 3)
+    all_rows = jnp.stack([swap(rows, 2 * r) if r else rows for r in range(pairs)], axis=1)
+    all_rows = all_rows.reshape(-1, 2 * key_cols)
+    image_part = lax.dot_general(
+        all_rows, weight, (((1,), (1,)), ((), ())), preferred_element_type=jnp.float32
+    ).astype(jnp.bfloat16)
+    image_part = image_part.reshape(mp_size, pairs * img_count * own_rows, width)
+    image_sum = lax.psum_scatter(image_part, "mp", scatter_dimension=0, tiled=False)
+    weight_part = lax.dot_general(
+        flat, all_rows, (((0,), (0,)), ((), ())), preferred_element_type=jnp.float32
+    )
+    weight_grad = lax.dynamic_slice_in_dim(weight_part, core * own_width, own_width, axis=0)
+    weight_grad = weight_grad + swap(
+        lax.dynamic_slice_in_dim(weight_part, (1 - core) * own_width, own_width, axis=0), 1
+    )
+    image_sum = image_sum.reshape(pairs, img_count, own_rows, width)
+    image_grad = jnp.zeros((img_count, own_rows, vis_width), jnp.bfloat16)
+    for r in range(pairs):
+        piece = swap(image_sum[r], 2 * r) if r else image_sum[r]
+        image_grad = lax.dynamic_update_slice_in_dim(
+            image_grad, piece, (pair ^ r) * width, axis=2
+        )
+    return (query_grad, image_grad, weight_grad[:, :key_cols], weight_grad[:, key_cols:])
 
 
 def solution(mesh):
@@ -163,8 +193,12 @@
         P("dp"),
         P("dp"),
     )
+
+    def body(*args):
+        return per_device(mesh.shape["dp"], *args)
+
     return jax.shard_map(
-        per_device,
+        body,
         mesh=mesh,
         in_specs=placed,
         out_specs=(P("dp", None, "mp"), P("dp", "mp", None), P("dp", "mp"), P("dp", "mp")),

time: 397 us -> 283 us (0.71)
  waiting for transfers between devices: 298 us -> 170 us
  starting transfers between devices: 0.34 us -> 15.4 us
  matrix products: 35.1 us -> 24 us
  local copies, waits for them, and re-layouts: 35.8 us -> 41.3 us
    unnamed x5 -> x2, waiting for transfers between devices: 97.5 us -> 0.03 us
    all_gather x2 -> x1, waiting for transfers between devices: 128 us -> 71.2 us  [per_device(): features = lax.all_gather(mine, 'mp', axis=0)]
    ppermute x0 -> x14, waiting for transfers between devices: none -> 42.3 us  [swap(): return lax.ppermute(value, 'dp', [(i, i ^ mask) for i in range(dp_size)])]
    reduce_scatter x1, waiting for transfers between devices: 72.5 us -> 56 us  [per_device(): lax.psum_scatter(image_part, 'mp', scatter_dimension=0, tiled=False)]
    ppermute x0 -> x14, starting transfers between devices: none -> 15.3 us  [swap(): return lax.ppermute(value, 'dp', [(i, i ^ mask) for i in range(dp_size)])]
    unnamed x36 -> x50, local copies, waits for them, and re-layouts: 20.9 us -> 9.17 us
    dot_general x5 -> x3, matrix products: 27.9 us -> 16.7 us  [the longest x1 6.43 us: per_device(): lax.dot_general(all_rows, weight, (((1,), (1,)), ((), ())), preferred_ele...]
    mul x2 -> x4, local copies, waits for them, and re-layouts: 0.82 us -> 6.01 us  [rms_back(): source * (factor * factor * factor)]
  transfers between devices with their start and end apart: 4 -> 16, of which waited for: 4 -> 11; matrix products, arithmetic and copies ran while one was open for 5% -> 7% of each run, Pallas kernels for 0% -> 0%
where the time goes in v1:
time: 283 us; the launch traced here: 282 us
  waiting for transfers between devices  170 us (60%)
  local copies, waits for them, and re-layouts  41.3 us (15%)
  matrix products  24 us (8%)
  other arithmetic  17.3 us (6%)
  starting transfers between devices  15.4 us (5%)
  between operations  14.5 us (5%)
    all_gather x1, waiting for transfers between devices, per_device(): features = lax.all_gather(mine, 'mp', axis=0)  71.2 us
    reduce_scatter x1, waiting for transfers between devices, per_device(): lax.psum_scatter(image_part, 'mp', scatter_dimension=0, tiled=False)  56 us
    ppermute x14, waiting for transfers between devices, swap(): return lax.ppermute(value, 'dp', [(i, i ^ mask) for i in range(dp_size)])  42.3 us
    ppermute x14, starting transfers between devices, swap(): return lax.ppermute(value, 'dp', [(i, i ^ mask) for i in range(dp_size)])  15.3 us
    unnamed x50, local copies, waits for them, and re-layouts  9.17 us
    dot_general x1, matrix products, per_device(): lax.dot_general(all_rows, weight, (((1,), (1,)), ((), ())), preferred_ele...  6.43 us
    mul x4, local copies, waits for them, and re-layouts, rms_back(): source * (factor * factor * factor)  6.01 us
  transfers between devices with their start and end apart: 16, of which 11 were waited for; matrix products, arithmetic and copies ran while one was open for 7% of the time, Pallas kernels for 0%

profile of v1, /device:TPU:0, one launch (start us, length us, event | category | flops | bytes accessed | tf_op | source)
XLA Modules:
  0.0 282.0 jit_solution(8124818265718558612)
XLA Ops:
  7.3 1.4 dynamic-slice_bitcast_fusion
  8.7 3.0 %collective-permute-start = (bf16[2,32,1920]{2,1,0:T(8,128)(2,1)S(1)}, bf16[2,32,1920]{2,1,0:T(8,128)(2,1)S(1)}, u32[]{:S(2)}, u32[]{:S(2)}) collective-permute-start(bf16[2,32,1920]{2,1,0:T(8,128)(2,1)S(1)} %get-tuple-element.39), channel_id=1, source_target_pairs={{0,8},{4,12},{8,0},{12,4},{16,24},{20,28},{24,16},{28,20},{1,9},{5... | collective-permute-start | bytes 737288 | tf_op jit(solution)/shard_map/ppermute | solution.py:83
  11.7 1.5 collective-permute-start.1
  13.3 5.2 %collective-permute-done = bf16[2,32,1920]{2,1,0:T(8,128)(2,1)S(1)} collective-permute-done((bf16[2,32,1920]{2,1,0:T(8,128)(2,1)S(1)}, bf16[2,32,1920]{2,1,0:T(8,128)(2,1)S(1)}, u32[]{:S(2)}, u32[]{:S(2)}) %collective-permute-start) | collective-permute-done | bytes 245792 | tf_op jit(solution)/shard_map/ppermute | solution.py:83
  18.5 5.9 %collective-permute-done.1 = bf16[2,32,1920]{2,1,0:T(8,128)(2,1)S(1)} collective-permute-done((bf16[2,32,1920]{2,1,0:T(8,128)(2,1)S(1)}, bf16[2,32,1920]{2,1,0:T(8,128)(2,1)S(1)}, u32[]{:S(2)}, u32[]{:S(2)}) %collective-permute-start.1) | collective-permute-done | bytes 245792 | tf_op jit(solution)/shard_map/ppermute | solution.py:83
  29.9 1.4 broadcast_multiply_fusion
  31.3 71.2 %all-gather.3.cloned.1.call-done = bf16[16,2,32,1920]{3,2,1,0:T(8,128)(2,1)} async-done(((bf16[4,2,32,1920]{3,2,1,0:T(8,128)(2,1)}), bf16[16,2,32,1920]{3,2,1,0:T(8,128)(2,1)}) %all-gather.3.cloned.1.call-update) | async-done | bytes 3932176 | tf_op jit(solution)/shard_map/all_gather | solution.py:98
  102.5 5.7 %convolution_convert_fusion.1 = bf16[1024,512]{1,0:T(8,128)(2,1)S(1)} fusion(bf16[1024,1920]{1,0:T(8,128)(2,1)} %bitcast.164, bf16[960,512]{1,0:T(8,128)(2,1)} %collective-permute-done.3, bf16[960,512]{1,0:T(8,128)(2,1)} %constant_dynamic-update-slice_fusion, pred[]{:T(512)S(6)} %eq.25), kind=kOutput, calls=%fused_computation.19 | convolution fusion | flops 2022637568 | bytes 6946817 | tf_op jit(solution)/shard_map/dot_general | solution.py:102
  108.2 1.6 collective-permute-start.4
  109.8 1.5 collective-permute-start.5
  112.1 1.2 copy.178
  114.0 3.5 %collective-permute-done.4 = bf16[4,2,32,512]{3,2,0,1:T(8,128)(2,1)S(1)} collective-permute-done((bf16[4,2,32,512]{3,2,0,1:T(8,128)(2,1)S(1)}, bf16[4,2,32,512]{3,2,0,1:T(8,128)(2,1)S(1)}, u32[]{:S(2)}, u32[]{:S(2)}) %collective-permute-start.4) | collective-permute-done | bytes 262176 | tf_op jit(solution)/shard_map/ppermute | solution.py:83
  117.5 5.8 %collective-permute-done.5 = bf16[4,2,32,512]{3,2,0,1:T(8,128)(2,1)S(1)} collective-permute-done((bf16[4,2,32,512]{3,2,0,1:T(8,128)(2,1)S(1)}, bf16[4,2,32,512]{3,2,0,1:T(8,128)(2,1)S(1)}, u32[]{:S(2)}, u32[]{:S(2)}) %collective-permute-start.5) | collective-permute-done | bytes 262176 | tf_op jit(solution)/shard_map/ppermute | solution.py:83
  127.0 1.5 bitcast_reduce_fusion
  129.3 2.0 fusion.25
  132.5 1.8 copy.137
  134.2 2.4 copy.145
  136.6 2.7 convolution_bitcast_fusion.1
  139.3 1.8 copy.146
  141.1 1.9 multiply_reduce_fusion.2
  143.7 1.4 multiply_reduce_fusion.3
  145.1 1.8 copy.138
  149.9 1.8 copy.139
  151.7 1.5 copy.141
  153.1 1.9 mul.316
  155.1 1.9 mul.317
  156.9 1.4 mul.270.clone
  158.3 1.8 copy.140
  160.1 1.7 copy.147
  161.8 1.6 convert_element_type.97
  163.5 1.3 subtract_convert_fusion
  167.8 1.5 collective-permute-start.9
  169.3 5.8 %collective-permute-done.7 = bf16[4,2,32,512]{3,2,1,0:T(8,128)(2,1)S(1)} collective-permute-done((bf16[4,2,32,512]{3,2,1,0:T(8,128)(2,1)S(1)}, bf16[4,2,32,512]{3,2,1,0:T(8,128)(2,1)S(1)}, u32[]{:S(2)}, u32[]{:S(2)}) %collective-permute-start.7) | collective-permute-done | bytes 262176 | tf_op jit(solution)/shard_map/ppermute | solution.py:83
  175.0 4.3 %collective-permute-done.8 = bf16[4,2,32,512]{3,2,1,0:T(8,128)(2,1)S(1)} collective-permute-done((bf16[4,2,32,512]{3,2,1,0:T(8,128)(2,1)S(1)}, bf16[4,2,32,512]{3,2,1,0:T(8,128)(2,1)S(1)}, u32[]{:S(2)}, u32[]{:S(2)}) %collective-permute-start.8) | collective-permute-done | bytes 262176 | tf_op jit(solution)/shard_map/ppermute | solution.py:83
  180.1 6.4 %convolution_convert_fusion = bf16[1024,1920]{1,0:T(8,128)(2,1)} fusion(bf16[1024,512]{1,0:T(8,128)(2,1)S(1)} %bitcast.143, bf16[960,512]{1,0:T(8,128)(2,1)} %collective-permute-done.3, bf16[960,512]{1,0:T(8,128)(2,1)} %constant_dynamic-update-slice_fusion, pred[]{:T(512)S(6)} %eq.25), kind=kOutput, calls=%fused_computation | convolution fusion | flops 2024079360 | bytes 6946817 | tf_op jit(solution)/shard_map/dot_general | solution.py:161
  186.6 4.6 %convolution_bitcast_fusion = f32[1920,512]{1,0:T(8,128)S(1)} fusion(bf16[4,4,2,32,1920]{4,3,2,1,0:T(8,128)(2,1)} %bitcast.165, bf16[4,1,2,32,512]{4,3,2,1,0:T(8,128)(2,1)} %bitcast.157, bf16[4,1,2,32,512]{4,3,2,1,0:T(8,128)(2,1)} %bitcast.155, bf16[4,1,2,32,512]{4,3,2,1,0:T(8,128)(2,1)} %bitcast.153, bf16[4,1,2,32,512]{4,3,2,1,0:T(8,128)(2,1)S(1)} %get-tuple-element.42), kind=kOutput, calls=%fused_computation.1 | convolution fusion | flops 2014838784 | bytes 8912896 | tf_op jit(solution)/shard_map/dot_general | solution.py:166
  191.2 1.8 copy-done
  193.0 1.4 constant_dynamic-slice_fusion
  195.9 1.3 copy.153
  197.2 1.6 collective-permute-done.13
  198.8 2.7 dynamic-slice_add_fusion
  201.5 56.0 %reduce-scatter.2.cloned.1.call-done = bf16[1,256,1920]{2,1,0:T(8,128)(2,1)} async-done(((bf16[4,256,1920]{2,1,0:T(8,128)(2,1)}), bf16[1,256,1920]{2,1,0:T(8,128)(2,1)}) %reduce-scatter.2.cloned.1.call-update) | async-done | bytes 983056 | tf_op jit(solution)/shard_map/reduce_scatter | solution.py:165
  257.5 1.4 fusion.28
  258.9 1.6 collective-permute-start.10
  260.4 1.4 fusion.26
  261.9 1.5 collective-permute-start.11
  264.0 3.8 %collective-permute-done.10 = bf16[2,32,1920]{2,1,0:T(8,128)(2,1)S(1)} collective-permute-done((bf16[2,32,1920]{2,1,0:T(8,128)(2,1)S(1)}, bf16[2,32,1920]{2,1,0:T(8,128)(2,1)S(1)}, u32[]{:S(2)}, u32[]{:S(2)}) %collective-permute-start.10) | collective-permute-done | bytes 245792 | tf_op jit(solution)/shard_map/ppermute | solution.py:83
  267.7 6.4 %collective-permute-done.11 = bf16[2,32,1920]{2,1,0:T(8,128)(2,1)S(1)} collective-permute-done((bf16[2,32,1920]{2,1,0:T(8,128)(2,1)S(1)}, bf16[2,32,1920]{2,1,0:T(8,128)(2,1)S(1)}, u32[]{:S(2)}, u32[]{:S(2)}) %collective-permute-start.11) | collective-permute-done | bytes 245792 | tf_op jit(solution)/shard_map/ppermute | solution.py:83
  (105 shorter events, 23.2 us)
Async XLA Ops:
  7.2 95.3 %all-gather.3.cloned.1.call-start = ((), (), s32[]{:S(2)}) async-start(), calls=%async_computation.2 | async-start | bytes 4915200 | tf_op jit(solution)/shard_map/all_gather | solution.py:98
  7.2 18.3 %copy-start.6 = (bf16[960,256]{1,0:T(8,128)(2,1)S(1)}, bf16[960,256]{1,0:T(8,128)(2,1)}, u32[]{:S(2)}) copy-start(bf16[960,256]{1,0:T(8,128)(2,1)} %param.13) | copy-start | bytes 1474564
  8.7 17.7 %copy-start.7 = (bf16[960,256]{1,0:T(8,128)(2,1)S(1)}, bf16[960,256]{1,0:T(8,128)(2,1)}, u32[]{:S(2)}) copy-start(bf16[960,256]{1,0:T(8,128)(2,1)} %param.14) | copy-start | bytes 1474564
  8.7 9.8 %collective-permute-start = (bf16[2,32,1920]{2,1,0:T(8,128)(2,1)S(1)}, bf16[2,32,1920]{2,1,0:T(8,128)(2,1)S(1)}, u32[]{:S(2)}, u32[]{:S(2)}) collective-permute-start(bf16[2,32,1920]{2,1,0:T(8,128)(2,1)S(1)} %get-tuple-element.39), channel_id=1, source_target_pairs={{0,8},{4,12},{8,0},{12,4},{16,24},{20,28},{24,16},{28,20},{1,9},{5... | collective-permute-start | bytes 737288 | tf_op jit(solution)/shard_map/ppermute | solution.py:83
  11.7 12.7 %collective-permute-start.1 = (bf16[2,32,1920]{2,1,0:T(8,128)(2,1)S(1)}, bf16[2,32,1920]{2,1,0:T(8,128)(2,1)S(1)}, u32[]{:S(2)}, u32[]{:S(2)}) collective-permute-start(bf16[2,32,1920]{2,1,0:T(8,128)(2,1)S(1)} %get-tuple-element.41), channel_id=1, source_target_pairs={{0,16},{4,20},{8,24},{12,28},{16,0},{20,4},{24,8},{28,12},{1,17},{... | collective-permute-start | bytes 737288 | tf_op jit(solution)/shard_map/ppermute | solution.py:83
  13.2 11.2 %collective-permute-start.2 = (bf16[2,32,1920]{2,1,0:T(8,128)(2,1)S(1)}, bf16[2,32,1920]{2,1,0:T(8,128)(2,1)S(1)}, u32[]{:S(2)}, u32[]{:S(2)}) collective-permute-start(bf16[2,32,1920]{2,1,0:T(8,128)(2,1)S(1)} %get-tuple-element.40), channel_id=1, source_target_pairs={{0,24},{4,28},{8,16},{12,20},{16,8},{20,12},{24,0},{28,4},{1,25},{... | collective-permute-start | bytes 737288 | tf_op jit(solution)/shard_map/ppermute | solution.py:83
  24.4 2.8 %copy-start.18 = (s32[2]{0:T(128)S(1)}, s32[2]{0:T(128)}, u32[]{:S(2)}) copy-start(s32[2]{0:T(128)} %param.18) | copy-start | bytes 28
  24.4 2.8 %copy-start.20 = (s32[2]{0:T(128)S(1)}, s32[2]{0:T(128)}, u32[]{:S(2)}) copy-start(s32[2]{0:T(128)} %param.17) | copy-start | bytes 28
  24.4 3.7 %copy-start.19 = (s32[2]{0:T(128)S(1)}, s32[2]{0:T(128)}, u32[]{:S(2)}) copy-start(s32[2]{0:T(128)} %param.19) | copy-start | bytes 28
  24.4 3.7 %copy-start.3 = (bf16[2,128,2048]{2,1,0:T(8,128)(2,1)S(1)}, bf16[2,128,2048]{2,1,0:T(8,128)(2,1)}, u32[]{:S(2)}) copy-start(bf16[2,128,2048]{2,1,0:T(8,128)(2,1)} %param.10) | copy-start | bytes 3145732
  25.5 232.0 %reduce-scatter.2.cloned.1.call-start = ((), (), s32[]{:S(2)}) async-start(), calls=%async_computation.1 | async-start | bytes 4915200 | tf_op jit(solution)/shard_map/reduce_scatter | solution.py:165
  26.4 2.9 %copy-start.14 = (f32[128]{0:T(128)S(1)}, f32[128]{0:T(128)}, u32[]{:S(2)}) copy-start(f32[128]{0:T(128)} %param.16) | copy-start | bytes 1540
  27.2 4.0 %collective-permute-start.3 = (bf16[960,512]{1,0:T(8,128)(2,1)}, bf16[960,512]{1,0:T(8,128)(2,1)}, u32[]{:S(2)}, u32[]{:S(2)}) collective-permute-start(bf16[960,512]{1,0:T(8,128)(2,1)} %constant_dynamic-update-slice_fusion), channel_id=1, source_target_pairs={{0,4},{4,0},{8,12},{12,8},{16,20},{20,16},{24,28},{28,24},{1,5},{5... | collective-permute-start | bytes 2949128 | tf_op jit(solution)/shard_map/ppermute | solution.py:83
  108.2 9.3 %collective-permute-start.4 = (bf16[4,2,32,512]{3,2,0,1:T(8,128)(2,1)S(1)}, bf16[4,2,32,512]{3,2,0,1:T(8,128)(2,1)S(1)}, u32[]{:S(2)}, u32[]{:S(2)}) collective-permute-start(bf16[4,2,32,512]{3,2,0,1:T(8,128)(2,1)S(1)} %bitcast.149), channel_id=1, source_target_pairs={{0,8},{4,12},{8,0},{12,4},{16,24},{20,28},{24,16},{28,20},{1,9},{5... | collective-permute-start | bytes 786440 | tf_op jit(solution)/shard_map/ppermute | solution.py:83
  109.8 13.4 %collective-permute-start.5 = (bf16[4,2,32,512]{3,2,0,1:T(8,128)(2,1)S(1)}, bf16[4,2,32,512]{3,2,0,1:T(8,128)(2,1)S(1)}, u32[]{:S(2)}, u32[]{:S(2)}) collective-permute-start(bf16[4,2,32,512]{3,2,0,1:T(8,128)(2,1)S(1)} %bitcast.150), channel_id=1, source_target_pairs={{0,16},{4,20},{8,24},{12,28},{16,0},{20,4},{24,8},{28,12},{1,17},{... | collective-permute-start | bytes 786440 | tf_op jit(solution)/shard_map/ppermute | solution.py:83
  111.4 11.9 %collective-permute-start.6 = (bf16[4,2,32,512]{3,2,0,1:T(8,128)(2,1)S(1)}, bf16[4,2,32,512]{3,2,0,1:T(8,128)(2,1)S(1)}, u32[]{:S(2)}, u32[]{:S(2)}) collective-permute-start(bf16[4,2,32,512]{3,2,0,1:T(8,128)(2,1)S(1)} %bitcast.151), channel_id=1, source_target_pairs={{0,24},{4,28},{8,16},{12,20},{16,8},{20,12},{24,0},{28,4},{1,25},{... | collective-permute-start | bytes 786440 | tf_op jit(solution)/shard_map/ppermute | solution.py:83
  113.3 12.3 %copy-start.15 = (f32[128]{0:T(128)S(1)}, f32[128]{0:T(128)}, u32[]{:S(2)}) copy-start(f32[128]{0:T(128)} %param.16) | copy-start | bytes 1540
  113.3 12.5 %copy-start.21 = (s32[2]{0:T(128)S(1)}, s32[2]{0:T(128)}, u32[]{:S(2)}) copy-start(s32[2]{0:T(128)} %param.17) | copy-start | bytes 28
  123.4 0.8 copy-start.1
  125.1 0.6 copy-start.12
  127.0 1.5 copy-start.4
  127.0 1.5 copy-start.13
  129.3 2.0 copy-start.16
  143.0 0.7 copy-start.2
  165.7 9.3 %collective-permute-start.7 = (bf16[4,2,32,512]{3,2,1,0:T(8,128)(2,1)S(1)}, bf16[4,2,32,512]{3,2,1,0:T(8,128)(2,1)S(1)}, u32[]{:S(2)}, u32[]{:S(2)}) collective-permute-start(bf16[4,2,32,512]{3,2,1,0:T(8,128)(2,1)S(1)} %get-tuple-element.43), channel_id=1, source_target_pairs={{0,8},{4,12},{8,0},{12,4},{16,24},{20,28},{24,16},{28,20},{1,9},{5... | collective-permute-start | bytes 786440 | tf_op jit(solution)/shard_map/ppermute | solution.py:83
  166.9 12.5 %collective-permute-start.8 = (bf16[4,2,32,512]{3,2,1,0:T(8,128)(2,1)S(1)}, bf16[4,2,32,512]{3,2,1,0:T(8,128)(2,1)S(1)}, u32[]{:S(2)}, u32[]{:S(2)}) collective-permute-start(bf16[4,2,32,512]{3,2,1,0:T(8,128)(2,1)S(1)} %get-tuple-element.43), channel_id=1, source_target_pairs={{0,16},{4,20},{8,24},{12,28},{16,0},{20,4},{24,8},{28,12},{1,17},{... | collective-permute-start | bytes 786440 | tf_op jit(solution)/shard_map/ppermute | solution.py:83
  167.8 11.6 %collective-permute-start.9 = (bf16[4,2,32,512]{3,2,1,0:T(8,128)(2,1)S(1)}, bf16[4,2,32,512]{3,2,1,0:T(8,128)(2,1)S(1)}, u32[]{:S(2)}, u32[]{:S(2)}) collective-permute-start(bf16[4,2,32,512]{3,2,1,0:T(8,128)(2,1)S(1)} %get-tuple-element.43), channel_id=1, source_target_pairs={{0,24},{4,28},{8,16},{12,20},{16,8},{20,12},{24,0},{28,4},{1,25},{... | collective-permute-start | bytes 786440 | tf_op jit(solution)/shard_map/ppermute | solution.py:83
  175.0 4.3 %copy-start.8 = (bf16[4,2,32,512]{3,2,1,0:T(8,128)(2,1)}, bf16[4,2,32,512]{3,2,1,0:T(8,128)(2,1)S(1)}, u32[]{:S(2)}) copy-start(bf16[4,2,32,512]{3,2,1,0:T(8,128)(2,1)S(1)} %collective-permute-done.7) | copy-start | bytes 786436
  179.3 0.7 copy-start.9
  179.3 0.8 copy-start.10
  191.2 1.9 copy-start
  193.0 1.4 copy-start.17
  194.5 4.3 %collective-permute-start.13 = (f32[960,512]{1,0:T(8,128)}, f32[960,512]{1,0:T(8,128)}, u32[]{:S(2)}, u32[]{:S(2)}) collective-permute-start(f32[960,512]{1,0:T(8,128)} %constant_dynamic-slice_fusion), channel_id=1, source_target_pairs={{0,4},{4,0},{8,12},{12,8},{16,20},{20,16},{24,28},{28,24},{1,5},{5... | collective-permute-start | bytes 5898248 | tf_op jit(solution)/shard_map/ppermute | solution.py:83
  194.5 0.7 copy-start.11
  258.9 8.8 %collective-permute-start.10 = (bf16[2,32,1920]{2,1,0:T(8,128)(2,1)S(1)}, bf16[2,32,1920]{2,1,0:T(8,128)(2,1)S(1)}, u32[]{:S(2)}, u32[]{:S(2)}) collective-permute-start(bf16[2,32,1920]{2,1,0:T(8,128)(2,1)S(1)} %bitcast.160), channel_id=1, source_target_pairs={{0,8},{4,12},{8,0},{12,4},{16,24},{20,28},{24,16},{28,20},{1,9},{5... | collective-permute-start | bytes 737288 | tf_op jit(solution)/shard_map/ppermute | solution.py:83
  261.9 12.3 %collective-permute-start.11 = (bf16[2,32,1920]{2,1,0:T(8,128)(2,1)S(1)}, bf16[2,32,1920]{2,1,0:T(8,128)(2,1)S(1)}, u32[]{:S(2)}, u32[]{:S(2)}) collective-permute-start(bf16[2,32,1920]{2,1,0:T(8,128)(2,1)S(1)} %bitcast.159), channel_id=1, source_target_pairs={{0,16},{4,20},{8,24},{12,28},{16,0},{20,4},{24,8},{28,12},{1,17},{... | collective-permute-start | bytes 737288 | tf_op jit(solution)/shard_map/ppermute | solution.py:83
  263.3 10.9 %collective-permute-start.12 = (bf16[2,32,1920]{2,1,0:T(8,128)(2,1)S(1)}, bf16[2,32,1920]{2,1,0:T(8,128)(2,1)S(1)}, u32[]{:S(2)}, u32[]{:S(2)}) collective-permute-start(bf16[2,32,1920]{2,1,0:T(8,128)(2,1)S(1)} %bitcast.158), channel_id=1, source_target_pairs={{0,24},{4,28},{8,16},{12,20},{16,8},{20,12},{24,0},{28,4},{1,25},{... | collective-permute-start | bytes 737288 | tf_op jit(solution)/shard_map/ppermute | solution.py:83
  274.2 0.9 copy-start.5
Sparse Core Ops, SparseCore 0:
  25.7 76.7 all-gather.2
  186.7 70.7 reduce-scatter.1

commit v2 on v1

--- a/solution.py
+++ b/solution.py
@@ -57,6 +57,7 @@
 
 def per_device(
     dp_size,
+    mp_size,
     queries,
     out_grad,
     images,
@@ -90,21 +91,30 @@
         jnp.concatenate((mate_weight, own_weight), axis=0),
     )
 
-    chunks = []
+    def ring(value, step):
+        return lax.ppermute(value, "mp", [(i, (i + step) % mp_size) for i in range(mp_size)])
+
+    half = mp_size // 2
+    blocks = []
     for r in range(pairs):
         piece = lax.dynamic_slice_in_dim(images, (pair ^ r) * width, width, axis=2)
-        chunks.append(swap(piece, 2 * r) if r else piece)
-    mine = jnp.stack(chunks)
-    features = lax.all_gather(mine, "mp", axis=0)
-    mp_size = features.shape[0]
+        piece = swap(piece, 2 * r) if r else piece
+        parts = [piece] + [None] * (mp_size - 1)
+        right = left = piece
+        for k in range(1, half + 1):
+            if k < half or r < pairs // 2:
+                parts[k] = right = ring(right, 1)
+            if k < half or r >= pairs // 2:
+                parts[mp_size - k] = left = ring(left, -1)
+        blocks.append(jnp.stack(parts))
     img_rows = mp_size * own_rows
-    flat = features.reshape(-1, width)
-    partial = jnp.dot(flat, weight, preferred_element_type=jnp.float32).astype(jnp.bfloat16)
-    partial = partial.reshape(mp_size, pairs, img_count, own_rows, 2 * key_cols)
     total = 0.0
     for r in range(pairs):
-        piece = partial[:, r]
+        piece = jnp.dot(
+            blocks[r].reshape(-1, width), weight, preferred_element_type=jnp.float32
+        ).astype(jnp.bfloat16)
         total = total + (swap(piece, 2 * r) if r else piece).astype(jnp.float32)
+    total = total.reshape(mp_size, img_count, own_rows, 2 * key_cols)
     total = total.transpose(1, 0, 2, 3).reshape(img_count, img_rows, 2 * key_cols)
     key_pre = total[..., :key_cols].reshape(img_count, img_rows, key_heads, head_dim)
     value_heads = (
@@ -123,9 +133,11 @@
         "bi,irgd->brgd", pick_half, value_heads, preferred_element_type=jnp.float32
     ).astype(jnp.bfloat16)
     seq_tiles = jnp.sum(picker.astype(jnp.int32) * tile_counts[None, :], axis=1)
-    key_live = (
-        jnp.arange(img_rows, dtype=jnp.int32)[None, :] < (seq_tiles * TILE_ROWS)[:, None]
-    ).astype(jnp.float32)
+    owners = (lax.axis_index("mp") - jnp.arange(mp_size, dtype=jnp.int32)) % mp_size
+    row_place = (
+        owners[:, None] * own_rows + jnp.arange(own_rows, dtype=jnp.int32)[None, :]
+    ).reshape(1, img_rows)
+    key_live = (row_place < (seq_tiles * TILE_ROWS)[:, None]).astype(jnp.float32)
     row_live = (jnp.arange(text_len, dtype=jnp.int32)[None, :] < lengths[:, None]).astype(
         jnp.bfloat16
     )
@@ -156,27 +168,49 @@
     )
     rows = jnp.concatenate((key_rows, value_rows), axis=2)
     rows = rows.reshape(img_count, mp_size, own_rows, 2 * key_cols).transpose(1, 0, 2, 3)
-    all_rows = jnp.stack([swap(rows, 2 * r) if r else rows for r in range(pairs)], axis=1)
-    all_rows = all_rows.reshape(-1, 2 * key_cols)
-    image_part = lax.dot_general(
-        all_rows, weight, (((1,), (1,)), ((), ())), preferred_element_type=jnp.float32
-    ).astype(jnp.bfloat16)
-    image_part = image_part.reshape(mp_size, pairs * img_count * own_rows, width)
-    image_sum = lax.psum_scatter(image_part, "mp", scatter_dimension=0, tiled=False)
+    all_rows = []
+    image_grad = jnp.zeros((img_count, own_rows, vis_width), jnp.bfloat16)
+    for r in range(pairs):
+        block_rows = (swap(rows, 2 * r) if r else rows).reshape(-1, 2 * key_cols)
+        all_rows.append(block_rows)
+        term = lax.dot_general(
+            block_rows, weight, (((1,), (1,)), ((), ())), preferred_element_type=jnp.float32
+        ).astype(jnp.bfloat16)
+        term = term.reshape(mp_size, img_count, own_rows, width)
+        total = term[0].astype(jnp.float32)
+        leftward = rightward = None
+        for k in range(half, 0, -1):
+            if k < half or r < pairs // 2:
+                own = term[k]
+                if leftward is not None:
+                    own = (own.astype(jnp.float32) + leftward.astype(jnp.float32)).astype(
+                        jnp.bfloat16
+                    )
+                leftward = ring(own, -1)
+            if k < half or r >= pairs // 2:
+                own = term[mp_size - k]
+                if rightward is not None:
+                    own = (own.astype(jnp.float32) + rightward.astype(jnp.float32)).astype(
+                        jnp.bfloat16
+                    )
+                rightward = ring(own, 1)
+        for arrived in (leftward, rightward):
+            if arrived is not None:
+                total = total + arrived.astype(jnp.float32)
+        piece = total.astype(jnp.bfloat16)
+        image_grad = lax.dynamic_update_slice_in_dim(
+            image_grad, swap(piece, 2 * r) if r else piece, (pair ^ r) * width, axis=2
+        )
     weight_part = lax.dot_general(
-        flat, all_rows, (((0,), (0,)), ((), ())), preferred_element_type=jnp.float32
+        jnp.stack(blocks).reshape(-1, width),
+        jnp.stack(all_rows).reshape(-1, 2 * key_cols),
+        (((0,), (0,)), ((), ())),
+        preferred_element_type=jnp.float32,
     )
     weight_grad = lax.dynamic_slice_in_dim(weight_part, core * own_width, own_width, axis=0)
     weight_grad = weight_grad + swap(
         lax.dynamic_slice_in_dim(weight_part, (1 - core) * own_width, own_width, axis=0), 1
     )
-    image_sum = image_sum.reshape(pairs, img_count, own_rows, width)
-    image_grad = jnp.zeros((img_count, own_rows, vis_width), jnp.bfloat16)
-    for r in range(pairs):
-        piece = swap(image_sum[r], 2 * r) if r else image_sum[r]
-        image_grad = lax.dynamic_update_slice_in_dim(
-            image_grad, piece, (pair ^ r) * width, axis=2
-        )
     return (query_grad, image_grad, weight_grad[:, :key_cols], weight_grad[:, key_cols:])
 
 
@@ -195,7 +229,7 @@
     )
 
     def body(*args):
-        return per_device(mesh.shape["dp"], *args)
+        return per_device(mesh.shape["dp"], mesh.shape["mp"], *args)
 
     return jax.shard_map(
         body,

time: 283 us -> 228 us (0.81)
  waiting for transfers between devices: 170 us -> 85.3 us
  starting transfers between devices: 15.4 us -> 57.5 us
  between operations: 14.5 us -> 1.44 us
  matrix products: 24 us -> 16 us
  other arithmetic: 17.3 us -> 24.3 us
    all_gather x1 -> x0, waiting for transfers between devices: 71.2 us -> none  [per_device(): features = lax.all_gather(mine, 'mp', axis=0)]
    ppermute x0 -> x24, waiting for transfers between devices: none -> 66.8 us  [ring(): lax.ppermute(value, 'mp', [(i, (i + step) % mp_size) for i in range(mp_si...]
    reduce_scatter x1 -> x0, waiting for transfers between devices: 56 us -> none  [per_device(): lax.psum_scatter(image_part, 'mp', scatter_dimension=0, tiled=False)]
    ppermute x0 -> x24, starting transfers between devices: none -> 41.5 us  [ring(): lax.ppermute(value, 'mp', [(i, (i + step) % mp_size) for i in range(mp_si...]
    ppermute x14, waiting for transfers between devices: 42.3 us -> 18.5 us  [swap(): return lax.ppermute(value, 'dp', [(i, i ^ mask) for i in range(dp_size)])]
    dot_general x3 -> x9, matrix products: 16.7 us -> 8.71 us  [the longest x4 3.41 us: per_device(): jnp.dot(blocks[r].reshape(-1, width), weight, preferred_element_type=jnp....]
    another operation x3 -> x6, other arithmetic: 2.17 us -> 7.18 us  [the longest x5 7.05 us: per_device(): jnp.stack(blocks).reshape(-1, width)]
    ppermute x0 -> x3, local copies, waits for them, and re-layouts: none -> 2.9 us  [swap(): return lax.ppermute(value, 'dp', [(i, i ^ mask) for i in range(dp_size)])]
  transfers between devices with their start and end apart: 16 -> 38, of which waited for: 11 -> 18; matrix products, arithmetic and copies ran while one was open for 7% -> 14% of each run, Pallas kernels for 0% -> 0%
where the time goes in v2:
time: 228 us; the launch traced here: 227 us
  waiting for transfers between devices  85.3 us (37%)
  starting transfers between devices  57.5 us (25%)
  local copies, waits for them, and re-layouts  42.1 us (18%)
  other arithmetic  24.3 us (11%)
  matrix products  16 us (7%)
    ppermute x24, waiting for transfers between devices, ring(): lax.ppermute(value, 'mp', [(i, (i + step) % mp_size) for i in range(mp_si...  66.8 us
    ppermute x24, starting transfers between devices, ring(): lax.ppermute(value, 'mp', [(i, (i + step) % mp_size) for i in range(mp_si...  41.5 us
    ppermute x14, waiting for transfers between devices, swap(): return lax.ppermute(value, 'dp', [(i, i ^ mask) for i in range(dp_size)])  18.5 us
    ppermute x14, starting transfers between devices, swap(): return lax.ppermute(value, 'dp', [(i, i ^ mask) for i in range(dp_size)])  16 us
    another operation x5, other arithmetic, per_device(): jnp.stack(blocks).reshape(-1, width)  7.05 us
    unnamed x61, local copies, waits for them, and re-layouts  6.61 us
    mul x4, local copies, waits for them, and re-layouts, rms_back(): source * (factor * factor * factor)  5.99 us
  transfers between devices with their start and end apart: 38, of which 18 were waited for; matrix products, arithmetic and copies ran while one was open for 14% of the time, Pallas kernels for 0%

profile of v2, /device:TPU:0, one launch (start us, length us, event | category | flops | bytes accessed | tf_op | source)
XLA Modules:
  0.0 226.7 jit_solution(826465446882255774)
XLA Ops:
  0.7 2.3 constant_dynamic-slice_fusion.3
  2.9 3.0 %collective-permute-start = (bf16[2,32,1920]{2,1,0:T(8,128)(2,1)S(1)}, bf16[2,32,1920]{2,1,0:T(8,128)(2,1)}, u32[]{:S(2)}, u32[]{:S(2)}) collective-permute-start(bf16[2,32,1920]{2,1,0:T(8,128)(2,1)S(1)} %get-tuple-element.55), channel_id=1, source_target_pairs={{0,1},{1,2},{2,3},{3,0},{4,5},{5,6},{6,7},{7,4},{8,9},{9,10},{10,1... | collective-permute-start | bytes 737288 | tf_op jit(solution)/shard_map/ppermute | solution.py:95
  6.0 2.0 collective-permute-start.2
  8.0 1.7 collective-permute-start.4
  17.2 1.6 collective-permute-start.1
  18.8 1.8 constant_dynamic-update-slice_fusion
  22.5 2.4 %collective-permute-start.7 = (bf16[2,32,1920]{2,1,0:T(8,128)(2,1)}, bf16[2,32,1920]{2,1,0:T(8,128)(2,1)S(1)}, u32[]{:S(2)}, u32[]{:S(2)}) collective-permute-start(bf16[2,32,1920]{2,1,0:T(8,128)(2,1)} %collective-permute-done.4), channel_id=1, source_target_pairs={{0,3},{1,0},{2,1},{3,2},{4,7},{5,4},{6,5},{7,6},{8,11},{9,8},{10,9... | collective-permute-start | bytes 737288 | tf_op jit(solution)/shard_map/ppermute | solution.py:95
  24.8 2.0 collective-permute-start.11
  26.8 1.6 collective-permute-done.5
  28.5 5.1 %collective-permute-done.1 = bf16[2,32,1920]{2,1,0:T(8,128)(2,1)} collective-permute-done((bf16[2,32,1920]{2,1,0:T(8,128)(2,1)}, bf16[2,32,1920]{2,1,0:T(8,128)(2,1)}, u32[]{:S(2)}, u32[]{:S(2)}) %collective-permute-start.1) | collective-permute-done | bytes 245792 | tf_op jit(solution)/shard_map/ppermute | solution.py:95
  36.4 10.9 %collective-permute-start.10 = (bf16[2,32,1920]{2,1,0:T(8,128)(2,1)}, bf16[2,32,1920]{2,1,0:T(8,128)(2,1)S(1)}, u32[]{:S(2)}, u32[]{:S(2)}) collective-permute-start(bf16[2,32,1920]{2,1,0:T(8,128)(2,1)} %collective-permute-done.9), channel_id=1, source_target_pairs={{0,1},{1,2},{2,3},{3,0},{4,5},{5,6},{6,7},{7,4},{8,9},{9,10},{10,1... | collective-permute-start | bytes 737288 | tf_op jit(solution)/shard_map/ppermute | solution.py:95
  47.3 1.8 collective-permute-start.15
  49.2 1.9 collective-permute-start.12
  51.1 3.5 %collective-permute-done.6 = bf16[2,32,1920]{2,1,0:T(8,128)(2,1)S(1)} collective-permute-done((bf16[2,32,1920]{2,1,0:T(8,128)(2,1)}, bf16[2,32,1920]{2,1,0:T(8,128)(2,1)S(1)}, u32[]{:S(2)}, u32[]{:S(2)}) %collective-permute-start.6) | collective-permute-done | bytes 245792 | tf_op jit(solution)/shard_map/ppermute | solution.py:95
  56.9 3.0 %collective-permute-done.10 = bf16[2,32,1920]{2,1,0:T(8,128)(2,1)S(1)} collective-permute-done((bf16[2,32,1920]{2,1,0:T(8,128)(2,1)}, bf16[2,32,1920]{2,1,0:T(8,128)(2,1)S(1)}, u32[]{:S(2)}, u32[]{:S(2)}) %collective-permute-start.10) | collective-permute-done | bytes 245792 | tf_op jit(solution)/shard_map/ppermute | solution.py:95
  59.9 8.1 %collective-permute-done.12 = bf16[2,32,1920]{2,1,0:T(8,128)(2,1)S(1)} collective-permute-done((bf16[2,32,1920]{2,1,0:T(8,128)(2,1)S(1)}, bf16[2,32,1920]{2,1,0:T(8,128)(2,1)S(1)}, u32[]{:S(2)}, u32[]{:S(2)}) %collective-permute-start.12) | collective-permute-done | bytes 245792 | tf_op jit(solution)/shard_map/ppermute | solution.py:95
  69.2 4.0 %collective-permute-done.17 = bf16[2,32,1920]{2,1,0:T(8,128)(2,1)S(1)} collective-permute-done((bf16[2,32,1920]{2,1,0:T(8,128)(2,1)S(1)}, bf16[2,32,1920]{2,1,0:T(8,128)(2,1)S(1)}, u32[]{:S(2)}, u32[]{:S(2)}) %collective-permute-start.17) | collective-permute-done | bytes 245792 | tf_op jit(solution)/shard_map/ppermute | solution.py:95
  77.5 1.6 collective-permute-start.13
  80.4 2.2 pad_maximum_fusion
  82.6 1.8 collective-permute-done.8
  84.4 6.7 %collective-permute-done.13 = bf16[256,512]{1,0:T(8,128)(2,1)S(1)} collective-permute-done((bf16[256,512]{1,0:T(8,128)(2,1)S(1)}, bf16[256,512]{1,0:T(8,128)(2,1)S(1)}, u32[]{:S(2)}, u32[]{:S(2)}) %collective-permute-start.13) | collective-permute-done | bytes 262176 | tf_op jit(solution)/shard_map/ppermute | solution.py:84
  97.6 2.0 fusion.44
  100.8 1.8 copy.121
  102.6 2.4 %copy.129 = bf16[2,2,8,128,128]{4,2,3,1,0:T(8,128)(2,1)} copy(bf16[2,2,8,128,128]{3,4,2,1,0:T(8,128)(2,1)} %get-tuple-element.26) | data formatting | bytes 2097152 | tf_op jit(solution)/shard_map/convert_element_type | solution.py:35
  105.0 2.7 %convolution_bitcast_fusion = f32[2,128,2,128]{1,3,2,0:T(8,128)} fusion(bf16[2,2,8,128,128]{4,2,3,1,0:T(8,128)(2,1)} %copy.129, bf16[2,128,2,8,128]{4,3,2,1,0:T(8,128)(2,1)} %bitcast.166), kind=kOutput, calls=%fused_computation.30 | convolution fusion | flops 134217728 | bytes 2359296 | tf_op jit(solution)/shard_map/bgjtr,btgjd->brgd/dot_general | solution.py:36
  107.8 1.8 copy.130
  109.6 1.9 multiply_reduce_fusion.2
  113.6 1.8 copy.122
  118.4 1.8 copy.123
  121.6 1.9 mul.325
  123.5 1.8 mul.326
  126.8 1.8 copy.124
  128.6 1.7 copy.131
  130.3 1.6 convert_element_type.222
  139.7 2.0 collective-permute-start.21
  144.3 5.0 %collective-permute-done.19 = bf16[2,32,1920]{2,1,0:T(8,128)(2,1)} collective-permute-done((bf16[2,32,1920]{2,1,0:T(8,128)(2,1)}, bf16[2,32,1920]{2,1,0:T(8,128)(2,1)}, u32[]{:S(2)}, u32[]{:S(2)}) %collective-permute-start.19) | collective-permute-done | bytes 245792 | tf_op jit(solution)/shard_map/ppermute | solution.py:95
  154.8 2.3 fusion.50
  160.3 3.0 %collective-permute-start.33 = (bf16[2,32,1920]{2,1,0:T(8,128)(2,1)S(1)}, bf16[2,32,1920]{2,1,0:T(8,128)(2,1)S(1)}, u32[]{:S(2)}, u32[]{:S(2)}) collective-permute-start(bf16[2,32,1920]{2,1,0:T(8,128)(2,1)S(1)} %bitcast.195), channel_id=1, source_target_pairs={{0,3},{1,0},{2,1},{3,2},{4,7},{5,4},{6,5},{7,6},{8,11},{9,8},{10,9... | collective-permute-start | bytes 737288 | tf_op jit(solution)/shard_map/ppermute | solution.py:95
  165.1 3.8 %collective-permute-start.28 = (bf16[2,32,1920]{2,1,0:T(8,128)(2,1)S(1)}, bf16[2,32,1920]{2,1,0:T(8,128)(2,1)S(1)}, u32[]{:S(2)}, u32[]{:S(2)}) collective-permute-start(bf16[2,32,1920]{2,1,0:T(8,128)(2,1)S(1)} %bitcast.198), channel_id=1, source_target_pairs={{0,3},{1,0},{2,1},{3,2},{4,7},{5,4},{6,5},{7,6},{8,11},{9,8},{10,9... | collective-permute-start | bytes 737288 | tf_op jit(solution)/shard_map/ppermute | solution.py:95
  170.2 10.5 %collective-permute-done.29 = bf16[2,32,1920]{2,1,0:T(8,128)(2,1)S(1)} collective-permute-done((bf16[2,32,1920]{2,1,0:T(8,128)(2,1)S(1)}, bf16[2,32,1920]{2,1,0:T(8,128)(2,1)S(1)}, u32[]{:S(2)}, u32[]{:S(2)}) %collective-permute-start.29) | collective-permute-done | bytes 245792 | tf_op jit(solution)/shard_map/ppermute | solution.py:95
  180.8 7.8 %collective-permute-done.23 = bf16[2,32,1920]{2,1,0:T(8,128)(2,1)S(1)} collective-permute-done((bf16[2,32,1920]{2,1,0:T(8,128)(2,1)S(1)}, bf16[2,32,1920]{2,1,0:T(8,128)(2,1)S(1)}, u32[]{:S(2)}, u32[]{:S(2)}) %collective-permute-start.23) | collective-permute-done | bytes 245792 | tf_op jit(solution)/shard_map/ppermute | solution.py:95
  189.3 3.3 %collective-permute-start.35 = (bf16[2,32,1920]{2,1,0:T(8,128)(2,1)S(1)}, bf16[2,32,1920]{2,1,0:T(8,128)(2,1)S(1)}, u32[]{:S(2)}, u32[]{:S(2)}) collective-permute-start(bf16[2,32,1920]{2,1,0:T(8,128)(2,1)S(1)} %fusion.17), channel_id=1, source_target_pairs={{0,1},{1,2},{2,3},{3,0},{4,5},{5,6},{6,7},{7,4},{8,9},{9,10},{10,1... | collective-permute-start | bytes 737288 | tf_op jit(solution)/shard_map/ppermute | solution.py:95
  192.5 9.5 %collective-permute-done.30 = bf16[2,32,1920]{2,1,0:T(8,128)(2,1)S(1)} collective-permute-done((bf16[2,32,1920]{2,1,0:T(8,128)(2,1)S(1)}, bf16[2,32,1920]{2,1,0:T(8,128)(2,1)S(1)}, u32[]{:S(2)}, u32[]{:S(2)}) %collective-permute-start.30) | collective-permute-done | bytes 245792 | tf_op jit(solution)/shard_map/ppermute | solution.py:95
  202.1 1.8 collective-permute-start.31
  203.9 6.8 %collective-permute-done.24 = bf16[2,32,1920]{2,1,0:T(8,128)(2,1)S(1)} collective-permute-done((bf16[2,32,1920]{2,1,0:T(8,128)(2,1)S(1)}, bf16[2,32,1920]{2,1,0:T(8,128)(2,1)S(1)}, u32[]{:S(2)}, u32[]{:S(2)}) %collective-permute-start.24) | collective-permute-done | bytes 245792 | tf_op jit(solution)/shard_map/ppermute | solution.py:95
  212.0 2.3 %collective-permute-start.36 = (bf16[2,32,1920]{2,1,0:T(8,128)(2,1)S(1)}, bf16[2,32,1920]{2,1,0:T(8,128)(2,1)S(1)}, u32[]{:S(2)}, u32[]{:S(2)}) collective-permute-start(bf16[2,32,1920]{2,1,0:T(8,128)(2,1)S(1)} %fusion.19), channel_id=1, source_target_pairs={{0,24},{4,28},{8,16},{12,20},{16,8},{20,12},{24,0},{28,4},{1,25},{... | collective-permute-start | bytes 737288 | tf_op jit(solution)/shard_map/ppermute | solution.py:84
  214.2 5.5 %collective-permute-done.26 = bf16[2,32,1920]{2,1,0:T(8,128)(2,1)S(1)} collective-permute-done((bf16[2,32,1920]{2,1,0:T(8,128)(2,1)S(1)}, bf16[2,32,1920]{2,1,0:T(8,128)(2,1)S(1)}, u32[]{:S(2)}, u32[]{:S(2)}) %collective-permute-start.26) | collective-permute-done | bytes 245792 | tf_op jit(solution)/shard_map/ppermute | solution.py:84
  219.9 4.5 %collective-permute-done.36 = bf16[2,32,1920]{2,1,0:T(8,128)(2,1)S(1)} collective-permute-done((bf16[2,32,1920]{2,1,0:T(8,128)(2,1)S(1)}, bf16[2,32,1920]{2,1,0:T(8,128)(2,1)S(1)}, u32[]{:S(2)}, u32[]{:S(2)}) %collective-permute-start.36) | collective-permute-done | bytes 245792 | tf_op jit(solution)/shard_map/ppermute | solution.py:84
  (184 shorter events, 63.0 us)
Async XLA Ops:
  0.6 10.9 %copy-start.3 = (bf16[2,128,2048]{2,1,0:T(8,128)(2,1)S(1)}, bf16[2,128,2048]{2,1,0:T(8,128)(2,1)}, u32[]{:S(2)}) copy-start(bf16[2,128,2048]{2,1,0:T(8,128)(2,1)} %param.10) | copy-start | bytes 3145732
  2.9 14.3 %collective-permute-start = (bf16[2,32,1920]{2,1,0:T(8,128)(2,1)S(1)}, bf16[2,32,1920]{2,1,0:T(8,128)(2,1)}, u32[]{:S(2)}, u32[]{:S(2)}) collective-permute-start(bf16[2,32,1920]{2,1,0:T(8,128)(2,1)S(1)} %get-tuple-element.55), channel_id=1, source_target_pairs={{0,1},{1,2},{2,3},{3,0},{4,5},{5,6},{6,7},{7,4},{8,9},{9,10},{10,1... | collective-permute-start | bytes 737288 | tf_op jit(solution)/shard_map/ppermute | solution.py:95
  6.0 18.9 %collective-permute-start.2 = (bf16[2,32,1920]{2,1,0:T(8,128)(2,1)S(1)}, bf16[2,32,1920]{2,1,0:T(8,128)(2,1)}, u32[]{:S(2)}, u32[]{:S(2)}) collective-permute-start(bf16[2,32,1920]{2,1,0:T(8,128)(2,1)S(1)} %get-tuple-element.55), channel_id=1, source_target_pairs={{0,3},{1,0},{2,1},{3,2},{4,7},{5,4},{6,5},{7,6},{8,11},{9,8},{10,9... | collective-permute-start | bytes 737288 | tf_op jit(solution)/shard_map/ppermute | solution.py:95
  8.0 9.2 %collective-permute-start.4 = (bf16[2,32,1920]{2,1,0:T(8,128)(2,1)}, bf16[2,32,1920]{2,1,0:T(8,128)(2,1)}, u32[]{:S(2)}, u32[]{:S(2)}) collective-permute-start(bf16[2,32,1920]{2,1,0:T(8,128)(2,1)} %get-tuple-element.54), channel_id=1, source_target_pairs={{0,8},{4,12},{8,0},{12,4},{16,24},{20,28},{24,16},{28,20},{1,9},{5... | collective-permute-start | bytes 737288 | tf_op jit(solution)/shard_map/ppermute | solution.py:84
  9.7 12.8 %collective-permute-start.9 = (bf16[2,32,1920]{2,1,0:T(8,128)(2,1)}, bf16[2,32,1920]{2,1,0:T(8,128)(2,1)}, u32[]{:S(2)}, u32[]{:S(2)}) collective-permute-start(bf16[2,32,1920]{2,1,0:T(8,128)(2,1)} %get-tuple-element.57), channel_id=1, source_target_pairs={{0,16},{4,20},{8,24},{12,28},{16,0},{20,4},{24,8},{28,12},{1,17},{... | collective-permute-start | bytes 737288 | tf_op jit(solution)/shard_map/ppermute | solution.py:84
  11.2 11.2 %collective-permute-start.14 = (bf16[2,32,1920]{2,1,0:T(8,128)(2,1)}, bf16[2,32,1920]{2,1,0:T(8,128)(2,1)}, u32[]{:S(2)}, u32[]{:S(2)}) collective-permute-start(bf16[2,32,1920]{2,1,0:T(8,128)(2,1)} %get-tuple-element.56), channel_id=1, source_target_pairs={{0,24},{4,28},{8,16},{12,20},{16,8},{20,12},{24,0},{28,4},{1,25},{... | collective-permute-start | bytes 737288 | tf_op jit(solution)/shard_map/ppermute | solution.py:84
  17.2 11.2 %collective-permute-start.5 = (bf16[2,32,1920]{2,1,0:T(8,128)(2,1)}, bf16[2,32,1920]{2,1,0:T(8,128)(2,1)}, u32[]{:S(2)}, u32[]{:S(2)}) collective-permute-start(bf16[2,32,1920]{2,1,0:T(8,128)(2,1)} %collective-permute-done.4), channel_id=1, source_target_pairs={{0,1},{1,2},{2,3},{3,0},{4,5},{5,6},{6,7},{7,4},{8,9},{9,10},{10,1... | collective-permute-start | bytes 737288 | tf_op jit(solution)/shard_map/ppermute | solution.py:95
  17.2 16.3 %collective-permute-start.1 = (bf16[2,32,1920]{2,1,0:T(8,128)(2,1)}, bf16[2,32,1920]{2,1,0:T(8,128)(2,1)}, u32[]{:S(2)}, u32[]{:S(2)}) collective-permute-start(bf16[2,32,1920]{2,1,0:T(8,128)(2,1)} %collective-permute-done), channel_id=1, source_target_pairs={{0,1},{1,2},{2,3},{3,0},{4,5},{5,6},{6,7},{7,4},{8,9},{9,10},{10,1... | collective-permute-start | bytes 737288 | tf_op jit(solution)/shard_map/ppermute | solution.py:95
  22.5 51.9 %collective-permute-start.3 = (bf16[960,512]{1,0:T(8,128)(2,1)}, bf16[960,512]{1,0:T(8,128)(2,1)S(1)}, u32[]{:S(2)}, u32[]{:S(2)}) collective-permute-start(bf16[960,512]{1,0:T(8,128)(2,1)} %constant_dynamic-update-slice_fusion), channel_id=1, source_target_pairs={{0,4},{4,0},{8,12},{12,8},{16,20},{20,16},{24,28},{28,24},{1,5},{5... | collective-permute-start | bytes 2949128 | tf_op jit(solution)/shard_map/ppermute | solution.py:84
  22.5 13.9 %collective-permute-start.7 = (bf16[2,32,1920]{2,1,0:T(8,128)(2,1)}, bf16[2,32,1920]{2,1,0:T(8,128)(2,1)S(1)}, u32[]{:S(2)}, u32[]{:S(2)}) collective-permute-start(bf16[2,32,1920]{2,1,0:T(8,128)(2,1)} %collective-permute-done.4), channel_id=1, source_target_pairs={{0,3},{1,0},{2,1},{3,2},{4,7},{5,4},{6,5},{7,6},{8,11},{9,8},{10,9... | collective-permute-start | bytes 737288 | tf_op jit(solution)/shard_map/ppermute | solution.py:95
  24.8 22.5 %collective-permute-start.11 = (bf16[2,32,1920]{2,1,0:T(8,128)(2,1)}, bf16[2,32,1920]{2,1,0:T(8,128)(2,1)S(1)}, u32[]{:S(2)}, u32[]{:S(2)}) collective-permute-start(bf16[2,32,1920]{2,1,0:T(8,128)(2,1)} %collective-permute-done.9), channel_id=1, source_target_pairs={{0,3},{1,0},{2,1},{3,2},{4,7},{5,4},{6,5},{7,6},{8,11},{9,8},{10,9... | collective-permute-start | bytes 737288 | tf_op jit(solution)/shard_map/ppermute | solution.py:95
  28.4 20.8 %collective-permute-start.16 = (bf16[2,32,1920]{2,1,0:T(8,128)(2,1)}, bf16[2,32,1920]{2,1,0:T(8,128)(2,1)S(1)}, u32[]{:S(2)}, u32[]{:S(2)}) collective-permute-start(bf16[2,32,1920]{2,1,0:T(8,128)(2,1)} %collective-permute-done.14), channel_id=1, source_target_pairs={{0,3},{1,0},{2,1},{3,2},{4,7},{5,4},{6,5},{7,6},{8,11},{9,8},{10,9... | collective-permute-start | bytes 737288 | tf_op jit(solution)/shard_map/ppermute | solution.py:95
  33.5 21.1 %collective-permute-start.6 = (bf16[2,32,1920]{2,1,0:T(8,128)(2,1)}, bf16[2,32,1920]{2,1,0:T(8,128)(2,1)S(1)}, u32[]{:S(2)}, u32[]{:S(2)}) collective-permute-start(bf16[2,32,1920]{2,1,0:T(8,128)(2,1)} %collective-permute-done.5), channel_id=1, source_target_pairs={{0,1},{1,2},{2,3},{3,0},{4,5},{5,6},{6,7},{7,4},{8,9},{9,10},{10,1... | collective-permute-start | bytes 737288 | tf_op jit(solution)/shard_map/ppermute | solution.py:95
  36.4 23.5 %collective-permute-start.10 = (bf16[2,32,1920]{2,1,0:T(8,128)(2,1)}, bf16[2,32,1920]{2,1,0:T(8,128)(2,1)S(1)}, u32[]{:S(2)}, u32[]{:S(2)}) collective-permute-start(bf16[2,32,1920]{2,1,0:T(8,128)(2,1)} %collective-permute-done.9), channel_id=1, source_target_pairs={{0,1},{1,2},{2,3},{3,0},{4,5},{5,6},{6,7},{7,4},{8,9},{9,10},{10,1... | collective-permute-start | bytes 737288 | tf_op jit(solution)/shard_map/ppermute | solution.py:95
  47.3 21.9 %collective-permute-start.15 = (bf16[2,32,1920]{2,1,0:T(8,128)(2,1)}, bf16[2,32,1920]{2,1,0:T(8,128)(2,1)S(1)}, u32[]{:S(2)}, u32[]{:S(2)}) collective-permute-start(bf16[2,32,1920]{2,1,0:T(8,128)(2,1)} %collective-permute-done.14), channel_id=1, source_target_pairs={{0,1},{1,2},{2,3},{3,0},{4,5},{5,6},{6,7},{7,4},{8,9},{9,10},{10,1... | collective-permute-start | bytes 737288 | tf_op jit(solution)/shard_map/ppermute | solution.py:95
  49.2 18.9 %collective-permute-start.12 = (bf16[2,32,1920]{2,1,0:T(8,128)(2,1)S(1)}, bf16[2,32,1920]{2,1,0:T(8,128)(2,1)S(1)}, u32[]{:S(2)}, u32[]{:S(2)}) collective-permute-start(bf16[2,32,1920]{2,1,0:T(8,128)(2,1)S(1)} %collective-permute-done.11), channel_id=1, source_target_pairs={{0,3},{1,0},{2,1},{3,2},{4,7},{5,4},{6,5},{7,6},{8,11},{9,8},{10,9... | collective-permute-start | bytes 737288 | tf_op jit(solution)/shard_map/ppermute | solution.py:95
  54.7 18.6 %collective-permute-start.17 = (bf16[2,32,1920]{2,1,0:T(8,128)(2,1)S(1)}, bf16[2,32,1920]{2,1,0:T(8,128)(2,1)S(1)}, u32[]{:S(2)}, u32[]{:S(2)}) collective-permute-start(bf16[2,32,1920]{2,1,0:T(8,128)(2,1)S(1)} %collective-permute-done.16), channel_id=1, source_target_pairs={{0,3},{1,0},{2,1},{3,2},{4,7},{5,4},{6,5},{7,6},{8,11},{9,8},{10,9... | collective-permute-start | bytes 737288 | tf_op jit(solution)/shard_map/ppermute | solution.py:95
  69.2 5.2 %copy-start.11 = (bf16[960,512]{1,0:T(8,128)(2,1)S(1)}, bf16[960,512]{1,0:T(8,128)(2,1)}, u32[]{:S(2)}) copy-start(bf16[960,512]{1,0:T(8,128)(2,1)} %constant_dynamic-update-slice_fusion) | copy-start | bytes 2949124
  74.4 16.7 %copy-start.22 = (bf16[960,512]{1,0:T(8,128)(2,1)}, bf16[960,512]{1,0:T(8,128)(2,1)S(1)}, u32[]{:S(2)}) copy-start(bf16[960,512]{1,0:T(8,128)(2,1)S(1)} %collective-permute-done.3) | copy-start | bytes 2949124
  75.2 9.2 %collective-permute-start.8 = (bf16[256,512]{1,0:T(8,128)(2,1)S(1)}, bf16[256,512]{1,0:T(8,128)(2,1)S(1)}, u32[]{:S(2)}, u32[]{:S(2)}) collective-permute-start(bf16[256,512]{1,0:T(8,128)(2,1)S(1)} %convolution_convert_fusion.6), channel_id=1, source_target_pairs={{0,8},{4,12},{8,0},{12,4},{16,24},{20,28},{24,16},{28,20},{1,9},{5... | collective-permute-start | bytes 786440 | tf_op jit(solution)/shard_map/ppermute | solution.py:84
  77.5 13.6 %collective-permute-start.13 = (bf16[256,512]{1,0:T(8,128)(2,1)S(1)}, bf16[256,512]{1,0:T(8,128)(2,1)S(1)}, u32[]{:S(2)}, u32[]{:S(2)}) collective-permute-start(bf16[256,512]{1,0:T(8,128)(2,1)S(1)} %convolution_convert_fusion.5), channel_id=1, source_target_pairs={{0,16},{4,20},{8,24},{12,28},{16,0},{20,4},{24,8},{28,12},{1,17},{... | collective-permute-start | bytes 786440 | tf_op jit(solution)/shard_map/ppermute | solution.py:84
  79.8 11.3 %collective-permute-start.18 = (bf16[256,512]{1,0:T(8,128)(2,1)S(1)}, bf16[256,512]{1,0:T(8,128)(2,1)S(1)}, u32[]{:S(2)}, u32[]{:S(2)}) collective-permute-start(bf16[256,512]{1,0:T(8,128)(2,1)S(1)} %convolution_convert_fusion.4), channel_id=1, source_target_pairs={{0,24},{4,28},{8,16},{12,20},{16,8},{20,12},{24,0},{28,4},{1,25},{... | collective-permute-start | bytes 786440 | tf_op jit(solution)/shard_map/ppermute | solution.py:84
  131.9 5.9 %copy-start.12 = (bf16[960,512]{1,0:T(8,128)(2,1)S(1)}, bf16[960,512]{1,0:T(8,128)(2,1)}, u32[]{:S(2)}) copy-start(bf16[960,512]{1,0:T(8,128)(2,1)} %constant_dynamic-update-slice_fusion) | copy-start | bytes 2949124
  131.9 5.9 %copy-start.23 = (bf16[960,512]{1,0:T(8,128)(2,1)S(1)}, bf16[960,512]{1,0:T(8,128)(2,1)}, u32[]{:S(2)}) copy-start(bf16[960,512]{1,0:T(8,128)(2,1)} %copy-done.22) | copy-start | bytes 2949124
  134.3 17.4 %collective-permute-start.22 = (bf16[4,2,32,512]{3,2,0,1:T(8,128)(2,1)S(1)}, bf16[4,2,32,512]{3,2,0,1:T(8,128)(2,1)}, u32[]{:S(2)}, u32[]{:S(2)}) collective-permute-start(bf16[4,2,32,512]{3,2,0,1:T(8,128)(2,1)S(1)} %maximum_bitcast_fusion), channel_id=1, source_target_pairs={{0,8},{4,12},{8,0},{12,4},{16,24},{20,28},{24,16},{28,20},{1,9},{5... | collective-permute-start | bytes 786440 | tf_op jit(solution)/shard_map/ppermute | solution.py:84
  134.9 17.8 %collective-permute-start.27 = (bf16[4,2,32,512]{3,2,0,1:T(8,128)(2,1)S(1)}, bf16[4,2,32,512]{3,2,0,1:T(8,128)(2,1)}, u32[]{:S(2)}, u32[]{:S(2)}) collective-permute-start(bf16[4,2,32,512]{3,2,0,1:T(8,128)(2,1)S(1)} %maximum_bitcast_fusion), channel_id=1, source_target_pairs={{0,16},{4,20},{8,24},{12,28},{16,0},{20,4},{24,8},{28,12},{1,17},{... | collective-permute-start | bytes 786440 | tf_op jit(solution)/shard_map/ppermute | solution.py:84
  136.4 17.2 %collective-permute-start.32 = (bf16[4,2,32,512]{3,2,0,1:T(8,128)(2,1)S(1)}, bf16[4,2,32,512]{3,2,0,1:T(8,128)(2,1)}, u32[]{:S(2)}, u32[]{:S(2)}) collective-permute-start(bf16[4,2,32,512]{3,2,0,1:T(8,128)(2,1)S(1)} %maximum_bitcast_fusion), channel_id=1, source_target_pairs={{0,24},{4,28},{8,16},{12,20},{16,8},{20,12},{24,0},{28,4},{1,25},{... | collective-permute-start | bytes 786440 | tf_op jit(solution)/shard_map/ppermute | solution.py:84
  137.9 3.9 %copy-start.17 = (f32[128]{0:T(128)S(1)}, f32[128]{0:T(128)}, u32[]{:S(2)}) copy-start(f32[128]{0:T(128)} %broadcast_multiply_fusion.3) | copy-start | bytes 1540
  139.7 9.6 %collective-permute-start.19 = (bf16[2,32,1920]{2,1,0:T(8,128)(2,1)}, bf16[2,32,1920]{2,1,0:T(8,128)(2,1)}, u32[]{:S(2)}, u32[]{:S(2)}) collective-permute-start(bf16[2,32,1920]{2,1,0:T(8,128)(2,1)} %bitcast.51), channel_id=1, source_target_pairs={{0,3},{1,0},{2,1},{3,2},{4,7},{5,4},{6,5},{7,6},{8,11},{9,8},{10,9... | collective-permute-start | bytes 737288 | tf_op jit(solution)/shard_map/ppermute | solution.py:95
  139.7 25.2 %collective-permute-start.21 = (bf16[2,32,1920]{2,1,0:T(8,128)(2,1)}, bf16[2,32,1920]{2,1,0:T(8,128)(2,1)}, u32[]{:S(2)}, u32[]{:S(2)}) collective-permute-start(bf16[2,32,1920]{2,1,0:T(8,128)(2,1)} %bitcast.52), channel_id=1, source_target_pairs={{0,1},{1,2},{2,3},{3,0},{4,5},{5,6},{6,7},{7,4},{8,9},{9,10},{10,1... | collective-permute-start | bytes 737288 | tf_op jit(solution)/shard_map/ppermute | solution.py:95
  142.9 6.4 %copy-start.9 = (bf16[64,1920]{1,0:T(8,128)(2,1)S(1)}, bf16[64,1920]{1,0:T(8,128)(2,1)}, u32[]{:S(2)}) copy-start(bf16[64,1920]{1,0:T(8,128)(2,1)} %get-tuple-element.53) | copy-start | bytes 737284
  143.0 11.7 %copy-start.6 = (bf16[4,2,32,512]{3,2,1,0:T(8,128)(2,1)S(1)}, bf16[4,2,32,512]{3,2,1,0:T(8,128)(2,1)}, u32[]{:S(2)}) copy-start(bf16[4,2,32,512]{3,2,1,0:T(8,128)(2,1)} %copy-done.5) | copy-start | bytes 786436
  149.3 5.5 %copy-start = (bf16[4,4,2,32,1920]{4,3,2,1,0:T(8,128)(2,1)S(1)}, bf16[4,4,2,32,1920]{4,3,2,1,0:T(8,128)(2,1)}, u32[]{:S(2)}) copy-start(bf16[4,4,2,32,1920]{4,3,2,1,0:T(8,128)(2,1)} %pad_maximum_fusion) | copy-start | bytes 11796484
  150.5 14.6 %collective-permute-start.20 = (bf16[2,32,1920]{2,1,0:T(8,128)(2,1)S(1)}, bf16[2,32,1920]{2,1,0:T(8,128)(2,1)S(1)}, u32[]{:S(2)}, u32[]{:S(2)}) collective-permute-start(bf16[2,32,1920]{2,1,0:T(8,128)(2,1)S(1)} %fusion.26), channel_id=1, source_target_pairs={{0,3},{1,0},{2,1},{3,2},{4,7},{5,4},{6,5},{7,6},{8,11},{9,8},{10,9... | collective-permute-start | bytes 737288 | tf_op jit(solution)/shard_map/ppermute | solution.py:95
  157.3 67.1 %collective-permute-start.37 = (f32[960,512]{1,0:T(8,128)S(1)}, f32[960,512]{1,0:T(8,128)S(1)}, u32[]{:S(2)}, u32[]{:S(2)}) collective-permute-start(f32[960,512]{1,0:T(8,128)S(1)} %constant_dynamic-slice_fusion), channel_id=1, source_target_pairs={{0,4},{4,0},{8,12},{12,8},{16,20},{20,16},{24,28},{28,24},{1,5},{5... | collective-permute-start | bytes 5898248 | tf_op jit(solution)/shard_map/ppermute | solution.py:84
  159.4 10.7 %collective-permute-start.34 = (bf16[2,32,1920]{2,1,0:T(8,128)(2,1)S(1)}, bf16[2,32,1920]{2,1,0:T(8,128)(2,1)S(1)}, u32[]{:S(2)}, u32[]{:S(2)}) collective-permute-start(bf16[2,32,1920]{2,1,0:T(8,128)(2,1)S(1)} %bitcast.201), channel_id=1, source_target_pairs={{0,1},{1,2},{2,3},{3,0},{4,5},{5,6},{6,7},{7,4},{8,9},{9,10},{10,1... | collective-permute-start | bytes 737288 | tf_op jit(solution)/shard_map/ppermute | solution.py:95
  160.3 51.6 %collective-permute-start.33 = (bf16[2,32,1920]{2,1,0:T(8,128)(2,1)S(1)}, bf16[2,32,1920]{2,1,0:T(8,128)(2,1)S(1)}, u32[]{:S(2)}, u32[]{:S(2)}) collective-permute-start(bf16[2,32,1920]{2,1,0:T(8,128)(2,1)S(1)} %bitcast.195), channel_id=1, source_target_pairs={{0,3},{1,0},{2,1},{3,2},{4,7},{5,4},{6,5},{7,6},{8,11},{9,8},{10,9... | collective-permute-start | bytes 737288 | tf_op jit(solution)/shard_map/ppermute | solution.py:95
  164.9 4.1 %copy-start.8 = (bf16[64,1920]{1,0:T(8,128)(2,1)S(1)}, bf16[64,1920]{1,0:T(8,128)(2,1)}, u32[]{:S(2)}) copy-start(bf16[64,1920]{1,0:T(8,128)(2,1)} %get-tuple-element.50) | copy-start | bytes 737284
  165.0 15.7 %collective-permute-start.29 = (bf16[2,32,1920]{2,1,0:T(8,128)(2,1)S(1)}, bf16[2,32,1920]{2,1,0:T(8,128)(2,1)S(1)}, u32[]{:S(2)}, u32[]{:S(2)}) collective-permute-start(bf16[2,32,1920]{2,1,0:T(8,128)(2,1)S(1)} %bitcast.202), channel_id=1, source_target_pairs={{0,1},{1,2},{2,3},{3,0},{4,5},{5,6},{6,7},{7,4},{8,9},{9,10},{10,1... | collective-permute-start | bytes 737288 | tf_op jit(solution)/shard_map/ppermute | solution.py:95
  165.1 24.2 %collective-permute-start.28 = (bf16[2,32,1920]{2,1,0:T(8,128)(2,1)S(1)}, bf16[2,32,1920]{2,1,0:T(8,128)(2,1)S(1)}, u32[]{:S(2)}, u32[]{:S(2)}) collective-permute-start(bf16[2,32,1920]{2,1,0:T(8,128)(2,1)S(1)} %bitcast.198), channel_id=1, source_target_pairs={{0,3},{1,0},{2,1},{3,2},{4,7},{5,4},{6,5},{7,6},{8,11},{9,8},{10,9... | collective-permute-start | bytes 737288 | tf_op jit(solution)/shard_map/ppermute | solution.py:95
  170.2 18.4 %collective-permute-start.23 = (bf16[2,32,1920]{2,1,0:T(8,128)(2,1)S(1)}, bf16[2,32,1920]{2,1,0:T(8,128)(2,1)S(1)}, u32[]{:S(2)}, u32[]{:S(2)}) collective-permute-start(bf16[2,32,1920]{2,1,0:T(8,128)(2,1)S(1)} %bitcast.203), channel_id=1, source_target_pairs={{0,3},{1,0},{2,1},{3,2},{4,7},{5,4},{6,5},{7,6},{8,11},{9,8},{10,9... | collective-permute-start | bytes 737288 | tf_op jit(solution)/shard_map/ppermute | solution.py:95
  180.7 21.4 %collective-permute-start.25 = (bf16[2,32,1920]{2,1,0:T(8,128)(2,1)S(1)}, bf16[2,32,1920]{2,1,0:T(8,128)(2,1)S(1)}, u32[]{:S(2)}, u32[]{:S(2)}) collective-permute-start(bf16[2,32,1920]{2,1,0:T(8,128)(2,1)S(1)} %bitcast.196), channel_id=1, source_target_pairs={{0,1},{1,2},{2,3},{3,0},{4,5},{5,6},{6,7},{7,4},{8,9},{9,10},{10,1... | collective-permute-start | bytes 737288 | tf_op jit(solution)/shard_map/ppermute | solution.py:95
  188.6 13.4 %collective-permute-start.30 = (bf16[2,32,1920]{2,1,0:T(8,128)(2,1)S(1)}, bf16[2,32,1920]{2,1,0:T(8,128)(2,1)S(1)}, u32[]{:S(2)}, u32[]{:S(2)}) collective-permute-start(bf16[2,32,1920]{2,1,0:T(8,128)(2,1)S(1)} %fusion.20), channel_id=1, source_target_pairs={{0,1},{1,2},{2,3},{3,0},{4,5},{5,6},{6,7},{7,4},{8,9},{9,10},{10,1... | collective-permute-start | bytes 737288 | tf_op jit(solution)/shard_map/ppermute | solution.py:95
  189.3 22.6 %collective-permute-start.35 = (bf16[2,32,1920]{2,1,0:T(8,128)(2,1)S(1)}, bf16[2,32,1920]{2,1,0:T(8,128)(2,1)S(1)}, u32[]{:S(2)}, u32[]{:S(2)}) collective-permute-start(bf16[2,32,1920]{2,1,0:T(8,128)(2,1)S(1)} %fusion.17), channel_id=1, source_target_pairs={{0,1},{1,2},{2,3},{3,0},{4,5},{5,6},{6,7},{7,4},{8,9},{9,10},{10,1... | collective-permute-start | bytes 737288 | tf_op jit(solution)/shard_map/ppermute | solution.py:95
  202.0 8.7 %collective-permute-start.24 = (bf16[2,32,1920]{2,1,0:T(8,128)(2,1)S(1)}, bf16[2,32,1920]{2,1,0:T(8,128)(2,1)S(1)}, u32[]{:S(2)}, u32[]{:S(2)}) collective-permute-start(bf16[2,32,1920]{2,1,0:T(8,128)(2,1)S(1)} %fusion.23), channel_id=1, source_target_pairs={{0,3},{1,0},{2,1},{3,2},{4,7},{5,4},{6,5},{7,6},{8,11},{9,8},{10,9... | collective-permute-start | bytes 737288 | tf_op jit(solution)/shard_map/ppermute | solution.py:95
  202.1 17.7 %collective-permute-start.31 = (bf16[2,32,1920]{2,1,0:T(8,128)(2,1)S(1)}, bf16[2,32,1920]{2,1,0:T(8,128)(2,1)S(1)}, u32[]{:S(2)}, u32[]{:S(2)}) collective-permute-start(bf16[2,32,1920]{2,1,0:T(8,128)(2,1)S(1)} %fusion.22), channel_id=1, source_target_pairs={{0,16},{4,20},{8,24},{12,28},{16,0},{20,4},{24,8},{28,12},{1,17},{... | collective-permute-start | bytes 737288 | tf_op jit(solution)/shard_map/ppermute | solution.py:84
  210.8 9.0 %collective-permute-start.26 = (bf16[2,32,1920]{2,1,0:T(8,128)(2,1)S(1)}, bf16[2,32,1920]{2,1,0:T(8,128)(2,1)S(1)}, u32[]{:S(2)}, u32[]{:S(2)}) collective-permute-start(bf16[2,32,1920]{2,1,0:T(8,128)(2,1)S(1)} %fusion.25), channel_id=1, source_target_pairs={{0,8},{4,12},{8,0},{12,4},{16,24},{20,28},{24,16},{28,20},{1,9},{5... | collective-permute-start | bytes 737288 | tf_op jit(solution)/shard_map/ppermute | solution.py:84
  212.0 12.4 %collective-permute-start.36 = (bf16[2,32,1920]{2,1,0:T(8,128)(2,1)S(1)}, bf16[2,32,1920]{2,1,0:T(8,128)(2,1)S(1)}, u32[]{:S(2)}, u32[]{:S(2)}) collective-permute-start(bf16[2,32,1920]{2,1,0:T(8,128)(2,1)S(1)} %fusion.19), channel_id=1, source_target_pairs={{0,24},{4,28},{8,16},{12,20},{16,8},{20,12},{24,0},{28,4},{1,25},{... | collective-permute-start | bytes 737288 | tf_op jit(solution)/shard_map/ppermute | solution.py:84
  (19 other events, 31.4 us)

commit v3 on v2

v3 whole, which is shorter than its diff:
```python
import functools
import math

import jax
import jax.numpy as jnp
from jax import lax
from jax.experimental import pallas as pl
from jax.experimental.pallas import tpu as pltpu
from jax.sharding import PartitionSpec as P

TILE_ROWS = 32


EPSILON = 1e-05


def rms_scale(source):
    return lax.rsqrt(jnp.mean(source * source, axis=-1, keepdims=True) + EPSILON)


def rms_back(source, factor, gain_vector, upstream):
    weighted = gain_vector * upstream
    return factor * weighted - source * (factor * factor * factor) * jnp.mean(
        source * weighted, axis=-1, keepdims=True
    )


def dot(left, right, left_dim, right_dim):
    return lax.dot_general(
        left,
        right,
        (((left_dim,), (right_dim,)), ((), ())),
        preferred_element_type=jnp.float32,
    )


def before_kernel(lengths, query, grad, gain, normed, masked):
    text_len, columns = query.shape[1:]
    head_dim = gain.shape[1]
    live = lax.broadcasted_iota(jnp.int32, (text_len, head_dim), 0) < lengths[pl.program_id(0)]
    for j in range(columns // head_dim):
        head = pl.ds(j * head_dim, head_dim)
        rows = pl.ds(j * text_len, text_len)
        source = query[0, :, head].astype(jnp.float32)
        normed[0, 0, rows, :] = (source * rms_scale(source) * gain[...]).astype(jnp.bfloat16)
        upstream = grad[0, :, head]
        masked[0, 0, rows, :] = jnp.where(live, upstream, jnp.zeros_like(upstream))


def before(queries, out_grad, gain, lengths, groups):
    seq_count, text_len, columns = queries.shape
    head_dim = gain.shape[1]
    span = columns // groups
    stacked = span // head_dim * text_len
    source = pl.BlockSpec((1, text_len, span), lambda b, g, *_: (b, 0, g))
    target = pl.BlockSpec((1, 1, stacked, head_dim), lambda b, g, *_: (b, g, 0, 0))
    shape = jax.ShapeDtypeStruct((seq_count, groups, stacked, head_dim), jnp.bfloat16)
    return pl.pallas_call(
        before_kernel,
        out_shape=(shape, shape),
        grid_spec=pltpu.PrefetchScalarGridSpec(
            num_scalar_prefetch=1,
            grid=(seq_count, groups),
            in_specs=[source, source, pl.BlockSpec((1, head_dim), lambda *_: (0, 0))],
            out_specs=(target, target),
        ),
        name="before",
    )(lengths, queries, out_grad, gain)


def attend_kernel(count, assignment, tiles, owners, *refs):
    key_parts, value_parts = refs[:count], refs[count : 2 * count]
    normed, masked, gain = refs[2 * count : 2 * count + 3]
    key_out, value_out, score_out, picked = refs[2 * count + 3 : 2 * count + 7]
    key_pre, key_normed, values, key_sum, value_sum = refs[2 * count + 7 :]
    parts, img_count, own_rows, head_dim = key_parts[0].shape
    img_rows = parts * own_rows
    step = pl.program_id(1)
    inv_root = 1.0 / math.sqrt(head_dim)

    @pl.when(step == 0)
    def _():
        for i in range(img_count):
            for target, sources in ((0, key_parts), (1, value_parts)):
                total = sources[0][:, i].astype(jnp.float32)
                for source in sources[1:]:
                    total = total + source[:, i].astype(jnp.float32)
                total = total.reshape(img_rows, head_dim)
                if target == 0:
                    key_pre[i] = total
                    key_normed[i] = (total * rms_scale(total) * gain[...]).astype(jnp.bfloat16)
                else:
                    values[i] = total.astype(jnp.bfloat16)
        key_sum[...] = jnp.zeros_like(key_sum)
        value_sum[...] = jnp.zeros_like(value_sum)

    image = assignment[step]
    keys = key_normed[image]
    picked[0, 0] = keys
    column = lax.broadcasted_iota(jnp.int32, (1, img_rows), 1)
    place = jnp.zeros_like(column)
    for k in range(parts):
        inside = (column >= k * own_rows) & (column < (k + 1) * own_rows)
        place = jnp.where(inside, column + (owners[k] - k) * own_rows, place)
    live = (place < tiles[image] * TILE_ROWS).astype(jnp.float32)
    queries = normed[0, 0]
    upstream = masked[0, 0]
    raised = jnp.exp(dot(queries, keys, 1, 1) * inv_root) * live
    prob = raised * (1.0 / jnp.sum(raised, axis=-1, keepdims=True))
    prob_grad = dot(upstream, values[image], 1, 1)
    inner = jnp.sum(prob * prob_grad, axis=-1, keepdims=True)
    score_grad = (prob * (prob_grad - inner)).astype(jnp.bfloat16)
    score_out[0, 0] = score_grad
    value_sum[image] += dot(prob.astype(jnp.bfloat16), upstream, 0, 0)
    key_sum[image] += dot(score_grad, queries, 0, 0) * inv_root

    @pl.when(step == pl.num_programs(1) - 1)
    def _():
        for i in range(img_count):
            source = key_pre[i]
            key_rows = rms_back(source, rms_scale(source), gain[...], key_sum[i])
            shape = (parts, own_rows, head_dim)
            key_out[:, i] = key_rows.astype(jnp.bfloat16).reshape(shape)
            value_out[:, i] = value_sum[i].astype(jnp.bfloat16).reshape(shape)


def attend(pieces, normed, masked, gain, assignment, tiles, owners):
    seq_count, groups, stacked, head_dim = normed.shape
    parts, img_count, own_rows, columns = pieces[0].shape
    img_rows = parts * own_rows
    count = len(pieces)
    part = (parts, img_count, own_rows, head_dim)
    keys = pl.BlockSpec(part, lambda g, b, *_: (0, 0, 0, g))
    values = pl.BlockSpec(part, lambda g, b, *_: (0, 0, 0, groups + g))
    stack = pl.BlockSpec((1, 1, stacked, head_dim), lambda g, b, *_: (b, g, 0, 0))
    rows = jax.ShapeDtypeStruct((parts, img_count, own_rows, columns // 2), jnp.bfloat16)
    return pl.pallas_call(
        functools.partial(attend_kernel, count),
        out_shape=(
            rows,
            rows,
            jax.ShapeDtypeStruct((seq_count, groups, stacked, img_rows), jnp.bfloat16),
            jax.ShapeDtypeStruct((seq_count, groups, img_rows, head_dim), jnp.bfloat16),
        ),
        grid_spec=pltpu.PrefetchScalarGridSpec(
            num_scalar_prefetch=3,
            grid=(groups, seq_count),
            in_specs=[keys] * count
            + [values] * count
            + [stack, stack, pl.BlockSpec((1, head_dim), lambda *_: (0, 0))],
            out_specs=(
                keys,
                keys,
                pl.BlockSpec((1, 1, stacked, img_rows), lambda g, b, *_: (b, g, 0, 0)),
                pl.BlockSpec((1, 1, img_rows, head_dim), lambda g, b, *_: (b, g, 0, 0)),
            ),
            scratch_shapes=[
                pltpu.VMEM((img_count, img_rows, head_dim), jnp.float32),
                pltpu.VMEM((img_count, img_rows, head_dim), jnp.bfloat16),
                pltpu.VMEM((img_count, img_rows, head_dim), jnp.bfloat16),
                pltpu.VMEM((img_count, img_rows, head_dim), jnp.float32),
                pltpu.VMEM((img_count, img_rows, head_dim), jnp.float32),
            ],
        ),
        compiler_params=pltpu.CompilerParams(vmem_limit_bytes=32 * 1024 * 1024),
        name="attend",
    )(assignment, tiles, owners, *pieces, *pieces, normed, masked, gain)


def after_kernel(query, score_grad, keys, gain, target):
    text_len, columns = query.shape[1:]
    head_dim = gain.shape[1]
    inv_root = 1.0 / math.sqrt(head_dim)
    for j in range(columns // head_dim):
        head = pl.ds(j * head_dim, head_dim)
        source = query[0, :, head].astype(jnp.float32)
        part = dot(score_grad[0, 0, pl.ds(j * text_len, text_len), :], keys[0, 0], 1, 0)
        grad = rms_back(source, rms_scale(source), gain[...], part * inv_root)
        target[0, :, head] = grad.astype(jnp.bfloat16)


def after(queries, score_grad, keys, gain):
    seq_count, text_len, columns = queries.shape
    groups, stacked, img_rows = score_grad.shape[1:]
    head_dim = gain.shape[1]
    source = pl.BlockSpec((1, text_len, columns // groups), lambda b, g: (b, 0, g))
    return pl.pallas_call(
        after_kernel,
        out_shape=jax.ShapeDtypeStruct(queries.shape, jnp.bfloat16),
        grid=(seq_count, groups),
        in_specs=[
            source,
            pl.BlockSpec((1, 1, stacked, img_rows), lambda b, g: (b, g, 0, 0)),
            pl.BlockSpec((1, 1, img_rows, head_dim), lambda b, g: (b, g, 0, 0)),
            pl.BlockSpec((1, head_dim), lambda *_: (0, 0)),
        ],
        out_specs=source,
        name="after",
    )(queries, score_grad, keys, gain)


def per_device(
    dp_size,
    mp_size,
    queries,
    out_grad,
    images,
    key_weight,
    value_weight,
    query_gain,
    key_gain,
    assignment,
    tile_counts,
    lengths,
):
    img_count, own_rows, vis_width = images.shape
    head_dim = query_gain.shape[0]
    own_width, key_cols = key_weight.shape
    key_heads = key_cols // head_dim
    pairs = dp_size // 2
    width = 2 * own_width
    place = lax.axis_index("dp")
    pair, core = place // 2, place % 2

    def swap(value, mask):
        return lax.ppermute(value, "dp", [(i, i ^ mask) for i in range(dp_size)])

    own_weight = jnp.concatenate((key_weight, value_weight), axis=1)
    mate_weight = swap(own_weight, 1)
    weight = jnp.where(
        core == 0,
        jnp.concatenate((own_weight, mate_weight), axis=0),
        jnp.concatenate((mate_weight, own_weight), axis=0),
    )

    def ring(value, step):
        return lax.ppermute(value, "mp", [(i, (i + step) % mp_size) for i in range(mp_size)])

    half = mp_size // 2
    blocks = []
    for r in range(pairs):
        piece = lax.dynamic_slice_in_dim(images, (pair ^ r) * width, width, axis=2)
        piece = swap(piece, 2 * r) if r else piece
        parts = [piece] + [None] * (mp_size - 1)
        right = left = piece
        for k in range(1, half + 1):
            if k < half or r < pairs // 2:
                parts[k] = right = ring(right, 1)
            if k < half or r >= pairs // 2:
                parts[mp_size - k] = left = ring(left, -1)
        blocks.append(jnp.stack(parts))
    img_rows = mp_size * own_rows
    pieces = []
    for r in range(pairs):
        piece = jnp.dot(
            blocks[r].reshape(-1, width), weight, preferred_element_type=jnp.float32
        ).astype(jnp.bfloat16)
        piece = swap(piece, 2 * r) if r else piece
        pieces.append(piece.reshape(mp_size, img_count, own_rows, 2 * key_cols))
    if pairs > 4:
        pieces = [sum(piece.astype(jnp.float32) for piece in pieces)]
    query_gain, key_gain = query_gain[None, :], key_gain[None, :]
    normed, masked = before(queries, out_grad, query_gain, lengths, key_heads)
    owners = (lax.axis_index("mp") - jnp.arange(mp_size, dtype=jnp.int32)) % mp_size
    key_rows, value_rows, score_grad, seq_keys = attend(
        pieces, normed, masked, key_gain, assignment, tile_counts, owners
    )
    query_grad = after(queries, score_grad, seq_keys, query_gain)
    rows = jnp.concatenate((key_rows, value_rows), axis=3)
    all_rows = []
    image_grad = jnp.zeros((img_count, own_rows, vis_width), jnp.bfloat16)
    for r in range(pairs):
        block_rows = (swap(rows, 2 * r) if r else rows).reshape(-1, 2 * key_cols)
        all_rows.append(block_rows)
        term = lax.dot_general(
            block_rows, weight, (((1,), (1,)), ((), ())), preferred_element_type=jnp.float32
        ).astype(jnp.bfloat16)
        term = term.reshape(mp_size, img_count, own_rows, width)
        total = term[0].astype(jnp.float32)
        leftward = rightward = None
        for k in range(half, 0, -1):
            if k < half or r < pairs // 2:
                own = term[k]
                if leftward is not None:
                    own = (own.astype(jnp.float32) + leftward.astype(jnp.float32)).astype(
                        jnp.bfloat16
                    )
                leftward = ring(own, -1)
            if k < half or r >= pairs // 2:
                own = term[mp_size - k]
                if rightward is not None:
                    own = (own.astype(jnp.float32) + rightward.astype(jnp.float32)).astype(
                        jnp.bfloat16
                    )
                rightward = ring(own, 1)
        for arrived in (leftward, rightward):
            if arrived is not None:
                total = total + arrived.astype(jnp.float32)
        piece = total.astype(jnp.bfloat16)
        image_grad = lax.dynamic_update_slice_in_dim(
            image_grad, swap(piece, 2 * r) if r else piece, (pair ^ r) * width, axis=2
        )
    weight_part = lax.dot_general(
        jnp.stack(blocks).reshape(-1, width),
        jnp.stack(all_rows).reshape(-1, 2 * key_cols),
        (((0,), (0,)), ((), ())),
        preferred_element_type=jnp.float32,
    )
    weight_grad = lax.dynamic_slice_in_dim(weight_part, core * own_width, own_width, axis=0)
    weight_grad = weight_grad + swap(
        lax.dynamic_slice_in_dim(weight_part, (1 - core) * own_width, own_width, axis=0), 1
    )
    return (query_grad, image_grad, weight_grad[:, :key_cols], weight_grad[:, key_cols:])


def solution(mesh):
    placed = (
        P("dp", None, "mp"),
        P("dp", None, "mp"),
        P("dp", "mp", None),
        P("dp", "mp"),
        P("dp", "mp"),
        P(),
        P(),
        P("dp"),
        P("dp"),
        P("dp"),
    )

    def body(*args):
        return per_device(mesh.shape["dp"], mesh.shape["mp"], *args)

    return jax.shard_map(
        body,
        mesh=mesh,
        in_specs=placed,
        out_specs=(P("dp", None, "mp"), P("dp", "mp", None), P("dp", "mp"), P("dp", "mp")),
        check_vma=False,
    )
```

time: 228 us -> 173 us (0.76)
  local copies, waits for them, and re-layouts: 42.1 us -> 6.64 us
  other arithmetic: 24.3 us -> 4.17 us
  Pallas kernels: 0 us -> 14.4 us
  waiting for transfers between devices: 85.3 us -> 79 us
  matrix products: 16 us -> 9.97 us
    pallas_call x0 -> x3, Pallas kernels: none -> 14.4 us  [the longest x1 5.23 us: attend(): pl.pallas_call(functools.partial(attend_kernel, count), out_shape=(rows,...]
    mul x9 -> x0, local copies, waits for them, and re-layouts: 13 us -> none  [the longest x4 5.99 us: rms_back(): source * (factor * factor * factor)]
    dot_general x7 -> x0, matrix products: 7.29 us -> none  [the longest x1 2.72 us: attend(): jnp.einsum('bgjtr,btgjd->brgd', prob_half, masked_grad, preferred_element...]
    ppermute x24, waiting for transfers between devices: 66.8 us -> 60.6 us  [ring(): lax.ppermute(value, 'mp', [(i, (i + step) % mp_size) for i in range(mp_si...]
    convert_element_type x4 -> x0, local copies, waits for them, and re-layouts: 5.88 us -> none  [the longest x2 3.34 us: per_device(): image_value.astype(jnp.bfloat16).reshape(img_count, img_rows, key_cols)]
    convert_element_type x7 -> x0, other arithmetic: 5.58 us -> none  [the longest x1 2.02 us: attend(): prob_half = prob_full.astype(jnp.bfloat16)]
    unnamed x61 -> x28, local copies, waits for them, and re-layouts: 6.61 us -> 2.38 us
    another operation x5, other arithmetic: 7.05 us -> 2.9 us  [per_device(): jnp.stack(blocks).reshape(-1, width)]
  transfers between devices with their start and end apart: 38 -> 38, of which waited for: 18 -> 17; matrix products, arithmetic and copies ran while one was open for 14% -> 7% of each run, Pallas kernels for 0% -> 5%
where the time goes in v3:
time: 173 us; the launch traced here: 172 us
  waiting for transfers between devices  79 us (46%)
  starting transfers between devices  57 us (33%)
  Pallas kernels  14.4 us (8%)
  matrix products  9.97 us (6%)
  local copies, waits for them, and re-layouts  6.64 us (4%)
  other arithmetic  4.17 us (2%)
    ppermute x24, waiting for transfers between devices, ring(): lax.ppermute(value, 'mp', [(i, (i + step) % mp_size) for i in range(mp_si...  60.6 us
    ppermute x24, starting transfers between devices, ring(): lax.ppermute(value, 'mp', [(i, (i + step) % mp_size) for i in range(mp_si...  42.1 us
    ppermute x14, waiting for transfers between devices, swap(): return lax.ppermute(value, 'dp', [(i, i ^ mask) for i in range(dp_size)])  18.4 us
    ppermute x14, starting transfers between devices, swap(): return lax.ppermute(value, 'dp', [(i, i ^ mask) for i in range(dp_size)])  14.9 us
    pallas_call x1, Pallas kernels, attend(): pl.pallas_call(functools.partial(attend_kernel, count), out_shape=(rows,...  5.23 us
    pallas_call x1, Pallas kernels, before(): pl.pallas_call(before_kernel, out_shape=(shape, shape), grid_spec=pltpu.P...  4.83 us
    dot_general x4, matrix products, per_device(): lax.dot_general(block_rows, weight, (((1,), (1,)), ((), ())), preferred_e...  4.58 us
    pallas_call x1, Pallas kernels, after(): pl.pallas_call(after_kernel, out_shape=jax.ShapeDtypeStruct(queries.shape...  4.32 us
  transfers between devices with their start and end apart: 38, of which 17 were waited for; matrix products, arithmetic and copies ran while one was open for 7% of the time, Pallas kernels for 5%

profile of v3, /device:TPU:0, one launch (start us, length us, event | category | flops | bytes accessed | tf_op | source)
XLA Modules:
  0.0 172.4 jit_solution(1447182347888891621)
XLA Ops:
  0.7 2.2 %constant_dynamic-slice_fusion.1 = (bf16[2,32,1920]{2,1,0:T(8,128)(2,1)}, bf16[2,32,1920]{2,1,0:T(8,128)(2,1)S(1)}, bf16[2,32,1920]{2,1,0:T(8,128)(2,1)S(1)}, bf16[2,32,1920]{2,1,0:T(8,128)(2,1)}) fusion(bf16[2,32,7680]{2,1,0:T(8,128)(2,1)} %param.12, s32[]{:T(128)S(6)} %select_n.55, s32[]{:T(128)S(6)} %select_n.53, s32[]{:T(128)S(6)} %select_n.49, ...), kind=kLoop, calls=%fused_computation.45 | loop fusion | bytes 1966096 | tf_op jit(solution)/shard_map/dynamic_slice | solution.py:242
  2.9 3.0 %collective-permute-start = (bf16[2,32,1920]{2,1,0:T(8,128)(2,1)S(1)}, bf16[2,32,1920]{2,1,0:T(8,128)(2,1)S(1)}, u32[]{:S(2)}, u32[]{:S(2)}) collective-permute-start(bf16[2,32,1920]{2,1,0:T(8,128)(2,1)S(1)} %get-tuple-element.44), channel_id=1, source_target_pairs={{0,1},{1,2},{2,3},{3,0},{4,5},{5,6},{6,7},{7,4},{8,9},{9,10},{10,1... | collective-permute-start | bytes 737288 | tf_op jit(solution)/shard_map/ppermute | solution.py:237
  5.9 1.5 collective-permute-start.4
  7.4 2.2 %collective-permute-start.2 = (bf16[2,32,1920]{2,1,0:T(8,128)(2,1)S(1)}, bf16[2,32,1920]{2,1,0:T(8,128)(2,1)S(1)}, u32[]{:S(2)}, u32[]{:S(2)}) collective-permute-start(bf16[2,32,1920]{2,1,0:T(8,128)(2,1)S(1)} %get-tuple-element.44), channel_id=1, source_target_pairs={{0,3},{1,0},{2,1},{3,2},{4,7},{5,4},{6,5},{7,6},{8,11},{9,8},{10,9... | collective-permute-start | bytes 737288 | tf_op jit(solution)/shard_map/ppermute | solution.py:237
  9.7 1.5 collective-permute-start.9
  11.5 4.8 %before.1 = (bf16[2,2,1024,128]{3,2,1,0:T(8,128)(2,1)}, bf16[2,2,1024,128]{3,2,1,0:T(8,128)(2,1)}) custom-call(s32[2]{0:T(128)} %lengths.1, bf16[2,128,2048]{2,1,0:T(8,128)(2,1)} %query.3, bf16[2,128,2048]{2,1,0:T(8,128)(2,1)} %grad.1, f32[1,128]{1,0:T(1,128)} %bitcast.133), custom_call_target="tpu_custom_call" | custom-call | tf_op jit(solution)/shard_map/before/pallas_call | solution.py:58
  16.4 3.2 %collective-permute-start.5 = (bf16[2,32,1920]{2,1,0:T(8,128)(2,1)S(1)}, bf16[2,32,1920]{2,1,0:T(8,128)(2,1)S(1)}, u32[]{:S(2)}, u32[]{:S(2)}) collective-permute-start(bf16[2,32,1920]{2,1,0:T(8,128)(2,1)S(1)} %collective-permute-done.4), channel_id=1, source_target_pairs={{0,1},{1,2},{2,3},{3,0},{4,5},{5,6},{6,7},{7,4},{8,9},{9,10},{10,1... | collective-permute-start | bytes 737288 | tf_op jit(solution)/shard_map/ppermute | solution.py:237
  19.8 2.3 %collective-permute-done.9 = bf16[2,32,1920]{2,1,0:T(8,128)(2,1)S(1)} collective-permute-done((bf16[2,32,1920]{2,1,0:T(8,128)(2,1)}, bf16[2,32,1920]{2,1,0:T(8,128)(2,1)S(1)}, u32[]{:S(2)}, u32[]{:S(2)}) %collective-permute-start.9) | collective-permute-done | bytes 245792 | tf_op jit(solution)/shard_map/ppermute | solution.py:226
  22.1 1.7 collective-permute-start.7
  24.2 3.0 %collective-permute-done.1 = bf16[2,32,1920]{2,1,0:T(8,128)(2,1)S(1)} collective-permute-done((bf16[2,32,1920]{2,1,0:T(8,128)(2,1)S(1)}, bf16[2,32,1920]{2,1,0:T(8,128)(2,1)S(1)}, u32[]{:S(2)}, u32[]{:S(2)}) %collective-permute-start.1) | collective-permute-done | bytes 245792 | tf_op jit(solution)/shard_map/ppermute | solution.py:237
  27.2 1.6 collective-permute-start.16
  28.8 3.6 %collective-permute-done.5 = bf16[2,32,1920]{2,1,0:T(8,128)(2,1)S(1)} collective-permute-done((bf16[2,32,1920]{2,1,0:T(8,128)(2,1)S(1)}, bf16[2,32,1920]{2,1,0:T(8,128)(2,1)S(1)}, u32[]{:S(2)}, u32[]{:S(2)}) %collective-permute-start.5) | collective-permute-done | bytes 245792 | tf_op jit(solution)/shard_map/ppermute | solution.py:237
  32.6 2.9 %collective-permute-done.7 = bf16[2,32,1920]{2,1,0:T(8,128)(2,1)S(1)} collective-permute-done((bf16[2,32,1920]{2,1,0:T(8,128)(2,1)S(1)}, bf16[2,32,1920]{2,1,0:T(8,128)(2,1)S(1)}, u32[]{:S(2)}, u32[]{:S(2)}) %collective-permute-start.7) | collective-permute-done | bytes 245792 | tf_op jit(solution)/shard_map/ppermute | solution.py:237
  35.4 11.2 %collective-permute-start.10 = (bf16[2,32,1920]{2,1,0:T(8,128)(2,1)S(1)}, bf16[2,32,1920]{2,1,0:T(8,128)(2,1)S(1)}, u32[]{:S(2)}, u32[]{:S(2)}) collective-permute-start(bf16[2,32,1920]{2,1,0:T(8,128)(2,1)S(1)} %collective-permute-done.9), channel_id=1, source_target_pairs={{0,1},{1,2},{2,3},{3,0},{4,5},{5,6},{6,7},{7,4},{8,9},{9,10},{10,1... | collective-permute-start | bytes 737288 | tf_op jit(solution)/shard_map/ppermute | solution.py:237
  46.6 2.4 %collective-permute-start.15 = (bf16[2,32,1920]{2,1,0:T(8,128)(2,1)S(1)}, bf16[2,32,1920]{2,1,0:T(8,128)(2,1)S(1)}, u32[]{:S(2)}, u32[]{:S(2)}) collective-permute-start(bf16[2,32,1920]{2,1,0:T(8,128)(2,1)S(1)} %collective-permute-done.14), channel_id=1, source_target_pairs={{0,1},{1,2},{2,3},{3,0},{4,5},{5,6},{6,7},{7,4},{8,9},{9,10},{10,1... | collective-permute-start | bytes 737288 | tf_op jit(solution)/shard_map/ppermute | solution.py:237
  49.0 1.4 collective-permute-start.12
  50.4 4.2 %collective-permute-done.6 = bf16[2,32,1920]{2,1,0:T(8,128)(2,1)S(1)} collective-permute-done((bf16[2,32,1920]{2,1,0:T(8,128)(2,1)S(1)}, bf16[2,32,1920]{2,1,0:T(8,128)(2,1)S(1)}, u32[]{:S(2)}, u32[]{:S(2)}) %collective-permute-start.6) | collective-permute-done | bytes 245792 | tf_op jit(solution)/shard_map/ppermute | solution.py:237
  54.6 1.9 %collective-permute-start.17 = (bf16[2,32,1920]{2,1,0:T(8,128)(2,1)S(1)}, bf16[2,32,1920]{2,1,0:T(8,128)(2,1)S(1)}, u32[]{:S(2)}, u32[]{:S(2)}) collective-permute-start(bf16[2,32,1920]{2,1,0:T(8,128)(2,1)S(1)} %collective-permute-done.16), channel_id=1, source_target_pairs={{0,3},{1,0},{2,1},{3,2},{4,7},{5,4},{6,5},{7,6},{8,11},{9,8},{10,9... | collective-permute-start | bytes 737288 | tf_op jit(solution)/shard_map/ppermute | solution.py:237
  56.7 3.1 %collective-permute-done.10 = bf16[2,32,1920]{2,1,0:T(8,128)(2,1)S(1)} collective-permute-done((bf16[2,32,1920]{2,1,0:T(8,128)(2,1)S(1)}, bf16[2,32,1920]{2,1,0:T(8,128)(2,1)S(1)}, u32[]{:S(2)}, u32[]{:S(2)}) %collective-permute-start.10) | collective-permute-done | bytes 245792 | tf_op jit(solution)/shard_map/ppermute | solution.py:237
  59.8 7.3 %collective-permute-done.12 = bf16[2,32,1920]{2,1,0:T(8,128)(2,1)S(1)} collective-permute-done((bf16[2,32,1920]{2,1,0:T(8,128)(2,1)S(1)}, bf16[2,32,1920]{2,1,0:T(8,128)(2,1)S(1)}, u32[]{:S(2)}, u32[]{:S(2)}) %collective-permute-start.12) | collective-permute-done | bytes 245792 | tf_op jit(solution)/shard_map/ppermute | solution.py:237
  67.3 4.9 %collective-permute-done.17 = bf16[2,32,1920]{2,1,0:T(8,128)(2,1)S(1)} collective-permute-done((bf16[2,32,1920]{2,1,0:T(8,128)(2,1)S(1)}, bf16[2,32,1920]{2,1,0:T(8,128)(2,1)S(1)}, u32[]{:S(2)}, u32[]{:S(2)}) %collective-permute-start.17) | collective-permute-done | bytes 245792 | tf_op jit(solution)/shard_map/ppermute | solution.py:237
  73.2 1.6 collective-permute-start.8
  75.5 1.6 collective-permute-start.13
  79.3 3.2 %collective-permute-done.8 = bf16[256,512]{1,0:T(8,128)(2,1)S(1)} collective-permute-done((bf16[256,512]{1,0:T(8,128)(2,1)S(1)}, bf16[256,512]{1,0:T(8,128)(2,1)S(1)}, u32[]{:S(2)}, u32[]{:S(2)}) %collective-permute-start.8) | collective-permute-done | bytes 262176 | tf_op jit(solution)/shard_map/ppermute | solution.py:226
  82.4 6.7 %collective-permute-done.13 = bf16[256,512]{1,0:T(8,128)(2,1)S(1)} collective-permute-done((bf16[256,512]{1,0:T(8,128)(2,1)S(1)}, bf16[256,512]{1,0:T(8,128)(2,1)S(1)}, u32[]{:S(2)}, u32[]{:S(2)}) %collective-permute-start.13) | collective-permute-done | bytes 262176 | tf_op jit(solution)/shard_map/ppermute | solution.py:226
  89.2 5.2 %attend.1 = (bf16[4,2,32,256]{3,2,1,0:T(8,128)(2,1)S(1)}, bf16[4,2,32,256]{3,2,1,0:T(8,128)(2,1)S(1)}, bf16[2,2,1024,128]{3,2,1,0:T(8,128)(2,1)S(1)}, bf16[2,2,128,128]{3,2,1,0:T(8,128)(2,1)S(1)}) custom-call(s32[2]{0:T(128)S(1)} %copy-done.4, s32[2]{0:T(128)S(1)} %copy-done.5, s32[4]{0:T(128)S(1)} %and_select_fusion.owners, ...), custom_call_target="tpu_custom_call" | custom-call | tf_op jit(solution)/shard_map/attend/pallas_call | solution.py:137
  95.6 2.2 %pad_maximum_fusion = bf16[4,4,2,32,1920]{4,3,2,1,0:T(8,128)(2,1)} fusion(bf16[1,4,2,32,1920]{4,3,2,1,0:T(8,128)(2,1)S(1)} %get-tuple-element.24, bf16[1,4,2,32,1920]{4,3,2,1,0:T(8,128)(2,1)S(1)} %get-tuple-element.22, bf16[1,4,2,32,1920]{4,3,2,1,0:T(8,128)(2,1)S(1)} %get-tuple-element.20, bf16[1,4,2,32,1920]{4,3,2,1,0:T(8,128)(2,1)S(1)} %get-tuple-element.18), kind=kLoop, calls=%fused_computation | loop fusion | flops 5898240 | bytes 7864320 | tf_op jit(solution)/shard_map/stack | solution.py:304
  98.5 1.3 collective-permute-start.27
  99.8 1.4 collective-permute-start.32
  101.2 2.0 %collective-permute-start.21 = (bf16[2,32,1920]{2,1,0:T(8,128)(2,1)S(1)}, bf16[2,32,1920]{2,1,0:T(8,128)(2,1)S(1)}, u32[]{:S(2)}, u32[]{:S(2)}) collective-permute-start(bf16[2,32,1920]{2,1,0:T(8,128)(2,1)S(1)} %bitcast.118), channel_id=1, source_target_pairs={{0,1},{1,2},{2,3},{3,0},{4,5},{5,6},{6,7},{7,4},{8,9},{9,10},{10,1... | collective-permute-start | bytes 737288 | tf_op jit(solution)/shard_map/ppermute | solution.py:237
  103.2 4.3 %after.1 = bf16[2,128,2048]{2,1,0:T(8,128)(2,1)} custom-call(bf16[2,128,2048]{2,1,0:T(8,128)(2,1)} %query.3, bf16[2,2,1024,128]{3,2,1,0:T(8,128)(2,1)} %copy-done, bf16[2,2,128,128]{3,2,1,0:T(8,128)(2,1)} %copy-done.3, f32[1,128]{1,0:T(1,128)} %bitcast.134), custom_call_target="tpu_custom_call" | custom-call | tf_op jit(solution)/shard_map/after/pallas_call | solution.py:187
  107.6 1.9 %collective-permute-start.20 = (bf16[2,32,1920]{2,1,0:T(8,128)(2,1)S(1)}, bf16[2,32,1920]{2,1,0:T(8,128)(2,1)S(1)}, u32[]{:S(2)}, u32[]{:S(2)}) collective-permute-start(bf16[2,32,1920]{2,1,0:T(8,128)(2,1)S(1)} %fusion.9), channel_id=1, source_target_pairs={{0,3},{1,0},{2,1},{3,2},{4,7},{5,4},{6,5},{7,6},{8,11},{9,8},{10,9... | collective-permute-start | bytes 737288 | tf_op jit(solution)/shard_map/ppermute | solution.py:237
  109.5 2.3 %convolution_convert_fusion.2 = bf16[256,1920]{1,0:T(8,128)(2,1)S(1)} fusion(bf16[256,512]{1,0:T(8,128)(2,1)S(1)} %bitcast.106, bf16[960,512]{1,0:T(8,128)(2,1)} %copy-done.11, bf16[960,512]{1,0:T(8,128)(2,1)S(1)} %constant_dynamic-update-slice_fusion, pred[]{:T(512)S(6)} %eq.7), kind=kOutput, calls=%fused_computation.3 | convolution fusion | flops 512655360 | bytes 3211265 | tf_op jit(solution)/shard_map/dot_general | solution.py:275
  112.1 3.6 %collective-permute-start.23 = (bf16[2,32,1920]{2,1,0:T(8,128)(2,1)S(1)}, bf16[2,32,1920]{2,1,0:T(8,128)(2,1)S(1)}, u32[]{:S(2)}, u32[]{:S(2)}) collective-permute-start(bf16[2,32,1920]{2,1,0:T(8,128)(2,1)S(1)} %bitcast.120), channel_id=1, source_target_pairs={{0,3},{1,0},{2,1},{3,2},{4,7},{5,4},{6,5},{7,6},{8,11},{9,8},{10,9... | collective-permute-start | bytes 737288 | tf_op jit(solution)/shard_map/ppermute | solution.py:237
  117.0 1.6 copy-done.7
  118.7 2.3 %fusion.23 = f32[1920,512]{1,0:T(8,128)S(1)} fusion(bf16[1024,1920]{1,0:T(8,128)(2,1)S(1)} %bitcast.87, bf16[1024,512]{1,0:T(8,128)(2,1)S(1)} %bitcast.88), kind=kOutput, calls=%fused_computation.62 | convolution fusion | flops 2013265920 | bytes 8912896 | tf_op jit(solution)/shard_map/dot_general | solution.py:303
  122.0 2.2 %collective-permute-start.28 = (bf16[2,32,1920]{2,1,0:T(8,128)(2,1)S(1)}, bf16[2,32,1920]{2,1,0:T(8,128)(2,1)S(1)}, u32[]{:S(2)}, u32[]{:S(2)}) collective-permute-start(bf16[2,32,1920]{2,1,0:T(8,128)(2,1)S(1)} %bitcast.115), channel_id=1, source_target_pairs={{0,3},{1,0},{2,1},{3,2},{4,7},{5,4},{6,5},{7,6},{8,11},{9,8},{10,9... | collective-permute-start | bytes 737288 | tf_op jit(solution)/shard_map/ppermute | solution.py:237
  124.4 7.2 %collective-permute-done.23 = bf16[2,32,1920]{2,1,0:T(8,128)(2,1)S(1)} collective-permute-done((bf16[2,32,1920]{2,1,0:T(8,128)(2,1)S(1)}, bf16[2,32,1920]{2,1,0:T(8,128)(2,1)S(1)}, u32[]{:S(2)}, u32[]{:S(2)}) %collective-permute-start.23) | collective-permute-done | bytes 245792 | tf_op jit(solution)/shard_map/ppermute | solution.py:237
  131.6 1.5 collective-permute-done.29
  133.2 10.3 %collective-permute-done.34 = bf16[2,32,1920]{2,1,0:T(8,128)(2,1)S(1)} collective-permute-done((bf16[2,32,1920]{2,1,0:T(8,128)(2,1)S(1)}, bf16[2,32,1920]{2,1,0:T(8,128)(2,1)S(1)}, u32[]{:S(2)}, u32[]{:S(2)}) %collective-permute-start.34) | collective-permute-done | bytes 245792 | tf_op jit(solution)/shard_map/ppermute | solution.py:237
  143.5 2.0 %collective-permute-start.24 = (bf16[2,32,1920]{2,1,0:T(8,128)(2,1)S(1)}, bf16[2,32,1920]{2,1,0:T(8,128)(2,1)S(1)}, u32[]{:S(2)}, u32[]{:S(2)}) collective-permute-start(bf16[2,32,1920]{2,1,0:T(8,128)(2,1)S(1)} %fusion.6), channel_id=1, source_target_pairs={{0,3},{1,0},{2,1},{3,2},{4,7},{5,4},{6,5},{7,6},{8,11},{9,8},{10,9... | collective-permute-start | bytes 737288 | tf_op jit(solution)/shard_map/ppermute | solution.py:237
  145.7 7.2 %collective-permute-done.24 = bf16[2,32,1920]{2,1,0:T(8,128)(2,1)S(1)} collective-permute-done((bf16[2,32,1920]{2,1,0:T(8,128)(2,1)S(1)}, bf16[2,32,1920]{2,1,0:T(8,128)(2,1)S(1)}, u32[]{:S(2)}, u32[]{:S(2)}) %collective-permute-start.24) | collective-permute-done | bytes 245792 | tf_op jit(solution)/shard_map/ppermute | solution.py:237
  154.6 3.7 %collective-permute-done.30 = bf16[2,32,1920]{2,1,0:T(8,128)(2,1)S(1)} collective-permute-done((bf16[2,32,1920]{2,1,0:T(8,128)(2,1)S(1)}, bf16[2,32,1920]{2,1,0:T(8,128)(2,1)S(1)}, u32[]{:S(2)}, u32[]{:S(2)}) %collective-permute-start.30) | collective-permute-done | bytes 245792 | tf_op jit(solution)/shard_map/ppermute | solution.py:237
  158.4 1.8 %collective-permute-start.31 = (bf16[2,32,1920]{2,1,0:T(8,128)(2,1)S(1)}, bf16[2,32,1920]{2,1,0:T(8,128)(2,1)S(1)}, u32[]{:S(2)}, u32[]{:S(2)}) collective-permute-start(bf16[2,32,1920]{2,1,0:T(8,128)(2,1)S(1)} %fusion.5), channel_id=1, source_target_pairs={{0,16},{4,20},{8,24},{12,28},{16,0},{20,4},{24,8},{28,12},{1,17},{... | collective-permute-start | bytes 737288 | tf_op jit(solution)/shard_map/ppermute | solution.py:226
  160.2 1.8 %collective-permute-done.35 = bf16[2,32,1920]{2,1,0:T(8,128)(2,1)S(1)} collective-permute-done((bf16[2,32,1920]{2,1,0:T(8,128)(2,1)S(1)}, bf16[2,32,1920]{2,1,0:T(8,128)(2,1)S(1)}, u32[]{:S(2)}, u32[]{:S(2)}) %collective-permute-start.35) | collective-permute-done | bytes 245792 | tf_op jit(solution)/shard_map/ppermute | solution.py:237
  162.0 1.5 collective-permute-start.36
  163.6 6.3 %collective-permute-done.31 = bf16[2,32,1920]{2,1,0:T(8,128)(2,1)S(1)} collective-permute-done((bf16[2,32,1920]{2,1,0:T(8,128)(2,1)S(1)}, bf16[2,32,1920]{2,1,0:T(8,128)(2,1)S(1)}, u32[]{:S(2)}, u32[]{:S(2)}) %collective-permute-start.31) | collective-permute-done | bytes 245792 | tf_op jit(solution)/shard_map/ppermute | solution.py:226
  171.0 1.4 fusion.18
  (97 shorter events, 13.3 us)
Async XLA Ops:
  0.7 19.0 %copy-start.9 = (bf16[960,256]{1,0:T(8,128)(2,1)S(1)}, bf16[960,256]{1,0:T(8,128)(2,1)}, u32[]{:S(2)}) copy-start(bf16[960,256]{1,0:T(8,128)(2,1)} %param.13) | copy-start | bytes 1474564
  2.9 16.8 %copy-start.10 = (bf16[960,256]{1,0:T(8,128)(2,1)S(1)}, bf16[960,256]{1,0:T(8,128)(2,1)}, u32[]{:S(2)}) copy-start(bf16[960,256]{1,0:T(8,128)(2,1)} %param.14) | copy-start | bytes 1474564
  2.9 13.4 %collective-permute-start = (bf16[2,32,1920]{2,1,0:T(8,128)(2,1)S(1)}, bf16[2,32,1920]{2,1,0:T(8,128)(2,1)S(1)}, u32[]{:S(2)}, u32[]{:S(2)}) collective-permute-start(bf16[2,32,1920]{2,1,0:T(8,128)(2,1)S(1)} %get-tuple-element.44), channel_id=1, source_target_pairs={{0,1},{1,2},{2,3},{3,0},{4,5},{5,6},{6,7},{7,4},{8,9},{9,10},{10,1... | collective-permute-start | bytes 737288 | tf_op jit(solution)/shard_map/ppermute | solution.py:237
  5.9 10.5 %collective-permute-start.4 = (bf16[2,32,1920]{2,1,0:T(8,128)(2,1)S(1)}, bf16[2,32,1920]{2,1,0:T(8,128)(2,1)S(1)}, u32[]{:S(2)}, u32[]{:S(2)}) collective-permute-start(bf16[2,32,1920]{2,1,0:T(8,128)(2,1)S(1)} %get-tuple-element.43), channel_id=1, source_target_pairs={{0,8},{4,12},{8,0},{12,4},{16,24},{20,28},{24,16},{28,20},{1,9},{5... | collective-permute-start | bytes 737288 | tf_op jit(solution)/shard_map/ppermute | solution.py:226
  7.4 12.3 %collective-permute-start.2 = (bf16[2,32,1920]{2,1,0:T(8,128)(2,1)S(1)}, bf16[2,32,1920]{2,1,0:T(8,128)(2,1)S(1)}, u32[]{:S(2)}, u32[]{:S(2)}) collective-permute-start(bf16[2,32,1920]{2,1,0:T(8,128)(2,1)S(1)} %get-tuple-element.44), channel_id=1, source_target_pairs={{0,3},{1,0},{2,1},{3,2},{4,7},{5,4},{6,5},{7,6},{8,11},{9,8},{10,9... | collective-permute-start | bytes 737288 | tf_op jit(solution)/shard_map/ppermute | solution.py:237
  9.7 12.4 %collective-permute-start.9 = (bf16[2,32,1920]{2,1,0:T(8,128)(2,1)}, bf16[2,32,1920]{2,1,0:T(8,128)(2,1)S(1)}, u32[]{:S(2)}, u32[]{:S(2)}) collective-permute-start(bf16[2,32,1920]{2,1,0:T(8,128)(2,1)} %get-tuple-element.45), channel_id=1, source_target_pairs={{0,16},{4,20},{8,24},{12,28},{16,0},{20,4},{24,8},{28,12},{1,17},{... | collective-permute-start | bytes 737288 | tf_op jit(solution)/shard_map/ppermute | solution.py:226
  11.2 12.6 %collective-permute-start.14 = (bf16[2,32,1920]{2,1,0:T(8,128)(2,1)}, bf16[2,32,1920]{2,1,0:T(8,128)(2,1)S(1)}, u32[]{:S(2)}, u32[]{:S(2)}) collective-permute-start(bf16[2,32,1920]{2,1,0:T(8,128)(2,1)} %get-tuple-element.42), channel_id=1, source_target_pairs={{0,24},{4,28},{8,16},{12,20},{16,8},{20,12},{24,0},{28,4},{1,25},{... | collective-permute-start | bytes 737288 | tf_op jit(solution)/shard_map/ppermute | solution.py:226
  16.3 10.9 %collective-permute-start.1 = (bf16[2,32,1920]{2,1,0:T(8,128)(2,1)S(1)}, bf16[2,32,1920]{2,1,0:T(8,128)(2,1)S(1)}, u32[]{:S(2)}, u32[]{:S(2)}) collective-permute-start(bf16[2,32,1920]{2,1,0:T(8,128)(2,1)S(1)} %collective-permute-done), channel_id=1, source_target_pairs={{0,1},{1,2},{2,3},{3,0},{4,5},{5,6},{6,7},{7,4},{8,9},{9,10},{10,1... | collective-permute-start | bytes 737288 | tf_op jit(solution)/shard_map/ppermute | solution.py:237
  16.4 16.0 %collective-permute-start.5 = (bf16[2,32,1920]{2,1,0:T(8,128)(2,1)S(1)}, bf16[2,32,1920]{2,1,0:T(8,128)(2,1)S(1)}, u32[]{:S(2)}, u32[]{:S(2)}) collective-permute-start(bf16[2,32,1920]{2,1,0:T(8,128)(2,1)S(1)} %collective-permute-done.4), channel_id=1, source_target_pairs={{0,1},{1,2},{2,3},{3,0},{4,5},{5,6},{6,7},{7,4},{8,9},{9,10},{10,1... | collective-permute-start | bytes 737288 | tf_op jit(solution)/shard_map/ppermute | solution.py:237
  19.7 52.6 %collective-permute-start.3 = (bf16[960,512]{1,0:T(8,128)(2,1)S(1)}, bf16[960,512]{1,0:T(8,128)(2,1)S(1)}, u32[]{:S(2)}, u32[]{:S(2)}) collective-permute-start(bf16[960,512]{1,0:T(8,128)(2,1)S(1)} %constant_dynamic-update-slice_fusion), channel_id=1, source_target_pairs={{0,4},{4,0},{8,12},{12,8},{16,20},{20,16},{24,28},{28,24},{1,5},{5... | collective-permute-start | bytes 2949128 | tf_op jit(solution)/shard_map/ppermute | solution.py:226
  22.1 13.3 %collective-permute-start.7 = (bf16[2,32,1920]{2,1,0:T(8,128)(2,1)S(1)}, bf16[2,32,1920]{2,1,0:T(8,128)(2,1)S(1)}, u32[]{:S(2)}, u32[]{:S(2)}) collective-permute-start(bf16[2,32,1920]{2,1,0:T(8,128)(2,1)S(1)} %collective-permute-done.4), channel_id=1, source_target_pairs={{0,3},{1,0},{2,1},{3,2},{4,7},{5,4},{6,5},{7,6},{8,11},{9,8},{10,9... | collective-permute-start | bytes 737288 | tf_op jit(solution)/shard_map/ppermute | solution.py:237
  23.8 22.8 %collective-permute-start.11 = (bf16[2,32,1920]{2,1,0:T(8,128)(2,1)S(1)}, bf16[2,32,1920]{2,1,0:T(8,128)(2,1)S(1)}, u32[]{:S(2)}, u32[]{:S(2)}) collective-permute-start(bf16[2,32,1920]{2,1,0:T(8,128)(2,1)S(1)} %collective-permute-done.9), channel_id=1, source_target_pairs={{0,3},{1,0},{2,1},{3,2},{4,7},{5,4},{6,5},{7,6},{8,11},{9,8},{10,9... | collective-permute-start | bytes 737288 | tf_op jit(solution)/shard_map/ppermute | solution.py:237
  27.2 21.8 %collective-permute-start.16 = (bf16[2,32,1920]{2,1,0:T(8,128)(2,1)S(1)}, bf16[2,32,1920]{2,1,0:T(8,128)(2,1)S(1)}, u32[]{:S(2)}, u32[]{:S(2)}) collective-permute-start(bf16[2,32,1920]{2,1,0:T(8,128)(2,1)S(1)} %collective-permute-done.14), channel_id=1, source_target_pairs={{0,3},{1,0},{2,1},{3,2},{4,7},{5,4},{6,5},{7,6},{8,11},{9,8},{10,9... | collective-permute-start | bytes 737288 | tf_op jit(solution)/shard_map/ppermute | solution.py:237
  32.4 22.3 %collective-permute-start.6 = (bf16[2,32,1920]{2,1,0:T(8,128)(2,1)S(1)}, bf16[2,32,1920]{2,1,0:T(8,128)(2,1)S(1)}, u32[]{:S(2)}, u32[]{:S(2)}) collective-permute-start(bf16[2,32,1920]{2,1,0:T(8,128)(2,1)S(1)} %collective-permute-done.5), channel_id=1, source_target_pairs={{0,1},{1,2},{2,3},{3,0},{4,5},{5,6},{6,7},{7,4},{8,9},{9,10},{10,1... | collective-permute-start | bytes 737288 | tf_op jit(solution)/shard_map/ppermute | solution.py:237
  35.4 24.4 %collective-permute-start.10 = (bf16[2,32,1920]{2,1,0:T(8,128)(2,1)S(1)}, bf16[2,32,1920]{2,1,0:T(8,128)(2,1)S(1)}, u32[]{:S(2)}, u32[]{:S(2)}) collective-permute-start(bf16[2,32,1920]{2,1,0:T(8,128)(2,1)S(1)} %collective-permute-done.9), channel_id=1, source_target_pairs={{0,1},{1,2},{2,3},{3,0},{4,5},{5,6},{6,7},{7,4},{8,9},{9,10},{10,1... | collective-permute-start | bytes 737288 | tf_op jit(solution)/shard_map/ppermute | solution.py:237
  46.6 20.6 %collective-permute-start.15 = (bf16[2,32,1920]{2,1,0:T(8,128)(2,1)S(1)}, bf16[2,32,1920]{2,1,0:T(8,128)(2,1)S(1)}, u32[]{:S(2)}, u32[]{:S(2)}) collective-permute-start(bf16[2,32,1920]{2,1,0:T(8,128)(2,1)S(1)} %collective-permute-done.14), channel_id=1, source_target_pairs={{0,1},{1,2},{2,3},{3,0},{4,5},{5,6},{6,7},{7,4},{8,9},{9,10},{10,1... | collective-permute-start | bytes 737288 | tf_op jit(solution)/shard_map/ppermute | solution.py:237
  49.0 18.1 %collective-permute-start.12 = (bf16[2,32,1920]{2,1,0:T(8,128)(2,1)S(1)}, bf16[2,32,1920]{2,1,0:T(8,128)(2,1)S(1)}, u32[]{:S(2)}, u32[]{:S(2)}) collective-permute-start(bf16[2,32,1920]{2,1,0:T(8,128)(2,1)S(1)} %collective-permute-done.11), channel_id=1, source_target_pairs={{0,3},{1,0},{2,1},{3,2},{4,7},{5,4},{6,5},{7,6},{8,11},{9,8},{10,9... | collective-permute-start | bytes 737288 | tf_op jit(solution)/shard_map/ppermute | solution.py:237
  54.6 17.5 %collective-permute-start.17 = (bf16[2,32,1920]{2,1,0:T(8,128)(2,1)S(1)}, bf16[2,32,1920]{2,1,0:T(8,128)(2,1)S(1)}, u32[]{:S(2)}, u32[]{:S(2)}) collective-permute-start(bf16[2,32,1920]{2,1,0:T(8,128)(2,1)S(1)} %collective-permute-done.16), channel_id=1, source_target_pairs={{0,3},{1,0},{2,1},{3,2},{4,7},{5,4},{6,5},{7,6},{8,11},{9,8},{10,9... | collective-permute-start | bytes 737288 | tf_op jit(solution)/shard_map/ppermute | solution.py:237
  72.4 22.1 %copy-start.11 = (bf16[960,512]{1,0:T(8,128)(2,1)}, bf16[960,512]{1,0:T(8,128)(2,1)S(1)}, u32[]{:S(2)}) copy-start(bf16[960,512]{1,0:T(8,128)(2,1)S(1)} %collective-permute-done.3) | copy-start | bytes 2949124
  73.2 9.2 %collective-permute-start.8 = (bf16[256,512]{1,0:T(8,128)(2,1)S(1)}, bf16[256,512]{1,0:T(8,128)(2,1)S(1)}, u32[]{:S(2)}, u32[]{:S(2)}) collective-permute-start(bf16[256,512]{1,0:T(8,128)(2,1)S(1)} %convolution_convert_fusion.6), channel_id=1, source_target_pairs={{0,8},{4,12},{8,0},{12,4},{16,24},{20,28},{24,16},{28,20},{1,9},{5... | collective-permute-start | bytes 786440 | tf_op jit(solution)/shard_map/ppermute | solution.py:226
  75.5 13.6 %collective-permute-start.13 = (bf16[256,512]{1,0:T(8,128)(2,1)S(1)}, bf16[256,512]{1,0:T(8,128)(2,1)S(1)}, u32[]{:S(2)}, u32[]{:S(2)}) collective-permute-start(bf16[256,512]{1,0:T(8,128)(2,1)S(1)} %convolution_convert_fusion.5), channel_id=1, source_target_pairs={{0,16},{4,20},{8,24},{12,28},{16,0},{20,4},{24,8},{28,12},{1,17},{... | collective-permute-start | bytes 786440 | tf_op jit(solution)/shard_map/ppermute | solution.py:226
  77.9 11.2 %collective-permute-start.18 = (bf16[256,512]{1,0:T(8,128)(2,1)S(1)}, bf16[256,512]{1,0:T(8,128)(2,1)S(1)}, u32[]{:S(2)}, u32[]{:S(2)}) collective-permute-start(bf16[256,512]{1,0:T(8,128)(2,1)S(1)} %convolution_convert_fusion.4), channel_id=1, source_target_pairs={{0,24},{4,28},{8,16},{12,20},{16,8},{20,12},{24,0},{28,4},{1,25},{... | collective-permute-start | bytes 786440 | tf_op jit(solution)/shard_map/ppermute | solution.py:226
  78.5 10.7 %copy-start.1 = (bf16[2,2,1024,128]{3,2,1,0:T(8,128)(2,1)S(1)}, bf16[2,2,1024,128]{3,2,1,0:T(8,128)(2,1)}, u32[]{:S(2)}) copy-start(bf16[2,2,1024,128]{3,2,1,0:T(8,128)(2,1)} %get-tuple-element.10.refs_8_) | copy-start | bytes 3145732
  78.5 10.7 %copy-start.2 = (bf16[2,2,1024,128]{3,2,1,0:T(8,128)(2,1)S(1)}, bf16[2,2,1024,128]{3,2,1,0:T(8,128)(2,1)}, u32[]{:S(2)}) copy-start(bf16[2,2,1024,128]{3,2,1,0:T(8,128)(2,1)} %get-tuple-element.11.refs_9_) | copy-start | bytes 3145732
  78.5 10.7 %copy-start.4 = (s32[2]{0:T(128)S(1)}, s32[2]{0:T(128)}, u32[]{:S(2)}) copy-start(s32[2]{0:T(128)} %assignment.1) | copy-start | bytes 28
  78.5 10.7 %copy-start.5 = (s32[2]{0:T(128)S(1)}, s32[2]{0:T(128)}, u32[]{:S(2)}) copy-start(s32[2]{0:T(128)} %tiles.1) | copy-start | bytes 28
  78.5 10.7 %copy-start.6 = (f32[128]{0:T(128)S(1)}, f32[128]{0:T(128)}, u32[]{:S(2)}) copy-start(f32[128]{0:T(128)} %param.16) | copy-start | bytes 1540
  95.5 12.1 %collective-permute-start.19 = (bf16[2,32,1920]{2,1,0:T(8,128)(2,1)S(1)}, bf16[2,32,1920]{2,1,0:T(8,128)(2,1)S(1)}, u32[]{:S(2)}, u32[]{:S(2)}) collective-permute-start(bf16[2,32,1920]{2,1,0:T(8,128)(2,1)S(1)} %bitcast.130), channel_id=1, source_target_pairs={{0,3},{1,0},{2,1},{3,2},{4,7},{5,4},{6,5},{7,6},{8,11},{9,8},{10,9... | collective-permute-start | bytes 737288 | tf_op jit(solution)/shard_map/ppermute | solution.py:237
  97.8 11.8 %collective-permute-start.22 = (bf16[4,2,32,512]{3,2,1,0:T(8,128)(2,1)S(1)}, bf16[4,2,32,512]{3,2,1,0:T(8,128)(2,1)S(1)}, u32[]{:S(2)}, u32[]{:S(2)}) collective-permute-start(bf16[4,2,32,512]{3,2,1,0:T(8,128)(2,1)S(1)} %constant_dynamic-update-slice_fusion.2), channel_id=1, source_target_pairs={{0,8},{4,12},{8,0},{12,4},{16,24},{20,28},{24,16},{28,20},{1,9},{5... | collective-permute-start | bytes 786440 | tf_op jit(solution)/shard_map/ppermute | solution.py:226
  98.5 13.6 %collective-permute-start.27 = (bf16[4,2,32,512]{3,2,1,0:T(8,128)(2,1)S(1)}, bf16[4,2,32,512]{3,2,1,0:T(8,128)(2,1)S(1)}, u32[]{:S(2)}, u32[]{:S(2)}) collective-permute-start(bf16[4,2,32,512]{3,2,1,0:T(8,128)(2,1)S(1)} %constant_dynamic-update-slice_fusion.2), channel_id=1, source_target_pairs={{0,16},{4,20},{8,24},{12,28},{16,0},{20,4},{24,8},{28,12},{1,17},{... | collective-permute-start | bytes 786440 | tf_op jit(solution)/shard_map/ppermute | solution.py:226
  99.8 16.8 %collective-permute-start.32 = (bf16[4,2,32,512]{3,2,1,0:T(8,128)(2,1)S(1)}, bf16[4,2,32,512]{3,2,1,0:T(8,128)(2,1)S(1)}, u32[]{:S(2)}, u32[]{:S(2)}) collective-permute-start(bf16[4,2,32,512]{3,2,1,0:T(8,128)(2,1)S(1)} %constant_dynamic-update-slice_fusion.2), channel_id=1, source_target_pairs={{0,24},{4,28},{8,16},{12,20},{16,8},{20,12},{24,0},{28,4},{1,25},{... | collective-permute-start | bytes 786440 | tf_op jit(solution)/shard_map/ppermute | solution.py:226
  101.2 20.7 %collective-permute-start.21 = (bf16[2,32,1920]{2,1,0:T(8,128)(2,1)S(1)}, bf16[2,32,1920]{2,1,0:T(8,128)(2,1)S(1)}, u32[]{:S(2)}, u32[]{:S(2)}) collective-permute-start(bf16[2,32,1920]{2,1,0:T(8,128)(2,1)S(1)} %bitcast.118), channel_id=1, source_target_pairs={{0,1},{1,2},{2,3},{3,0},{4,5},{5,6},{6,7},{7,4},{8,9},{9,10},{10,1... | collective-permute-start | bytes 737288 | tf_op jit(solution)/shard_map/ppermute | solution.py:237
  107.6 16.6 %collective-permute-start.20 = (bf16[2,32,1920]{2,1,0:T(8,128)(2,1)S(1)}, bf16[2,32,1920]{2,1,0:T(8,128)(2,1)S(1)}, u32[]{:S(2)}, u32[]{:S(2)}) collective-permute-start(bf16[2,32,1920]{2,1,0:T(8,128)(2,1)S(1)} %fusion.9), channel_id=1, source_target_pairs={{0,3},{1,0},{2,1},{3,2},{4,7},{5,4},{6,5},{7,6},{8,11},{9,8},{10,9... | collective-permute-start | bytes 737288 | tf_op jit(solution)/shard_map/ppermute | solution.py:237
  111.8 4.0 %copy-start.12 = (bf16[960,512]{1,0:T(8,128)(2,1)S(1)}, bf16[960,512]{1,0:T(8,128)(2,1)}, u32[]{:S(2)}) copy-start(bf16[960,512]{1,0:T(8,128)(2,1)} %copy-done.11) | copy-start | bytes 2949124
  111.9 33.8 %collective-permute-start.25 = (bf16[2,32,1920]{2,1,0:T(8,128)(2,1)S(1)}, bf16[2,32,1920]{2,1,0:T(8,128)(2,1)S(1)}, u32[]{:S(2)}, u32[]{:S(2)}) collective-permute-start(bf16[2,32,1920]{2,1,0:T(8,128)(2,1)S(1)} %bitcast.116), channel_id=1, source_target_pairs={{0,1},{1,2},{2,3},{3,0},{4,5},{5,6},{6,7},{7,4},{8,9},{9,10},{10,1... | collective-permute-start | bytes 737288 | tf_op jit(solution)/shard_map/ppermute | solution.py:237
  112.1 19.5 %collective-permute-start.23 = (bf16[2,32,1920]{2,1,0:T(8,128)(2,1)S(1)}, bf16[2,32,1920]{2,1,0:T(8,128)(2,1)S(1)}, u32[]{:S(2)}, u32[]{:S(2)}) collective-permute-start(bf16[2,32,1920]{2,1,0:T(8,128)(2,1)S(1)} %bitcast.120), channel_id=1, source_target_pairs={{0,3},{1,0},{2,1},{3,2},{4,7},{5,4},{6,5},{7,6},{8,11},{9,8},{10,9... | collective-permute-start | bytes 737288 | tf_op jit(solution)/shard_map/ppermute | solution.py:237
  116.5 2.1 %copy-start.7 = (bf16[4,4,2,32,1920]{4,3,2,1,0:T(8,128)(2,1)S(1)}, bf16[4,4,2,32,1920]{4,3,2,1,0:T(8,128)(2,1)}, u32[]{:S(2)}) copy-start(bf16[4,4,2,32,1920]{4,3,2,1,0:T(8,128)(2,1)} %pad_maximum_fusion) | copy-start | bytes 11796484
  116.6 16.5 %collective-permute-start.29 = (bf16[2,32,1920]{2,1,0:T(8,128)(2,1)S(1)}, bf16[2,32,1920]{2,1,0:T(8,128)(2,1)S(1)}, u32[]{:S(2)}, u32[]{:S(2)}) collective-permute-start(bf16[2,32,1920]{2,1,0:T(8,128)(2,1)S(1)} %bitcast.122), channel_id=1, source_target_pairs={{0,1},{1,2},{2,3},{3,0},{4,5},{5,6},{6,7},{7,4},{8,9},{9,10},{10,1... | collective-permute-start | bytes 737288 | tf_op jit(solution)/shard_map/ppermute | solution.py:237
  122.0 31.6 %collective-permute-start.28 = (bf16[2,32,1920]{2,1,0:T(8,128)(2,1)S(1)}, bf16[2,32,1920]{2,1,0:T(8,128)(2,1)S(1)}, u32[]{:S(2)}, u32[]{:S(2)}) collective-permute-start(bf16[2,32,1920]{2,1,0:T(8,128)(2,1)S(1)} %bitcast.115), channel_id=1, source_target_pairs={{0,3},{1,0},{2,1},{3,2},{4,7},{5,4},{6,5},{7,6},{8,11},{9,8},{10,9... | collective-permute-start | bytes 737288 | tf_op jit(solution)/shard_map/ppermute | solution.py:237
  124.2 19.3 %collective-permute-start.34 = (bf16[2,32,1920]{2,1,0:T(8,128)(2,1)S(1)}, bf16[2,32,1920]{2,1,0:T(8,128)(2,1)S(1)}, u32[]{:S(2)}, u32[]{:S(2)}) collective-permute-start(bf16[2,32,1920]{2,1,0:T(8,128)(2,1)S(1)} %bitcast.126), channel_id=1, source_target_pairs={{0,1},{1,2},{2,3},{3,0},{4,5},{5,6},{6,7},{7,4},{8,9},{9,10},{10,1... | collective-permute-start | bytes 737288 | tf_op jit(solution)/shard_map/ppermute | solution.py:237
  131.6 28.6 %collective-permute-start.33 = (bf16[2,32,1920]{2,1,0:T(8,128)(2,1)S(1)}, bf16[2,32,1920]{2,1,0:T(8,128)(2,1)S(1)}, u32[]{:S(2)}, u32[]{:S(2)}) collective-permute-start(bf16[2,32,1920]{2,1,0:T(8,128)(2,1)S(1)} %bitcast.117), channel_id=1, source_target_pairs={{0,3},{1,0},{2,1},{3,2},{4,7},{5,4},{6,5},{7,6},{8,11},{9,8},{10,9... | collective-permute-start | bytes 737288 | tf_op jit(solution)/shard_map/ppermute | solution.py:237
  133.2 36.8 %collective-permute-start.37 = (f32[960,512]{1,0:T(8,128)S(1)}, f32[960,512]{1,0:T(8,128)S(1)}, u32[]{:S(2)}, u32[]{:S(2)}) collective-permute-start(f32[960,512]{1,0:T(8,128)S(1)} %constant_dynamic-slice_fusion), channel_id=1, source_target_pairs={{0,4},{4,0},{8,12},{12,8},{16,20},{20,16},{24,28},{28,24},{1,5},{5... | collective-permute-start | bytes 5898248 | tf_op jit(solution)/shard_map/ppermute | solution.py:226
  143.5 9.4 %collective-permute-start.24 = (bf16[2,32,1920]{2,1,0:T(8,128)(2,1)S(1)}, bf16[2,32,1920]{2,1,0:T(8,128)(2,1)S(1)}, u32[]{:S(2)}, u32[]{:S(2)}) collective-permute-start(bf16[2,32,1920]{2,1,0:T(8,128)(2,1)S(1)} %fusion.6), channel_id=1, source_target_pairs={{0,3},{1,0},{2,1},{3,2},{4,7},{5,4},{6,5},{7,6},{8,11},{9,8},{10,9... | collective-permute-start | bytes 737288 | tf_op jit(solution)/shard_map/ppermute | solution.py:237
  145.6 12.6 %collective-permute-start.30 = (bf16[2,32,1920]{2,1,0:T(8,128)(2,1)S(1)}, bf16[2,32,1920]{2,1,0:T(8,128)(2,1)S(1)}, u32[]{:S(2)}, u32[]{:S(2)}) collective-permute-start(bf16[2,32,1920]{2,1,0:T(8,128)(2,1)S(1)} %fusion.3), channel_id=1, source_target_pairs={{0,1},{1,2},{2,3},{3,0},{4,5},{5,6},{6,7},{7,4},{8,9},{9,10},{10,1... | collective-permute-start | bytes 737288 | tf_op jit(solution)/shard_map/ppermute | solution.py:237
  152.9 9.0 %collective-permute-start.35 = (bf16[2,32,1920]{2,1,0:T(8,128)(2,1)S(1)}, bf16[2,32,1920]{2,1,0:T(8,128)(2,1)S(1)}, u32[]{:S(2)}, u32[]{:S(2)}) collective-permute-start(bf16[2,32,1920]{2,1,0:T(8,128)(2,1)S(1)} %fusion), channel_id=1, source_target_pairs={{0,1},{1,2},{2,3},{3,0},{4,5},{5,6},{6,7},{7,4},{8,9},{9,10},{10,1... | collective-permute-start | bytes 737288 | tf_op jit(solution)/shard_map/ppermute | solution.py:237
  153.6 10.0 %collective-permute-start.26 = (bf16[2,32,1920]{2,1,0:T(8,128)(2,1)S(1)}, bf16[2,32,1920]{2,1,0:T(8,128)(2,1)S(1)}, u32[]{:S(2)}, u32[]{:S(2)}) collective-permute-start(bf16[2,32,1920]{2,1,0:T(8,128)(2,1)S(1)} %fusion.8), channel_id=1, source_target_pairs={{0,8},{4,12},{8,0},{12,4},{16,24},{20,28},{24,16},{28,20},{1,9},{5... | collective-permute-start | bytes 737288 | tf_op jit(solution)/shard_map/ppermute | solution.py:226
  158.4 11.5 %collective-permute-start.31 = (bf16[2,32,1920]{2,1,0:T(8,128)(2,1)S(1)}, bf16[2,32,1920]{2,1,0:T(8,128)(2,1)S(1)}, u32[]{:S(2)}, u32[]{:S(2)}) collective-permute-start(bf16[2,32,1920]{2,1,0:T(8,128)(2,1)S(1)} %fusion.5), channel_id=1, source_target_pairs={{0,16},{4,20},{8,24},{12,28},{16,0},{20,4},{24,8},{28,12},{1,17},{... | collective-permute-start | bytes 737288 | tf_op jit(solution)/shard_map/ppermute | solution.py:226
  162.0 7.9 %collective-permute-start.36 = (bf16[2,32,1920]{2,1,0:T(8,128)(2,1)S(1)}, bf16[2,32,1920]{2,1,0:T(8,128)(2,1)S(1)}, u32[]{:S(2)}, u32[]{:S(2)}) collective-permute-start(bf16[2,32,1920]{2,1,0:T(8,128)(2,1)S(1)} %fusion.2), channel_id=1, source_target_pairs={{0,24},{4,28},{8,16},{12,20},{16,8},{20,12},{24,0},{28,4},{1,25},{... | collective-permute-start | bytes 737288 | tf_op jit(solution)/shard_map/ppermute | solution.py:226
  (3 other events, 3.0 us)

commit v4 on v3

--- a/solution.py
+++ b/solution.py
@@ -217,99 +217,87 @@
     head_dim = query_gain.shape[0]
     own_width, key_cols = key_weight.shape
     key_heads = key_cols // head_dim
+    cols = 2 * key_cols
     pairs = dp_size // 2
     width = 2 * own_width
     place = lax.axis_index("dp")
     pair, core = place // 2, place % 2
+    line = lax.axis_index("mp")
+    is_inner = (line == 1) | (line == 2)
 
     def swap(value, mask):
         return lax.ppermute(value, "dp", [(i, i ^ mask) for i in range(dp_size)])
 
+    def inward(value):
+        return lax.ppermute(value, "mp", [(0, 1), (3, 2)])
+
+    def outward(value):
+        return lax.ppermute(value, "mp", [(1, 0), (2, 3)])
+
+    def across(value):
+        return lax.ppermute(value, "mp", [(1, 2), (2, 1)])
+
     own_weight = jnp.concatenate((key_weight, value_weight), axis=1)
-    mate_weight = swap(own_weight, 1)
+    both_weight = jnp.concatenate((own_weight, inward(own_weight)), axis=1)
+    mate_weight = swap(both_weight, 1)
     weight = jnp.where(
         core == 0,
-        jnp.concatenate((own_weight, mate_weight), axis=0),
-        jnp.concatenate((mate_weight, own_weight), axis=0),
-    )
-
-    def ring(value, step):
-        return lax.ppermute(value, "mp", [(i, (i + step) % mp_size) for i in range(mp_size)])
-
-    half = mp_size // 2
+        jnp.concatenate((both_weight, mate_weight), axis=0),
+        jnp.concatenate((mate_weight, both_weight), axis=0),
+    )
+
     blocks = []
+    own_pieces = []
+    outer_total = 0.0
     for r in range(pairs):
         piece = lax.dynamic_slice_in_dim(images, (pair ^ r) * width, width, axis=2)
         piece = swap(piece, 2 * r) if r else piece
-        parts = [piece] + [None] * (mp_size - 1)
-        right = left = piece
-        for k in range(1, half + 1):
-            if k < half or r < pairs // 2:
-                parts[k] = right = ring(right, 1)
-            if k < half or r >= pairs // 2:
-                parts[mp_size - k] = left = ring(left, -1)
-        blocks.append(jnp.stack(parts))
-    img_rows = mp_size * own_rows
-    pieces = []
-    for r in range(pairs):
-        piece = jnp.dot(
-            blocks[r].reshape(-1, width), weight, preferred_element_type=jnp.float32
-        ).astype(jnp.bfloat16)
-        piece = swap(piece, 2 * r) if r else piece
-        pieces.append(piece.reshape(mp_size, img_count, own_rows, 2 * key_cols))
-    if pairs > 4:
-        pieces = [sum(piece.astype(jnp.float32) for piece in pieces)]
+        outer = inward(piece)
+        block = jnp.stack((piece, outer, across(piece), across(outer)))
+        blocks.append(block)
+        part = jnp.dot(block.reshape(-1, width), weight, preferred_element_type=jnp.float32)
+        part = part.astype(jnp.bfloat16)
+        part = swap(part, 2 * r) if r else part
+        own_pieces.append(part[:, :cols])
+        outer_total = outer_total + part[:, cols:].astype(jnp.float32)
+    given = outward(outer_total.astype(jnp.bfloat16))
+    own_total = sum(piece.astype(jnp.float32) for piece in own_pieces)
+    total = jnp.where(is_inner, own_total, given.astype(jnp.float32))
+    total = total.reshape(mp_size, img_count, own_rows, cols)
     query_gain, key_gain = query_gain[None, :], key_gain[None, :]
     normed, masked = before(queries, out_grad, query_gain, lengths, key_heads)
-    owners = (lax.axis_index("mp") - jnp.arange(mp_size, dtype=jnp.int32)) % mp_size
+    owners = jnp.where(
+        line < 2, jnp.array((1, 0, 2, 3), jnp.int32), jnp.array((2, 3, 1, 0), jnp.int32)
+    )
     key_rows, value_rows, score_grad, seq_keys = attend(
-        pieces, normed, masked, key_gain, assignment, tile_counts, owners
+        [total], normed, masked, key_gain, assignment, tile_counts, owners
     )
     query_grad = after(queries, score_grad, seq_keys, query_gain)
-    rows = jnp.concatenate((key_rows, value_rows), axis=3)
+
+    rows = jnp.concatenate((key_rows, value_rows), axis=3).reshape(-1, cols)
+    both_rows = jnp.concatenate((rows, inward(rows)), axis=1)
     all_rows = []
     image_grad = jnp.zeros((img_count, own_rows, vis_width), jnp.bfloat16)
     for r in range(pairs):
-        block_rows = (swap(rows, 2 * r) if r else rows).reshape(-1, 2 * key_cols)
+        block_rows = swap(both_rows, 2 * r) if r else both_rows
         all_rows.append(block_rows)
-        term = lax.dot_general(
-            block_rows, weight, (((1,), (1,)), ((), ())), preferred_element_type=jnp.float32
-        ).astype(jnp.bfloat16)
-        term = term.reshape(mp_size, img_count, own_rows, width)
-        total = term[0].astype(jnp.float32)
-        leftward = rightward = None
-        for k in range(half, 0, -1):
-            if k < half or r < pairs // 2:
-                own = term[k]
-                if leftward is not None:
-                    own = (own.astype(jnp.float32) + leftward.astype(jnp.float32)).astype(
-                        jnp.bfloat16
-                    )
-                leftward = ring(own, -1)
-            if k < half or r >= pairs // 2:
-                own = term[mp_size - k]
-                if rightward is not None:
-                    own = (own.astype(jnp.float32) + rightward.astype(jnp.float32)).astype(
-                        jnp.bfloat16
-                    )
-                rightward = ring(own, 1)
-        for arrived in (leftward, rightward):
-            if arrived is not None:
-                total = total + arrived.astype(jnp.float32)
-        piece = total.astype(jnp.bfloat16)
+        term = dot(block_rows, weight, 1, 1).reshape(mp_size, img_count, own_rows, width)
+        far = across(term[3].astype(jnp.bfloat16)).astype(jnp.float32)
+        near = across(term[2].astype(jnp.bfloat16)).astype(jnp.float32)
+        given = outward((term[1] + far).astype(jnp.bfloat16))
+        piece = jnp.where(is_inner, (term[0] + near).astype(jnp.bfloat16), given)
         image_grad = lax.dynamic_update_slice_in_dim(
             image_grad, swap(piece, 2 * r) if r else piece, (pair ^ r) * width, axis=2
         )
-    weight_part = lax.dot_general(
-        jnp.stack(blocks).reshape(-1, width),
-        jnp.stack(all_rows).reshape(-1, 2 * key_cols),
-        (((0,), (0,)), ((), ())),
-        preferred_element_type=jnp.float32,
+    weight_part = dot(
+        jnp.stack(blocks).reshape(-1, width), jnp.stack(all_rows).reshape(-1, 2 * cols), 0, 0
     )
     weight_grad = lax.dynamic_slice_in_dim(weight_part, core * own_width, own_width, axis=0)
     weight_grad = weight_grad + swap(
         lax.dynamic_slice_in_dim(weight_part, (1 - core) * own_width, own_width, axis=0), 1
     )
+    given = outward(weight_grad[:, cols:].astype(jnp.bfloat16)).astype(jnp.float32)
+    weight_grad = jnp.where(is_inner, weight_grad[:, :cols], given)
     return (query_grad, image_grad, weight_grad[:, :key_cols], weight_grad[:, key_cols:])
 
 

time: 173 us -> 262 us (1.51)
  waiting for transfers between devices: 79 us -> 137 us
  other arithmetic: 4.17 us -> 16.9 us
  matrix products: 9.97 us -> 18.8 us
  local copies, waits for them, and re-layouts: 6.64 us -> 13.3 us
    ppermute x24 -> x28, waiting for transfers between devices: 60.6 us -> 96.8 us  [the longest x6 71.1 us: outward(): return lax.ppermute(value, 'mp', [(1, 0), (2, 3)])]
    ppermute x14, waiting for transfers between devices: 18.4 us -> 40.1 us  [swap(): return lax.ppermute(value, 'dp', [(i, i ^ mask) for i in range(dp_size)])]
    dot_general x9, matrix products: 9.97 us -> 18.8 us  [the longest x5 13.8 us: dot(): lax.dot_general(left, right, (((left_dim,), (right_dim,)), ((), ())), pre...]
    select_n x1 -> x7, other arithmetic: 0.01 us -> 6.06 us  [the longest x1 4.06 us: per_device(): jnp.where(core == 0, jnp.concatenate((both_weight, mate_weight), axis=0),...]
    unnamed x28 -> x42, local copies, waits for them, and re-layouts: 2.38 us -> 7.98 us
    ppermute x24 -> x28, starting transfers between devices: 42.1 us -> 43.3 us  [the longest x6 23.5 us: inward(): return lax.ppermute(value, 'mp', [(0, 1), (3, 2)])]
  transfers between devices with their start and end apart: 38 -> 42, of which waited for: 17 -> 16; matrix products, arithmetic and copies ran while one was open for 7% -> 13% of each run, Pallas kernels for 5% -> 4%
where the time goes in v4:
time: 262 us; the launch traced here: 261 us
  waiting for transfers between devices  137 us (52%)
  starting transfers between devices  58.9 us (22%)
  matrix products  18.8 us (7%)
  other arithmetic  16.9 us (6%)
  Pallas kernels  14.2 us (5%)
  local copies, waits for them, and re-layouts  13.3 us (5%)
    ppermute x6, waiting for transfers between devices, outward(): return lax.ppermute(value, 'mp', [(1, 0), (2, 3)])  71.1 us
    ppermute x14, waiting for transfers between devices, swap(): return lax.ppermute(value, 'dp', [(i, i ^ mask) for i in range(dp_size)])  40.1 us
    ppermute x6, waiting for transfers between devices, inward(): return lax.ppermute(value, 'mp', [(0, 1), (3, 2)])  25.6 us
    ppermute x6, starting transfers between devices, inward(): return lax.ppermute(value, 'mp', [(0, 1), (3, 2)])  23.5 us
    ppermute x14, starting transfers between devices, swap(): return lax.ppermute(value, 'dp', [(i, i ^ mask) for i in range(dp_size)])  15.6 us
    dot_general x5, matrix products, dot(): lax.dot_general(left, right, (((left_dim,), (right_dim,)), ((), ())), pre...  13.8 us
    ppermute x16, starting transfers between devices, across(): return lax.ppermute(value, 'mp', [(1, 2), (2, 1)])  11.9 us
    unnamed x42, local copies, waits for them, and re-layouts  7.98 us
  transfers between devices with their start and end apart: 42, of which 16 were waited for; matrix products, arithmetic and copies ran while one was open for 13% of the time, Pallas kernels for 4%

profile of v4, /device:TPU:0, one launch (start us, length us, event | category | flops | bytes accessed | tf_op | source)
XLA Modules:
  0.0 260.6 jit_solution(16574120712182074237)
XLA Ops:
  0.6 1.3 pad_maximum_fusion.3
  2.0 5.0 %collective-permute-start.3 = (bf16[960,512]{1,0:T(8,128)(2,1)S(1)}, bf16[960,512]{1,0:T(8,128)(2,1)S(1)}, u32[]{:S(2)}, u32[]{:S(2)}) collective-permute-start(bf16[960,512]{1,0:T(8,128)(2,1)S(1)} %pad_maximum_fusion.3), channel_id=1, source_target_pairs={{0,1},{3,2},{4,5},{7,6},{8,9},{11,10},{12,13},{15,14},{16,17},{19,... | collective-permute-start | bytes 2949128 | tf_op jit(solution)/shard_map/ppermute | solution.py:232
  7.0 1.9 constant_dynamic-update-slice_fusion.2
  8.9 1.9 constant_dynamic-update-slice_fusion.1
  10.8 17.1 %collective-permute-done.3 = bf16[960,512]{1,0:T(8,128)(2,1)S(1)} collective-permute-done((bf16[960,512]{1,0:T(8,128)(2,1)S(1)}, bf16[960,512]{1,0:T(8,128)(2,1)S(1)}, u32[]{:S(2)}, u32[]{:S(2)}) %collective-permute-start.3) | collective-permute-done | bytes 983072 | tf_op jit(solution)/shard_map/ppermute | solution.py:232
  29.1 2.5 collective-permute-start.15
  32.1 6.4 %collective-permute-done.15 = bf16[2,32,1920]{2,1,0:T(8,128)(2,1)S(1)} collective-permute-done((bf16[2,32,1920]{2,1,0:T(8,128)(2,1)S(1)}, bf16[2,32,1920]{2,1,0:T(8,128)(2,1)S(1)}, u32[]{:S(2)}, u32[]{:S(2)}) %collective-permute-start.15) | collective-permute-done | bytes 245792 | tf_op jit(solution)/shard_map/ppermute | solution.py:229
  38.5 4.4 %collective-permute-start.16 = (bf16[2,32,1920]{2,1,0:T(8,128)(2,1)S(1)}, bf16[2,32,1920]{2,1,0:T(8,128)(2,1)S(1)}, u32[]{:S(2)}, u32[]{:S(2)}) collective-permute-start(bf16[2,32,1920]{2,1,0:T(8,128)(2,1)S(1)} %collective-permute-done.15), channel_id=1, source_target_pairs={{0,1},{3,2},{4,5},{7,6},{8,9},{11,10},{12,13},{15,14},{16,17},{19,... | collective-permute-start | bytes 737288 | tf_op jit(solution)/shard_map/ppermute | solution.py:232
  42.9 1.6 collective-permute-start.5
  45.2 4.1 %collective-permute-start.11 = (bf16[2,32,1920]{2,1,0:T(8,128)(2,1)S(1)}, bf16[2,32,1920]{2,1,0:T(8,128)(2,1)S(1)}, u32[]{:S(2)}, u32[]{:S(2)}) collective-permute-start(bf16[2,32,1920]{2,1,0:T(8,128)(2,1)S(1)} %collective-permute-done.10), channel_id=1, source_target_pairs={{0,1},{3,2},{4,5},{7,6},{8,9},{11,10},{12,13},{15,14},{16,17},{19,... | collective-permute-start | bytes 737288 | tf_op jit(solution)/shard_map/ppermute | solution.py:232
  50.2 5.6 %collective-permute-start = (bf16[2,32,1920]{2,1,0:T(8,128)(2,1)S(1)}, bf16[2,32,1920]{2,1,0:T(8,128)(2,1)S(1)}, u32[]{:S(2)}, u32[]{:S(2)}) collective-permute-start(bf16[2,32,1920]{2,1,0:T(8,128)(2,1)S(1)} %get-tuple-element.42), channel_id=1, source_target_pairs={{0,1},{3,2},{4,5},{7,6},{8,9},{11,10},{12,13},{15,14},{16,17},{19,... | collective-permute-start | bytes 737288 | tf_op jit(solution)/shard_map/ppermute | solution.py:232
  56.6 3.0 %collective-permute-start.6 = (bf16[2,32,1920]{2,1,0:T(8,128)(2,1)S(1)}, bf16[2,32,1920]{2,1,0:T(8,128)(2,1)S(1)}, u32[]{:S(2)}, u32[]{:S(2)}) collective-permute-start(bf16[2,32,1920]{2,1,0:T(8,128)(2,1)S(1)} %collective-permute-done.5), channel_id=1, source_target_pairs={{0,1},{3,2},{4,5},{7,6},{8,9},{11,10},{12,13},{15,14},{16,17},{19,... | collective-permute-start | bytes 737288 | tf_op jit(solution)/shard_map/ppermute | solution.py:232
  62.9 2.0 collective-permute-done.6
  66.7 4.1 %maximum_select_fusion = bf16[1920,1024]{1,0:T(8,128)(2,1)S(1)} fusion(bf16[960,1024]{1,0:T(8,128)(2,1)} %collective-permute-done.4, bf16[960,1024]{1,0:T(8,128)(2,1)} %constant_dynamic-update-slice_fusion, pred[]{:T(512)S(6)} %eq.13), kind=kLoop, calls=%fused_computation | loop fusion | flops 17694720 | bytes 7864321 | tf_op jit(solution)/shard_map/jit(_where)/select_n | solution.py:243
  70.8 1.2 convolution_convert_fusion
  72.1 3.3 %collective-permute-start.19 = (bf16[256,1024]{1,0:T(8,128)(2,1)S(1)}, bf16[256,1024]{1,0:T(8,128)(2,1)S(1)}, u32[]{:S(2)}, u32[]{:S(2)}) collective-permute-start(bf16[256,1024]{1,0:T(8,128)(2,1)S(1)} %convolution_convert_fusion), channel_id=1, source_target_pairs={{0,24},{4,28},{8,16},{12,20},{16,8},{20,12},{24,0},{28,4},{1,25},{... | collective-permute-start | bytes 1572872 | tf_op jit(solution)/shard_map/ppermute | solution.py:229
  81.0 7.2 %collective-permute-done.19 = bf16[256,1024]{1,0:T(8,128)(2,1)S(1)} collective-permute-done((bf16[256,1024]{1,0:T(8,128)(2,1)S(1)}, bf16[256,1024]{1,0:T(8,128)(2,1)S(1)}, u32[]{:S(2)}, u32[]{:S(2)}) %collective-permute-start.19) | collective-permute-done | bytes 524320 | tf_op jit(solution)/shard_map/ppermute | solution.py:229
  88.2 8.1 %collective-permute-done.14 = bf16[256,1024]{1,0:T(8,128)(2,1)S(1)} collective-permute-done((bf16[256,1024]{1,0:T(8,128)(2,1)S(1)}, bf16[256,1024]{1,0:T(8,128)(2,1)S(1)}, u32[]{:S(2)}, u32[]{:S(2)}) %collective-permute-start.14) | collective-permute-done | bytes 524320 | tf_op jit(solution)/shard_map/ppermute | solution.py:229
  97.4 1.3 collective-permute-start.20
  98.7 4.8 %before.1 = (bf16[2,2,1024,128]{3,2,1,0:T(8,128)(2,1)}, bf16[2,2,1024,128]{3,2,1,0:T(8,128)(2,1)}) custom-call(s32[2]{0:T(128)} %lengths.1, bf16[2,128,2048]{2,1,0:T(8,128)(2,1)} %query.3, bf16[2,128,2048]{2,1,0:T(8,128)(2,1)} %grad.1, f32[1,128]{1,0:T(1,128)} %bitcast.118), custom_call_target="tpu_custom_call" | custom-call | tf_op jit(solution)/shard_map/before/pallas_call | solution.py:58
  103.6 25.9 %collective-permute-done.20 = bf16[256,512]{1,0:T(8,128)(2,1)} collective-permute-done((bf16[256,512]{1,0:T(8,128)(2,1)}, bf16[256,512]{1,0:T(8,128)(2,1)}, u32[]{:S(2)}, u32[]{:S(2)}) %collective-permute-start.20) | collective-permute-done | bytes 262176 | tf_op jit(solution)/shard_map/ppermute | solution.py:235
  129.5 1.4 convert_select_fusion
  133.4 5.0 %attend.1 = (bf16[4,2,32,256]{3,2,1,0:T(8,128)(2,1)S(1)}, bf16[4,2,32,256]{3,2,1,0:T(8,128)(2,1)S(1)}, bf16[2,2,1024,128]{3,2,1,0:T(8,128)(2,1)S(1)}, bf16[2,2,128,128]{3,2,1,0:T(8,128)(2,1)S(1)}) custom-call(s32[2]{0:T(128)S(1)} %copy-done.4, s32[2]{0:T(128)S(1)} %copy-done.5, s32[4]{0:T(128)S(1)} %broadcast_select_fusion.owners, ...), custom_call_target="tpu_custom_call" | custom-call | tf_op jit(solution)/shard_map/attend/pallas_call | solution.py:137
  140.0 1.5 collective-permute-start.21
  141.5 5.3 %collective-permute-done.21 = bf16[256,512]{1,0:T(8,128)(2,1)S(1)} collective-permute-done((bf16[256,512]{1,0:T(8,128)(2,1)S(1)}, bf16[256,512]{1,0:T(8,128)(2,1)S(1)}, u32[]{:S(2)}, u32[]{:S(2)}) %collective-permute-start.21) | collective-permute-done | bytes 262176 | tf_op jit(solution)/shard_map/ppermute | solution.py:232
  146.8 3.4 %fusion.20 = (bf16[256,1920]{1,0:T(8,128)(2,1)S(1)}, f32[256,1920]{1,0:T(8,128)S(1)}) fusion(bf16[1920,1024]{1,0:T(8,128)(2,1)} %copy-done.7, bf16[256,512]{1,0:T(8,128)(2,1)S(1)} %collective-permute-done.21, bf16[256,512]{1,0:T(8,128)(2,1)S(1)} %bitcast.77), kind=kOutput, calls=%fused_computation.59 | convolution fusion | flops 1008173056 | bytes 7405568 | tf_op jit(solution)/shard_map/dot_general | solution.py:29
  151.6 1.4 collective-permute-start.22
  154.1 1.5 collective-permute-start.25
  157.2 1.5 collective-permute-start.24
  158.7 2.2 pad_maximum_fusion
  160.9 4.4 %after.1 = bf16[2,128,2048]{2,1,0:T(8,128)(2,1)} custom-call(bf16[2,128,2048]{2,1,0:T(8,128)(2,1)} %query.3, bf16[2,2,1024,128]{3,2,1,0:T(8,128)(2,1)} %copy-done, bf16[2,2,128,128]{3,2,1,0:T(8,128)(2,1)} %copy-done.3, f32[1,128]{1,0:T(1,128)} %bitcast.119), custom_call_target="tpu_custom_call" | custom-call | tf_op jit(solution)/shard_map/after/pallas_call | solution.py:187
  167.3 3.1 %collective-permute-done.24 = bf16[2,32,1920]{2,1,0:T(8,128)(2,1)} collective-permute-done((bf16[2,32,1920]{2,1,0:T(8,128)(2,1)}, bf16[2,32,1920]{2,1,0:T(8,128)(2,1)}, u32[]{:S(2)}, u32[]{:S(2)}) %collective-permute-start.24) | collective-permute-done | bytes 245792 | tf_op jit(solution)/shard_map/ppermute | solution.py:235
  171.7 3.5 %fusion.21 = (bf16[256,1920]{1,0:T(8,128)(2,1)S(1)}, f32[256,1920]{1,0:T(8,128)S(1)}) fusion(bf16[256,1024]{1,0:T(8,128)(2,1)S(1)} %collective-permute-done.25, bf16[1920,1024]{1,0:T(8,128)(2,1)} %copy-done.7), kind=kOutput, calls=%fused_computation.60 | convolution fusion | flops 1007124480 | bytes 7405568 | tf_op jit(solution)/shard_map/dot_general | solution.py:29
  176.8 12.2 %collective-permute-done.30 = bf16[256,1024]{1,0:T(8,128)(2,1)S(1)} collective-permute-done((bf16[256,1024]{1,0:T(8,128)(2,1)}, bf16[256,1024]{1,0:T(8,128)(2,1)S(1)}, u32[]{:S(2)}, u32[]{:S(2)}) %collective-permute-start.30) | collective-permute-done | bytes 524320 | tf_op jit(solution)/shard_map/ppermute | solution.py:229
  189.0 1.3 fusion.22
  192.4 4.3 %fusion.24 = f32[1920,1024]{1,0:T(8,128)S(1)} fusion(bf16[1024,1920]{1,0:T(8,128)(2,1)S(1)} %bitcast.75, bf16[1024,1024]{1,0:T(8,128)(2,1)S(1)} %bitcast.82), kind=kOutput, calls=%fused_computation.63 | convolution fusion | flops 4026531840 | bytes 13893632 | tf_op jit(solution)/shard_map/dot_general | solution.py:29
  197.3 1.3 fusion.23
  200.3 1.3 collective-permute-start.28
  201.7 1.3 collective-permute-start.33
  203.0 25.2 %collective-permute-done.28 = bf16[2,32,1920]{2,1,0:T(8,128)(2,1)S(1)} collective-permute-done((bf16[2,32,1920]{2,1,0:T(8,128)(2,1)S(1)}, bf16[2,32,1920]{2,1,0:T(8,128)(2,1)S(1)}, u32[]{:S(2)}, u32[]{:S(2)}) %collective-permute-start.28) | collective-permute-done | bytes 245792 | tf_op jit(solution)/shard_map/ppermute | solution.py:235
  228.2 1.3 collective-permute-start.38
  230.2 3.2 %collective-permute-done.33 = bf16[2,32,1920]{2,1,0:T(8,128)(2,1)S(1)} collective-permute-done((bf16[2,32,1920]{2,1,0:T(8,128)(2,1)S(1)}, bf16[2,32,1920]{2,1,0:T(8,128)(2,1)S(1)}, u32[]{:S(2)}, u32[]{:S(2)}) %collective-permute-start.33) | collective-permute-done | bytes 245792 | tf_op jit(solution)/shard_map/ppermute | solution.py:235
  234.8 1.3 dynamic-slice_add_fusion
  236.2 1.3 collective-permute-start.41
  237.6 1.6 collective-permute-start.39
  239.2 5.9 %collective-permute-done.34 = bf16[2,32,1920]{2,1,0:T(8,128)(2,1)S(1)} collective-permute-done((bf16[2,32,1920]{2,1,0:T(8,128)(2,1)S(1)}, bf16[2,32,1920]{2,1,0:T(8,128)(2,1)S(1)}, u32[]{:S(2)}, u32[]{:S(2)}) %collective-permute-start.34) | collective-permute-done | bytes 245792 | tf_op jit(solution)/shard_map/ppermute | solution.py:229
  245.2 13.6 %collective-permute-done.41 = bf16[960,512]{1,0:T(8,128)(2,1)S(1)} collective-permute-done((bf16[960,512]{1,0:T(8,128)(2,1)S(1)}, bf16[960,512]{1,0:T(8,128)(2,1)S(1)}, u32[]{:S(2)}, u32[]{:S(2)}) %collective-permute-start.41) | collective-permute-done | bytes 983072 | tf_op jit(solution)/shard_map/ppermute | solution.py:235
  259.1 1.4 fusion.11
  (130 shorter events, 35.7 us)
Async XLA Ops:
  0.6 28.4 %copy-start.13 = (bf16[2,32,7680]{2,1,0:T(8,128)(2,1)S(1)}, bf16[2,32,7680]{2,1,0:T(8,128)(2,1)}, u32[]{:S(2)}) copy-start(bf16[2,32,7680]{2,1,0:T(8,128)(2,1)} %param.14) | copy-start | bytes 2949124
  2.0 25.9 %collective-permute-start.3 = (bf16[960,512]{1,0:T(8,128)(2,1)S(1)}, bf16[960,512]{1,0:T(8,128)(2,1)S(1)}, u32[]{:S(2)}, u32[]{:S(2)}) collective-permute-start(bf16[960,512]{1,0:T(8,128)(2,1)S(1)} %pad_maximum_fusion.3), channel_id=1, source_target_pairs={{0,1},{3,2},{4,5},{7,6},{8,9},{11,10},{12,13},{15,14},{16,17},{19,... | collective-permute-start | bytes 2949128 | tf_op jit(solution)/shard_map/ppermute | solution.py:232
  29.0 37.7 %collective-permute-start.4 = (bf16[960,1024]{1,0:T(8,128)(2,1)}, bf16[960,1024]{1,0:T(8,128)(2,1)}, u32[]{:S(2)}, u32[]{:S(2)}) collective-permute-start(bf16[960,1024]{1,0:T(8,128)(2,1)} %constant_dynamic-update-slice_fusion), channel_id=1, source_target_pairs={{0,4},{4,0},{8,12},{12,8},{16,20},{20,16},{24,28},{28,24},{1,5},{5... | collective-permute-start | bytes 5898248 | tf_op jit(solution)/shard_map/ppermute | solution.py:229
  29.1 9.4 %collective-permute-start.15 = (bf16[2,32,1920]{2,1,0:T(8,128)(2,1)S(1)}, bf16[2,32,1920]{2,1,0:T(8,128)(2,1)S(1)}, u32[]{:S(2)}, u32[]{:S(2)}) collective-permute-start(bf16[2,32,1920]{2,1,0:T(8,128)(2,1)S(1)} %get-tuple-element.44), channel_id=1, source_target_pairs={{0,24},{4,28},{8,16},{12,20},{16,8},{20,12},{24,0},{28,4},{1,25},{... | collective-permute-start | bytes 737288 | tf_op jit(solution)/shard_map/ppermute | solution.py:229
  31.6 13.6 %collective-permute-start.10 = (bf16[2,32,1920]{2,1,0:T(8,128)(2,1)S(1)}, bf16[2,32,1920]{2,1,0:T(8,128)(2,1)S(1)}, u32[]{:S(2)}, u32[]{:S(2)}) collective-permute-start(bf16[2,32,1920]{2,1,0:T(8,128)(2,1)S(1)} %get-tuple-element.45), channel_id=1, source_target_pairs={{0,16},{4,20},{8,24},{12,28},{16,0},{20,4},{24,8},{28,12},{1,17},{... | collective-permute-start | bytes 737288 | tf_op jit(solution)/shard_map/ppermute | solution.py:229
  38.5 10.7 %collective-permute-start.16 = (bf16[2,32,1920]{2,1,0:T(8,128)(2,1)S(1)}, bf16[2,32,1920]{2,1,0:T(8,128)(2,1)S(1)}, u32[]{:S(2)}, u32[]{:S(2)}) collective-permute-start(bf16[2,32,1920]{2,1,0:T(8,128)(2,1)S(1)} %collective-permute-done.15), channel_id=1, source_target_pairs={{0,1},{3,2},{4,5},{7,6},{8,9},{11,10},{12,13},{15,14},{16,17},{19,... | collective-permute-start | bytes 737288 | tf_op jit(solution)/shard_map/ppermute | solution.py:232
  42.9 7.3 %collective-permute-start.5 = (bf16[2,32,1920]{2,1,0:T(8,128)(2,1)S(1)}, bf16[2,32,1920]{2,1,0:T(8,128)(2,1)S(1)}, u32[]{:S(2)}, u32[]{:S(2)}) collective-permute-start(bf16[2,32,1920]{2,1,0:T(8,128)(2,1)S(1)} %get-tuple-element.43), channel_id=1, source_target_pairs={{0,8},{4,12},{8,0},{12,4},{16,24},{20,28},{24,16},{28,20},{1,9},{5... | collective-permute-start | bytes 737288 | tf_op jit(solution)/shard_map/ppermute | solution.py:229
  44.5 11.4 %collective-permute-start.17 = (bf16[2,32,1920]{2,1,0:T(8,128)(2,1)S(1)}, bf16[2,32,1920]{2,1,0:T(8,128)(2,1)S(1)}, u32[]{:S(2)}, u32[]{:S(2)}) collective-permute-start(bf16[2,32,1920]{2,1,0:T(8,128)(2,1)S(1)} %collective-permute-done.15), channel_id=1, source_target_pairs={{1,2},{2,1},{5,6},{6,5},{9,10},{10,9},{13,14},{14,13},{17,18},{18,... | collective-permute-start | bytes 737288 | tf_op jit(solution)/shard_map/ppermute | solution.py:238
  45.2 11.4 %collective-permute-start.11 = (bf16[2,32,1920]{2,1,0:T(8,128)(2,1)S(1)}, bf16[2,32,1920]{2,1,0:T(8,128)(2,1)S(1)}, u32[]{:S(2)}, u32[]{:S(2)}) collective-permute-start(bf16[2,32,1920]{2,1,0:T(8,128)(2,1)S(1)} %collective-permute-done.10), channel_id=1, source_target_pairs={{0,1},{3,2},{4,5},{7,6},{8,9},{11,10},{12,13},{15,14},{16,17},{19,... | collective-permute-start | bytes 737288 | tf_op jit(solution)/shard_map/ppermute | solution.py:232
  49.3 10.3 %collective-permute-start.18 = (bf16[2,32,1920]{2,1,0:T(8,128)(2,1)S(1)}, bf16[2,32,1920]{2,1,0:T(8,128)(2,1)S(1)}, u32[]{:S(2)}, u32[]{:S(2)}) collective-permute-start(bf16[2,32,1920]{2,1,0:T(8,128)(2,1)S(1)} %collective-permute-done.16), channel_id=1, source_target_pairs={{1,2},{2,1},{5,6},{6,5},{9,10},{10,9},{13,14},{14,13},{17,18},{18,... | collective-permute-start | bytes 737288 | tf_op jit(solution)/shard_map/ppermute | solution.py:238
  50.2 11.3 %collective-permute-start = (bf16[2,32,1920]{2,1,0:T(8,128)(2,1)S(1)}, bf16[2,32,1920]{2,1,0:T(8,128)(2,1)S(1)}, u32[]{:S(2)}, u32[]{:S(2)}) collective-permute-start(bf16[2,32,1920]{2,1,0:T(8,128)(2,1)S(1)} %get-tuple-element.42), channel_id=1, source_target_pairs={{0,1},{3,2},{4,5},{7,6},{8,9},{11,10},{12,13},{15,14},{16,17},{19,... | collective-permute-start | bytes 737288 | tf_op jit(solution)/shard_map/ppermute | solution.py:232
  55.9 6.4 %collective-permute-start.12 = (bf16[2,32,1920]{2,1,0:T(8,128)(2,1)S(1)}, bf16[2,32,1920]{2,1,0:T(8,128)(2,1)S(1)}, u32[]{:S(2)}, u32[]{:S(2)}) collective-permute-start(bf16[2,32,1920]{2,1,0:T(8,128)(2,1)S(1)} %collective-permute-done.10), channel_id=1, source_target_pairs={{1,2},{2,1},{5,6},{6,5},{9,10},{10,9},{13,14},{14,13},{17,18},{18,... | collective-permute-start | bytes 737288 | tf_op jit(solution)/shard_map/ppermute | solution.py:238
  56.6 8.4 %collective-permute-start.6 = (bf16[2,32,1920]{2,1,0:T(8,128)(2,1)S(1)}, bf16[2,32,1920]{2,1,0:T(8,128)(2,1)S(1)}, u32[]{:S(2)}, u32[]{:S(2)}) collective-permute-start(bf16[2,32,1920]{2,1,0:T(8,128)(2,1)S(1)} %collective-permute-done.5), channel_id=1, source_target_pairs={{0,1},{3,2},{4,5},{7,6},{8,9},{11,10},{12,13},{15,14},{16,17},{19,... | collective-permute-start | bytes 737288 | tf_op jit(solution)/shard_map/ppermute | solution.py:232
  59.5 6.1 %collective-permute-start.13 = (bf16[2,32,1920]{2,1,0:T(8,128)(2,1)S(1)}, bf16[2,32,1920]{2,1,0:T(8,128)(2,1)S(1)}, u32[]{:S(2)}, u32[]{:S(2)}) collective-permute-start(bf16[2,32,1920]{2,1,0:T(8,128)(2,1)S(1)} %collective-permute-done.11), channel_id=1, source_target_pairs={{1,2},{2,1},{5,6},{6,5},{9,10},{10,9},{13,14},{14,13},{17,18},{18,... | collective-permute-start | bytes 737288 | tf_op jit(solution)/shard_map/ppermute | solution.py:238
  61.6 17.0 %collective-permute-start.1 = (bf16[2,32,1920]{2,1,0:T(8,128)(2,1)S(1)}, bf16[2,32,1920]{2,1,0:T(8,128)(2,1)S(1)}, u32[]{:S(2)}, u32[]{:S(2)}) collective-permute-start(bf16[2,32,1920]{2,1,0:T(8,128)(2,1)S(1)} %get-tuple-element.42), channel_id=1, source_target_pairs={{1,2},{2,1},{5,6},{6,5},{9,10},{10,9},{13,14},{14,13},{17,18},{18,... | collective-permute-start | bytes 737288 | tf_op jit(solution)/shard_map/ppermute | solution.py:238
  62.2 4.3 %collective-permute-start.7 = (bf16[2,32,1920]{2,1,0:T(8,128)(2,1)S(1)}, bf16[2,32,1920]{2,1,0:T(8,128)(2,1)S(1)}, u32[]{:S(2)}, u32[]{:S(2)}) collective-permute-start(bf16[2,32,1920]{2,1,0:T(8,128)(2,1)S(1)} %collective-permute-done.5), channel_id=1, source_target_pairs={{1,2},{2,1},{5,6},{6,5},{9,10},{10,9},{13,14},{14,13},{17,18},{18,... | collective-permute-start | bytes 737288 | tf_op jit(solution)/shard_map/ppermute | solution.py:238
  65.0 13.6 %collective-permute-start.2 = (bf16[2,32,1920]{2,1,0:T(8,128)(2,1)S(1)}, bf16[2,32,1920]{2,1,0:T(8,128)(2,1)S(1)}, u32[]{:S(2)}, u32[]{:S(2)}) collective-permute-start(bf16[2,32,1920]{2,1,0:T(8,128)(2,1)S(1)} %collective-permute-done), channel_id=1, source_target_pairs={{1,2},{2,1},{5,6},{6,5},{9,10},{10,9},{13,14},{14,13},{17,18},{18,... | collective-permute-start | bytes 737288 | tf_op jit(solution)/shard_map/ppermute | solution.py:238
  65.6 0.9 collective-permute-start.8
  72.1 16.2 %collective-permute-start.19 = (bf16[256,1024]{1,0:T(8,128)(2,1)S(1)}, bf16[256,1024]{1,0:T(8,128)(2,1)S(1)}, u32[]{:S(2)}, u32[]{:S(2)}) collective-permute-start(bf16[256,1024]{1,0:T(8,128)(2,1)S(1)} %convolution_convert_fusion), channel_id=1, source_target_pairs={{0,24},{4,28},{8,16},{12,20},{16,8},{20,12},{24,0},{28,4},{1,25},{... | collective-permute-start | bytes 1572872 | tf_op jit(solution)/shard_map/ppermute | solution.py:229
  76.6 19.7 %collective-permute-start.14 = (bf16[256,1024]{1,0:T(8,128)(2,1)S(1)}, bf16[256,1024]{1,0:T(8,128)(2,1)S(1)}, u32[]{:S(2)}, u32[]{:S(2)}) collective-permute-start(bf16[256,1024]{1,0:T(8,128)(2,1)S(1)} %convolution_convert_fusion.1), channel_id=1, source_target_pairs={{0,16},{4,20},{8,24},{12,28},{16,0},{20,4},{24,8},{28,12},{1,17},{... | collective-permute-start | bytes 1572872 | tf_op jit(solution)/shard_map/ppermute | solution.py:229
  77.9 18.5 %collective-permute-start.9 = (bf16[256,1024]{1,0:T(8,128)(2,1)S(1)}, bf16[256,1024]{1,0:T(8,128)(2,1)S(1)}, u32[]{:S(2)}, u32[]{:S(2)}) collective-permute-start(bf16[256,1024]{1,0:T(8,128)(2,1)S(1)} %convolution_convert_fusion.2), channel_id=1, source_target_pairs={{0,8},{4,12},{8,0},{12,4},{16,24},{20,28},{24,16},{28,20},{1,9},{5... | collective-permute-start | bytes 1572872 | tf_op jit(solution)/shard_map/ppermute | solution.py:229
  79.7 23.8 %copy-start.18 = (s32[4]{0:T(128)S(1)}, s32[4]{0:T(128)}, u32[]{:S(2)}) copy-start(s32[4]{0:T(128)} %constant.49.clone) | copy-start | bytes 52
  79.7 23.8 %copy-start.19 = (s32[4]{0:T(128)S(1)}, s32[4]{0:T(128)}, u32[]{:S(2)}) copy-start(s32[4]{0:T(128)} %constant.50.clone) | copy-start | bytes 52
  81.0 49.9 %copy-start.4 = (s32[2]{0:T(128)S(1)}, s32[2]{0:T(128)}, u32[]{:S(2)}) copy-start(s32[2]{0:T(128)} %assignment.1) | copy-start | bytes 28
  81.0 49.9 %copy-start.5 = (s32[2]{0:T(128)S(1)}, s32[2]{0:T(128)}, u32[]{:S(2)}) copy-start(s32[2]{0:T(128)} %tiles.1) | copy-start | bytes 28
  81.0 49.9 %copy-start.6 = (f32[128]{0:T(128)S(1)}, f32[128]{0:T(128)}, u32[]{:S(2)}) copy-start(f32[128]{0:T(128)} %param.18) | copy-start | bytes 1540
  97.4 32.1 %collective-permute-start.20 = (bf16[256,512]{1,0:T(8,128)(2,1)}, bf16[256,512]{1,0:T(8,128)(2,1)}, u32[]{:S(2)}, u32[]{:S(2)}) collective-permute-start(bf16[256,512]{1,0:T(8,128)(2,1)} %add_convert_fusion), channel_id=1, source_target_pairs={{1,0},{2,3},{5,4},{6,7},{9,8},{10,11},{13,12},{14,15},{17,16},{18,... | collective-permute-start | bytes 786440 | tf_op jit(solution)/shard_map/ppermute | solution.py:235
  140.0 6.8 %collective-permute-start.21 = (bf16[256,512]{1,0:T(8,128)(2,1)S(1)}, bf16[256,512]{1,0:T(8,128)(2,1)S(1)}, u32[]{:S(2)}, u32[]{:S(2)}) collective-permute-start(bf16[256,512]{1,0:T(8,128)(2,1)S(1)} %bitcast.76), channel_id=1, source_target_pairs={{0,1},{3,2},{4,5},{7,6},{8,9},{11,10},{12,13},{15,14},{16,17},{19,... | collective-permute-start | bytes 786440 | tf_op jit(solution)/shard_map/ppermute | solution.py:232
  151.0 5.5 %collective-permute-start.23 = (bf16[2,32,1920]{2,1,0:T(8,128)(2,1)S(1)}, bf16[2,32,1920]{2,1,0:T(8,128)(2,1)S(1)}, u32[]{:S(2)}, u32[]{:S(2)}) collective-permute-start(bf16[2,32,1920]{2,1,0:T(8,128)(2,1)S(1)} %bitcast.116), channel_id=1, source_target_pairs={{1,2},{2,1},{5,6},{6,5},{9,10},{10,9},{13,14},{14,13},{17,18},{18,... | collective-permute-start | bytes 737288 | tf_op jit(solution)/shard_map/ppermute | solution.py:238
  151.6 15.7 %collective-permute-start.22 = (bf16[2,32,1920]{2,1,0:T(8,128)(2,1)}, bf16[2,32,1920]{2,1,0:T(8,128)(2,1)}, u32[]{:S(2)}, u32[]{:S(2)}) collective-permute-start(bf16[2,32,1920]{2,1,0:T(8,128)(2,1)} %bitcast.25), channel_id=1, source_target_pairs={{1,2},{2,1},{5,6},{6,5},{9,10},{10,9},{13,14},{14,13},{17,18},{18,... | collective-permute-start | bytes 737288 | tf_op jit(solution)/shard_map/ppermute | solution.py:238
  154.1 17.6 %collective-permute-start.25 = (bf16[256,1024]{1,0:T(8,128)(2,1)}, bf16[256,1024]{1,0:T(8,128)(2,1)S(1)}, u32[]{:S(2)}, u32[]{:S(2)}) collective-permute-start(bf16[256,1024]{1,0:T(8,128)(2,1)} %get-tuple-element.47), channel_id=1, source_target_pairs={{0,8},{4,12},{8,0},{12,4},{16,24},{20,28},{24,16},{28,20},{1,9},{5... | collective-permute-start | bytes 1572872 | tf_op jit(solution)/shard_map/ppermute | solution.py:229
  157.2 13.2 %collective-permute-start.24 = (bf16[2,32,1920]{2,1,0:T(8,128)(2,1)}, bf16[2,32,1920]{2,1,0:T(8,128)(2,1)}, u32[]{:S(2)}, u32[]{:S(2)}) collective-permute-start(bf16[2,32,1920]{2,1,0:T(8,128)(2,1)} %add_convert_fusion.7), channel_id=1, source_target_pairs={{1,0},{2,3},{5,4},{6,7},{9,8},{10,11},{13,12},{14,15},{17,16},{18,... | collective-permute-start | bytes 737288 | tf_op jit(solution)/shard_map/ppermute | solution.py:235
  165.3 23.7 %collective-permute-start.30 = (bf16[256,1024]{1,0:T(8,128)(2,1)}, bf16[256,1024]{1,0:T(8,128)(2,1)S(1)}, u32[]{:S(2)}, u32[]{:S(2)}) collective-permute-start(bf16[256,1024]{1,0:T(8,128)(2,1)} %get-tuple-element.47), channel_id=1, source_target_pairs={{0,16},{4,20},{8,24},{12,28},{16,0},{20,4},{24,8},{28,12},{1,17},{... | collective-permute-start | bytes 1572872 | tf_op jit(solution)/shard_map/ppermute | solution.py:229
  166.1 26.0 %collective-permute-start.35 = (bf16[256,1024]{1,0:T(8,128)(2,1)}, bf16[256,1024]{1,0:T(8,128)(2,1)S(1)}, u32[]{:S(2)}, u32[]{:S(2)}) collective-permute-start(bf16[256,1024]{1,0:T(8,128)(2,1)} %get-tuple-element.47), channel_id=1, source_target_pairs={{0,24},{4,28},{8,16},{12,20},{16,8},{20,12},{24,0},{28,4},{1,25},{... | collective-permute-start | bytes 1572872 | tf_op jit(solution)/shard_map/ppermute | solution.py:229
  175.3 23.5 %collective-permute-start.27 = (bf16[2,32,1920]{2,1,0:T(8,128)(2,1)S(1)}, bf16[2,32,1920]{2,1,0:T(8,128)(2,1)S(1)}, u32[]{:S(2)}, u32[]{:S(2)}) collective-permute-start(bf16[2,32,1920]{2,1,0:T(8,128)(2,1)S(1)} %bitcast.114), channel_id=1, source_target_pairs={{1,2},{2,1},{5,6},{6,5},{9,10},{10,9},{13,14},{14,13},{17,18},{18,... | collective-permute-start | bytes 737288 | tf_op jit(solution)/shard_map/ppermute | solution.py:238
  176.0 25.7 %collective-permute-start.26 = (bf16[2,32,1920]{2,1,0:T(8,128)(2,1)S(1)}, bf16[2,32,1920]{2,1,0:T(8,128)(2,1)S(1)}, u32[]{:S(2)}, u32[]{:S(2)}) collective-permute-start(bf16[2,32,1920]{2,1,0:T(8,128)(2,1)S(1)} %bitcast.112), channel_id=1, source_target_pairs={{1,2},{2,1},{5,6},{6,5},{9,10},{10,9},{13,14},{14,13},{17,18},{18,... | collective-permute-start | bytes 737288 | tf_op jit(solution)/shard_map/ppermute | solution.py:238
  190.3 9.2 %collective-permute-start.32 = (bf16[2,32,1920]{2,1,0:T(8,128)(2,1)S(1)}, bf16[2,32,1920]{2,1,0:T(8,128)(2,1)S(1)}, u32[]{:S(2)}, u32[]{:S(2)}) collective-permute-start(bf16[2,32,1920]{2,1,0:T(8,128)(2,1)S(1)} %bitcast.115), channel_id=1, source_target_pairs={{1,2},{2,1},{5,6},{6,5},{9,10},{10,9},{13,14},{14,13},{17,18},{18,... | collective-permute-start | bytes 737288 | tf_op jit(solution)/shard_map/ppermute | solution.py:238
  191.2 38.4 %collective-permute-start.31 = (bf16[2,32,1920]{2,1,0:T(8,128)(2,1)S(1)}, bf16[2,32,1920]{2,1,0:T(8,128)(2,1)S(1)}, u32[]{:S(2)}, u32[]{:S(2)}) collective-permute-start(bf16[2,32,1920]{2,1,0:T(8,128)(2,1)S(1)} %bitcast.111), channel_id=1, source_target_pairs={{1,2},{2,1},{5,6},{6,5},{9,10},{10,9},{13,14},{14,13},{17,18},{18,... | collective-permute-start | bytes 737288 | tf_op jit(solution)/shard_map/ppermute | solution.py:238
  197.2 37.6 %collective-permute-start.40 = (f32[960,1024]{1,0:T(8,128)S(1)}, f32[960,1024]{1,0:T(8,128)S(1)}, u32[]{:S(2)}, u32[]{:S(2)}) collective-permute-start(f32[960,1024]{1,0:T(8,128)S(1)} %constant_dynamic-slice_fusion), channel_id=1, source_target_pairs={{0,4},{4,0},{8,12},{12,8},{16,20},{20,16},{24,28},{28,24},{1,5},{5... | collective-permute-start | bytes 11796488 | tf_op jit(solution)/shard_map/ppermute | solution.py:229
  198.8 1.5 collective-permute-start.37
  199.5 38.0 %collective-permute-start.36 = (bf16[2,32,1920]{2,1,0:T(8,128)(2,1)S(1)}, bf16[2,32,1920]{2,1,0:T(8,128)(2,1)S(1)}, u32[]{:S(2)}, u32[]{:S(2)}) collective-permute-start(bf16[2,32,1920]{2,1,0:T(8,128)(2,1)S(1)} %bitcast.113), channel_id=1, source_target_pairs={{1,2},{2,1},{5,6},{6,5},{9,10},{10,9},{13,14},{14,13},{17,18},{18,... | collective-permute-start | bytes 737288 | tf_op jit(solution)/shard_map/ppermute | solution.py:238
  200.3 27.9 %collective-permute-start.28 = (bf16[2,32,1920]{2,1,0:T(8,128)(2,1)S(1)}, bf16[2,32,1920]{2,1,0:T(8,128)(2,1)S(1)}, u32[]{:S(2)}, u32[]{:S(2)}) collective-permute-start(bf16[2,32,1920]{2,1,0:T(8,128)(2,1)S(1)} %add_convert_fusion.5), channel_id=1, source_target_pairs={{1,0},{2,3},{5,4},{6,7},{9,8},{10,11},{13,12},{14,15},{17,16},{18,... | collective-permute-start | bytes 737288 | tf_op jit(solution)/shard_map/ppermute | solution.py:235
  201.7 31.8 %collective-permute-start.33 = (bf16[2,32,1920]{2,1,0:T(8,128)(2,1)S(1)}, bf16[2,32,1920]{2,1,0:T(8,128)(2,1)S(1)}, u32[]{:S(2)}, u32[]{:S(2)}) collective-permute-start(bf16[2,32,1920]{2,1,0:T(8,128)(2,1)S(1)} %add_convert_fusion.3), channel_id=1, source_target_pairs={{1,0},{2,3},{5,4},{6,7},{9,8},{10,11},{13,12},{14,15},{17,16},{18,... | collective-permute-start | bytes 737288 | tf_op jit(solution)/shard_map/ppermute | solution.py:235
  228.2 9.3 %collective-permute-start.38 = (bf16[2,32,1920]{2,1,0:T(8,128)(2,1)S(1)}, bf16[2,32,1920]{2,1,0:T(8,128)(2,1)S(1)}, u32[]{:S(2)}, u32[]{:S(2)}) collective-permute-start(bf16[2,32,1920]{2,1,0:T(8,128)(2,1)S(1)} %add_convert_fusion.1), channel_id=1, source_target_pairs={{1,0},{2,3},{5,4},{6,7},{9,8},{10,11},{13,12},{14,15},{17,16},{18,... | collective-permute-start | bytes 737288 | tf_op jit(solution)/shard_map/ppermute | solution.py:235
  229.6 9.6 %collective-permute-start.29 = (bf16[2,32,1920]{2,1,0:T(8,128)(2,1)S(1)}, bf16[2,32,1920]{2,1,0:T(8,128)(2,1)S(1)}, u32[]{:S(2)}, u32[]{:S(2)}) collective-permute-start(bf16[2,32,1920]{2,1,0:T(8,128)(2,1)S(1)} %fusion.2), channel_id=1, source_target_pairs={{0,8},{4,12},{8,0},{12,4},{16,24},{20,28},{24,16},{28,20},{1,9},{5... | collective-permute-start | bytes 737288 | tf_op jit(solution)/shard_map/ppermute | solution.py:229
  233.6 11.5 %collective-permute-start.34 = (bf16[2,32,1920]{2,1,0:T(8,128)(2,1)S(1)}, bf16[2,32,1920]{2,1,0:T(8,128)(2,1)S(1)}, u32[]{:S(2)}, u32[]{:S(2)}) collective-permute-start(bf16[2,32,1920]{2,1,0:T(8,128)(2,1)S(1)} %fusion.3), channel_id=1, source_target_pairs={{0,16},{4,20},{8,24},{12,28},{16,0},{20,4},{24,8},{28,12},{1,17},{... | collective-permute-start | bytes 737288 | tf_op jit(solution)/shard_map/ppermute | solution.py:229
  236.2 22.6 %collective-permute-start.41 = (bf16[960,512]{1,0:T(8,128)(2,1)S(1)}, bf16[960,512]{1,0:T(8,128)(2,1)S(1)}, u32[]{:S(2)}, u32[]{:S(2)}) collective-permute-start(bf16[960,512]{1,0:T(8,128)(2,1)S(1)} %slice.175), channel_id=1, source_target_pairs={{1,0},{2,3},{5,4},{6,7},{9,8},{10,11},{13,12},{14,15},{17,16},{18,... | collective-permute-start | bytes 2949128 | tf_op jit(solution)/shard_map/ppermute | solution.py:235
  237.6 7.5 %collective-permute-start.39 = (bf16[2,32,1920]{2,1,0:T(8,128)(2,1)S(1)}, bf16[2,32,1920]{2,1,0:T(8,128)(2,1)S(1)}, u32[]{:S(2)}, u32[]{:S(2)}) collective-permute-start(bf16[2,32,1920]{2,1,0:T(8,128)(2,1)S(1)} %fusion.4), channel_id=1, source_target_pairs={{0,24},{4,28},{8,16},{12,20},{16,8},{20,12},{24,0},{28,4},{1,25},{... | collective-permute-start | bytes 737288 | tf_op jit(solution)/shard_map/ppermute | solution.py:229
  (14 other events, 92.2 us)

commit v5 on v3

--- a/solution.py
+++ b/solution.py
@@ -9,6 +9,7 @@
 from jax.sharding import PartitionSpec as P
 
 TILE_ROWS = 32
+CHUNKS = 4
 
 
 EPSILON = 1e-05
@@ -200,7 +201,6 @@
 
 
 def per_device(
-    dp_size,
     mp_size,
     queries,
     out_grad,
@@ -215,78 +215,55 @@
 ):
     img_count, own_rows, vis_width = images.shape
     head_dim = query_gain.shape[0]
-    own_width, key_cols = key_weight.shape
+    key_cols = key_weight.shape[1]
     key_heads = key_cols // head_dim
-    pairs = dp_size // 2
-    width = 2 * own_width
-    place = lax.axis_index("dp")
-    pair, core = place // 2, place % 2
-
-    def swap(value, mask):
-        return lax.ppermute(value, "dp", [(i, i ^ mask) for i in range(dp_size)])
-
-    own_weight = jnp.concatenate((key_weight, value_weight), axis=1)
-    mate_weight = swap(own_weight, 1)
-    weight = jnp.where(
-        core == 0,
-        jnp.concatenate((own_weight, mate_weight), axis=0),
-        jnp.concatenate((mate_weight, own_weight), axis=0),
-    )
+    cols = 2 * key_cols
+    half = mp_size // 2
+    width = vis_width // CHUNKS
 
     def ring(value, step):
         return lax.ppermute(value, "mp", [(i, (i + step) % mp_size) for i in range(mp_size)])
 
-    half = mp_size // 2
+    own_weight = jnp.concatenate((key_weight, value_weight), axis=1)
+    weight = lax.all_gather(own_weight, "dp", axis=0, tiled=True)
+
     blocks = []
-    for r in range(pairs):
-        piece = lax.dynamic_slice_in_dim(images, (pair ^ r) * width, width, axis=2)
-        piece = swap(piece, 2 * r) if r else piece
+    total = 0.0
+    for c in range(CHUNKS):
+        piece = images[:, :, c * width : (c + 1) * width]
         parts = [piece] + [None] * (mp_size - 1)
         right = left = piece
         for k in range(1, half + 1):
-            if k < half or r < pairs // 2:
+            if k < half or c < CHUNKS // 2:
                 parts[k] = right = ring(right, 1)
-            if k < half or r >= pairs // 2:
+            if k < half or c >= CHUNKS // 2:
                 parts[mp_size - k] = left = ring(left, -1)
-        blocks.append(jnp.stack(parts))
-    img_rows = mp_size * own_rows
-    pieces = []
-    for r in range(pairs):
-        piece = jnp.dot(
-            blocks[r].reshape(-1, width), weight, preferred_element_type=jnp.float32
-        ).astype(jnp.bfloat16)
-        piece = swap(piece, 2 * r) if r else piece
-        pieces.append(piece.reshape(mp_size, img_count, own_rows, 2 * key_cols))
-    if pairs > 4:
-        pieces = [sum(piece.astype(jnp.float32) for piece in pieces)]
+        blocks.append(jnp.stack(parts).reshape(-1, width))
+        total = total + dot(blocks[c], weight[c * width : (c + 1) * width], 1, 0)
+    total = total.reshape(mp_size, img_count, own_rows, cols)
     query_gain, key_gain = query_gain[None, :], key_gain[None, :]
     normed, masked = before(queries, out_grad, query_gain, lengths, key_heads)
     owners = (lax.axis_index("mp") - jnp.arange(mp_size, dtype=jnp.int32)) % mp_size
     key_rows, value_rows, score_grad, seq_keys = attend(
-        pieces, normed, masked, key_gain, assignment, tile_counts, owners
+        [total], normed, masked, key_gain, assignment, tile_counts, owners
     )
     query_grad = after(queries, score_grad, seq_keys, query_gain)
-    rows = jnp.concatenate((key_rows, value_rows), axis=3)
-    all_rows = []
-    image_grad = jnp.zeros((img_count, own_rows, vis_width), jnp.bfloat16)
-    for r in range(pairs):
-        block_rows = (swap(rows, 2 * r) if r else rows).reshape(-1, 2 * key_cols)
-        all_rows.append(block_rows)
-        term = lax.dot_general(
-            block_rows, weight, (((1,), (1,)), ((), ())), preferred_element_type=jnp.float32
-        ).astype(jnp.bfloat16)
-        term = term.reshape(mp_size, img_count, own_rows, width)
+    rows = jnp.concatenate((key_rows, value_rows), axis=3).reshape(-1, cols)
+    image_grad = []
+    for c in range(CHUNKS):
+        term = dot(rows, weight[c * width : (c + 1) * width], 1, 1)
+        term = term.astype(jnp.bfloat16).reshape(mp_size, img_count, own_rows, width)
         total = term[0].astype(jnp.float32)
         leftward = rightward = None
         for k in range(half, 0, -1):
-            if k < half or r < pairs // 2:
+            if k < half or c < CHUNKS // 2:
                 own = term[k]
                 if leftward is not None:
                     own = (own.astype(jnp.float32) + leftward.astype(jnp.float32)).astype(
                         jnp.bfloat16
                     )
                 leftward = ring(own, -1)
-            if k < half or r >= pairs // 2:
+            if k < half or c >= CHUNKS // 2:
                 own = term[mp_size - k]
                 if rightward is not None:
                     own = (own.astype(jnp.float32) + rightward.astype(jnp.float32)).astype(
@@ -296,20 +273,13 @@
         for arrived in (leftward, rightward):
             if arrived is not None:
                 total = total + arrived.astype(jnp.float32)
-        piece = total.astype(jnp.bfloat16)
-        image_grad = lax.dynamic_update_slice_in_dim(
-            image_grad, swap(piece, 2 * r) if r else piece, (pair ^ r) * width, axis=2
-        )
-    weight_part = lax.dot_general(
-        jnp.stack(blocks).reshape(-1, width),
-        jnp.stack(all_rows).reshape(-1, 2 * key_cols),
-        (((0,), (0,)), ((), ())),
-        preferred_element_type=jnp.float32,
-    )
-    weight_grad = lax.dynamic_slice_in_dim(weight_part, core * own_width, own_width, axis=0)
-    weight_grad = weight_grad + swap(
-        lax.dynamic_slice_in_dim(weight_part, (1 - core) * own_width, own_width, axis=0), 1
-    )
+        image_grad.append(total.astype(jnp.bfloat16))
+    image_grad = jnp.concatenate(image_grad, axis=2)
+    weight_part = jnp.concatenate(
+        [dot(block, rows, 0, 0).astype(jnp.bfloat16) for block in blocks], axis=0
+    )
+    weight_grad = lax.psum_scatter(weight_part, "dp", scatter_dimension=0, tiled=True)
+    weight_grad = weight_grad.astype(jnp.float32)
     return (query_grad, image_grad, weight_grad[:, :key_cols], weight_grad[:, key_cols:])
 
 
@@ -328,7 +298,7 @@
     )
 
     def body(*args):
-        return per_device(mesh.shape["dp"], mesh.shape["mp"], *args)
+        return per_device(mesh.shape["mp"], *args)
 
     return jax.shard_map(
         body,

time: 173 us -> 193 us (1.12)
  starting transfers between devices: 57 us -> 43 us
  between operations: 1.16 us -> 14.7 us
  matrix products: 9.97 us -> 23.1 us
  other arithmetic: 4.17 us -> 13.3 us
    ppermute x14 -> x0, waiting for transfers between devices: 18.4 us -> none  [swap(): return lax.ppermute(value, 'dp', [(i, i ^ mask) for i in range(dp_size)])]
    ppermute x24, waiting for transfers between devices: 60.6 us -> 77.6 us  [ring(): lax.ppermute(value, 'mp', [(i, (i + step) % mp_size) for i in range(mp_si...]
    ppermute x14 -> x0, starting transfers between devices: 14.9 us -> none  [swap(): return lax.ppermute(value, 'dp', [(i, i ^ mask) for i in range(dp_size)])]
    dot_general x9 -> x12, matrix products: 9.97 us -> 23.1 us  [dot(): lax.dot_general(left, right, (((left_dim,), (right_dim,)), ((), ())), pre...]
    concatenate x0 -> x3, other arithmetic: none -> 7.28 us  [the longest x1 4 us: per_device(): jnp.concatenate([dot(block, rows, 0, 0).astype(jnp.bfloat16) for block in...]
    convert_element_type x3 -> x4, other arithmetic: 0.31 us -> 3.21 us  [per_device(): image_grad.append(total.astype(jnp.bfloat16))]
    dynamic_slice x2 -> x0, local copies, waits for them, and re-layouts: 2.37 us -> none  [the longest x1 2.21 us: per_device(): piece = lax.dynamic_slice_in_dim(images, (pair ^ r) * width, width, axis=2)]
  transfers between devices with their start and end apart: 38 -> 26, of which waited for: 17 -> 13; matrix products, arithmetic and copies ran while one was open for 7% -> 9% of each run, Pallas kernels for 5% -> 5%
where the time goes in v5:
time: 193 us; the launch traced here: 192 us
  waiting for transfers between devices  77.6 us (40%)
  starting transfers between devices  43 us (22%)
  matrix products  23.1 us (12%)
  between operations  14.7 us (8%)
  Pallas kernels  14.4 us (7%)
  other arithmetic  13.3 us (7%)
  local copies, waits for them, and re-layouts  6.32 us (3%)
    ppermute x24, waiting for transfers between devices, ring(): lax.ppermute(value, 'mp', [(i, (i + step) % mp_size) for i in range(mp_si...  77.6 us
    ppermute x24, starting transfers between devices, ring(): lax.ppermute(value, 'mp', [(i, (i + step) % mp_size) for i in range(mp_si...  42.9 us
    dot_general x12, matrix products, dot(): lax.dot_general(left, right, (((left_dim,), (right_dim,)), ((), ())), pre...  23.1 us
    pallas_call x1, Pallas kernels, attend(): pl.pallas_call(functools.partial(attend_kernel, count), out_shape=(rows,...  5 us
    pallas_call x1, Pallas kernels, before(): pl.pallas_call(before_kernel, out_shape=(shape, shape), grid_spec=pltpu.P...  4.96 us
    pallas_call x1, Pallas kernels, after(): pl.pallas_call(after_kernel, out_shape=jax.ShapeDtypeStruct(queries.shape...  4.42 us
    concatenate x1, other arithmetic, per_device(): jnp.concatenate([dot(block, rows, 0, 0).astype(jnp.bfloat16) for block in...  4 us
  transfers between devices with their start and end apart: 26, of which 13 were waited for; matrix products, arithmetic and copies ran while one was open for 9% of the time, Pallas kernels for 5%

profile of v5, /device:TPU:0, one launch (start us, length us, event | category | flops | bytes accessed | tf_op | source)
XLA Modules:
  0.0 192.4 jit_solution(4698624693056090206)
XLA Ops:
  7.2 2.3 %pad_maximum_fusion.2 = bf16[960,512]{1,0:T(8,128)(2,1)} fusion(bf16[960,256]{1,0:T(8,128)(2,1)} %param.14, bf16[960,256]{1,0:T(8,128)(2,1)} %param.13), kind=kLoop, calls=%fused_computation.25 | loop fusion | flops 1966080 | bytes 1966080 | tf_op jit(solution)/shard_map/concatenate | solution.py:227
  9.6 0.9 slice_bitcast_fusion.3
  10.5 5.0 %collective-permute-start.7 = (bf16[2,32,1920]{2,1,0:T(8,128)(2,1)S(1)}, bf16[2,32,1920]{2,1,0:T(8,128)(2,1)S(1)}, u32[]{:S(2)}, u32[]{:S(2)}) collective-permute-start(bf16[2,32,1920]{2,1,0:T(8,128)(2,1)S(1)} %get-tuple-element.41), channel_id=1, source_target_pairs={{0,3},{1,0},{2,1},{3,2},{4,7},{5,4},{6,5},{7,6},{8,11},{9,8},{10,9... | collective-permute-start | bytes 737288 | tf_op jit(solution)/shard_map/ppermute | solution.py:225
  16.0 1.6 collective-permute-start.6
  17.6 4.4 %collective-permute-done.7 = bf16[2,32,1920]{2,1,0:T(8,128)(2,1)S(1)} collective-permute-done((bf16[2,32,1920]{2,1,0:T(8,128)(2,1)S(1)}, bf16[2,32,1920]{2,1,0:T(8,128)(2,1)S(1)}, u32[]{:S(2)}, u32[]{:S(2)}) %collective-permute-start.7) | collective-permute-done | bytes 245792 | tf_op jit(solution)/shard_map/ppermute | solution.py:225
  22.0 4.4 %collective-permute-start.8 = (bf16[2,32,1920]{2,1,0:T(8,128)(2,1)S(1)}, bf16[2,32,1920]{2,1,0:T(8,128)(2,1)S(1)}, u32[]{:S(2)}, u32[]{:S(2)}) collective-permute-start(bf16[2,32,1920]{2,1,0:T(8,128)(2,1)S(1)} %collective-permute-done.7), channel_id=1, source_target_pairs={{0,3},{1,0},{2,1},{3,2},{4,7},{5,4},{6,5},{7,6},{8,11},{9,8},{10,9... | collective-permute-start | bytes 737288 | tf_op jit(solution)/shard_map/ppermute | solution.py:225
  26.3 3.8 %collective-permute-start.5 = (bf16[2,32,1920]{2,1,0:T(8,128)(2,1)}, bf16[2,32,1920]{2,1,0:T(8,128)(2,1)}, u32[]{:S(2)}, u32[]{:S(2)}) collective-permute-start(bf16[2,32,1920]{2,1,0:T(8,128)(2,1)} %get-tuple-element.38), channel_id=1, source_target_pairs={{0,3},{1,0},{2,1},{3,2},{4,7},{5,4},{6,5},{7,6},{8,11},{9,8},{10,9... | collective-permute-start | bytes 737288 | tf_op jit(solution)/shard_map/ppermute | solution.py:225
  30.2 5.0 %before.1 = (bf16[2,2,1024,128]{3,2,1,0:T(8,128)(2,1)}, bf16[2,2,1024,128]{3,2,1,0:T(8,128)(2,1)}) custom-call(s32[2]{0:T(128)} %lengths.1, bf16[2,128,2048]{2,1,0:T(8,128)(2,1)} %query.3, bf16[2,128,2048]{2,1,0:T(8,128)(2,1)} %grad.1, f32[1,128]{1,0:T(1,128)} %bitcast.127), custom_call_target="tpu_custom_call" | custom-call | tf_op jit(solution)/shard_map/before/pallas_call | solution.py:59
  35.3 2.5 %collective-permute-done.8 = bf16[2,32,1920]{2,1,0:T(8,128)(2,1)S(1)} collective-permute-done((bf16[2,32,1920]{2,1,0:T(8,128)(2,1)S(1)}, bf16[2,32,1920]{2,1,0:T(8,128)(2,1)S(1)}, u32[]{:S(2)}, u32[]{:S(2)}) %collective-permute-start.8) | collective-permute-done | bytes 245792 | tf_op jit(solution)/shard_map/ppermute | solution.py:225
  37.8 4.3 %collective-permute-start.11 = (bf16[2,32,1920]{2,1,0:T(8,128)(2,1)S(1)}, bf16[2,32,1920]{2,1,0:T(8,128)(2,1)S(1)}, u32[]{:S(2)}, u32[]{:S(2)}) collective-permute-start(bf16[2,32,1920]{2,1,0:T(8,128)(2,1)S(1)} %collective-permute-done.10), channel_id=1, source_target_pairs={{0,3},{1,0},{2,1},{3,2},{4,7},{5,4},{6,5},{7,6},{8,11},{9,8},{10,9... | collective-permute-start | bytes 737288 | tf_op jit(solution)/shard_map/ppermute | solution.py:225
  42.2 1.8 collective-permute-done.3
  44.1 3.5 %collective-permute-start.2 = (bf16[2,32,1920]{2,1,0:T(8,128)(2,1)}, bf16[2,32,1920]{2,1,0:T(8,128)(2,1)S(1)}, u32[]{:S(2)}, u32[]{:S(2)}) collective-permute-start(bf16[2,32,1920]{2,1,0:T(8,128)(2,1)} %get-tuple-element.39), channel_id=1, source_target_pairs={{0,3},{1,0},{2,1},{3,2},{4,7},{5,4},{6,5},{7,6},{8,11},{9,8},{10,9... | collective-permute-start | bytes 737288 | tf_op jit(solution)/shard_map/ppermute | solution.py:225
  47.5 12.3 %collective-permute-done = bf16[2,32,1920]{2,1,0:T(8,128)(2,1)S(1)} collective-permute-done((bf16[2,32,1920]{2,1,0:T(8,128)(2,1)}, bf16[2,32,1920]{2,1,0:T(8,128)(2,1)S(1)}, u32[]{:S(2)}, u32[]{:S(2)}) %collective-permute-start) | collective-permute-done | bytes 245792 | tf_op jit(solution)/shard_map/ppermute | solution.py:225
  59.8 1.6 collective-permute-start.4
  61.4 1.2 collective-permute-start.1
  62.6 1.6 collective-permute-done.11
  64.4 5.2 %collective-permute-done.2 = bf16[2,32,1920]{2,1,0:T(8,128)(2,1)S(1)} collective-permute-done((bf16[2,32,1920]{2,1,0:T(8,128)(2,1)}, bf16[2,32,1920]{2,1,0:T(8,128)(2,1)S(1)}, u32[]{:S(2)}, u32[]{:S(2)}) %collective-permute-start.2) | collective-permute-done | bytes 245792 | tf_op jit(solution)/shard_map/ppermute | solution.py:225
  69.6 10.1 %collective-permute-done.1 = bf16[2,32,1920]{2,1,0:T(8,128)(2,1)S(1)} collective-permute-done((bf16[2,32,1920]{2,1,0:T(8,128)(2,1)S(1)}, bf16[2,32,1920]{2,1,0:T(8,128)(2,1)S(1)}, u32[]{:S(2)}, u32[]{:S(2)}) %collective-permute-start.1) | collective-permute-done | bytes 245792 | tf_op jit(solution)/shard_map/ppermute | solution.py:225
  81.1 2.2 %pad_maximum_fusion.3 = bf16[4,2,32,1920]{3,2,1,0:T(8,128)(2,1)} fusion(bf16[1,2,32,1920]{3,2,1,0:T(8,128)(2,1)} %bitcast.8, bf16[1,2,32,1920]{3,2,1,0:T(8,128)(2,1)S(1)} %bitcast.115, bf16[1,2,32,1920]{3,2,1,0:T(8,128)(2,1)} %bitcast.6, bf16[1,2,32,1920]{3,2,1,0:T(8,128)(2,1)S(1)} %get-tuple-element.35), kind=kLoop, calls=%fused_computation.26 | loop fusion | flops 1474560 | bytes 1966080 | tf_op jit(solution)/shard_map/stack | solution.py:241
  83.3 2.3 %fusion.4 = f32[256,512]{1,0:T(8,128)S(1)} fusion(bf16[256,1920]{1,0:T(8,128)(2,1)S(1)} %bitcast.84, bf16[7680,512]{1,0:T(8,128)(2,1)} %all-gather.2.cloned.1.call-done), kind=kOutput, calls=%fused_computation.13 | convolution fusion | flops 503316480 | bytes 3473408 | tf_op jit(solution)/shard_map/dot_general | solution.py:30
  85.6 2.3 %fusion.1 = f32[256,512]{1,0:T(8,128)S(1)} fusion(bf16[256,1920]{1,0:T(8,128)(2,1)S(1)} %bitcast.85, bf16[7680,512]{1,0:T(8,128)(2,1)} %all-gather.2.cloned.1.call-done), kind=kOutput, calls=%fused_computation.10 | convolution fusion | flops 503316480 | bytes 3473408 | tf_op jit(solution)/shard_map/dot_general | solution.py:30
  87.9 2.3 %fusion.7 = f32[256,512]{1,0:T(8,128)S(1)} fusion(bf16[256,1920]{1,0:T(8,128)(2,1)S(1)} %bitcast.86, bf16[7680,512]{1,0:T(8,128)(2,1)} %all-gather.2.cloned.1.call-done), kind=kOutput, calls=%fused_computation.16 | convolution fusion | flops 503316480 | bytes 3473408 | tf_op jit(solution)/shard_map/dot_general | solution.py:30
  90.3 2.4 %fusion.18 = f32[256,512]{1,0:T(8,128)S(1)} fusion(f32[256,512]{1,0:T(8,128)S(1)} %fusion.1, f32[256,512]{1,0:T(8,128)S(1)} %fusion.4, f32[256,512]{1,0:T(8,128)S(1)} %fusion.7, bf16[256,1920]{1,0:T(8,128)(2,1)S(1)} %bitcast.83, bf16[7680,512]{1,0:T(8,128)(2,1)} %all-gather.2.cloned.1.call-done), kind=kOutput, calls=%fused_computation.23 | convolution fusion | flops 503709696 | bytes 5046272 | tf_op jit(solution)/shard_map/dot_general | solution.py:30
  92.8 5.0 %attend.1 = (bf16[4,2,32,256]{3,2,1,0:T(8,128)(2,1)S(1)}, bf16[4,2,32,256]{3,2,1,0:T(8,128)(2,1)S(1)}, bf16[2,2,1024,128]{3,2,1,0:T(8,128)(2,1)S(1)}, bf16[2,2,128,128]{3,2,1,0:T(8,128)(2,1)S(1)}) custom-call(s32[2]{0:T(128)S(1)} %copy-done.4, s32[2]{0:T(128)S(1)} %copy-done.5, s32[4]{0:T(128)S(1)} %and_select_fusion.owners, f32[4,2,32,512]{3,2,1,0:T(8,128)S(1)} %bitcast.80, ...), custom_call_target="tpu_custom_call" | custom-call | tf_op jit(solution)/shard_map/attend/pallas_call | solution.py:138
  100.6 1.9 bitcast_convert_fusion.2
  102.5 0.7 bitcast_convert_fusion.3
  103.2 4.0 %pad_maximum_fusion = bf16[7680,512]{1,0:T(8,128)(2,1)} fusion(bf16[1920,512]{1,0:T(8,128)(2,1)S(1)} %bitcast_convert_fusion, bf16[1920,512]{1,0:T(8,128)(2,1)S(1)} %bitcast_convert_fusion.1, bf16[1920,512]{1,0:T(8,128)(2,1)S(1)} %bitcast_convert_fusion.2, bf16[1920,512]{1,0:T(8,128)(2,1)S(1)} %bitcast_convert_fusion.3), kind=kLoop, calls=%fused_computation | loop fusion | flops 31457280 | bytes 15728640 | tf_op jit(solution)/shard_map/concatenate | solution.py:278
  107.2 2.3 %convolution_convert_fusion = bf16[256,1920]{1,0:T(8,128)(2,1)S(1)} fusion(bf16[256,512]{1,0:T(8,128)(2,1)S(1)} %bitcast.123, bf16[7680,512]{1,0:T(8,128)(2,1)} %all-gather.2.cloned.1.call-done), kind=kOutput, calls=%fused_computation.5 | convolution fusion | flops 503808000 | bytes 3211264 | tf_op jit(solution)/shard_map/dot_general | solution.py:30
  109.6 1.7 collective-permute-start.22
  111.3 2.2 %collective-permute-start.21 = (bf16[2,32,1920]{2,1,0:T(8,128)(2,1)S(1)}, bf16[2,32,1920]{2,1,0:T(8,128)(2,1)}, u32[]{:S(2)}, u32[]{:S(2)}) collective-permute-start(bf16[2,32,1920]{2,1,0:T(8,128)(2,1)S(1)} %bitcast.108), channel_id=1, source_target_pairs={{0,3},{1,0},{2,1},{3,2},{4,7},{5,4},{6,5},{7,6},{8,11},{9,8},{10,9... | collective-permute-start | bytes 737288 | tf_op jit(solution)/shard_map/ppermute | solution.py:225
  113.5 2.4 %convolution_convert_fusion.1 = bf16[256,1920]{1,0:T(8,128)(2,1)S(1)} fusion(bf16[256,512]{1,0:T(8,128)(2,1)S(1)} %bitcast.124, bf16[7680,512]{1,0:T(8,128)(2,1)} %all-gather.2.cloned.1.call-done), kind=kOutput, calls=%fused_computation.6 | convolution fusion | flops 503808000 | bytes 3211264 | tf_op jit(solution)/shard_map/dot_general | solution.py:30
  116.0 3.8 %collective-permute-start.18 = (bf16[2,32,1920]{2,1,0:T(8,128)(2,1)S(1)}, bf16[2,32,1920]{2,1,0:T(8,128)(2,1)}, u32[]{:S(2)}, u32[]{:S(2)}) collective-permute-start(bf16[2,32,1920]{2,1,0:T(8,128)(2,1)S(1)} %bitcast.104), channel_id=1, source_target_pairs={{0,3},{1,0},{2,1},{3,2},{4,7},{5,4},{6,5},{7,6},{8,11},{9,8},{10,9... | collective-permute-start | bytes 737288 | tf_op jit(solution)/shard_map/ppermute | solution.py:225
  119.8 2.7 %convolution_convert_fusion.2 = bf16[256,1920]{1,0:T(8,128)(2,1)S(1)} fusion(bf16[256,512]{1,0:T(8,128)(2,1)S(1)} %bitcast.125, bf16[7680,512]{1,0:T(8,128)(2,1)} %all-gather.2.cloned.1.call-done), kind=kOutput, calls=%fused_computation.7 | convolution fusion | flops 503808000 | bytes 3211264 | tf_op jit(solution)/shard_map/dot_general | solution.py:30
  122.7 4.4 %after.1 = bf16[2,128,2048]{2,1,0:T(8,128)(2,1)} custom-call(bf16[2,128,2048]{2,1,0:T(8,128)(2,1)} %query.3, bf16[2,2,1024,128]{3,2,1,0:T(8,128)(2,1)} %copy-done, bf16[2,2,128,128]{3,2,1,0:T(8,128)(2,1)} %copy-done.3, f32[1,128]{1,0:T(1,128)} %bitcast.128), custom_call_target="tpu_custom_call" | custom-call | tf_op jit(solution)/shard_map/after/pallas_call | solution.py:188
  127.1 2.4 %convolution_convert_fusion.3 = bf16[256,1920]{1,0:T(8,128)(2,1)S(1)} fusion(bf16[256,512]{1,0:T(8,128)(2,1)} %bitcast.126, bf16[7680,512]{1,0:T(8,128)(2,1)} %all-gather.2.cloned.1.call-done), kind=kOutput, calls=%fused_computation.8 | convolution fusion | flops 503808000 | bytes 3211264 | tf_op jit(solution)/shard_map/dot_general | solution.py:30
  129.6 3.8 %collective-permute-start.15 = (bf16[2,32,1920]{2,1,0:T(8,128)(2,1)S(1)}, bf16[2,32,1920]{2,1,0:T(8,128)(2,1)S(1)}, u32[]{:S(2)}, u32[]{:S(2)}) collective-permute-start(bf16[2,32,1920]{2,1,0:T(8,128)(2,1)S(1)} %bitcast.121), channel_id=1, source_target_pairs={{0,3},{1,0},{2,1},{3,2},{4,7},{5,4},{6,5},{7,6},{8,11},{9,8},{10,9... | collective-permute-start | bytes 737288 | tf_op jit(solution)/shard_map/ppermute | solution.py:225
  134.2 11.0 %collective-permute-done.15 = bf16[2,32,1920]{2,1,0:T(8,128)(2,1)S(1)} collective-permute-done((bf16[2,32,1920]{2,1,0:T(8,128)(2,1)S(1)}, bf16[2,32,1920]{2,1,0:T(8,128)(2,1)S(1)}, u32[]{:S(2)}, u32[]{:S(2)}) %collective-permute-start.15) | collective-permute-done | bytes 245792 | tf_op jit(solution)/shard_map/ppermute | solution.py:225
  145.2 3.2 %collective-permute-start.12 = (bf16[2,32,1920]{2,1,0:T(8,128)(2,1)S(1)}, bf16[2,32,1920]{2,1,0:T(8,128)(2,1)S(1)}, u32[]{:S(2)}, u32[]{:S(2)}) collective-permute-start(bf16[2,32,1920]{2,1,0:T(8,128)(2,1)S(1)} %bitcast.122), channel_id=1, source_target_pairs={{0,3},{1,0},{2,1},{3,2},{4,7},{5,4},{6,5},{7,6},{8,11},{9,8},{10,9... | collective-permute-start | bytes 737288 | tf_op jit(solution)/shard_map/ppermute | solution.py:225
  148.5 7.7 %collective-permute-done.12 = bf16[2,32,1920]{2,1,0:T(8,128)(2,1)S(1)} collective-permute-done((bf16[2,32,1920]{2,1,0:T(8,128)(2,1)S(1)}, bf16[2,32,1920]{2,1,0:T(8,128)(2,1)S(1)}, u32[]{:S(2)}, u32[]{:S(2)}) %collective-permute-start.12) | collective-permute-done | bytes 245792 | tf_op jit(solution)/shard_map/ppermute | solution.py:225
  157.4 9.4 %collective-permute-done.23 = bf16[2,32,1920]{2,1,0:T(8,128)(2,1)S(1)} collective-permute-done((bf16[2,32,1920]{2,1,0:T(8,128)(2,1)S(1)}, bf16[2,32,1920]{2,1,0:T(8,128)(2,1)S(1)}, u32[]{:S(2)}, u32[]{:S(2)}) %collective-permute-start.23) | collective-permute-done | bytes 245792 | tf_op jit(solution)/shard_map/ppermute | solution.py:225
  166.9 1.0 fusion.23
  168.3 3.8 %collective-permute-done.20 = bf16[2,32,1920]{2,1,0:T(8,128)(2,1)S(1)} collective-permute-done((bf16[2,32,1920]{2,1,0:T(8,128)(2,1)S(1)}, bf16[2,32,1920]{2,1,0:T(8,128)(2,1)S(1)}, u32[]{:S(2)}, u32[]{:S(2)}) %collective-permute-start.20) | collective-permute-done | bytes 245792 | tf_op jit(solution)/shard_map/ppermute | solution.py:225
  172.1 1.1 fusion.26
  173.2 3.5 %collective-permute-done.16 = bf16[2,32,1920]{2,1,0:T(8,128)(2,1)S(1)} collective-permute-done((bf16[2,32,1920]{2,1,0:T(8,128)(2,1)S(1)}, bf16[2,32,1920]{2,1,0:T(8,128)(2,1)S(1)}, u32[]{:S(2)}, u32[]{:S(2)}) %collective-permute-start.16) | collective-permute-done | bytes 245792 | tf_op jit(solution)/shard_map/ppermute | solution.py:225
  176.7 1.0 fusion.29
  177.8 4.1 %collective-permute-done.13 = bf16[2,32,1920]{2,1,0:T(8,128)(2,1)S(1)} collective-permute-done((bf16[2,32,1920]{2,1,0:T(8,128)(2,1)S(1)}, bf16[2,32,1920]{2,1,0:T(8,128)(2,1)S(1)}, u32[]{:S(2)}, u32[]{:S(2)}) %collective-permute-start.13) | collective-permute-done | bytes 245792 | tf_op jit(solution)/shard_map/ppermute | solution.py:225
  182.0 1.0 pad_maximum_fusion.6
  183.0 2.6 %fusion.34 = (f32[960,256]{1,0:T(8,128)}, f32[960,256]{1,0:T(8,128)}) fusion(bf16[960,512]{1,0:T(8,128)(2,1)} %reduce-scatter.2.cloned.1.call-done), kind=kLoop, calls=%fused_computation.60 | loop fusion | bytes 3932160 | tf_op jit(solution)/shard_map/slice | solution.py:283
  (113 shorter events, 8.0 us)
Async XLA Ops:
  7.2 2.4 %copy-start.7 = (bf16[2,32,7680]{2,1,0:T(8,128)(2,1)S(1)}, bf16[2,32,7680]{2,1,0:T(8,128)(2,1)}, u32[]{:S(2)}) copy-start(bf16[2,32,7680]{2,1,0:T(8,128)(2,1)} %param.12) | copy-start | bytes 2949124
  7.2 76.1 %all-gather.2.cloned.1.call-start = ((), (), s32[]{:S(2)}) async-start(), calls=%async_computation.1 | async-start | bytes 8847360 | tf_op jit(solution)/shard_map/all_gather | solution.py:228
  9.5 173.5 %reduce-scatter.2.cloned.1.call-start = ((), (), s32[]{:S(2)}) async-start(), calls=%async_computation.2 | async-start | bytes 8847360 | tf_op jit(solution)/shard_map/reduce_scatter | solution.py:281
  10.5 31.7 %copy-start.9 = (bf16[1,2,32,1920]{3,2,1,0:T(8,128)(2,1)}, bf16[1,2,32,1920]{3,2,1,0:T(8,128)(2,1)S(1)}, u32[]{:S(2)}) copy-start(bf16[1,2,32,1920]{3,2,1,0:T(8,128)(2,1)S(1)} %get-tuple-element.36) | copy-start | bytes 737284
  10.5 11.5 %collective-permute-start.7 = (bf16[2,32,1920]{2,1,0:T(8,128)(2,1)S(1)}, bf16[2,32,1920]{2,1,0:T(8,128)(2,1)S(1)}, u32[]{:S(2)}, u32[]{:S(2)}) collective-permute-start(bf16[2,32,1920]{2,1,0:T(8,128)(2,1)S(1)} %get-tuple-element.41), channel_id=1, source_target_pairs={{0,3},{1,0},{2,1},{3,2},{4,7},{5,4},{6,5},{7,6},{8,11},{9,8},{10,9... | collective-permute-start | bytes 737288 | tf_op jit(solution)/shard_map/ppermute | solution.py:225
  15.5 19.6 %collective-permute-start.10 = (bf16[2,32,1920]{2,1,0:T(8,128)(2,1)S(1)}, bf16[2,32,1920]{2,1,0:T(8,128)(2,1)S(1)}, u32[]{:S(2)}, u32[]{:S(2)}) collective-permute-start(bf16[2,32,1920]{2,1,0:T(8,128)(2,1)S(1)} %get-tuple-element.40), channel_id=1, source_target_pairs={{0,3},{1,0},{2,1},{3,2},{4,7},{5,4},{6,5},{7,6},{8,11},{9,8},{10,9... | collective-permute-start | bytes 737288 | tf_op jit(solution)/shard_map/ppermute | solution.py:225
  16.0 19.2 %collective-permute-start.6 = (bf16[2,32,1920]{2,1,0:T(8,128)(2,1)S(1)}, bf16[2,32,1920]{2,1,0:T(8,128)(2,1)S(1)}, u32[]{:S(2)}, u32[]{:S(2)}) collective-permute-start(bf16[2,32,1920]{2,1,0:T(8,128)(2,1)S(1)} %get-tuple-element.41), channel_id=1, source_target_pairs={{0,1},{1,2},{2,3},{3,0},{4,5},{5,6},{6,7},{7,4},{8,9},{9,10},{10,1... | collective-permute-start | bytes 737288 | tf_op jit(solution)/shard_map/ppermute | solution.py:225
  22.0 20.3 %copy-start.13 = (bf16[2,32,1920]{2,1,0:T(8,128)(2,1)}, bf16[2,32,1920]{2,1,0:T(8,128)(2,1)S(1)}, u32[]{:S(2)}) copy-start(bf16[2,32,1920]{2,1,0:T(8,128)(2,1)S(1)} %collective-permute-done.7) | copy-start | bytes 737284
  22.0 15.8 %collective-permute-start.8 = (bf16[2,32,1920]{2,1,0:T(8,128)(2,1)S(1)}, bf16[2,32,1920]{2,1,0:T(8,128)(2,1)S(1)}, u32[]{:S(2)}, u32[]{:S(2)}) collective-permute-start(bf16[2,32,1920]{2,1,0:T(8,128)(2,1)S(1)} %collective-permute-done.7), channel_id=1, source_target_pairs={{0,3},{1,0},{2,1},{3,2},{4,7},{5,4},{6,5},{7,6},{8,11},{9,8},{10,9... | collective-permute-start | bytes 737288 | tf_op jit(solution)/shard_map/ppermute | solution.py:225
  26.3 17.7 %collective-permute-start.3 = (bf16[2,32,1920]{2,1,0:T(8,128)(2,1)}, bf16[2,32,1920]{2,1,0:T(8,128)(2,1)}, u32[]{:S(2)}, u32[]{:S(2)}) collective-permute-start(bf16[2,32,1920]{2,1,0:T(8,128)(2,1)} %get-tuple-element.38), channel_id=1, source_target_pairs={{0,1},{1,2},{2,3},{3,0},{4,5},{5,6},{6,7},{7,4},{8,9},{9,10},{10,1... | collective-permute-start | bytes 737288 | tf_op jit(solution)/shard_map/ppermute | solution.py:225
  26.3 53.6 %collective-permute-start.5 = (bf16[2,32,1920]{2,1,0:T(8,128)(2,1)}, bf16[2,32,1920]{2,1,0:T(8,128)(2,1)}, u32[]{:S(2)}, u32[]{:S(2)}) collective-permute-start(bf16[2,32,1920]{2,1,0:T(8,128)(2,1)} %get-tuple-element.38), channel_id=1, source_target_pairs={{0,3},{1,0},{2,1},{3,2},{4,7},{5,4},{6,5},{7,6},{8,11},{9,8},{10,9... | collective-permute-start | bytes 737288 | tf_op jit(solution)/shard_map/ppermute | solution.py:225
  30.2 34.1 %copy-start.11 = (bf16[1,2,32,1920]{3,2,1,0:T(8,128)(2,1)S(1)}, bf16[1,2,32,1920]{3,2,1,0:T(8,128)(2,1)}, u32[]{:S(2)}) copy-start(bf16[1,2,32,1920]{3,2,1,0:T(8,128)(2,1)} %get-tuple-element.37) | copy-start | bytes 737284
  35.2 29.2 %copy-start.17 = (bf16[2,32,1920]{2,1,0:T(8,128)(2,1)}, bf16[2,32,1920]{2,1,0:T(8,128)(2,1)S(1)}, u32[]{:S(2)}) copy-start(bf16[2,32,1920]{2,1,0:T(8,128)(2,1)S(1)} %collective-permute-done.10) | copy-start | bytes 737284
  35.2 26.2 %collective-permute-start.9 = (bf16[2,32,1920]{2,1,0:T(8,128)(2,1)S(1)}, bf16[2,32,1920]{2,1,0:T(8,128)(2,1)S(1)}, u32[]{:S(2)}, u32[]{:S(2)}) collective-permute-start(bf16[2,32,1920]{2,1,0:T(8,128)(2,1)S(1)} %get-tuple-element.40), channel_id=1, source_target_pairs={{0,1},{1,2},{2,3},{3,0},{4,5},{5,6},{6,7},{7,4},{8,9},{9,10},{10,1... | collective-permute-start | bytes 737288 | tf_op jit(solution)/shard_map/ppermute | solution.py:225
  35.2 29.1 %copy-start.15 = (bf16[2,32,1920]{2,1,0:T(8,128)(2,1)}, bf16[2,32,1920]{2,1,0:T(8,128)(2,1)S(1)}, u32[]{:S(2)}) copy-start(bf16[2,32,1920]{2,1,0:T(8,128)(2,1)S(1)} %collective-permute-done.6) | copy-start | bytes 737284
  35.2 24.6 %collective-permute-start = (bf16[2,32,1920]{2,1,0:T(8,128)(2,1)}, bf16[2,32,1920]{2,1,0:T(8,128)(2,1)S(1)}, u32[]{:S(2)}, u32[]{:S(2)}) collective-permute-start(bf16[2,32,1920]{2,1,0:T(8,128)(2,1)} %get-tuple-element.39), channel_id=1, source_target_pairs={{0,1},{1,2},{2,3},{3,0},{4,5},{5,6},{6,7},{7,4},{8,9},{9,10},{10,1... | collective-permute-start | bytes 737288 | tf_op jit(solution)/shard_map/ppermute | solution.py:225
  37.8 26.4 %copy-start.19 = (bf16[2,32,1920]{2,1,0:T(8,128)(2,1)}, bf16[2,32,1920]{2,1,0:T(8,128)(2,1)S(1)}, u32[]{:S(2)}) copy-start(bf16[2,32,1920]{2,1,0:T(8,128)(2,1)S(1)} %collective-permute-done.8) | copy-start | bytes 737284
  37.8 26.4 %collective-permute-start.11 = (bf16[2,32,1920]{2,1,0:T(8,128)(2,1)S(1)}, bf16[2,32,1920]{2,1,0:T(8,128)(2,1)S(1)}, u32[]{:S(2)}, u32[]{:S(2)}) collective-permute-start(bf16[2,32,1920]{2,1,0:T(8,128)(2,1)S(1)} %collective-permute-done.10), channel_id=1, source_target_pairs={{0,3},{1,0},{2,1},{3,2},{4,7},{5,4},{6,5},{7,6},{8,11},{9,8},{10,9... | collective-permute-start | bytes 737288 | tf_op jit(solution)/shard_map/ppermute | solution.py:225
  44.1 25.5 %collective-permute-start.2 = (bf16[2,32,1920]{2,1,0:T(8,128)(2,1)}, bf16[2,32,1920]{2,1,0:T(8,128)(2,1)S(1)}, u32[]{:S(2)}, u32[]{:S(2)}) collective-permute-start(bf16[2,32,1920]{2,1,0:T(8,128)(2,1)} %get-tuple-element.39), channel_id=1, source_target_pairs={{0,3},{1,0},{2,1},{3,2},{4,7},{5,4},{6,5},{7,6},{8,11},{9,8},{10,9... | collective-permute-start | bytes 737288 | tf_op jit(solution)/shard_map/ppermute | solution.py:225
  59.8 20.1 %copy-start.21 = (bf16[2,32,1920]{2,1,0:T(8,128)(2,1)}, bf16[2,32,1920]{2,1,0:T(8,128)(2,1)S(1)}, u32[]{:S(2)}) copy-start(bf16[2,32,1920]{2,1,0:T(8,128)(2,1)S(1)} %collective-permute-done) | copy-start | bytes 737284
  59.8 20.1 %collective-permute-start.4 = (bf16[2,32,1920]{2,1,0:T(8,128)(2,1)}, bf16[2,32,1920]{2,1,0:T(8,128)(2,1)S(1)}, u32[]{:S(2)}, u32[]{:S(2)}) collective-permute-start(bf16[2,32,1920]{2,1,0:T(8,128)(2,1)} %collective-permute-done.3), channel_id=1, source_target_pairs={{0,1},{1,2},{2,3},{3,0},{4,5},{5,6},{6,7},{7,4},{8,9},{9,10},{10,1... | collective-permute-start | bytes 737288 | tf_op jit(solution)/shard_map/ppermute | solution.py:225
  61.4 18.5 %copy-start.23 = (bf16[2,32,1920]{2,1,0:T(8,128)(2,1)}, bf16[2,32,1920]{2,1,0:T(8,128)(2,1)S(1)}, u32[]{:S(2)}) copy-start(bf16[2,32,1920]{2,1,0:T(8,128)(2,1)S(1)} %collective-permute-done.9) | copy-start | bytes 737284
  61.4 18.3 %collective-permute-start.1 = (bf16[2,32,1920]{2,1,0:T(8,128)(2,1)S(1)}, bf16[2,32,1920]{2,1,0:T(8,128)(2,1)S(1)}, u32[]{:S(2)}, u32[]{:S(2)}) collective-permute-start(bf16[2,32,1920]{2,1,0:T(8,128)(2,1)S(1)} %collective-permute-done), channel_id=1, source_target_pairs={{0,1},{1,2},{2,3},{3,0},{4,5},{5,6},{6,7},{7,4},{8,9},{9,10},{10,1... | collective-permute-start | bytes 737288 | tf_op jit(solution)/shard_map/ppermute | solution.py:225
  64.2 15.7 %copy-start.27 = (bf16[2,32,1920]{2,1,0:T(8,128)(2,1)}, bf16[2,32,1920]{2,1,0:T(8,128)(2,1)S(1)}, u32[]{:S(2)}) copy-start(bf16[2,32,1920]{2,1,0:T(8,128)(2,1)S(1)} %collective-permute-done.11) | copy-start | bytes 737284
  69.6 10.3 %copy-start.25 = (bf16[2,32,1920]{2,1,0:T(8,128)(2,1)}, bf16[2,32,1920]{2,1,0:T(8,128)(2,1)S(1)}, u32[]{:S(2)}) copy-start(bf16[2,32,1920]{2,1,0:T(8,128)(2,1)S(1)} %collective-permute-done.2) | copy-start | bytes 737284
  85.6 2.4 %copy-start.8 = (bf16[4,2,32,1920]{3,2,1,0:T(8,128)(2,1)S(1)}, bf16[4,2,32,1920]{3,2,1,0:T(8,128)(2,1)}, u32[]{:S(2)}) copy-start(bf16[4,2,32,1920]{3,2,1,0:T(8,128)(2,1)} %pad_maximum_fusion.3) | copy-start | bytes 2949124
  90.2 2.5 %copy-start.1 = (bf16[2,2,1024,128]{3,2,1,0:T(8,128)(2,1)S(1)}, bf16[2,2,1024,128]{3,2,1,0:T(8,128)(2,1)}, u32[]{:S(2)}) copy-start(bf16[2,2,1024,128]{3,2,1,0:T(8,128)(2,1)} %get-tuple-element.10.refs_2_) | copy-start | bytes 3145732
  90.2 2.5 %copy-start.2 = (bf16[2,2,1024,128]{3,2,1,0:T(8,128)(2,1)S(1)}, bf16[2,2,1024,128]{3,2,1,0:T(8,128)(2,1)}, u32[]{:S(2)}) copy-start(bf16[2,2,1024,128]{3,2,1,0:T(8,128)(2,1)} %get-tuple-element.11.refs_3_) | copy-start | bytes 3145732
  90.2 2.5 %copy-start.4 = (s32[2]{0:T(128)S(1)}, s32[2]{0:T(128)}, u32[]{:S(2)}) copy-start(s32[2]{0:T(128)} %assignment.1) | copy-start | bytes 28
  90.2 2.5 %copy-start.5 = (s32[2]{0:T(128)S(1)}, s32[2]{0:T(128)}, u32[]{:S(2)}) copy-start(s32[2]{0:T(128)} %tiles.1) | copy-start | bytes 28
  90.2 2.5 %copy-start.6 = (f32[128]{0:T(128)S(1)}, f32[128]{0:T(128)}, u32[]{:S(2)}) copy-start(f32[128]{0:T(128)} %param.16) | copy-start | bytes 1540
  92.7 5.2 %copy-start.12 = (bf16[1,2,32,1920]{3,2,1,0:T(8,128)(2,1)S(1)}, bf16[1,2,32,1920]{3,2,1,0:T(8,128)(2,1)}, u32[]{:S(2)}) copy-start(bf16[1,2,32,1920]{3,2,1,0:T(8,128)(2,1)} %get-tuple-element.37) | copy-start | bytes 737284
  92.7 5.2 %copy-start.18 = (bf16[2,32,1920]{2,1,0:T(8,128)(2,1)S(1)}, bf16[2,32,1920]{2,1,0:T(8,128)(2,1)}, u32[]{:S(2)}) copy-start(bf16[2,32,1920]{2,1,0:T(8,128)(2,1)} %copy-done.17) | copy-start | bytes 737284
  92.7 5.2 %copy-start.24 = (bf16[2,32,1920]{2,1,0:T(8,128)(2,1)S(1)}, bf16[2,32,1920]{2,1,0:T(8,128)(2,1)}, u32[]{:S(2)}) copy-start(bf16[2,32,1920]{2,1,0:T(8,128)(2,1)} %copy-done.23) | copy-start | bytes 737284
  92.7 5.2 %copy-start.28 = (bf16[2,32,1920]{2,1,0:T(8,128)(2,1)S(1)}, bf16[2,32,1920]{2,1,0:T(8,128)(2,1)}, u32[]{:S(2)}) copy-start(bf16[2,32,1920]{2,1,0:T(8,128)(2,1)} %copy-done.27) | copy-start | bytes 737284
  97.9 22.0 %copy-start.33 = (bf16[4,2,32,512]{3,2,1,0:T(8,128)(2,1)}, bf16[4,2,32,512]{3,2,1,0:T(8,128)(2,1)S(1)}, u32[]{:S(2)}) copy-start(bf16[4,2,32,512]{3,2,1,0:T(8,128)(2,1)S(1)} %constant_dynamic-update-slice_fusion) | copy-start | bytes 786436
  109.6 20.0 %collective-permute-start.22 = (bf16[2,32,1920]{2,1,0:T(8,128)(2,1)S(1)}, bf16[2,32,1920]{2,1,0:T(8,128)(2,1)S(1)}, u32[]{:S(2)}, u32[]{:S(2)}) collective-permute-start(bf16[2,32,1920]{2,1,0:T(8,128)(2,1)S(1)} %bitcast.119), channel_id=1, source_target_pairs={{0,1},{1,2},{2,3},{3,0},{4,5},{5,6},{6,7},{7,4},{8,9},{9,10},{10,1... | collective-permute-start | bytes 737288 | tf_op jit(solution)/shard_map/ppermute | solution.py:225
  111.3 45.6 %collective-permute-start.21 = (bf16[2,32,1920]{2,1,0:T(8,128)(2,1)S(1)}, bf16[2,32,1920]{2,1,0:T(8,128)(2,1)}, u32[]{:S(2)}, u32[]{:S(2)}) collective-permute-start(bf16[2,32,1920]{2,1,0:T(8,128)(2,1)S(1)} %bitcast.108), channel_id=1, source_target_pairs={{0,3},{1,0},{2,1},{3,2},{4,7},{5,4},{6,5},{7,6},{8,11},{9,8},{10,9... | collective-permute-start | bytes 737288 | tf_op jit(solution)/shard_map/ppermute | solution.py:225
  116.0 17.5 %collective-permute-start.19 = (bf16[2,32,1920]{2,1,0:T(8,128)(2,1)S(1)}, bf16[2,32,1920]{2,1,0:T(8,128)(2,1)S(1)}, u32[]{:S(2)}, u32[]{:S(2)}) collective-permute-start(bf16[2,32,1920]{2,1,0:T(8,128)(2,1)S(1)} %bitcast.120), channel_id=1, source_target_pairs={{0,1},{1,2},{2,3},{3,0},{4,5},{5,6},{6,7},{7,4},{8,9},{9,10},{10,1... | collective-permute-start | bytes 737288 | tf_op jit(solution)/shard_map/ppermute | solution.py:225
  116.0 51.9 %collective-permute-start.18 = (bf16[2,32,1920]{2,1,0:T(8,128)(2,1)S(1)}, bf16[2,32,1920]{2,1,0:T(8,128)(2,1)}, u32[]{:S(2)}, u32[]{:S(2)}) collective-permute-start(bf16[2,32,1920]{2,1,0:T(8,128)(2,1)S(1)} %bitcast.104), channel_id=1, source_target_pairs={{0,3},{1,0},{2,1},{3,2},{4,7},{5,4},{6,5},{7,6},{8,11},{9,8},{10,9... | collective-permute-start | bytes 737288 | tf_op jit(solution)/shard_map/ppermute | solution.py:225
  122.6 50.6 %collective-permute-start.17 = (bf16[2,32,1920]{2,1,0:T(8,128)(2,1)S(1)}, bf16[2,32,1920]{2,1,0:T(8,128)(2,1)}, u32[]{:S(2)}, u32[]{:S(2)}) collective-permute-start(bf16[2,32,1920]{2,1,0:T(8,128)(2,1)S(1)} %bitcast.103), channel_id=1, source_target_pairs={{0,1},{1,2},{2,3},{3,0},{4,5},{5,6},{6,7},{7,4},{8,9},{9,10},{10,1... | collective-permute-start | bytes 737288 | tf_op jit(solution)/shard_map/ppermute | solution.py:225
  129.6 15.6 %collective-permute-start.15 = (bf16[2,32,1920]{2,1,0:T(8,128)(2,1)S(1)}, bf16[2,32,1920]{2,1,0:T(8,128)(2,1)S(1)}, u32[]{:S(2)}, u32[]{:S(2)}) collective-permute-start(bf16[2,32,1920]{2,1,0:T(8,128)(2,1)S(1)} %bitcast.121), channel_id=1, source_target_pairs={{0,3},{1,0},{2,1},{3,2},{4,7},{5,4},{6,5},{7,6},{8,11},{9,8},{10,9... | collective-permute-start | bytes 737288 | tf_op jit(solution)/shard_map/ppermute | solution.py:225
  133.5 44.3 %collective-permute-start.14 = (bf16[2,32,1920]{2,1,0:T(8,128)(2,1)S(1)}, bf16[2,32,1920]{2,1,0:T(8,128)(2,1)S(1)}, u32[]{:S(2)}, u32[]{:S(2)}) collective-permute-start(bf16[2,32,1920]{2,1,0:T(8,128)(2,1)S(1)} %bitcast.107), channel_id=1, source_target_pairs={{0,1},{1,2},{2,3},{3,0},{4,5},{5,6},{6,7},{7,4},{8,9},{9,10},{10,1... | collective-permute-start | bytes 737288 | tf_op jit(solution)/shard_map/ppermute | solution.py:225
  145.2 11.0 %collective-permute-start.12 = (bf16[2,32,1920]{2,1,0:T(8,128)(2,1)S(1)}, bf16[2,32,1920]{2,1,0:T(8,128)(2,1)S(1)}, u32[]{:S(2)}, u32[]{:S(2)}) collective-permute-start(bf16[2,32,1920]{2,1,0:T(8,128)(2,1)S(1)} %bitcast.122), channel_id=1, source_target_pairs={{0,3},{1,0},{2,1},{3,2},{4,7},{5,4},{6,5},{7,6},{8,11},{9,8},{10,9... | collective-permute-start | bytes 737288 | tf_op jit(solution)/shard_map/ppermute | solution.py:225
  156.2 10.7 %collective-permute-start.23 = (bf16[2,32,1920]{2,1,0:T(8,128)(2,1)S(1)}, bf16[2,32,1920]{2,1,0:T(8,128)(2,1)S(1)}, u32[]{:S(2)}, u32[]{:S(2)}) collective-permute-start(bf16[2,32,1920]{2,1,0:T(8,128)(2,1)S(1)} %fusion.21), channel_id=1, source_target_pairs={{0,1},{1,2},{2,3},{3,0},{4,5},{5,6},{6,7},{7,4},{8,9},{9,10},{10,1... | collective-permute-start | bytes 737288 | tf_op jit(solution)/shard_map/ppermute | solution.py:225
  156.8 15.3 %collective-permute-start.20 = (bf16[2,32,1920]{2,1,0:T(8,128)(2,1)S(1)}, bf16[2,32,1920]{2,1,0:T(8,128)(2,1)S(1)}, u32[]{:S(2)}, u32[]{:S(2)}) collective-permute-start(bf16[2,32,1920]{2,1,0:T(8,128)(2,1)S(1)} %fusion.24), channel_id=1, source_target_pairs={{0,1},{1,2},{2,3},{3,0},{4,5},{5,6},{6,7},{7,4},{8,9},{9,10},{10,1... | collective-permute-start | bytes 737288 | tf_op jit(solution)/shard_map/ppermute | solution.py:225
  166.9 9.8 %collective-permute-start.16 = (bf16[2,32,1920]{2,1,0:T(8,128)(2,1)S(1)}, bf16[2,32,1920]{2,1,0:T(8,128)(2,1)S(1)}, u32[]{:S(2)}, u32[]{:S(2)}) collective-permute-start(bf16[2,32,1920]{2,1,0:T(8,128)(2,1)S(1)} %fusion.27), channel_id=1, source_target_pairs={{0,3},{1,0},{2,1},{3,2},{4,7},{5,4},{6,5},{7,6},{8,11},{9,8},{10,9... | collective-permute-start | bytes 737288 | tf_op jit(solution)/shard_map/ppermute | solution.py:225
  167.9 14.0 %collective-permute-start.13 = (bf16[2,32,1920]{2,1,0:T(8,128)(2,1)S(1)}, bf16[2,32,1920]{2,1,0:T(8,128)(2,1)S(1)}, u32[]{:S(2)}, u32[]{:S(2)}) collective-permute-start(bf16[2,32,1920]{2,1,0:T(8,128)(2,1)S(1)} %fusion.30), channel_id=1, source_target_pairs={{0,3},{1,0},{2,1},{3,2},{4,7},{5,4},{6,5},{7,6},{8,11},{9,8},{10,9... | collective-permute-start | bytes 737288 | tf_op jit(solution)/shard_map/ppermute | solution.py:225
  (12 other events, 16.0 us)
Sparse Core Ops, SparseCore 0:
  10.5 54.8 all-gather.1
  107.3 70.4 reduce-scatter.1

commit v6 on v5

--- a/solution.py
+++ b/solution.py
@@ -9,7 +9,6 @@
 from jax.sharding import PartitionSpec as P
 
 TILE_ROWS = 32
-CHUNKS = 4
 
 
 EPSILON = 1e-05
@@ -72,26 +71,26 @@
 def attend_kernel(count, assignment, tiles, owners, *refs):
     key_parts, value_parts = refs[:count], refs[count : 2 * count]
     normed, masked, gain = refs[2 * count : 2 * count + 3]
-    key_out, value_out, score_out, picked = refs[2 * count + 3 : 2 * count + 7]
-    key_pre, key_normed, values, key_sum, value_sum = refs[2 * count + 7 :]
-    parts, img_count, own_rows, head_dim = key_parts[0].shape
+    rows_out, score_out, picked = refs[2 * count + 3 : 2 * count + 6]
+    key_pre, key_normed, values, key_sum, value_sum = refs[2 * count + 6 :]
+    img_count, own_rows, head_dim = key_parts[0].shape[1:]
+    parts = rows_out.shape[0]
     img_rows = parts * own_rows
-    step = pl.program_id(1)
+    group, step = pl.program_id(0), pl.program_id(1)
     inv_root = 1.0 / math.sqrt(head_dim)
 
     @pl.when(step == 0)
     def _():
         for i in range(img_count):
-            for target, sources in ((0, key_parts), (1, value_parts)):
-                total = sources[0][:, i].astype(jnp.float32)
-                for source in sources[1:]:
-                    total = total + source[:, i].astype(jnp.float32)
-                total = total.reshape(img_rows, head_dim)
-                if target == 0:
-                    key_pre[i] = total
-                    key_normed[i] = (total * rms_scale(total) * gain[...]).astype(jnp.bfloat16)
-                else:
-                    values[i] = total.astype(jnp.bfloat16)
+            keys, upper = [
+                jnp.concatenate(
+                    [source[:, i].reshape(-1, head_dim) for source in sources], axis=0
+                )
+                for sources in (key_parts, value_parts)
+            ]
+            key_pre[i] = keys
+            key_normed[i] = (keys * rms_scale(keys) * gain[...]).astype(jnp.bfloat16)
+            values[i] = upper.astype(jnp.bfloat16)
         key_sum[...] = jnp.zeros_like(key_sum)
         value_sum[...] = jnp.zeros_like(value_sum)
 
@@ -117,41 +116,43 @@
 
     @pl.when(step == pl.num_programs(1) - 1)
     def _():
+        shape = (parts, own_rows, head_dim)
+        key_cols = pl.ds(pl.multiple_of(group * head_dim, head_dim), head_dim)
+        value_cols = pl.ds(
+            pl.multiple_of((pl.num_programs(0) + group) * head_dim, head_dim), head_dim
+        )
         for i in range(img_count):
             source = key_pre[i]
             key_rows = rms_back(source, rms_scale(source), gain[...], key_sum[i])
-            shape = (parts, own_rows, head_dim)
-            key_out[:, i] = key_rows.astype(jnp.bfloat16).reshape(shape)
-            value_out[:, i] = value_sum[i].astype(jnp.bfloat16).reshape(shape)
+            rows_out[:, i, :, key_cols] = key_rows.astype(jnp.bfloat16).reshape(shape)
+            rows_out[:, i, :, value_cols] = value_sum[i].astype(jnp.bfloat16).reshape(shape)
 
 
 def attend(pieces, normed, masked, gain, assignment, tiles, owners):
     seq_count, groups, stacked, head_dim = normed.shape
-    parts, img_count, own_rows, columns = pieces[0].shape
+    img_count, own_rows, columns = pieces[0].shape[1:]
+    parts = sum(piece.shape[0] for piece in pieces)
     img_rows = parts * own_rows
-    count = len(pieces)
-    part = (parts, img_count, own_rows, head_dim)
-    keys = pl.BlockSpec(part, lambda g, b, *_: (0, 0, 0, g))
-    values = pl.BlockSpec(part, lambda g, b, *_: (0, 0, 0, groups + g))
+    shapes = [(piece.shape[0], img_count, own_rows, head_dim) for piece in pieces]
+    keys = [pl.BlockSpec(shape, lambda g, b, *_: (0, 0, 0, g)) for shape in shapes]
+    values = [pl.BlockSpec(shape, lambda g, b, *_: (0, 0, 0, groups + g)) for shape in shapes]
     stack = pl.BlockSpec((1, 1, stacked, head_dim), lambda g, b, *_: (b, g, 0, 0))
-    rows = jax.ShapeDtypeStruct((parts, img_count, own_rows, columns // 2), jnp.bfloat16)
+    rows = (parts, img_count, own_rows, columns)
     return pl.pallas_call(
-        functools.partial(attend_kernel, count),
+        functools.partial(attend_kernel, len(pieces)),
         out_shape=(
-            rows,
-            rows,
+            jax.ShapeDtypeStruct(rows, jnp.bfloat16),
             jax.ShapeDtypeStruct((seq_count, groups, stacked, img_rows), jnp.bfloat16),
             jax.ShapeDtypeStruct((seq_count, groups, img_rows, head_dim), jnp.bfloat16),
         ),
         grid_spec=pltpu.PrefetchScalarGridSpec(
             num_scalar_prefetch=3,
             grid=(groups, seq_count),
-            in_specs=[keys] * count
-            + [values] * count
+            in_specs=keys
+            + values
             + [stack, stack, pl.BlockSpec((1, head_dim), lambda *_: (0, 0))],
             out_specs=(
-                keys,
-                keys,
+                pl.BlockSpec(rows, lambda *_: (0, 0, 0, 0)),
                 pl.BlockSpec((1, 1, stacked, img_rows), lambda g, b, *_: (b, g, 0, 0)),
                 pl.BlockSpec((1, 1, img_rows, head_dim), lambda g, b, *_: (b, g, 0, 0)),
             ),
@@ -200,7 +201,44 @@
     )(queries, score_grad, keys, gain)
 
 
+def terms_kernel(rows, weight, own, left, right, leaving_right, leaving_left):
+    parts, img_count, own_rows, cols = rows.shape
+    first = leaving_right.shape[0]
+    term = dot(rows[...].reshape(-1, cols), weight[...], 1, 1).astype(jnp.bfloat16)
+    term = term.reshape(parts, img_count, own_rows, -1)
+    own[...] = term[0]
+    left[...] = term[1]
+    right[...] = term[2]
+    leaving_right[...] = term[3, :first]
+    leaving_left[...] = term[3, first:]
+
+
+def terms(rows, weight, chunks):
+    parts, img_count, own_rows, cols = rows.shape
+    vis_width = weight.shape[0]
+    width = vis_width // chunks
+    first = img_count // 2
+    counts = (img_count, img_count, img_count, first, img_count - first)
+    return pl.pallas_call(
+        terms_kernel,
+        out_shape=[
+            jax.ShapeDtypeStruct((count, own_rows, vis_width), jnp.bfloat16) for count in counts
+        ],
+        grid=(chunks,),
+        in_specs=[
+            pl.BlockSpec(rows.shape, lambda c: (0, 0, 0, 0)),
+            pl.BlockSpec((width, cols), lambda c: (c, 0)),
+        ],
+        out_specs=[
+            pl.BlockSpec((count, own_rows, width), lambda c: (0, 0, c)) for count in counts
+        ],
+        compiler_params=pltpu.CompilerParams(vmem_limit_bytes=32 * 1024 * 1024),
+        name="terms",
+    )(rows, weight)
+
+
 def per_device(
+    dp_size,
     mp_size,
     queries,
     out_grad,
@@ -215,71 +253,83 @@
 ):
     img_count, own_rows, vis_width = images.shape
     head_dim = query_gain.shape[0]
-    key_cols = key_weight.shape[1]
+    own_width, key_cols = key_weight.shape
     key_heads = key_cols // head_dim
     cols = 2 * key_cols
-    half = mp_size // 2
-    width = vis_width // CHUNKS
+    pairs = dp_size // 2
+    place = lax.axis_index("dp")
+    pair, core = place // 2, place % 2
+    line = lax.axis_index("mp")
+    first = img_count // 2
 
     def ring(value, step):
         return lax.ppermute(value, "mp", [(i, (i + step) % mp_size) for i in range(mp_size)])
 
-    own_weight = jnp.concatenate((key_weight, value_weight), axis=1)
-    weight = lax.all_gather(own_weight, "dp", axis=0, tiled=True)
-
-    blocks = []
-    total = 0.0
-    for c in range(CHUNKS):
-        piece = images[:, :, c * width : (c + 1) * width]
-        parts = [piece] + [None] * (mp_size - 1)
-        right = left = piece
-        for k in range(1, half + 1):
-            if k < half or c < CHUNKS // 2:
-                parts[k] = right = ring(right, 1)
-            if k < half or c >= CHUNKS // 2:
-                parts[mp_size - k] = left = ring(left, -1)
-        blocks.append(jnp.stack(parts).reshape(-1, width))
-        total = total + dot(blocks[c], weight[c * width : (c + 1) * width], 1, 0)
-    total = total.reshape(mp_size, img_count, own_rows, cols)
+    def swap(value, mask):
+        return lax.ppermute(value, "dp", [(i, i ^ mask) for i in range(dp_size)])
+
+    from_left, from_right = ring(images, 1), ring(images, -1)
     query_gain, key_gain = query_gain[None, :], key_gain[None, :]
     normed, masked = before(queries, out_grad, query_gain, lengths, key_heads)
-    owners = (lax.axis_index("mp") - jnp.arange(mp_size, dtype=jnp.int32)) % mp_size
-    key_rows, value_rows, score_grad, seq_keys = attend(
-        [total], normed, masked, key_gain, assignment, tile_counts, owners
+
+    own_weight = jnp.concatenate((key_weight, value_weight), axis=1)
+    if pairs > 4:
+        weight = lax.all_gather(own_weight, "dp", axis=0, tiled=True)
+    else:
+        sent = [swap(own_weight, 2 * r) for r in range(1, pairs)]
+        weight = jnp.zeros((2 * pairs, own_width, cols), jnp.bfloat16)
+        from_left, from_right, sent, weight, normed, masked = lax.optimization_barrier(
+            (from_left, from_right, sent, weight, normed, masked)
+        )
+        mine = jnp.stack([own_weight, *sent])
+        mates = swap(mine, 1)
+        for r in range(pairs):
+            for source, side in ((mine, core), (mates, 1 - core)):
+                weight = lax.dynamic_update_slice_in_dim(
+                    weight, source[r : r + 1], 2 * (pair ^ r) + side, axis=0
+                )
+        weight = weight.reshape(vis_width, cols)
+    opposite = (ring(from_left[:first], 1), ring(from_right[first:], -1))
+
+    near = jnp.stack((images, from_left, from_right)).reshape(-1, vis_width)
+    near_total = dot(near, weight, 1, 0)
+    near_total, opposite = lax.optimization_barrier((near_total, opposite))
+    near_total = near_total.reshape(3, img_count, own_rows, cols)
+    far = jnp.concatenate(opposite).reshape(-1, vis_width)
+    far_total = dot(far, weight, 1, 0).reshape(1, img_count, own_rows, cols)
+    owners = (line + jnp.array((0, -1, 1, 2), jnp.int32)) % mp_size
+    rows, score_grad, seq_keys = attend(
+        [near_total, far_total], normed, masked, key_gain, assignment, tile_counts, owners
     )
     query_grad = after(queries, score_grad, seq_keys, query_gain)
-    rows = jnp.concatenate((key_rows, value_rows), axis=3).reshape(-1, cols)
-    image_grad = []
-    for c in range(CHUNKS):
-        term = dot(rows, weight[c * width : (c + 1) * width], 1, 1)
-        term = term.astype(jnp.bfloat16).reshape(mp_size, img_count, own_rows, width)
-        total = term[0].astype(jnp.float32)
-        leftward = rightward = None
-        for k in range(half, 0, -1):
-            if k < half or c < CHUNKS // 2:
-                own = term[k]
-                if leftward is not None:
-                    own = (own.astype(jnp.float32) + leftward.astype(jnp.float32)).astype(
-                        jnp.bfloat16
-                    )
-                leftward = ring(own, -1)
-            if k < half or c >= CHUNKS // 2:
-                own = term[mp_size - k]
-                if rightward is not None:
-                    own = (own.astype(jnp.float32) + rightward.astype(jnp.float32)).astype(
-                        jnp.bfloat16
-                    )
-                rightward = ring(own, 1)
-        for arrived in (leftward, rightward):
-            if arrived is not None:
-                total = total + arrived.astype(jnp.float32)
-        image_grad.append(total.astype(jnp.bfloat16))
-    image_grad = jnp.concatenate(image_grad, axis=2)
-    weight_part = jnp.concatenate(
-        [dot(block, rows, 0, 0).astype(jnp.bfloat16) for block in blocks], axis=0
-    )
-    weight_grad = lax.psum_scatter(weight_part, "dp", scatter_dimension=0, tiled=True)
-    weight_grad = weight_grad.astype(jnp.float32)
+
+    own, to_left, to_right, leaving_right, leaving_left = terms(rows, weight, 4)
+    right_half = ring(leaving_right, 1).astype(jnp.float32)
+    left_half = ring(leaving_left, -1).astype(jnp.float32)
+    to_right = jnp.concatenate(
+        ((to_right[:first].astype(jnp.float32) + right_half).astype(jnp.bfloat16), to_right[first:])
+    )
+    to_left = jnp.concatenate(
+        (to_left[:first], (to_left[first:].astype(jnp.float32) + left_half).astype(jnp.bfloat16))
+    )
+    from_left = ring(to_right, 1).astype(jnp.float32)
+    from_right = ring(to_left, -1).astype(jnp.float32)
+    image_grad = (own.astype(jnp.float32) + from_left + from_right).astype(jnp.bfloat16)
+
+    all_rows = rows.reshape(-1, cols)
+    weight_part = dot(jnp.concatenate((near, far)), all_rows, 0, 0)
+    if pairs > 4:
+        weight_grad = lax.psum_scatter(weight_part, "dp", scatter_dimension=0, tiled=True)
+    else:
+        weight_part = weight_part.astype(jnp.bfloat16).reshape(pairs, 2, own_width, cols)
+        both = lax.dynamic_index_in_dim(weight_part, core, 1, keepdims=False).astype(jnp.float32)
+        both = both + swap(
+            lax.dynamic_index_in_dim(weight_part, 1 - core, 1, keepdims=False), 1
+        ).astype(jnp.float32)
+        weight_grad = lax.dynamic_index_in_dim(both, pair, 0, keepdims=False)
+        for r in range(1, pairs):
+            sent = lax.dynamic_index_in_dim(both, pair ^ r, 0, keepdims=False)
+            weight_grad = weight_grad + swap(sent.astype(jnp.bfloat16), 2 * r).astype(jnp.float32)
     return (query_grad, image_grad, weight_grad[:, :key_cols], weight_grad[:, key_cols:])
 
 
@@ -298,7 +348,7 @@
     )
 
     def body(*args):
-        return per_device(mesh.shape["mp"], *args)
+        return per_device(mesh.shape["dp"], mesh.shape["mp"], *args)
 
     return jax.shard_map(
         body,

time: 193 us -> 180 us (0.933)
  waiting for transfers between devices: 77.6 us -> 103 us
  starting transfers between devices: 43 us -> 20.4 us
  matrix products: 23.1 us -> 5.6 us
  between operations: 14.7 us -> 0.94 us
  local copies, waits for them, and re-layouts: 6.32 us -> 17.9 us
  Pallas kernels: 14.4 us -> 17.4 us
    ppermute x0 -> x8, waiting for transfers between devices: none -> 45.3 us  [swap(): return lax.ppermute(value, 'dp', [(i, i ^ mask) for i in range(dp_size)])]
    ppermute x24 -> x8, starting transfers between devices: 42.9 us -> 12.2 us  [ring(): lax.ppermute(value, 'mp', [(i, (i + step) % mp_size) for i in range(mp_si...]
    ppermute x24 -> x8, waiting for transfers between devices: 77.6 us -> 57.4 us  [ring(): lax.ppermute(value, 'mp', [(i, (i + step) % mp_size) for i in range(mp_si...]
    dot_general x12 -> x3, matrix products: 23.1 us -> 5.6 us  [dot(): lax.dot_general(left, right, (((left_dim,), (right_dim,)), ((), ())), pre...]
    ppermute x0 -> x8, starting transfers between devices: none -> 8.16 us  [swap(): return lax.ppermute(value, 'dp', [(i, i ^ mask) for i in range(dp_size)])]
    dynamic_update_slice x0 -> x8, local copies, waits for them, and re-layouts: none -> 6.74 us  [per_device(): lax.dynamic_update_slice_in_dim(weight, source[r:r + 1], 2 * (pair ^ r) +...]
    concatenate x3 -> x2, other arithmetic: 7.28 us -> 1.12 us  [the longest x1 1.03 us: per_device(): jnp.concatenate(((to_right[:first].astype(jnp.float32) + right_half).asty...]
    add x0 -> x2, other arithmetic: none -> 5.16 us  [the longest x1 4.53 us: per_device(): both + swap(lax.dynamic_index_in_dim(weight_part, 1 - core, 1, keepdims=F...]
  transfers between devices with their start and end apart: 26 -> 16, of which waited for: 13 -> 12; matrix products, arithmetic and copies ran while one was open for 9% -> 15% of each run, Pallas kernels for 5% -> 5%
where the time goes in v6:
time: 180 us; the launch traced here: 179 us
  waiting for transfers between devices  103 us (57%)
  starting transfers between devices  20.4 us (11%)
  local copies, waits for them, and re-layouts  17.9 us (10%)
  Pallas kernels  17.4 us (10%)
  other arithmetic  14.3 us (8%)
  matrix products  5.6 us (3%)
    ppermute x8, waiting for transfers between devices, ring(): lax.ppermute(value, 'mp', [(i, (i + step) % mp_size) for i in range(mp_si...  57.4 us
    ppermute x8, waiting for transfers between devices, swap(): return lax.ppermute(value, 'dp', [(i, i ^ mask) for i in range(dp_size)])  45.3 us
    ppermute x8, starting transfers between devices, ring(): lax.ppermute(value, 'mp', [(i, (i + step) % mp_size) for i in range(mp_si...  12.2 us
    ppermute x8, starting transfers between devices, swap(): return lax.ppermute(value, 'dp', [(i, i ^ mask) for i in range(dp_size)])  8.16 us
    dynamic_update_slice x8, local copies, waits for them, and re-layouts, per_device(): lax.dynamic_update_slice_in_dim(weight, source[r:r + 1], 2 * (pair ^ r) +...  6.74 us
    dot_general x3, matrix products, dot(): lax.dot_general(left, right, (((left_dim,), (right_dim,)), ((), ())), pre...  5.6 us
    pallas_call x1, Pallas kernels, attend(): pl.pallas_call(functools.partial(attend_kernel, len(pieces)), out_shape=(...  4.97 us
    pallas_call x1, Pallas kernels, before(): pl.pallas_call(before_kernel, out_shape=(shape, shape), grid_spec=pltpu.P...  4.83 us
  transfers between devices with their start and end apart: 16, of which 12 were waited for; matrix products, arithmetic and copies ran while one was open for 15% of the time, Pallas kernels for 5%

profile of v6, /device:TPU:0, one launch (start us, length us, event | category | flops | bytes accessed | tf_op | source)
XLA Modules:
  0.0 179.3 jit_solution(10770832928526205045)
XLA Ops:
  0.6 1.1 constant_dynamic-update-slice_fusion.1
  1.7 1.1 constant_dynamic-update-slice_fusion
  2.8 4.0 %collective-permute-start.4 = (bf16[960,512]{1,0:T(8,128)(2,1)S(1)}, bf16[960,512]{1,0:T(8,128)(2,1)S(1)}, u32[]{:S(2)}, u32[]{:S(2)}) collective-permute-start(bf16[960,512]{1,0:T(8,128)(2,1)S(1)} %constant_dynamic-update-slice_fusion), channel_id=1, source_target_pairs={{0,24},{4,28},{8,16},{12,20},{16,8},{20,12},{24,0},{28,4},{1,25},{... | collective-permute-start | bytes 2949128 | tf_op jit(solution)/shard_map/ppermute | solution.py:269
  6.7 0.5 collective-permute-start.3
  7.4 4.0 %collective-permute-start.1 = (bf16[2,32,7680]{2,1,0:T(8,128)(2,1)}, bf16[2,32,7680]{2,1,0:T(8,128)(2,1)}, u32[]{:S(2)}, u32[]{:S(2)}) collective-permute-start(bf16[2,32,7680]{2,1,0:T(8,128)(2,1)} %param.13), channel_id=1, source_target_pairs={{0,3},{1,0},{2,1},{3,2},{4,7},{5,4},{6,5},{7,6},{8,11},{9,8},{10,9... | collective-permute-start | bytes 2949128 | tf_op jit(solution)/shard_map/ppermute | solution.py:266
  11.4 4.8 %before.1 = (bf16[2,2,1024,128]{3,2,1,0:T(8,128)(2,1)}, bf16[2,2,1024,128]{3,2,1,0:T(8,128)(2,1)}) custom-call(s32[2]{0:T(128)} %lengths.1, bf16[2,128,2048]{2,1,0:T(8,128)(2,1)} %query.3, bf16[2,128,2048]{2,1,0:T(8,128)(2,1)} %grad.1, f32[1,128]{1,0:T(1,128)} %bitcast.63), custom_call_target="tpu_custom_call" | custom-call | tf_op jit(solution)/shard_map/before/pallas_call | solution.py:58
  16.2 13.1 %collective-permute-done.4 = bf16[960,512]{1,0:T(8,128)(2,1)S(1)} collective-permute-done((bf16[960,512]{1,0:T(8,128)(2,1)S(1)}, bf16[960,512]{1,0:T(8,128)(2,1)S(1)}, u32[]{:S(2)}, u32[]{:S(2)}) %collective-permute-start.4) | collective-permute-done | bytes 983072 | tf_op jit(solution)/shard_map/ppermute | solution.py:269
  29.4 20.2 %collective-permute-done.3 = bf16[960,512]{1,0:T(8,128)(2,1)S(1)} collective-permute-done((bf16[960,512]{1,0:T(8,128)(2,1)S(1)}, bf16[960,512]{1,0:T(8,128)(2,1)S(1)}, u32[]{:S(2)}, u32[]{:S(2)}) %collective-permute-start.3) | collective-permute-done | bytes 983072 | tf_op jit(solution)/shard_map/ppermute | solution.py:269
  49.6 0.4 collective-permute-done.2
  50.0 3.9 %collective-permute-done = bf16[2,32,7680]{2,1,0:T(8,128)(2,1)} collective-permute-done((bf16[2,32,7680]{2,1,0:T(8,128)(2,1)}, bf16[2,32,7680]{2,1,0:T(8,128)(2,1)}, u32[]{:S(2)}, u32[]{:S(2)}) %collective-permute-start) | collective-permute-done | bytes 983072 | tf_op jit(solution)/shard_map/ppermute | solution.py:266
  53.8 3.2 %pad_maximum_fusion = bf16[4,960,512]{2,1,0:T(8,128)(2,1)} fusion(bf16[1,960,512]{2,1,0:T(8,128)(2,1)S(1)} %bitcast.57, bf16[1,960,512]{2,1,0:T(8,128)(2,1)S(1)} %bitcast.58, bf16[1,960,512]{2,1,0:T(8,128)(2,1)} %bitcast.6, bf16[1,960,512]{2,1,0:T(8,128)(2,1)S(1)} %bitcast.56), kind=kLoop, calls=%fused_computation.2 | loop fusion | flops 5898240 | bytes 7864320 | tf_op jit(solution)/shard_map/stack | solution.py:284
  57.0 1.1 slice.40
  58.1 1.1 slice.41
  59.2 1.8 %collective-permute-start.7 = (bf16[1,32,7680]{2,1,0:T(8,128)(2,1)S(1)}, bf16[1,32,7680]{2,1,0:T(8,128)(2,1)S(1)}, u32[]{:S(2)}, u32[]{:S(2)}) collective-permute-start(bf16[1,32,7680]{2,1,0:T(8,128)(2,1)S(1)} %slice.41), channel_id=1, source_target_pairs={{0,3},{1,0},{2,1},{3,2},{4,7},{5,4},{6,5},{7,6},{8,11},{9,8},{10,9... | collective-permute-start | bytes 1474568 | tf_op jit(solution)/shard_map/ppermute | solution.py:266
  61.3 0.7 broadcast_in_dim.9
  62.0 1.8 %pad_maximum_fusion.1 = bf16[3,2,32,7680]{3,2,1,0:T(8,128)(2,1)S(1)} fusion(bf16[1,2,32,7680]{3,2,1,0:T(8,128)(2,1)} %bitcast.3, bf16[1,2,32,7680]{3,2,1,0:T(8,128)(2,1)} %bitcast.2, bf16[1,2,32,7680]{3,2,1,0:T(8,128)(2,1)S(1)} %bitcast.62), kind=kLoop, calls=%fused_computation.7 | loop fusion | flops 2949120 | bytes 5898240 | tf_op jit(solution)/shard_map/stack | solution.py:294
  64.1 1.3 slice_dynamic-update-slice_fusion.3
  65.4 1.3 constant_dynamic-update-slice_fusion.6
  66.7 1.3 slice_dynamic-update-slice_fusion.2
  68.1 1.3 slice_dynamic-update-slice_fusion.1
  69.5 1.3 slice_dynamic-update-slice_fusion
  70.8 1.7 fusion.11
  72.5 0.6 collective-permute-done.7
  73.1 10.6 %collective-permute-done.6 = bf16[1,32,7680]{2,1,0:T(8,128)(2,1)S(1)} collective-permute-done((bf16[1,32,7680]{2,1,0:T(8,128)(2,1)S(1)}, bf16[1,32,7680]{2,1,0:T(8,128)(2,1)S(1)}, u32[]{:S(2)}, u32[]{:S(2)}) %collective-permute-start.6) | collective-permute-done | bytes 491552 | tf_op jit(solution)/shard_map/ppermute | solution.py:266
  83.8 1.5 convolution_bitcast_fusion.refs_1_.refs_3_
  85.3 5.0 %attend.1 = (bf16[4,2,32,512]{3,2,1,0:T(8,128)(2,1)S(1)}, bf16[2,2,1024,128]{3,2,1,0:T(8,128)(2,1)S(1)}, bf16[2,2,128,128]{3,2,1,0:T(8,128)(2,1)S(1)}) custom-call(s32[2]{0:T(128)S(1)} %copy-done.4, s32[2]{0:T(128)S(1)} %copy-done.5, s32[4]{0:T(128)S(1)} %and_select_fusion.owners, f32[3,2,32,512]{3,2,1,0:T(8,128)S(1)} %bitcast.50, ...), custom_call_target="tpu_custom_call" | custom-call | tf_op jit(solution)/shard_map/attend/pallas_call | solution.py:141
  90.3 3.3 %terms.1 = (bf16[2,32,7680]{2,1,0:T(8,128)(2,1)S(1)}, bf16[2,32,7680]{2,1,0:T(8,128)(2,1)S(1)}, bf16[2,32,7680]{2,1,0:T(8,128)(2,1)S(1)}, bf16[1,32,7680]{2,1,0:T(8,128)(2,1)S(1)}, bf16[1,32,7680]{2,1,0:T(8,128)(2,1)S(1)}) custom-call(bf16[4,2,32,512]{3,2,1,0:T(8,128)(2,1)S(1)} %get-tuple-element.40.rows, bf16[7680,512]{1,0:T(8,128)(2,1)S(1)} %bitcast.49), custom_call_target="tpu_custom_call" | custom-call | tf_op jit(solution)/shard_map/terms/pallas_call | solution.py:222
  93.7 1.6 collective-permute-start.8
  95.3 2.3 %collective-permute-start.10 = (bf16[1,32,7680]{2,1,0:T(8,128)(2,1)S(1)}, bf16[1,32,7680]{2,1,0:T(8,128)(2,1)S(1)}, u32[]{:S(2)}, u32[]{:S(2)}) collective-permute-start(bf16[1,32,7680]{2,1,0:T(8,128)(2,1)S(1)} %get-tuple-element.45), channel_id=1, source_target_pairs={{0,3},{1,0},{2,1},{3,2},{4,7},{5,4},{6,5},{7,6},{8,11},{9,8},{10,9... | collective-permute-start | bytes 1474568 | tf_op jit(solution)/shard_map/ppermute | solution.py:266
  97.6 2.5 %convolution_convert_fusion = bf16[7680,512]{1,0:T(8,128)(2,1)S(1)} fusion(bf16[256,512]{1,0:T(8,128)(2,1)S(1)} %bitcast.52, bf16[64,7680]{1,0:T(8,128)(2,1)S(1)} %bitcast.59, bf16[192,7680]{1,0:T(8,128)(2,1)S(1)} %bitcast.61), kind=kOutput, calls=%fused_computation | convolution fusion | flops 2025062400 | bytes 12058624 | tf_op jit(solution)/shard_map/dot_general | solution.py:29
  100.1 2.4 %dynamic-slice_bitcast_fusion = bf16[4,960,512]{2,1,0:T(8,128)(2,1)} fusion(bf16[4,2,960,512]{3,2,1,0:T(8,128)(2,1)S(1)} %bitcast.54, s32[]{:T(128)S(6)} %select_n.73), kind=kLoop, calls=%fused_computation.6 | loop fusion | bytes 7864324 | tf_op jit(solution)/shard_map/jit(dynamic_index_in_dim)/squeeze | solution.py:327
  102.5 1.8 %copy-done.7 = bf16[7680,512]{1,0:T(8,128)(2,1)} copy-done((bf16[7680,512]{1,0:T(8,128)(2,1)}, bf16[7680,512]{1,0:T(8,128)(2,1)S(1)}, u32[]{:S(2)}) %copy-start.7) | copy-done | bytes 7864344
  104.3 14.1 %collective-permute-done.10 = bf16[1,32,7680]{2,1,0:T(8,128)(2,1)S(1)} collective-permute-done((bf16[1,32,7680]{2,1,0:T(8,128)(2,1)S(1)}, bf16[1,32,7680]{2,1,0:T(8,128)(2,1)S(1)}, u32[]{:S(2)}, u32[]{:S(2)}) %collective-permute-start.10) | collective-permute-done | bytes 491552 | tf_op jit(solution)/shard_map/ppermute | solution.py:266
  118.6 2.2 %collective-permute-start.11 = (bf16[2,32,7680]{2,1,0:T(8,128)(2,1)S(1)}, bf16[2,32,7680]{2,1,0:T(8,128)(2,1)}, u32[]{:S(2)}, u32[]{:S(2)}) collective-permute-start(bf16[2,32,7680]{2,1,0:T(8,128)(2,1)S(1)} %pad_maximum_fusion.3), channel_id=1, source_target_pairs={{0,3},{1,0},{2,1},{3,2},{4,7},{5,4},{6,5},{7,6},{8,11},{9,8},{10,9... | collective-permute-start | bytes 2949128 | tf_op jit(solution)/shard_map/ppermute | solution.py:266
  121.0 1.0 pad_maximum_fusion.2
  122.0 4.3 %after.1 = bf16[2,128,2048]{2,1,0:T(8,128)(2,1)} custom-call(bf16[2,128,2048]{2,1,0:T(8,128)(2,1)} %query.3, bf16[2,2,1024,128]{3,2,1,0:T(8,128)(2,1)} %copy-done, bf16[2,2,128,128]{3,2,1,0:T(8,128)(2,1)} %copy-done.3, f32[1,128]{1,0:T(1,128)} %bitcast.64), custom_call_target="tpu_custom_call" | custom-call | tf_op jit(solution)/shard_map/after/pallas_call | solution.py:189
  126.4 4.5 %convert_add_fusion = f32[4,960,512]{2,1,0:T(8,128)S(1)} fusion(bf16[4,960,512]{2,1,0:T(8,128)(2,1)} %collective-permute-done.12, bf16[4,2,960,512]{3,2,1,0:T(8,128)(2,1)} %bitcast.55, s32[]{:T(128)S(6)} %select_n.72), kind=kLoop, calls=%fused_computation.1 | loop fusion | flops 5898240 | bytes 15728644 | tf_op jit(solution)/shard_map/add | solution.py:326
  130.9 0.4 fusion.5
  131.3 1.5 collective-permute-start.13
  132.8 1.5 collective-permute-start.15
  134.3 0.5 collective-permute-start.14
  134.8 9.1 %collective-permute-done.11 = bf16[2,32,7680]{2,1,0:T(8,128)(2,1)} collective-permute-done((bf16[2,32,7680]{2,1,0:T(8,128)(2,1)S(1)}, bf16[2,32,7680]{2,1,0:T(8,128)(2,1)}, u32[]{:S(2)}, u32[]{:S(2)}) %collective-permute-start.11) | collective-permute-done | bytes 983072 | tf_op jit(solution)/shard_map/ppermute | solution.py:266
  143.9 19.2 %collective-permute-done.9 = bf16[2,32,7680]{2,1,0:T(8,128)(2,1)} collective-permute-done((bf16[2,32,7680]{2,1,0:T(8,128)(2,1)}, bf16[2,32,7680]{2,1,0:T(8,128)(2,1)}, u32[]{:S(2)}, u32[]{:S(2)}) %collective-permute-start.9) | collective-permute-done | bytes 983072 | tf_op jit(solution)/shard_map/ppermute | solution.py:266
  163.1 2.8 %add_convert_fusion = bf16[2,32,7680]{2,1,0:T(8,128)(2,1)} fusion(bf16[2,32,7680]{2,1,0:T(8,128)(2,1)} %collective-permute-done.11, bf16[2,32,7680]{2,1,0:T(8,128)(2,1)} %collective-permute-done.9, bf16[2,32,7680]{2,1,0:T(8,128)(2,1)S(1)} %get-tuple-element.41), kind=kLoop, calls=%fused_computation.14 | loop fusion | flops 2949120 | bytes 3932160 | tf_op jit(solution)/shard_map/convert_element_type | solution.py:317
  165.9 9.9 %collective-permute-done.15 = bf16[960,512]{1,0:T(8,128)(2,1)S(1)} collective-permute-done((bf16[960,512]{1,0:T(8,128)(2,1)S(1)}, bf16[960,512]{1,0:T(8,128)(2,1)S(1)}, u32[]{:S(2)}, u32[]{:S(2)}) %collective-permute-start.15) | collective-permute-done | bytes 983072 | tf_op jit(solution)/shard_map/ppermute | solution.py:269
  175.9 1.4 collective-permute-done.14
  177.2 0.6 fusion.4
  177.8 1.4 fusion.10
  (41 shorter events, 1.5 us)
Async XLA Ops:
  2.8 26.6 %collective-permute-start.4 = (bf16[960,512]{1,0:T(8,128)(2,1)S(1)}, bf16[960,512]{1,0:T(8,128)(2,1)S(1)}, u32[]{:S(2)}, u32[]{:S(2)}) collective-permute-start(bf16[960,512]{1,0:T(8,128)(2,1)S(1)} %constant_dynamic-update-slice_fusion), channel_id=1, source_target_pairs={{0,24},{4,28},{8,16},{12,20},{16,8},{20,12},{24,0},{28,4},{1,25},{... | collective-permute-start | bytes 2949128 | tf_op jit(solution)/shard_map/ppermute | solution.py:269
  6.7 42.8 %collective-permute-start.3 = (bf16[960,512]{1,0:T(8,128)(2,1)S(1)}, bf16[960,512]{1,0:T(8,128)(2,1)S(1)}, u32[]{:S(2)}, u32[]{:S(2)}) collective-permute-start(bf16[960,512]{1,0:T(8,128)(2,1)S(1)} %constant_dynamic-update-slice_fusion), channel_id=1, source_target_pairs={{0,16},{4,20},{8,24},{12,28},{16,0},{20,4},{24,8},{28,12},{1,17},{... | collective-permute-start | bytes 2949128 | tf_op jit(solution)/shard_map/ppermute | solution.py:269
  7.2 42.7 %collective-permute-start.2 = (bf16[960,512]{1,0:T(8,128)(2,1)S(1)}, bf16[960,512]{1,0:T(8,128)(2,1)}, u32[]{:S(2)}, u32[]{:S(2)}) collective-permute-start(bf16[960,512]{1,0:T(8,128)(2,1)S(1)} %constant_dynamic-update-slice_fusion), channel_id=1, source_target_pairs={{0,8},{4,12},{8,0},{12,4},{16,24},{20,28},{24,16},{28,20},{1,9},{5... | collective-permute-start | bytes 2949128 | tf_op jit(solution)/shard_map/ppermute | solution.py:269
  7.4 42.6 %collective-permute-start.1 = (bf16[2,32,7680]{2,1,0:T(8,128)(2,1)}, bf16[2,32,7680]{2,1,0:T(8,128)(2,1)}, u32[]{:S(2)}, u32[]{:S(2)}) collective-permute-start(bf16[2,32,7680]{2,1,0:T(8,128)(2,1)} %param.13), channel_id=1, source_target_pairs={{0,3},{1,0},{2,1},{3,2},{4,7},{5,4},{6,5},{7,6},{8,11},{9,8},{10,9... | collective-permute-start | bytes 2949128 | tf_op jit(solution)/shard_map/ppermute | solution.py:266
  11.4 42.5 %collective-permute-start = (bf16[2,32,7680]{2,1,0:T(8,128)(2,1)}, bf16[2,32,7680]{2,1,0:T(8,128)(2,1)}, u32[]{:S(2)}, u32[]{:S(2)}) collective-permute-start(bf16[2,32,7680]{2,1,0:T(8,128)(2,1)} %param.13), channel_id=1, source_target_pairs={{0,1},{1,2},{2,3},{3,0},{4,5},{5,6},{6,7},{7,4},{8,9},{9,10},{10,1... | collective-permute-start | bytes 2949128 | tf_op jit(solution)/shard_map/ppermute | solution.py:266
  53.8 3.2 %copy-start.9 = (s32[4]{0:T(128)S(1)}, s32[4]{0:T(128)}, u32[]{:S(2)}) copy-start(s32[4]{0:T(128)} %constant.73.clone) | copy-start | bytes 52
  57.0 7.1 %collective-permute-start.5 = (bf16[4,960,512]{2,1,0:T(8,128)(2,1)}, bf16[4,960,512]{2,1,0:T(8,128)(2,1)}, u32[]{:S(2)}, u32[]{:S(2)}) collective-permute-start(bf16[4,960,512]{2,1,0:T(8,128)(2,1)} %pad_maximum_fusion), channel_id=1, source_target_pairs={{0,4},{4,0},{8,12},{12,8},{16,20},{20,16},{24,28},{28,24},{1,5},{5... | collective-permute-start | bytes 11796488 | tf_op jit(solution)/shard_map/ppermute | solution.py:269
  59.2 2.9 %copy-start.8 = (bf16[2,32,7680]{2,1,0:T(8,128)(2,1)S(1)}, bf16[2,32,7680]{2,1,0:T(8,128)(2,1)}, u32[]{:S(2)}) copy-start(bf16[2,32,7680]{2,1,0:T(8,128)(2,1)} %param.13) | copy-start | bytes 2949124
  59.2 13.9 %collective-permute-start.7 = (bf16[1,32,7680]{2,1,0:T(8,128)(2,1)S(1)}, bf16[1,32,7680]{2,1,0:T(8,128)(2,1)S(1)}, u32[]{:S(2)}, u32[]{:S(2)}) collective-permute-start(bf16[1,32,7680]{2,1,0:T(8,128)(2,1)S(1)} %slice.41), channel_id=1, source_target_pairs={{0,3},{1,0},{2,1},{3,2},{4,7},{5,4},{6,5},{7,6},{8,11},{9,8},{10,9... | collective-permute-start | bytes 1474568 | tf_op jit(solution)/shard_map/ppermute | solution.py:266
  61.0 22.7 %collective-permute-start.6 = (bf16[1,32,7680]{2,1,0:T(8,128)(2,1)S(1)}, bf16[1,32,7680]{2,1,0:T(8,128)(2,1)S(1)}, u32[]{:S(2)}, u32[]{:S(2)}) collective-permute-start(bf16[1,32,7680]{2,1,0:T(8,128)(2,1)S(1)} %slice.40), channel_id=1, source_target_pairs={{0,1},{1,2},{2,3},{3,0},{4,5},{5,6},{6,7},{7,4},{8,9},{9,10},{10,1... | collective-permute-start | bytes 1474568 | tf_op jit(solution)/shard_map/ppermute | solution.py:266
  83.8 1.5 copy-start.1
  83.8 1.5 copy-start.2
  83.8 1.5 copy-start.4
  83.8 1.5 copy-start.5
  83.8 1.5 copy-start.6
  90.3 3.3 %copy-start = (bf16[2,2,1024,128]{3,2,1,0:T(8,128)(2,1)}, bf16[2,2,1024,128]{3,2,1,0:T(8,128)(2,1)S(1)}, u32[]{:S(2)}) copy-start(bf16[2,2,1024,128]{3,2,1,0:T(8,128)(2,1)S(1)} %get-tuple-element.38.score_grad) | copy-start | bytes 3145732
  90.3 3.3 %copy-start.3 = (bf16[2,2,128,128]{3,2,1,0:T(8,128)(2,1)}, bf16[2,2,128,128]{3,2,1,0:T(8,128)(2,1)S(1)}, u32[]{:S(2)}) copy-start(bf16[2,2,128,128]{3,2,1,0:T(8,128)(2,1)S(1)} %get-tuple-element.39.keys) | copy-start | bytes 393220
  93.7 27.1 %collective-permute-start.8 = (bf16[1,32,7680]{2,1,0:T(8,128)(2,1)S(1)}, bf16[1,32,7680]{2,1,0:T(8,128)(2,1)S(1)}, u32[]{:S(2)}, u32[]{:S(2)}) collective-permute-start(bf16[1,32,7680]{2,1,0:T(8,128)(2,1)S(1)} %get-tuple-element.43), channel_id=1, source_target_pairs={{0,1},{1,2},{2,3},{3,0},{4,5},{5,6},{6,7},{7,4},{8,9},{9,10},{10,1... | collective-permute-start | bytes 1474568 | tf_op jit(solution)/shard_map/ppermute | solution.py:266
  95.3 23.1 %collective-permute-start.10 = (bf16[1,32,7680]{2,1,0:T(8,128)(2,1)S(1)}, bf16[1,32,7680]{2,1,0:T(8,128)(2,1)S(1)}, u32[]{:S(2)}, u32[]{:S(2)}) collective-permute-start(bf16[1,32,7680]{2,1,0:T(8,128)(2,1)S(1)} %get-tuple-element.45), channel_id=1, source_target_pairs={{0,3},{1,0},{2,1},{3,2},{4,7},{5,4},{6,5},{7,6},{8,11},{9,8},{10,9... | collective-permute-start | bytes 1474568 | tf_op jit(solution)/shard_map/ppermute | solution.py:266
  100.1 4.2 %copy-start.7 = (bf16[7680,512]{1,0:T(8,128)(2,1)}, bf16[7680,512]{1,0:T(8,128)(2,1)S(1)}, u32[]{:S(2)}) copy-start(bf16[7680,512]{1,0:T(8,128)(2,1)S(1)} %convolution_convert_fusion) | copy-start | bytes 23592964
  104.3 22.0 %collective-permute-start.12 = (bf16[4,960,512]{2,1,0:T(8,128)(2,1)}, bf16[4,960,512]{2,1,0:T(8,128)(2,1)}, u32[]{:S(2)}, u32[]{:S(2)}) collective-permute-start(bf16[4,960,512]{2,1,0:T(8,128)(2,1)} %dynamic-slice_bitcast_fusion), channel_id=1, source_target_pairs={{0,4},{4,0},{8,12},{12,8},{16,20},{20,16},{24,28},{28,24},{1,5},{5... | collective-permute-start | bytes 11796488 | tf_op jit(solution)/shard_map/ppermute | solution.py:269
  118.6 25.3 %collective-permute-start.11 = (bf16[2,32,7680]{2,1,0:T(8,128)(2,1)S(1)}, bf16[2,32,7680]{2,1,0:T(8,128)(2,1)}, u32[]{:S(2)}, u32[]{:S(2)}) collective-permute-start(bf16[2,32,7680]{2,1,0:T(8,128)(2,1)S(1)} %pad_maximum_fusion.3), channel_id=1, source_target_pairs={{0,3},{1,0},{2,1},{3,2},{4,7},{5,4},{6,5},{7,6},{8,11},{9,8},{10,9... | collective-permute-start | bytes 2949128 | tf_op jit(solution)/shard_map/ppermute | solution.py:266
  122.0 41.1 %collective-permute-start.9 = (bf16[2,32,7680]{2,1,0:T(8,128)(2,1)}, bf16[2,32,7680]{2,1,0:T(8,128)(2,1)}, u32[]{:S(2)}, u32[]{:S(2)}) collective-permute-start(bf16[2,32,7680]{2,1,0:T(8,128)(2,1)} %pad_maximum_fusion.2), channel_id=1, source_target_pairs={{0,1},{1,2},{2,3},{3,0},{4,5},{5,6},{6,7},{7,4},{8,9},{9,10},{10,1... | collective-permute-start | bytes 2949128 | tf_op jit(solution)/shard_map/ppermute | solution.py:266
  131.3 34.6 %collective-permute-start.13 = (bf16[960,512]{1,0:T(8,128)(2,1)S(1)}, bf16[960,512]{1,0:T(8,128)(2,1)S(1)}, u32[]{:S(2)}, u32[]{:S(2)}) collective-permute-start(bf16[960,512]{1,0:T(8,128)(2,1)S(1)} %get-tuple-element.46), channel_id=1, source_target_pairs={{0,8},{4,12},{8,0},{12,4},{16,24},{20,28},{24,16},{28,20},{1,9},{5... | collective-permute-start | bytes 2949128 | tf_op jit(solution)/shard_map/ppermute | solution.py:269
  132.8 43.0 %collective-permute-start.15 = (bf16[960,512]{1,0:T(8,128)(2,1)S(1)}, bf16[960,512]{1,0:T(8,128)(2,1)S(1)}, u32[]{:S(2)}, u32[]{:S(2)}) collective-permute-start(bf16[960,512]{1,0:T(8,128)(2,1)S(1)} %get-tuple-element.47), channel_id=1, source_target_pairs={{0,24},{4,28},{8,16},{12,20},{16,8},{20,12},{24,0},{28,4},{1,25},{... | collective-permute-start | bytes 2949128 | tf_op jit(solution)/shard_map/ppermute | solution.py:269
  134.3 42.9 %collective-permute-start.14 = (bf16[960,512]{1,0:T(8,128)(2,1)S(1)}, bf16[960,512]{1,0:T(8,128)(2,1)S(1)}, u32[]{:S(2)}, u32[]{:S(2)}) collective-permute-start(bf16[960,512]{1,0:T(8,128)(2,1)S(1)} %get-tuple-element.48), channel_id=1, source_target_pairs={{0,16},{4,20},{8,24},{12,28},{16,0},{20,4},{24,8},{28,12},{1,17},{... | collective-permute-start | bytes 2949128 | tf_op jit(solution)/shard_map/ppermute | solution.py:269

commit v7 on v6

--- a/solution.py
+++ b/solution.py
@@ -201,26 +201,21 @@
     )(queries, score_grad, keys, gain)
 
 
-def terms_kernel(rows, weight, own, left, right, leaving_right, leaving_left):
+def terms_kernel(splits, rows, weight, *outs):
     parts, img_count, own_rows, cols = rows.shape
-    first = leaving_right.shape[0]
     term = dot(rows[...].reshape(-1, cols), weight[...], 1, 1).astype(jnp.bfloat16)
     term = term.reshape(parts, img_count, own_rows, -1)
-    own[...] = term[0]
-    left[...] = term[1]
-    right[...] = term[2]
-    leaving_right[...] = term[3, :first]
-    leaving_left[...] = term[3, first:]
-
-
-def terms(rows, weight, chunks):
+    for (part, low, high), out in zip(splits, outs):
+        out[...] = term[part, low:high]
+
+
+def terms(rows, weight, splits, chunks):
     parts, img_count, own_rows, cols = rows.shape
     vis_width = weight.shape[0]
     width = vis_width // chunks
-    first = img_count // 2
-    counts = (img_count, img_count, img_count, first, img_count - first)
+    counts = [high - low for _, low, high in splits]
     return pl.pallas_call(
-        terms_kernel,
+        functools.partial(terms_kernel, splits),
         out_shape=[
             jax.ShapeDtypeStruct((count, own_rows, vis_width), jnp.bfloat16) for count in counts
         ],
@@ -235,6 +230,67 @@
         compiler_params=pltpu.CompilerParams(vmem_limit_bytes=32 * 1024 * 1024),
         name="terms",
     )(rows, weight)
+
+
+def weights_kernel(place, near, far, rows, own, mate, total):
+    low, width = near.shape[0], own.shape[1]
+    total[...] = dot(near[...], rows[:low], 0, 0) + dot(far[...], rows[low:], 0, 0)
+    core = place[0]
+    own[0] = total[pl.ds(pl.multiple_of(core * width, width), width)].astype(own.dtype)
+    mate[0] = total[pl.ds(pl.multiple_of((1 - core) * width, width), width)].astype(mate.dtype)
+
+
+def weights(near, far, rows, place, pairs):
+    vis_width, cols = near.shape[1], rows.shape[1]
+    width = vis_width // pairs
+    shape = jax.ShapeDtypeStruct((pairs, width // 2, cols), jnp.bfloat16)
+    target = pl.BlockSpec((1, width // 2, cols), lambda p, *_: (p, 0, 0))
+    return pl.pallas_call(
+        weights_kernel,
+        out_shape=(shape, shape),
+        grid_spec=pltpu.PrefetchScalarGridSpec(
+            num_scalar_prefetch=1,
+            grid=(pairs,),
+            in_specs=[
+                pl.BlockSpec((near.shape[0], width), lambda p, *_: (0, p)),
+                pl.BlockSpec((far.shape[0], width), lambda p, *_: (0, p)),
+                pl.BlockSpec(rows.shape, lambda *_: (0, 0)),
+            ],
+            out_specs=(target, target),
+            scratch_shapes=[pltpu.VMEM((width, cols), jnp.float32)],
+        ),
+        compiler_params=pltpu.CompilerParams(vmem_limit_bytes=32 * 1024 * 1024),
+        name="weights",
+    )(place, near, far, rows)
+
+
+def merge_kernel(place, held, given, out):
+    out[...] = (held[...].astype(jnp.float32) + given[...].astype(jnp.float32)).astype(out.dtype)
+
+
+def merge(held, given, place):
+    pairs, own_width, cols = held.shape
+    return [
+        pl.pallas_call(
+            merge_kernel,
+            out_shape=jax.ShapeDtypeStruct((1, own_width, cols), kind),
+            grid_spec=pltpu.PrefetchScalarGridSpec(
+                num_scalar_prefetch=1,
+                grid=(1,),
+                in_specs=[
+                    pl.BlockSpec(
+                        (1, own_width, cols),
+                        lambda i, place, r=r: (jnp.bitwise_xor(place[1], r), 0, 0),
+                    )
+                ]
+                * 2,
+                out_specs=pl.BlockSpec((1, own_width, cols), lambda *_: (0, 0, 0)),
+            ),
+            compiler_params=pltpu.CompilerParams(vmem_limit_bytes=32 * 1024 * 1024),
+            name="merge",
+        )(place, held, given)[0]
+        for r, kind in enumerate([jnp.float32] + [jnp.bfloat16] * (pairs - 1))
+    ]
 
 
 def per_device(
@@ -273,23 +329,26 @@
     normed, masked = before(queries, out_grad, query_gain, lengths, key_heads)
 
     own_weight = jnp.concatenate((key_weight, value_weight), axis=1)
-    if pairs > 4:
+    leaving = (from_left[:first], from_right[first:])
+    if pairs != 4:
         weight = lax.all_gather(own_weight, "dp", axis=0, tiled=True)
+        opposite = (ring(leaving[0], 1), ring(leaving[1], -1))
     else:
-        sent = [swap(own_weight, 2 * r) for r in range(1, pairs)]
+        side, up, across = (swap(own_weight, 2 * r) for r in range(1, pairs))
+        twice = jnp.stack((own_weight, side))
         weight = jnp.zeros((2 * pairs, own_width, cols), jnp.bfloat16)
-        from_left, from_right, sent, weight, normed, masked = lax.optimization_barrier(
-            (from_left, from_right, sent, weight, normed, masked)
+        leaving, twice, up, across, normed, masked, weight = lax.optimization_barrier(
+            (leaving, twice, up, across, normed, masked, weight)
         )
-        mine = jnp.stack([own_weight, *sent])
-        mates = swap(mine, 1)
-        for r in range(pairs):
-            for source, side in ((mine, core), (mates, 1 - core)):
-                weight = lax.dynamic_update_slice_in_dim(
-                    weight, source[r : r + 1], 2 * (pair ^ r) + side, axis=0
-                )
+        opposite = (ring(leaving[0], 1), ring(leaving[1], -1))
+        for r, pieces in ((0, twice), (2, up[None]), (3, across[None])):
+            mates = swap(pieces, 1)
+            for k in range(pieces.shape[0]):
+                for source, half in ((pieces, core), (mates, 1 - core)):
+                    weight = lax.dynamic_update_slice_in_dim(
+                        weight, source[k : k + 1], 2 * (pair ^ (r + k)) + half, axis=0
+                    )
         weight = weight.reshape(vis_width, cols)
-    opposite = (ring(from_left[:first], 1), ring(from_right[first:], -1))
 
     near = jnp.stack((images, from_left, from_right)).reshape(-1, vis_width)
     near_total = dot(near, weight, 1, 0)
@@ -301,35 +360,45 @@
     rows, score_grad, seq_keys = attend(
         [near_total, far_total], normed, masked, key_gain, assignment, tile_counts, owners
     )
-    query_grad = after(queries, score_grad, seq_keys, query_gain)
-
-    own, to_left, to_right, leaving_right, leaving_left = terms(rows, weight, 4)
-    right_half = ring(leaving_right, 1).astype(jnp.float32)
-    left_half = ring(leaving_left, -1).astype(jnp.float32)
-    to_right = jnp.concatenate(
-        ((to_right[:first].astype(jnp.float32) + right_half).astype(jnp.bfloat16), to_right[first:])
-    )
-    to_left = jnp.concatenate(
-        (to_left[:first], (to_left[first:].astype(jnp.float32) + left_half).astype(jnp.bfloat16))
-    )
-    from_left = ring(to_right, 1).astype(jnp.float32)
-    from_right = ring(to_left, -1).astype(jnp.float32)
-    image_grad = (own.astype(jnp.float32) + from_left + from_right).astype(jnp.bfloat16)
+    halves = ((0, 0, first), (0, first, img_count))
+    leaving_right, leaving_left = terms(rows[3:], weight, halves, 4)
+    wholes = tuple((part, 0, img_count) for part in range(3))
+    own, to_left, to_right = terms(rows[:3], weight, wholes, 4)
 
     all_rows = rows.reshape(-1, cols)
-    weight_part = dot(jnp.concatenate((near, far)), all_rows, 0, 0)
-    if pairs > 4:
+    if pairs != 4:
+        weight_part = dot(jnp.concatenate((near, far)), all_rows, 0, 0)
         weight_grad = lax.psum_scatter(weight_part, "dp", scatter_dimension=0, tiled=True)
     else:
-        weight_part = weight_part.astype(jnp.bfloat16).reshape(pairs, 2, own_width, cols)
-        both = lax.dynamic_index_in_dim(weight_part, core, 1, keepdims=False).astype(jnp.float32)
-        both = both + swap(
-            lax.dynamic_index_in_dim(weight_part, 1 - core, 1, keepdims=False), 1
-        ).astype(jnp.float32)
-        weight_grad = lax.dynamic_index_in_dim(both, pair, 0, keepdims=False)
+        where = jnp.stack((core, pair))
+        all_rows, leaving_right, leaving_left = lax.optimization_barrier(
+            (all_rows, leaving_right, leaving_left)
+        )
+        kept, given = weights(near, far, all_rows, where, pairs)
+        sent = merge(kept, swap(given, 1), where)
+        score_grad, sent = lax.optimization_barrier((score_grad, sent))
+        weight_grad = sent[0]
         for r in range(1, pairs):
-            sent = lax.dynamic_index_in_dim(both, pair ^ r, 0, keepdims=False)
-            weight_grad = weight_grad + swap(sent.astype(jnp.bfloat16), 2 * r).astype(jnp.float32)
+            weight_grad = weight_grad + swap(sent[r], 2 * r).astype(jnp.float32)
+    query_grad = after(queries, score_grad, seq_keys, query_gain)
+
+    right_half, left_half = lax.optimization_barrier(
+        (ring(leaving_right, 1), ring(leaving_left, -1))
+    )
+
+    def added(held, half):
+        return (held.astype(jnp.float32) + half.astype(jnp.float32)).astype(jnp.bfloat16)
+
+    to_right = jnp.concatenate((added(to_right[:first], right_half), to_right[first:]))
+    to_left = jnp.concatenate((to_left[:first], added(to_left[first:], left_half)))
+    to_right, to_left = lax.optimization_barrier((to_right, to_left))
+    from_left, from_right = ring(to_right, 1), ring(to_left, -1)
+    from_left, from_right, weight_grad, query_grad = lax.optimization_barrier(
+        (from_left, from_right, weight_grad, query_grad)
+    )
+    image_grad = (
+        own.astype(jnp.float32) + from_left.astype(jnp.float32) + from_right.astype(jnp.float32)
+    ).astype(jnp.bfloat16)
     return (query_grad, image_grad, weight_grad[:, :key_cols], weight_grad[:, key_cols:])
 
 

time: 180 us -> 184 us (1.022)
  Pallas kernels: 17.4 us -> 32.6 us
  other arithmetic: 14.3 us -> 9.48 us
  waiting for transfers between devices: 103 us -> 98.4 us
  starting transfers between devices: 20.4 us -> 24.5 us
  local copies, waits for them, and re-layouts: 17.9 us -> 14 us
  matrix products: 5.6 us -> 3.13 us
    pallas_call x1 -> x7, Pallas kernels: 3.29 us -> 18.3 us  [the longest x1 6.59 us: weights(): pl.pallas_call(weights_kernel, out_shape=(shape, shape), grid_spec=pltpu....]
    ppermute x8 -> x10, waiting for transfers between devices: 45.3 us -> 36.3 us  [swap(): return lax.ppermute(value, 'dp', [(i, i ^ mask) for i in range(dp_size)])]
    ppermute x8, waiting for transfers between devices: 57.4 us -> 62.1 us  [ring(): lax.ppermute(value, 'mp', [(i, (i + step) % mp_size) for i in range(mp_si...]
    ppermute x8, starting transfers between devices: 12.2 us -> 16.7 us  [ring(): lax.ppermute(value, 'mp', [(i, (i + step) % mp_size) for i in range(mp_si...]
    add x2 -> x1, other arithmetic: 5.16 us -> 2.31 us  [per_device(): weight_grad = weight_grad + swap(sent[r], 2 * r).astype(jnp.float32)]
    dot_general x3 -> x2, matrix products: 5.6 us -> 3.13 us  [dot(): lax.dot_general(left, right, (((left_dim,), (right_dim,)), ((), ())), pre...]
    squeeze x1 -> x0, local copies, waits for them, and re-layouts: 2.41 us -> none  [per_device(): lax.dynamic_index_in_dim(weight_part, 1 - core, 1, keepdims=False)]
    ppermute x8 -> x10, starting transfers between devices: 8.16 us -> 7.78 us  [swap(): return lax.ppermute(value, 'dp', [(i, i ^ mask) for i in range(dp_size)])]
  transfers between devices with their start and end apart: 16 -> 18, of which waited for: 12 -> 11; matrix products, arithmetic and copies ran while one was open for 15% -> 11% of each run, Pallas kernels for 5% -> 7%
where the time goes in v7:
time: 184 us; the launch traced here: 183 us
  waiting for transfers between devices  98.4 us (53%)
  Pallas kernels  32.6 us (18%)
  starting transfers between devices  24.5 us (13%)
  local copies, waits for them, and re-layouts  14 us (8%)
  other arithmetic  9.48 us (5%)
  matrix products  3.13 us (2%)
    ppermute x8, waiting for transfers between devices, ring(): lax.ppermute(value, 'mp', [(i, (i + step) % mp_size) for i in range(mp_si...  62.1 us
    ppermute x10, waiting for transfers between devices, swap(): return lax.ppermute(value, 'dp', [(i, i ^ mask) for i in range(dp_size)])  36.3 us
    ppermute x8, starting transfers between devices, ring(): lax.ppermute(value, 'mp', [(i, (i + step) % mp_size) for i in range(mp_si...  16.7 us
    ppermute x10, starting transfers between devices, swap(): return lax.ppermute(value, 'dp', [(i, i ^ mask) for i in range(dp_size)])  7.78 us
    pallas_call x1, Pallas kernels, weights(): pl.pallas_call(weights_kernel, out_shape=(shape, shape), grid_spec=pltpu....  6.59 us
    pallas_call x2, Pallas kernels, terms(): pl.pallas_call(functools.partial(terms_kernel, splits), out_shape=[jax.Sh...  6.59 us
    dynamic_update_slice x8, local copies, waits for them, and re-layouts, per_device(): lax.dynamic_update_slice_in_dim(weight, source[k:k + 1], 2 * (pair ^ r +...  5.56 us
    pallas_call x4, Pallas kernels, merge(): pl.pallas_call(merge_kernel, out_shape=jax.ShapeDtypeStruct((1, own_width...  5.14 us
  transfers between devices with their start and end apart: 18, of which 11 were waited for; matrix products, arithmetic and copies ran while one was open for 11% of the time, Pallas kernels for 7%

profile of v7, /device:TPU:0, one launch (start us, length us, event | category | flops | bytes accessed | tf_op | source)
XLA Modules:
  0.0 183.1 jit_solution(17395544051421575310)
XLA Ops:
  0.6 3.1 %collective-permute-start = (bf16[2,32,7680]{2,1,0:T(8,128)(2,1)}, bf16[2,32,7680]{2,1,0:T(8,128)(2,1)S(1)}, u32[]{:S(2)}, u32[]{:S(2)}) collective-permute-start(bf16[2,32,7680]{2,1,0:T(8,128)(2,1)} %param.13), channel_id=1, source_target_pairs={{0,1},{1,2},{2,3},{3,0},{4,5},{5,6},{6,7},{7,4},{8,9},{9,10},{10,1... | collective-permute-start | bytes 2949128 | tf_op jit(solution)/shard_map/ppermute | solution.py:322
  3.7 2.1 %collective-permute-start.1 = (bf16[2,32,7680]{2,1,0:T(8,128)(2,1)}, bf16[2,32,7680]{2,1,0:T(8,128)(2,1)S(1)}, u32[]{:S(2)}, u32[]{:S(2)}) collective-permute-start(bf16[2,32,7680]{2,1,0:T(8,128)(2,1)} %param.13), channel_id=1, source_target_pairs={{0,3},{1,0},{2,1},{3,2},{4,7},{5,4},{6,5},{7,6},{8,11},{9,8},{10,9... | collective-permute-start | bytes 2949128 | tf_op jit(solution)/shard_map/ppermute | solution.py:322
  5.8 1.8 %constant_dynamic-update-slice_fusion.1 = bf16[960,512]{1,0:T(8,128)(2,1)} fusion(bf16[960,256]{1,0:T(8,128)(2,1)} %param.14), kind=kLoop, calls=%fused_computation.14 | loop fusion | bytes 983040
  7.6 1.8 %constant_dynamic-update-slice_fusion = bf16[960,512]{1,0:T(8,128)(2,1)} fusion(bf16[960,512]{1,0:T(8,128)(2,1)} %constant_dynamic-update-slice_fusion.1, bf16[960,256]{1,0:T(8,128)(2,1)} %param.15), kind=kLoop, calls=%fused_computation.13 | loop fusion | bytes 983040 | tf_op jit(solution)/shard_map/concatenate | solution.py:331
  9.5 1.6 collective-permute-start.2
  11.1 1.5 collective-permute-start.3
  13.0 5.0 %before.1 = (bf16[2,2,1024,128]{3,2,1,0:T(8,128)(2,1)}, bf16[2,2,1024,128]{3,2,1,0:T(8,128)(2,1)}) custom-call(s32[2]{0:T(128)} %lengths.1, bf16[2,128,2048]{2,1,0:T(8,128)(2,1)} %query.3, bf16[2,128,2048]{2,1,0:T(8,128)(2,1)} %grad.1, f32[1,128]{1,0:T(1,128)} %bitcast.47), custom_call_target="tpu_custom_call" | custom-call | tf_op jit(solution)/shard_map/before/pallas_call | solution.py:58
  17.9 10.6 %collective-permute-done = bf16[2,32,7680]{2,1,0:T(8,128)(2,1)S(1)} collective-permute-done((bf16[2,32,7680]{2,1,0:T(8,128)(2,1)}, bf16[2,32,7680]{2,1,0:T(8,128)(2,1)S(1)}, u32[]{:S(2)}, u32[]{:S(2)}) %collective-permute-start) | collective-permute-done | bytes 983072 | tf_op jit(solution)/shard_map/ppermute | solution.py:322
  28.6 19.6 %collective-permute-done.1 = bf16[2,32,7680]{2,1,0:T(8,128)(2,1)S(1)} collective-permute-done((bf16[2,32,7680]{2,1,0:T(8,128)(2,1)}, bf16[2,32,7680]{2,1,0:T(8,128)(2,1)S(1)}, u32[]{:S(2)}, u32[]{:S(2)}) %collective-permute-start.1) | collective-permute-done | bytes 983072 | tf_op jit(solution)/shard_map/ppermute | solution.py:322
  48.2 0.9 slice.57
  50.0 1.7 pad_maximum_fusion.1
  51.7 3.6 %collective-permute-done.3 = bf16[960,512]{1,0:T(8,128)(2,1)} collective-permute-done((bf16[960,512]{1,0:T(8,128)(2,1)}, bf16[960,512]{1,0:T(8,128)(2,1)}, u32[]{:S(2)}, u32[]{:S(2)}) %collective-permute-start.3) | collective-permute-done | bytes 983072 | tf_op jit(solution)/shard_map/ppermute | solution.py:325
  56.1 3.8 %collective-permute-start.9 = (bf16[1,32,7680]{2,1,0:T(8,128)(2,1)}, bf16[1,32,7680]{2,1,0:T(8,128)(2,1)S(1)}, u32[]{:S(2)}, u32[]{:S(2)}) collective-permute-start(bf16[1,32,7680]{2,1,0:T(8,128)(2,1)} %slice.57), channel_id=1, source_target_pairs={{0,3},{1,0},{2,1},{3,2},{4,7},{5,4},{6,5},{7,6},{8,11},{9,8},{10,9... | collective-permute-start | bytes 1474568 | tf_op jit(solution)/shard_map/ppermute | solution.py:322
  61.0 1.3 slice_dynamic-update-slice_fusion.1
  62.4 1.3 slice_dynamic-update-slice_fusion
  63.7 1.3 constant_dynamic-update-slice_fusion.7
  65.1 1.3 constant_dynamic-update-slice_fusion.5
  66.5 1.7 fusion.2
  68.2 3.7 %collective-permute-done.8 = bf16[1,32,7680]{2,1,0:T(8,128)(2,1)S(1)} collective-permute-done((bf16[1,32,7680]{2,1,0:T(8,128)(2,1)S(1)}, bf16[1,32,7680]{2,1,0:T(8,128)(2,1)S(1)}, u32[]{:S(2)}, u32[]{:S(2)}) %collective-permute-start.8) | collective-permute-done | bytes 491552 | tf_op jit(solution)/shard_map/ppermute | solution.py:322
  71.9 8.4 %collective-permute-done.9 = bf16[1,32,7680]{2,1,0:T(8,128)(2,1)S(1)} collective-permute-done((bf16[1,32,7680]{2,1,0:T(8,128)(2,1)}, bf16[1,32,7680]{2,1,0:T(8,128)(2,1)S(1)}, u32[]{:S(2)}, u32[]{:S(2)}) %collective-permute-start.9) | collective-permute-done | bytes 491552 | tf_op jit(solution)/shard_map/ppermute | solution.py:322
  80.5 1.5 convolution_bitcast_fusion.refs_1_.refs_3_
  82.0 5.0 %attend.1 = (bf16[4,2,32,512]{3,2,1,0:T(8,128)(2,1)S(1)}, bf16[2,2,1024,128]{3,2,1,0:T(8,128)(2,1)S(1)}, bf16[2,2,128,128]{3,2,1,0:T(8,128)(2,1)S(1)}) custom-call(s32[2]{0:T(128)S(1)} %copy-done.6, s32[2]{0:T(128)S(1)} %copy-done.7, s32[4]{0:T(128)S(1)} %and_select_fusion.owners, f32[3,2,32,512]{3,2,1,0:T(8,128)S(1)} %bitcast.38, ...), custom_call_target="tpu_custom_call" | custom-call | tf_op jit(solution)/shard_map/attend/pallas_call | solution.py:141
  87.7 3.1 %terms.3 = (bf16[1,32,7680]{2,1,0:T(8,128)(2,1)S(1)}, bf16[1,32,7680]{2,1,0:T(8,128)(2,1)S(1)}) custom-call(bf16[1,2,32,512]{3,2,1,0:T(8,128)(2,1)S(1)} %slice.50.rows, bf16[7680,512]{1,0:T(8,128)(2,1)S(1)} %bitcast.32), custom_call_target="tpu_custom_call" | custom-call | tf_op jit(solution)/shard_map/terms/pallas_call | solution.py:217
  90.8 6.6 %weights.1 = (bf16[4,960,512]{2,1,0:T(8,128)(2,1)S(1)}, bf16[4,960,512]{2,1,0:T(8,128)(2,1)S(1)}) custom-call(s32[2]{0:T(128)S(1)} %pad_add_fusion.place, bf16[192,7680]{1,0:T(8,128)(2,1)S(1)} %bitcast.35, bf16[64,7680]{1,0:T(8,128)(2,1)S(1)} %bitcast.36, bf16[256,512]{1,0:T(8,128)(2,1)S(1)} %bitcast.40), custom_call_target="tpu_custom_call" | custom-call | tf_op jit(solution)/shard_map/weights/pallas_call | solution.py:248
  97.5 1.0 collective-permute-start.10
  98.5 2.9 %collective-permute-start.11 = (bf16[1,32,7680]{2,1,0:T(8,128)(2,1)S(1)}, bf16[1,32,7680]{2,1,0:T(8,128)(2,1)S(1)}, u32[]{:S(2)}, u32[]{:S(2)}) collective-permute-start(bf16[1,32,7680]{2,1,0:T(8,128)(2,1)S(1)} %get-tuple-element.61), channel_id=1, source_target_pairs={{0,3},{1,0},{2,1},{3,2},{4,7},{5,4},{6,5},{7,6},{8,11},{9,8},{10,9... | collective-permute-start | bytes 1474568 | tf_op jit(solution)/shard_map/ppermute | solution.py:322
  101.3 3.5 %terms.2 = (bf16[2,32,7680]{2,1,0:T(8,128)(2,1)S(1)}, bf16[2,32,7680]{2,1,0:T(8,128)(2,1)S(1)}, bf16[2,32,7680]{2,1,0:T(8,128)(2,1)S(1)}) custom-call(bf16[3,2,32,512]{3,2,1,0:T(8,128)(2,1)S(1)} %slice.48.rows, bf16[7680,512]{1,0:T(8,128)(2,1)S(1)} %bitcast.33), custom_call_target="tpu_custom_call" | custom-call | tf_op jit(solution)/shard_map/terms/pallas_call | solution.py:217
  104.9 8.4 %collective-permute-done.10 = bf16[1,32,7680]{2,1,0:T(8,128)(2,1)S(1)} collective-permute-done((bf16[1,32,7680]{2,1,0:T(8,128)(2,1)S(1)}, bf16[1,32,7680]{2,1,0:T(8,128)(2,1)S(1)}, u32[]{:S(2)}, u32[]{:S(2)}) %collective-permute-start.10) | collective-permute-done | bytes 491552 | tf_op jit(solution)/shard_map/ppermute | solution.py:322
  113.4 9.0 %collective-permute-done.11 = bf16[1,32,7680]{2,1,0:T(8,128)(2,1)S(1)} collective-permute-done((bf16[1,32,7680]{2,1,0:T(8,128)(2,1)S(1)}, bf16[1,32,7680]{2,1,0:T(8,128)(2,1)S(1)}, u32[]{:S(2)}, u32[]{:S(2)}) %collective-permute-start.11) | collective-permute-done | bytes 491552 | tf_op jit(solution)/shard_map/ppermute | solution.py:322
  122.6 1.0 pad_maximum_fusion.3
  123.6 0.8 merge.7
  124.4 1.7 merge.6
  126.2 1.8 merge.5
  128.0 0.8 merge.4
  128.8 1.3 collective-permute-start.15
  130.1 0.8 collective-permute-start.16
  130.9 1.4 collective-permute-start.17
  132.3 1.0 pad_maximum_fusion.2
  133.3 1.6 collective-permute-start.12
  135.0 2.2 %collective-permute-start.13 = (bf16[2,32,7680]{2,1,0:T(8,128)(2,1)}, bf16[2,32,7680]{2,1,0:T(8,128)(2,1)}, u32[]{:S(2)}, u32[]{:S(2)}) collective-permute-start(bf16[2,32,7680]{2,1,0:T(8,128)(2,1)} %pad_maximum_fusion.3), channel_id=1, source_target_pairs={{0,3},{1,0},{2,1},{3,2},{4,7},{5,4},{6,5},{7,6},{8,11},{9,8},{10,9... | collective-permute-start | bytes 2949128 | tf_op jit(solution)/shard_map/ppermute | solution.py:322
  137.2 4.3 %after.1 = bf16[2,128,2048]{2,1,0:T(8,128)(2,1)} custom-call(bf16[2,128,2048]{2,1,0:T(8,128)(2,1)} %query.3, bf16[2,2,1024,128]{3,2,1,0:T(8,128)(2,1)} %copy-done, bf16[2,2,128,128]{3,2,1,0:T(8,128)(2,1)} %copy-done.5, f32[1,128]{1,0:T(1,128)} %bitcast.48), custom_call_target="tpu_custom_call" | custom-call | tf_op jit(solution)/shard_map/after/pallas_call | solution.py:189
  141.5 12.3 %collective-permute-done.15 = bf16[960,512]{1,0:T(8,128)(2,1)} collective-permute-done((bf16[960,512]{1,0:T(8,128)(2,1)}, bf16[960,512]{1,0:T(8,128)(2,1)}, u32[]{:S(2)}, u32[]{:S(2)}) %collective-permute-start.15) | collective-permute-done | bytes 983072 | tf_op jit(solution)/shard_map/ppermute | solution.py:325
  153.8 18.8 %collective-permute-done.16 = bf16[960,512]{1,0:T(8,128)(2,1)} collective-permute-done((bf16[960,512]{1,0:T(8,128)(2,1)}, bf16[960,512]{1,0:T(8,128)(2,1)}, u32[]{:S(2)}, u32[]{:S(2)}) %collective-permute-start.16) | collective-permute-done | bytes 983072 | tf_op jit(solution)/shard_map/ppermute | solution.py:325
  172.6 1.6 collective-permute-done.17
  174.3 2.3 %convert_add_fusion = f32[960,512]{1,0:T(8,128)S(1)} fusion(bf16[960,512]{1,0:T(8,128)(2,1)} %collective-permute-done.17, bf16[960,512]{1,0:T(8,128)(2,1)} %collective-permute-done.16, f32[960,512]{1,0:T(8,128)S(1)} %bitcast.37, bf16[960,512]{1,0:T(8,128)(2,1)} %collective-permute-done.15), kind=kLoop, calls=%fused_computation.3 | loop fusion | flops 2949120 | bytes 6881280 | tf_op jit(solution)/shard_map/add | solution.py:382
  176.6 2.3 %collective-permute-done.13 = bf16[2,32,7680]{2,1,0:T(8,128)(2,1)} collective-permute-done((bf16[2,32,7680]{2,1,0:T(8,128)(2,1)}, bf16[2,32,7680]{2,1,0:T(8,128)(2,1)}, u32[]{:S(2)}, u32[]{:S(2)}) %collective-permute-start.13) | collective-permute-done | bytes 983072 | tf_op jit(solution)/shard_map/ppermute | solution.py:322
  178.9 1.4 fusion.1
  180.3 2.8 %add_convert_fusion = bf16[2,32,7680]{2,1,0:T(8,128)(2,1)} fusion(bf16[2,32,7680]{2,1,0:T(8,128)(2,1)} %collective-permute-done.13, bf16[2,32,7680]{2,1,0:T(8,128)(2,1)} %collective-permute-done.12, bf16[2,32,7680]{2,1,0:T(8,128)(2,1)S(1)} %copy-done.4), kind=kLoop, calls=%fused_computation.2 | loop fusion | flops 2949120 | bytes 3932160 | tf_op jit(solution)/shard_map/convert_element_type | solution.py:401
  (57 shorter events, 4.6 us)
Async XLA Ops:
  0.6 27.9 %collective-permute-start = (bf16[2,32,7680]{2,1,0:T(8,128)(2,1)}, bf16[2,32,7680]{2,1,0:T(8,128)(2,1)S(1)}, u32[]{:S(2)}, u32[]{:S(2)}) collective-permute-start(bf16[2,32,7680]{2,1,0:T(8,128)(2,1)} %param.13), channel_id=1, source_target_pairs={{0,1},{1,2},{2,3},{3,0},{4,5},{5,6},{6,7},{7,4},{8,9},{9,10},{10,1... | collective-permute-start | bytes 2949128 | tf_op jit(solution)/shard_map/ppermute | solution.py:322
  3.7 44.5 %collective-permute-start.1 = (bf16[2,32,7680]{2,1,0:T(8,128)(2,1)}, bf16[2,32,7680]{2,1,0:T(8,128)(2,1)S(1)}, u32[]{:S(2)}, u32[]{:S(2)}) collective-permute-start(bf16[2,32,7680]{2,1,0:T(8,128)(2,1)} %param.13), channel_id=1, source_target_pairs={{0,3},{1,0},{2,1},{3,2},{4,7},{5,4},{6,5},{7,6},{8,11},{9,8},{10,9... | collective-permute-start | bytes 2949128 | tf_op jit(solution)/shard_map/ppermute | solution.py:322
  9.5 39.6 %collective-permute-start.2 = (bf16[960,512]{1,0:T(8,128)(2,1)}, bf16[960,512]{1,0:T(8,128)(2,1)S(1)}, u32[]{:S(2)}, u32[]{:S(2)}) collective-permute-start(bf16[960,512]{1,0:T(8,128)(2,1)} %constant_dynamic-update-slice_fusion), channel_id=1, source_target_pairs={{0,8},{4,12},{8,0},{12,4},{16,24},{20,28},{24,16},{28,20},{1,9},{5... | collective-permute-start | bytes 2949128 | tf_op jit(solution)/shard_map/ppermute | solution.py:325
  11.1 44.2 %collective-permute-start.3 = (bf16[960,512]{1,0:T(8,128)(2,1)}, bf16[960,512]{1,0:T(8,128)(2,1)}, u32[]{:S(2)}, u32[]{:S(2)}) collective-permute-start(bf16[960,512]{1,0:T(8,128)(2,1)} %constant_dynamic-update-slice_fusion), channel_id=1, source_target_pairs={{0,16},{4,20},{8,24},{12,28},{16,0},{20,4},{24,8},{28,12},{1,17},{... | collective-permute-start | bytes 2949128 | tf_op jit(solution)/shard_map/ppermute | solution.py:325
  12.6 42.6 %collective-permute-start.4 = (bf16[960,512]{1,0:T(8,128)(2,1)}, bf16[960,512]{1,0:T(8,128)(2,1)}, u32[]{:S(2)}, u32[]{:S(2)}) collective-permute-start(bf16[960,512]{1,0:T(8,128)(2,1)} %constant_dynamic-update-slice_fusion), channel_id=1, source_target_pairs={{0,24},{4,28},{8,16},{12,20},{16,8},{20,12},{24,0},{28,4},{1,25},{... | collective-permute-start | bytes 2949128 | tf_op jit(solution)/shard_map/ppermute | solution.py:325
  13.0 42.4 %copy-start.13 = (s32[4]{0:T(128)S(1)}, s32[4]{0:T(128)}, u32[]{:S(2)}) copy-start(s32[4]{0:T(128)} %constant.56.clone) | copy-start | bytes 52
  48.2 1.1 copy-start.9
  49.1 0.9 copy-start.12
  55.3 5.7 %collective-permute-start.5 = (bf16[2,960,512]{2,1,0:T(8,128)(2,1)S(1)}, bf16[2,960,512]{2,1,0:T(8,128)(2,1)}, u32[]{:S(2)}, u32[]{:S(2)}) collective-permute-start(bf16[2,960,512]{2,1,0:T(8,128)(2,1)S(1)} %pad_maximum_fusion.1), channel_id=1, source_target_pairs={{0,4},{4,0},{8,12},{12,8},{16,20},{20,16},{24,28},{28,24},{1,5},{5... | collective-permute-start | bytes 5898248 | tf_op jit(solution)/shard_map/ppermute | solution.py:325
  55.4 9.6 %collective-permute-start.6 = (bf16[1,960,512]{2,1,0:T(8,128)(2,1)}, bf16[1,960,512]{2,1,0:T(8,128)(2,1)S(1)}, u32[]{:S(2)}, u32[]{:S(2)}) collective-permute-start(bf16[1,960,512]{2,1,0:T(8,128)(2,1)} %bitcast.7), channel_id=1, source_target_pairs={{0,4},{4,0},{8,12},{12,8},{16,20},{20,16},{24,28},{28,24},{1,5},{5... | collective-permute-start | bytes 2949128 | tf_op jit(solution)/shard_map/ppermute | solution.py:325
  56.0 4.7 %copy-start.10 = (bf16[2,32,7680]{2,1,0:T(8,128)(2,1)S(1)}, bf16[2,32,7680]{2,1,0:T(8,128)(2,1)}, u32[]{:S(2)}) copy-start(bf16[2,32,7680]{2,1,0:T(8,128)(2,1)} %copy-done.9) | copy-start | bytes 2949124
  56.0 4.7 %copy-start.11 = (bf16[2,32,7680]{2,1,0:T(8,128)(2,1)S(1)}, bf16[2,32,7680]{2,1,0:T(8,128)(2,1)}, u32[]{:S(2)}) copy-start(bf16[2,32,7680]{2,1,0:T(8,128)(2,1)} %param.13) | copy-start | bytes 2949124
  56.0 10.5 %collective-permute-start.7 = (bf16[1,960,512]{2,1,0:T(8,128)(2,1)}, bf16[1,960,512]{2,1,0:T(8,128)(2,1)S(1)}, u32[]{:S(2)}, u32[]{:S(2)}) collective-permute-start(bf16[1,960,512]{2,1,0:T(8,128)(2,1)} %bitcast.8), channel_id=1, source_target_pairs={{0,4},{4,0},{8,12},{12,8},{16,20},{20,16},{24,28},{28,24},{1,5},{5... | collective-permute-start | bytes 2949128 | tf_op jit(solution)/shard_map/ppermute | solution.py:325
  56.1 15.9 %collective-permute-start.8 = (bf16[1,32,7680]{2,1,0:T(8,128)(2,1)S(1)}, bf16[1,32,7680]{2,1,0:T(8,128)(2,1)S(1)}, u32[]{:S(2)}, u32[]{:S(2)}) collective-permute-start(bf16[1,32,7680]{2,1,0:T(8,128)(2,1)S(1)} %slice.56), channel_id=1, source_target_pairs={{0,1},{1,2},{2,3},{3,0},{4,5},{5,6},{6,7},{7,4},{8,9},{9,10},{10,1... | collective-permute-start | bytes 1474568 | tf_op jit(solution)/shard_map/ppermute | solution.py:322
  56.1 24.3 %collective-permute-start.9 = (bf16[1,32,7680]{2,1,0:T(8,128)(2,1)}, bf16[1,32,7680]{2,1,0:T(8,128)(2,1)S(1)}, u32[]{:S(2)}, u32[]{:S(2)}) collective-permute-start(bf16[1,32,7680]{2,1,0:T(8,128)(2,1)} %slice.57), channel_id=1, source_target_pairs={{0,3},{1,0},{2,1},{3,2},{4,7},{5,4},{6,5},{7,6},{8,11},{9,8},{10,9... | collective-permute-start | bytes 1474568 | tf_op jit(solution)/shard_map/ppermute | solution.py:322
  80.4 1.5 copy-start.1
  80.5 1.5 copy-start.2
  80.5 1.5 copy-start.6
  80.5 1.5 copy-start.7
  80.5 1.5 copy-start.8
  87.0 0.7 copy-start.5
  87.7 3.1 %copy-start = (bf16[2,2,1024,128]{3,2,1,0:T(8,128)(2,1)}, bf16[2,2,1024,128]{3,2,1,0:T(8,128)(2,1)S(1)}, u32[]{:S(2)}) copy-start(bf16[2,2,1024,128]{3,2,1,0:T(8,128)(2,1)S(1)} %get-tuple-element.75.score_grad) | copy-start | bytes 3145732
  97.4 26.2 %collective-permute-start.14 = (bf16[4,960,512]{2,1,0:T(8,128)(2,1)S(1)}, bf16[4,960,512]{2,1,0:T(8,128)(2,1)S(1)}, u32[]{:S(2)}, u32[]{:S(2)}) collective-permute-start(bf16[4,960,512]{2,1,0:T(8,128)(2,1)S(1)} %get-tuple-element.70), channel_id=1, source_target_pairs={{0,4},{4,0},{8,12},{12,8},{16,20},{20,16},{24,28},{28,24},{1,5},{5... | collective-permute-start | bytes 11796488 | tf_op jit(solution)/shard_map/ppermute | solution.py:325
  97.5 15.9 %collective-permute-start.10 = (bf16[1,32,7680]{2,1,0:T(8,128)(2,1)S(1)}, bf16[1,32,7680]{2,1,0:T(8,128)(2,1)S(1)}, u32[]{:S(2)}, u32[]{:S(2)}) collective-permute-start(bf16[1,32,7680]{2,1,0:T(8,128)(2,1)S(1)} %get-tuple-element.60), channel_id=1, source_target_pairs={{0,1},{1,2},{2,3},{3,0},{4,5},{5,6},{6,7},{7,4},{8,9},{9,10},{10,1... | collective-permute-start | bytes 1474568 | tf_op jit(solution)/shard_map/ppermute | solution.py:322
  98.5 23.9 %collective-permute-start.11 = (bf16[1,32,7680]{2,1,0:T(8,128)(2,1)S(1)}, bf16[1,32,7680]{2,1,0:T(8,128)(2,1)S(1)}, u32[]{:S(2)}, u32[]{:S(2)}) collective-permute-start(bf16[1,32,7680]{2,1,0:T(8,128)(2,1)S(1)} %get-tuple-element.61), channel_id=1, source_target_pairs={{0,3},{1,0},{2,1},{3,2},{4,7},{5,4},{6,5},{7,6},{8,11},{9,8},{10,9... | collective-permute-start | bytes 1474568 | tf_op jit(solution)/shard_map/ppermute | solution.py:322
  104.9 18.8 %copy-start.3 = (bf16[2,32,7680]{2,1,0:T(8,128)(2,1)}, bf16[2,32,7680]{2,1,0:T(8,128)(2,1)S(1)}, u32[]{:S(2)}) copy-start(bf16[2,32,7680]{2,1,0:T(8,128)(2,1)S(1)} %get-tuple-element.78) | copy-start | bytes 2949124
  128.8 25.1 %collective-permute-start.15 = (bf16[960,512]{1,0:T(8,128)(2,1)}, bf16[960,512]{1,0:T(8,128)(2,1)}, u32[]{:S(2)}, u32[]{:S(2)}) collective-permute-start(bf16[960,512]{1,0:T(8,128)(2,1)} %bitcast.19), channel_id=1, source_target_pairs={{0,8},{4,12},{8,0},{12,4},{16,24},{20,28},{24,16},{28,20},{1,9},{5... | collective-permute-start | bytes 2949128 | tf_op jit(solution)/shard_map/ppermute | solution.py:325
  130.1 42.6 %collective-permute-start.16 = (bf16[960,512]{1,0:T(8,128)(2,1)}, bf16[960,512]{1,0:T(8,128)(2,1)}, u32[]{:S(2)}, u32[]{:S(2)}) collective-permute-start(bf16[960,512]{1,0:T(8,128)(2,1)} %bitcast.20), channel_id=1, source_target_pairs={{0,16},{4,20},{8,24},{12,28},{16,0},{20,4},{24,8},{28,12},{1,17},{... | collective-permute-start | bytes 2949128 | tf_op jit(solution)/shard_map/ppermute | solution.py:325
  130.9 43.4 %collective-permute-start.17 = (bf16[960,512]{1,0:T(8,128)(2,1)S(1)}, bf16[960,512]{1,0:T(8,128)(2,1)}, u32[]{:S(2)}, u32[]{:S(2)}) collective-permute-start(bf16[960,512]{1,0:T(8,128)(2,1)S(1)} %bitcast.41), channel_id=1, source_target_pairs={{0,24},{4,28},{8,16},{12,20},{16,8},{20,12},{24,0},{28,4},{1,25},{... | collective-permute-start | bytes 2949128 | tf_op jit(solution)/shard_map/ppermute | solution.py:325
  133.3 43.2 %collective-permute-start.12 = (bf16[2,32,7680]{2,1,0:T(8,128)(2,1)}, bf16[2,32,7680]{2,1,0:T(8,128)(2,1)}, u32[]{:S(2)}, u32[]{:S(2)}) collective-permute-start(bf16[2,32,7680]{2,1,0:T(8,128)(2,1)} %pad_maximum_fusion.2), channel_id=1, source_target_pairs={{0,1},{1,2},{2,3},{3,0},{4,5},{5,6},{6,7},{7,4},{8,9},{9,10},{10,1... | collective-permute-start | bytes 2949128 | tf_op jit(solution)/shard_map/ppermute | solution.py:322
  135.0 43.9 %collective-permute-start.13 = (bf16[2,32,7680]{2,1,0:T(8,128)(2,1)}, bf16[2,32,7680]{2,1,0:T(8,128)(2,1)}, u32[]{:S(2)}, u32[]{:S(2)}) collective-permute-start(bf16[2,32,7680]{2,1,0:T(8,128)(2,1)} %pad_maximum_fusion.3), channel_id=1, source_target_pairs={{0,3},{1,0},{2,1},{3,2},{4,7},{5,4},{6,5},{7,6},{8,11},{9,8},{10,9... | collective-permute-start | bytes 2949128 | tf_op jit(solution)/shard_map/ppermute | solution.py:322
  141.5 38.8 %copy-start.4 = (bf16[2,32,7680]{2,1,0:T(8,128)(2,1)S(1)}, bf16[2,32,7680]{2,1,0:T(8,128)(2,1)}, u32[]{:S(2)}) copy-start(bf16[2,32,7680]{2,1,0:T(8,128)(2,1)} %copy-done.3) | copy-start | bytes 2949124

commit v8 on v7

--- a/solution.py
+++ b/solution.py
@@ -201,6 +201,21 @@
     )(queries, score_grad, keys, gain)
 
 
+def beside_kernel(left, right, out):
+    cut = left.shape[1]
+    out[:, :cut] = left[...]
+    out[:, cut:] = right[...]
+
+
+def beside(left, right):
+    rows, columns = left.shape
+    return pl.pallas_call(
+        beside_kernel,
+        out_shape=jax.ShapeDtypeStruct((rows, 2 * columns), left.dtype),
+        name="beside",
+    )(left, right)
+
+
 def terms_kernel(splits, rows, weight, *outs):
     parts, img_count, own_rows, cols = rows.shape
     term = dot(rows[...].reshape(-1, cols), weight[...], 1, 1).astype(jnp.bfloat16)
@@ -232,44 +247,12 @@
     )(rows, weight)
 
 
-def weights_kernel(place, near, far, rows, own, mate, total):
-    low, width = near.shape[0], own.shape[1]
-    total[...] = dot(near[...], rows[:low], 0, 0) + dot(far[...], rows[low:], 0, 0)
-    core = place[0]
-    own[0] = total[pl.ds(pl.multiple_of(core * width, width), width)].astype(own.dtype)
-    mate[0] = total[pl.ds(pl.multiple_of((1 - core) * width, width), width)].astype(mate.dtype)
-
-
-def weights(near, far, rows, place, pairs):
-    vis_width, cols = near.shape[1], rows.shape[1]
-    width = vis_width // pairs
-    shape = jax.ShapeDtypeStruct((pairs, width // 2, cols), jnp.bfloat16)
-    target = pl.BlockSpec((1, width // 2, cols), lambda p, *_: (p, 0, 0))
-    return pl.pallas_call(
-        weights_kernel,
-        out_shape=(shape, shape),
-        grid_spec=pltpu.PrefetchScalarGridSpec(
-            num_scalar_prefetch=1,
-            grid=(pairs,),
-            in_specs=[
-                pl.BlockSpec((near.shape[0], width), lambda p, *_: (0, p)),
-                pl.BlockSpec((far.shape[0], width), lambda p, *_: (0, p)),
-                pl.BlockSpec(rows.shape, lambda *_: (0, 0)),
-            ],
-            out_specs=(target, target),
-            scratch_shapes=[pltpu.VMEM((width, cols), jnp.float32)],
-        ),
-        compiler_params=pltpu.CompilerParams(vmem_limit_bytes=32 * 1024 * 1024),
-        name="weights",
-    )(place, near, far, rows)
-
-
 def merge_kernel(place, held, given, out):
-    out[...] = (held[...].astype(jnp.float32) + given[...].astype(jnp.float32)).astype(out.dtype)
+    out[0] = (held[0, 0].astype(jnp.float32) + given[0].astype(jnp.float32)).astype(out.dtype)
 
 
 def merge(held, given, place):
-    pairs, own_width, cols = held.shape
+    pairs, _, own_width, cols = held.shape
     return [
         pl.pallas_call(
             merge_kernel,
@@ -279,11 +262,14 @@
                 grid=(1,),
                 in_specs=[
                     pl.BlockSpec(
+                        (1, 1, own_width, cols),
+                        lambda i, place, r=r: (jnp.bitwise_xor(place[1], r), place[0], 0, 0),
+                    ),
+                    pl.BlockSpec(
                         (1, own_width, cols),
                         lambda i, place, r=r: (jnp.bitwise_xor(place[1], r), 0, 0),
-                    )
-                ]
-                * 2,
+                    ),
+                ],
                 out_specs=pl.BlockSpec((1, own_width, cols), lambda *_: (0, 0, 0)),
             ),
             compiler_params=pltpu.CompilerParams(vmem_limit_bytes=32 * 1024 * 1024),
@@ -328,7 +314,7 @@
     query_gain, key_gain = query_gain[None, :], key_gain[None, :]
     normed, masked = before(queries, out_grad, query_gain, lengths, key_heads)
 
-    own_weight = jnp.concatenate((key_weight, value_weight), axis=1)
+    own_weight = beside(key_weight, value_weight)
     leaving = (from_left[:first], from_right[first:])
     if pairs != 4:
         weight = lax.all_gather(own_weight, "dp", axis=0, tiled=True)
@@ -365,23 +351,6 @@
     wholes = tuple((part, 0, img_count) for part in range(3))
     own, to_left, to_right = terms(rows[:3], weight, wholes, 4)
 
-    all_rows = rows.reshape(-1, cols)
-    if pairs != 4:
-        weight_part = dot(jnp.concatenate((near, far)), all_rows, 0, 0)
-        weight_grad = lax.psum_scatter(weight_part, "dp", scatter_dimension=0, tiled=True)
-    else:
-        where = jnp.stack((core, pair))
-        all_rows, leaving_right, leaving_left = lax.optimization_barrier(
-            (all_rows, leaving_right, leaving_left)
-        )
-        kept, given = weights(near, far, all_rows, where, pairs)
-        sent = merge(kept, swap(given, 1), where)
-        score_grad, sent = lax.optimization_barrier((score_grad, sent))
-        weight_grad = sent[0]
-        for r in range(1, pairs):
-            weight_grad = weight_grad + swap(sent[r], 2 * r).astype(jnp.float32)
-    query_grad = after(queries, score_grad, seq_keys, query_gain)
-
     right_half, left_half = lax.optimization_barrier(
         (ring(leaving_right, 1), ring(leaving_left, -1))
     )
@@ -393,12 +362,24 @@
     to_left = jnp.concatenate((to_left[:first], added(to_left[first:], left_half)))
     to_right, to_left = lax.optimization_barrier((to_right, to_left))
     from_left, from_right = ring(to_right, 1), ring(to_left, -1)
-    from_left, from_right, weight_grad, query_grad = lax.optimization_barrier(
-        (from_left, from_right, weight_grad, query_grad)
-    )
     image_grad = (
         own.astype(jnp.float32) + from_left.astype(jnp.float32) + from_right.astype(jnp.float32)
     ).astype(jnp.bfloat16)
+
+    weight_part = dot(jnp.concatenate((near, far)), rows.reshape(-1, cols), 0, 0)
+    if pairs != 4:
+        weight_grad = lax.psum_scatter(weight_part, "dp", scatter_dimension=0, tiled=True)
+    else:
+        weight_part = weight_part.astype(jnp.bfloat16).reshape(pairs, 2, own_width, cols)
+        given = swap(lax.dynamic_index_in_dim(weight_part, 1 - core, 1, keepdims=False), 1)
+        given, to_right, to_left = lax.optimization_barrier((given, to_right, to_left))
+        weight_grad, *sent = merge(weight_part, given, jnp.stack((core, pair)))
+        score_grad, sent = lax.optimization_barrier((score_grad, sent))
+        sent = [swap(piece, 2 * r) for r, piece in enumerate(sent, 1)]
+        image_grad, sent = lax.optimization_barrier((image_grad, sent))
+        for piece in sent:
+            weight_grad = weight_grad + piece.astype(jnp.float32)
+    query_grad = after(queries, score_grad, seq_keys, query_gain)
     return (query_grad, image_grad, weight_grad[:, :key_cols], weight_grad[:, key_cols:])
 
 

time: 184 us -> 170 us (0.924)
  local copies, waits for them, and re-layouts: 14 us -> 9.23 us
  Pallas kernels: 32.6 us -> 28.1 us
  other arithmetic: 9.48 us -> 5.8 us
  waiting for transfers between devices: 98.4 us -> 95.3 us
  matrix products: 3.13 us -> 5.62 us
    ppermute x10, waiting for transfers between devices: 36.3 us -> 4.17 us  [swap(): return lax.ppermute(value, 'dp', [(i, i ^ mask) for i in range(dp_size)])]
    ppermute x8, waiting for transfers between devices: 62.1 us -> 91.1 us  [ring(): lax.ppermute(value, 'mp', [(i, (i + step) % mp_size) for i in range(mp_si...]
    pallas_call x1, Pallas kernels: 6.59 us -> 2.2 us  [beside(): pl.pallas_call(beside_kernel, out_shape=jax.ShapeDtypeStruct((rows, 2 * c...]
    unnamed x30 -> x29, local copies, waits for them, and re-layouts: 3.53 us -> 0.33 us
    dot_general x2 -> x3, matrix products: 3.13 us -> 5.62 us  [dot(): lax.dot_general(left, right, (((left_dim,), (right_dim,)), ((), ())), pre...]
  transfers between devices with their start and end apart: 18 -> 18, of which waited for: 11 -> 11; matrix products, arithmetic and copies ran while one was open for 11% -> 9% of each run, Pallas kernels for 7% -> 12%
where the time goes in v8:
time: 170 us
  waiting for transfers between devices  95.3 us (56%)
  Pallas kernels  28.1 us (17%)
  starting transfers between devices  24.5 us (14%)
  local copies, waits for them, and re-layouts  9.23 us (5%)
  other arithmetic  5.8 us (3%)
  matrix products  5.62 us (3%)
    ppermute x8, waiting for transfers between devices, ring(): lax.ppermute(value, 'mp', [(i, (i + step) % mp_size) for i in range(mp_si...  91.1 us
    ppermute x8, starting transfers between devices, ring(): lax.ppermute(value, 'mp', [(i, (i + step) % mp_size) for i in range(mp_si...  16.7 us
    ppermute x10, starting transfers between devices, swap(): return lax.ppermute(value, 'dp', [(i, i ^ mask) for i in range(dp_size)])  7.72 us
    pallas_call x2, Pallas kernels, terms(): pl.pallas_call(functools.partial(terms_kernel, splits), out_shape=[jax.Sh...  6.57 us
    dot_general x3, matrix products, dot(): lax.dot_general(left, right, (((left_dim,), (right_dim,)), ((), ())), pre...  5.62 us
    dynamic_update_slice x8, local copies, waits for them, and re-layouts, per_device(): lax.dynamic_update_slice_in_dim(weight, source[k:k + 1], 2 * (pair ^ r +...  5.54 us
    pallas_call x4, Pallas kernels, merge(): pl.pallas_call(merge_kernel, out_shape=jax.ShapeDtypeStruct((1, own_width...  5.09 us
    pallas_call x1, Pallas kernels, attend(): pl.pallas_call(functools.partial(attend_kernel, len(pieces)), out_shape=(...  4.97 us
  transfers between devices with their start and end apart: 18, of which 11 were waited for; matrix products, arithmetic and copies ran while one was open for 9% of the time, Pallas kernels for 12%

profile of v8, /device:TPU:0, one launch (start us, length us, event | category | flops | bytes accessed | tf_op | source)
XLA Modules:
  0.0 169.5 jit_solution(5835149414787145418)
XLA Ops:
  0.6 3.1 %collective-permute-start = (bf16[2,32,7680]{2,1,0:T(8,128)(2,1)}, bf16[2,32,7680]{2,1,0:T(8,128)(2,1)S(1)}, u32[]{:S(2)}, u32[]{:S(2)}) collective-permute-start(bf16[2,32,7680]{2,1,0:T(8,128)(2,1)} %param.13), channel_id=1, source_target_pairs={{0,1},{1,2},{2,3},{3,0},{4,5},{5,6},{6,7},{7,4},{8,9},{9,10},{10,1... | collective-permute-start | bytes 2949128 | tf_op jit(solution)/shard_map/ppermute | solution.py:308
  3.7 2.1 %collective-permute-start.1 = (bf16[2,32,7680]{2,1,0:T(8,128)(2,1)}, bf16[2,32,7680]{2,1,0:T(8,128)(2,1)S(1)}, u32[]{:S(2)}, u32[]{:S(2)}) collective-permute-start(bf16[2,32,7680]{2,1,0:T(8,128)(2,1)} %param.13), channel_id=1, source_target_pairs={{0,3},{1,0},{2,1},{3,2},{4,7},{5,4},{6,5},{7,6},{8,11},{9,8},{10,9... | collective-permute-start | bytes 2949128 | tf_op jit(solution)/shard_map/ppermute | solution.py:308
  5.8 2.2 %beside.1 = bf16[960,512]{1,0:T(8,128)(2,1)} custom-call(bf16[960,256]{1,0:T(8,128)(2,1)} %left.1, bf16[960,256]{1,0:T(8,128)(2,1)} %right.1), custom_call_target="tpu_custom_call" | custom-call | tf_op jit(solution)/shard_map/beside/pallas_call | solution.py:212
  8.0 1.6 collective-permute-start.2
  9.6 1.5 collective-permute-start.3
  11.2 0.3 collective-permute-start.4
  11.5 5.0 %before.1 = (bf16[2,2,1024,128]{3,2,1,0:T(8,128)(2,1)}, bf16[2,2,1024,128]{3,2,1,0:T(8,128)(2,1)}) custom-call(s32[2]{0:T(128)} %lengths.1, bf16[2,128,2048]{2,1,0:T(8,128)(2,1)} %query.3, bf16[2,128,2048]{2,1,0:T(8,128)(2,1)} %grad.1, f32[1,128]{1,0:T(1,128)} %bitcast.60), custom_call_target="tpu_custom_call" | custom-call | tf_op jit(solution)/shard_map/before/pallas_call | solution.py:58
  16.5 12.1 %collective-permute-done = bf16[2,32,7680]{2,1,0:T(8,128)(2,1)S(1)} collective-permute-done((bf16[2,32,7680]{2,1,0:T(8,128)(2,1)}, bf16[2,32,7680]{2,1,0:T(8,128)(2,1)S(1)}, u32[]{:S(2)}, u32[]{:S(2)}) %collective-permute-start) | collective-permute-done | bytes 983072 | tf_op jit(solution)/shard_map/ppermute | solution.py:308
  28.6 19.6 %collective-permute-done.1 = bf16[2,32,7680]{2,1,0:T(8,128)(2,1)S(1)} collective-permute-done((bf16[2,32,7680]{2,1,0:T(8,128)(2,1)}, bf16[2,32,7680]{2,1,0:T(8,128)(2,1)S(1)}, u32[]{:S(2)}, u32[]{:S(2)}) %collective-permute-start.1) | collective-permute-done | bytes 983072 | tf_op jit(solution)/shard_map/ppermute | solution.py:308
  48.2 0.9 slice.57
  49.3 1.4 pad_maximum_fusion.1
  50.7 3.1 %collective-permute-done.3 = bf16[960,512]{1,0:T(8,128)(2,1)} collective-permute-done((bf16[960,512]{1,0:T(8,128)(2,1)}, bf16[960,512]{1,0:T(8,128)(2,1)}, u32[]{:S(2)}, u32[]{:S(2)}) %collective-permute-start.3) | collective-permute-done | bytes 983072 | tf_op jit(solution)/shard_map/ppermute | solution.py:311
  53.8 0.6 collective-permute-start.6
  54.5 3.8 %collective-permute-start.9 = (bf16[1,32,7680]{2,1,0:T(8,128)(2,1)}, bf16[1,32,7680]{2,1,0:T(8,128)(2,1)S(1)}, u32[]{:S(2)}, u32[]{:S(2)}) collective-permute-start(bf16[1,32,7680]{2,1,0:T(8,128)(2,1)} %slice.57), channel_id=1, source_target_pairs={{0,3},{1,0},{2,1},{3,2},{4,7},{5,4},{6,5},{7,6},{8,11},{9,8},{10,9... | collective-permute-start | bytes 1474568 | tf_op jit(solution)/shard_map/ppermute | solution.py:308
  58.3 0.7 broadcast_in_dim.16
  59.5 0.4 collective-permute-done.5
  59.8 1.3 slice_dynamic-update-slice_fusion.1
  61.2 1.3 slice_dynamic-update-slice_fusion
  62.5 1.3 constant_dynamic-update-slice_fusion.5
  63.9 1.3 constant_dynamic-update-slice_fusion.3
  65.3 1.7 fusion.8
  67.0 3.4 %collective-permute-done.8 = bf16[1,32,7680]{2,1,0:T(8,128)(2,1)S(1)} collective-permute-done((bf16[1,32,7680]{2,1,0:T(8,128)(2,1)S(1)}, bf16[1,32,7680]{2,1,0:T(8,128)(2,1)S(1)}, u32[]{:S(2)}, u32[]{:S(2)}) %collective-permute-start.8) | collective-permute-done | bytes 491552 | tf_op jit(solution)/shard_map/ppermute | solution.py:308
  70.4 8.4 %collective-permute-done.9 = bf16[1,32,7680]{2,1,0:T(8,128)(2,1)S(1)} collective-permute-done((bf16[1,32,7680]{2,1,0:T(8,128)(2,1)}, bf16[1,32,7680]{2,1,0:T(8,128)(2,1)S(1)}, u32[]{:S(2)}, u32[]{:S(2)}) %collective-permute-start.9) | collective-permute-done | bytes 491552 | tf_op jit(solution)/shard_map/ppermute | solution.py:308
  78.9 1.5 convolution_bitcast_fusion.refs_1_.refs_3_
  80.4 5.0 %attend.1 = (bf16[4,2,32,512]{3,2,1,0:T(8,128)(2,1)S(1)}, bf16[2,2,1024,128]{3,2,1,0:T(8,128)(2,1)S(1)}, bf16[2,2,128,128]{3,2,1,0:T(8,128)(2,1)S(1)}) custom-call(s32[2]{0:T(128)S(1)} %copy-done.4, s32[2]{0:T(128)S(1)} %copy-done.5, s32[4]{0:T(128)S(1)} %and_select_fusion.owners, f32[3,2,32,512]{3,2,1,0:T(8,128)S(1)} %bitcast.48, ...), custom_call_target="tpu_custom_call" | custom-call | tf_op jit(solution)/shard_map/attend/pallas_call | solution.py:141
  85.5 3.1 %terms.3 = (bf16[1,32,7680]{2,1,0:T(8,128)(2,1)S(1)}, bf16[1,32,7680]{2,1,0:T(8,128)(2,1)S(1)}) custom-call(bf16[1,2,32,512]{3,2,1,0:T(8,128)(2,1)S(1)} %slice.50.rows, bf16[7680,512]{1,0:T(8,128)(2,1)S(1)} %bitcast.46), custom_call_target="tpu_custom_call" | custom-call | tf_op jit(solution)/shard_map/terms/pallas_call | solution.py:232
  88.6 1.0 collective-permute-start.11
  89.6 2.9 %collective-permute-start.12 = (bf16[1,32,7680]{2,1,0:T(8,128)(2,1)S(1)}, bf16[1,32,7680]{2,1,0:T(8,128)(2,1)S(1)}, u32[]{:S(2)}, u32[]{:S(2)}) collective-permute-start(bf16[1,32,7680]{2,1,0:T(8,128)(2,1)S(1)} %get-tuple-element.55), channel_id=1, source_target_pairs={{0,3},{1,0},{2,1},{3,2},{4,7},{5,4},{6,5},{7,6},{8,11},{9,8},{10,9... | collective-permute-start | bytes 1474568 | tf_op jit(solution)/shard_map/ppermute | solution.py:308
  92.5 3.5 %terms.2 = (bf16[2,32,7680]{2,1,0:T(8,128)(2,1)S(1)}, bf16[2,32,7680]{2,1,0:T(8,128)(2,1)S(1)}, bf16[2,32,7680]{2,1,0:T(8,128)(2,1)S(1)}) custom-call(bf16[3,2,32,512]{3,2,1,0:T(8,128)(2,1)S(1)} %slice.48.rows, bf16[7680,512]{1,0:T(8,128)(2,1)S(1)} %bitcast.47), custom_call_target="tpu_custom_call" | custom-call | tf_op jit(solution)/shard_map/terms/pallas_call | solution.py:232
  96.0 2.5 %convolution_convert_fusion = bf16[7680,512]{1,0:T(8,128)(2,1)S(1)} fusion(bf16[256,512]{1,0:T(8,128)(2,1)S(1)} %bitcast.51, bf16[64,7680]{1,0:T(8,128)(2,1)S(1)} %bitcast.54, bf16[192,7680]{1,0:T(8,128)(2,1)S(1)} %bitcast.56), kind=kOutput, calls=%fused_computation | convolution fusion | flops 2025062400 | bytes 12058624 | tf_op jit(solution)/shard_map/dot_general | solution.py:29
  98.9 5.8 %collective-permute-done.11 = bf16[1,32,7680]{2,1,0:T(8,128)(2,1)S(1)} collective-permute-done((bf16[1,32,7680]{2,1,0:T(8,128)(2,1)S(1)}, bf16[1,32,7680]{2,1,0:T(8,128)(2,1)S(1)}, u32[]{:S(2)}, u32[]{:S(2)}) %collective-permute-start.11) | collective-permute-done | bytes 491552 | tf_op jit(solution)/shard_map/ppermute | solution.py:308
  104.6 8.1 %collective-permute-done.12 = bf16[1,32,7680]{2,1,0:T(8,128)(2,1)S(1)} collective-permute-done((bf16[1,32,7680]{2,1,0:T(8,128)(2,1)S(1)}, bf16[1,32,7680]{2,1,0:T(8,128)(2,1)S(1)}, u32[]{:S(2)}, u32[]{:S(2)}) %collective-permute-start.12) | collective-permute-done | bytes 491552 | tf_op jit(solution)/shard_map/ppermute | solution.py:308
  113.1 1.6 collective-permute-start.13
  114.7 2.3 %collective-permute-start.14 = (bf16[2,32,7680]{2,1,0:T(8,128)(2,1)S(1)}, bf16[2,32,7680]{2,1,0:T(8,128)(2,1)S(1)}, u32[]{:S(2)}, u32[]{:S(2)}) collective-permute-start(bf16[2,32,7680]{2,1,0:T(8,128)(2,1)S(1)} %pad_maximum_fusion.3), channel_id=1, source_target_pairs={{0,3},{1,0},{2,1},{3,2},{4,7},{5,4},{6,5},{7,6},{8,11},{9,8},{10,9... | collective-permute-start | bytes 2949128 | tf_op jit(solution)/shard_map/ppermute | solution.py:308
  117.1 0.8 merge.6
  117.9 1.7 %merge.5 = bf16[1,960,512]{2,1,0:T(8,128)(2,1)} custom-call(s32[2]{0:T(128)S(1)} %pad_add_fusion.place, bf16[4,2,960,512]{3,2,1,0:T(8,128)(2,1)S(1)} %bitcast.41, bf16[4,960,512]{2,1,0:T(8,128)(2,1)S(1)} %collective-permute-done.10.given), custom_call_target="tpu_custom_call" | custom-call | tf_op jit(solution)/shard_map/merge/pallas_call | solution.py:257
  119.6 1.7 %merge.4 = bf16[1,960,512]{2,1,0:T(8,128)(2,1)} custom-call(s32[2]{0:T(128)S(1)} %pad_add_fusion.place, bf16[4,2,960,512]{3,2,1,0:T(8,128)(2,1)S(1)} %bitcast.42, bf16[4,960,512]{2,1,0:T(8,128)(2,1)S(1)} %collective-permute-done.10.given), custom_call_target="tpu_custom_call" | custom-call | tf_op jit(solution)/shard_map/merge/pallas_call | solution.py:257
  121.4 1.2 collective-permute-start.15
  122.6 0.8 collective-permute-start.16
  123.5 1.4 collective-permute-start.17
  124.9 14.8 %collective-permute-done.13 = bf16[2,32,7680]{2,1,0:T(8,128)(2,1)S(1)} collective-permute-done((bf16[2,32,7680]{2,1,0:T(8,128)(2,1)S(1)}, bf16[2,32,7680]{2,1,0:T(8,128)(2,1)S(1)}, u32[]{:S(2)}, u32[]{:S(2)}) %collective-permute-start.13) | collective-permute-done | bytes 983072 | tf_op jit(solution)/shard_map/ppermute | solution.py:308
  139.7 19.0 %collective-permute-done.14 = bf16[2,32,7680]{2,1,0:T(8,128)(2,1)S(1)} collective-permute-done((bf16[2,32,7680]{2,1,0:T(8,128)(2,1)S(1)}, bf16[2,32,7680]{2,1,0:T(8,128)(2,1)S(1)}, u32[]{:S(2)}, u32[]{:S(2)}) %collective-permute-start.14) | collective-permute-done | bytes 983072 | tf_op jit(solution)/shard_map/ppermute | solution.py:308
  158.7 1.3 add_convert_fusion
  160.0 0.8 merge.7
  160.8 4.3 %after.1 = bf16[2,128,2048]{2,1,0:T(8,128)(2,1)} custom-call(bf16[2,128,2048]{2,1,0:T(8,128)(2,1)} %query.3, bf16[2,2,1024,128]{3,2,1,0:T(8,128)(2,1)} %copy-done, bf16[2,2,128,128]{3,2,1,0:T(8,128)(2,1)} %copy-done.3, f32[1,128]{1,0:T(1,128)} %bitcast.61), custom_call_target="tpu_custom_call" | custom-call | tf_op jit(solution)/shard_map/after/pallas_call | solution.py:189
  165.2 0.7 collective-permute-done.17
  165.8 2.3 %fusion.4 = f32[960,512]{1,0:T(8,128)S(1)} fusion(f32[1,960,512]{2,1,0:T(8,128)S(1)} %merge.7, bf16[960,512]{1,0:T(8,128)(2,1)} %collective-permute-done.17, bf16[960,512]{1,0:T(8,128)(2,1)} %collective-permute-done.16, bf16[960,512]{1,0:T(8,128)(2,1)} %collective-permute-done.15), kind=kLoop, calls=%fused_computation.9 | loop fusion | flops 2949120 | bytes 6881280 | tf_op jit(solution)/shard_map/add | solution.py:381
  168.1 1.4 fusion.7
  (57 shorter events, 2.1 us)
Async XLA Ops:
  0.6 27.9 %collective-permute-start = (bf16[2,32,7680]{2,1,0:T(8,128)(2,1)}, bf16[2,32,7680]{2,1,0:T(8,128)(2,1)S(1)}, u32[]{:S(2)}, u32[]{:S(2)}) collective-permute-start(bf16[2,32,7680]{2,1,0:T(8,128)(2,1)} %param.13), channel_id=1, source_target_pairs={{0,1},{1,2},{2,3},{3,0},{4,5},{5,6},{6,7},{7,4},{8,9},{9,10},{10,1... | collective-permute-start | bytes 2949128 | tf_op jit(solution)/shard_map/ppermute | solution.py:308
  3.7 44.5 %collective-permute-start.1 = (bf16[2,32,7680]{2,1,0:T(8,128)(2,1)}, bf16[2,32,7680]{2,1,0:T(8,128)(2,1)S(1)}, u32[]{:S(2)}, u32[]{:S(2)}) collective-permute-start(bf16[2,32,7680]{2,1,0:T(8,128)(2,1)} %param.13), channel_id=1, source_target_pairs={{0,3},{1,0},{2,1},{3,2},{4,7},{5,4},{6,5},{7,6},{8,11},{9,8},{10,9... | collective-permute-start | bytes 2949128 | tf_op jit(solution)/shard_map/ppermute | solution.py:308
  8.0 41.3 %copy-start.7 = (bf16[960,512]{1,0:T(8,128)(2,1)S(1)}, bf16[960,512]{1,0:T(8,128)(2,1)}, u32[]{:S(2)}) copy-start(bf16[960,512]{1,0:T(8,128)(2,1)} %beside.1) | copy-start | bytes 2949124
  8.0 41.1 %collective-permute-start.2 = (bf16[960,512]{1,0:T(8,128)(2,1)}, bf16[960,512]{1,0:T(8,128)(2,1)}, u32[]{:S(2)}, u32[]{:S(2)}) collective-permute-start(bf16[960,512]{1,0:T(8,128)(2,1)} %beside.1), channel_id=1, source_target_pairs={{0,8},{4,12},{8,0},{12,4},{16,24},{20,28},{24,16},{28,20},{1,9},{5... | collective-permute-start | bytes 2949128 | tf_op jit(solution)/shard_map/ppermute | solution.py:311
  9.6 44.2 %collective-permute-start.3 = (bf16[960,512]{1,0:T(8,128)(2,1)}, bf16[960,512]{1,0:T(8,128)(2,1)}, u32[]{:S(2)}, u32[]{:S(2)}) collective-permute-start(bf16[960,512]{1,0:T(8,128)(2,1)} %beside.1), channel_id=1, source_target_pairs={{0,16},{4,20},{8,24},{12,28},{16,0},{20,4},{24,8},{28,12},{1,17},{... | collective-permute-start | bytes 2949128 | tf_op jit(solution)/shard_map/ppermute | solution.py:311
  11.2 42.6 %collective-permute-start.4 = (bf16[960,512]{1,0:T(8,128)(2,1)}, bf16[960,512]{1,0:T(8,128)(2,1)}, u32[]{:S(2)}, u32[]{:S(2)}) collective-permute-start(bf16[960,512]{1,0:T(8,128)(2,1)} %beside.1), channel_id=1, source_target_pairs={{0,24},{4,28},{8,16},{12,20},{16,8},{20,12},{24,0},{28,4},{1,25},{... | collective-permute-start | bytes 2949128 | tf_op jit(solution)/shard_map/ppermute | solution.py:311
  11.5 42.3 %copy-start.13 = (s32[4]{0:T(128)S(1)}, s32[4]{0:T(128)}, u32[]{:S(2)}) copy-start(s32[4]{0:T(128)} %constant.61.clone) | copy-start | bytes 52
  28.6 20.5 %copy-start.8 = (bf16[2,32,7680]{2,1,0:T(8,128)(2,1)}, bf16[2,32,7680]{2,1,0:T(8,128)(2,1)S(1)}, u32[]{:S(2)}) copy-start(bf16[2,32,7680]{2,1,0:T(8,128)(2,1)S(1)} %collective-permute-done) | copy-start | bytes 2949124
  48.2 1.1 copy-start.10
  53.8 6.0 %collective-permute-start.5 = (bf16[2,960,512]{2,1,0:T(8,128)(2,1)S(1)}, bf16[2,960,512]{2,1,0:T(8,128)(2,1)}, u32[]{:S(2)}, u32[]{:S(2)}) collective-permute-start(bf16[2,960,512]{2,1,0:T(8,128)(2,1)S(1)} %pad_maximum_fusion.1), channel_id=1, source_target_pairs={{0,4},{4,0},{8,12},{12,8},{16,20},{20,16},{24,28},{28,24},{1,5},{5... | collective-permute-start | bytes 5898248 | tf_op jit(solution)/shard_map/ppermute | solution.py:311
  53.8 10.0 %collective-permute-start.6 = (bf16[1,960,512]{2,1,0:T(8,128)(2,1)}, bf16[1,960,512]{2,1,0:T(8,128)(2,1)S(1)}, u32[]{:S(2)}, u32[]{:S(2)}) collective-permute-start(bf16[1,960,512]{2,1,0:T(8,128)(2,1)} %bitcast.7), channel_id=1, source_target_pairs={{0,4},{4,0},{8,12},{12,8},{16,20},{20,16},{24,28},{28,24},{1,5},{5... | collective-permute-start | bytes 2949128 | tf_op jit(solution)/shard_map/ppermute | solution.py:311
  54.4 4.7 %copy-start.9 = (bf16[2,32,7680]{2,1,0:T(8,128)(2,1)S(1)}, bf16[2,32,7680]{2,1,0:T(8,128)(2,1)}, u32[]{:S(2)}) copy-start(bf16[2,32,7680]{2,1,0:T(8,128)(2,1)} %copy-done.8) | copy-start | bytes 2949124
  54.4 4.7 %copy-start.11 = (bf16[2,32,7680]{2,1,0:T(8,128)(2,1)S(1)}, bf16[2,32,7680]{2,1,0:T(8,128)(2,1)}, u32[]{:S(2)}) copy-start(bf16[2,32,7680]{2,1,0:T(8,128)(2,1)} %copy-done.10) | copy-start | bytes 2949124
  54.4 4.7 %copy-start.12 = (bf16[2,32,7680]{2,1,0:T(8,128)(2,1)S(1)}, bf16[2,32,7680]{2,1,0:T(8,128)(2,1)}, u32[]{:S(2)}) copy-start(bf16[2,32,7680]{2,1,0:T(8,128)(2,1)} %param.13) | copy-start | bytes 2949124
  54.4 10.8 %collective-permute-start.7 = (bf16[1,960,512]{2,1,0:T(8,128)(2,1)}, bf16[1,960,512]{2,1,0:T(8,128)(2,1)S(1)}, u32[]{:S(2)}, u32[]{:S(2)}) collective-permute-start(bf16[1,960,512]{2,1,0:T(8,128)(2,1)} %bitcast.8), channel_id=1, source_target_pairs={{0,4},{4,0},{8,12},{12,8},{16,20},{20,16},{24,28},{28,24},{1,5},{5... | collective-permute-start | bytes 2949128 | tf_op jit(solution)/shard_map/ppermute | solution.py:311
  54.5 15.9 %collective-permute-start.8 = (bf16[1,32,7680]{2,1,0:T(8,128)(2,1)S(1)}, bf16[1,32,7680]{2,1,0:T(8,128)(2,1)S(1)}, u32[]{:S(2)}, u32[]{:S(2)}) collective-permute-start(bf16[1,32,7680]{2,1,0:T(8,128)(2,1)S(1)} %slice.56), channel_id=1, source_target_pairs={{0,1},{1,2},{2,3},{3,0},{4,5},{5,6},{6,7},{7,4},{8,9},{9,10},{10,1... | collective-permute-start | bytes 1474568 | tf_op jit(solution)/shard_map/ppermute | solution.py:308
  54.5 24.3 %collective-permute-start.9 = (bf16[1,32,7680]{2,1,0:T(8,128)(2,1)}, bf16[1,32,7680]{2,1,0:T(8,128)(2,1)S(1)}, u32[]{:S(2)}, u32[]{:S(2)}) collective-permute-start(bf16[1,32,7680]{2,1,0:T(8,128)(2,1)} %slice.57), channel_id=1, source_target_pairs={{0,3},{1,0},{2,1},{3,2},{4,7},{5,4},{6,5},{7,6},{8,11},{9,8},{10,9... | collective-permute-start | bytes 1474568 | tf_op jit(solution)/shard_map/ppermute | solution.py:308
  78.9 1.5 copy-start.1
  78.9 1.5 copy-start.2
  78.9 1.5 copy-start.4
  78.9 1.5 copy-start.5
  78.9 1.5 copy-start.6
  85.4 3.2 %copy-start = (bf16[2,2,1024,128]{3,2,1,0:T(8,128)(2,1)}, bf16[2,2,1024,128]{3,2,1,0:T(8,128)(2,1)S(1)}, u32[]{:S(2)}) copy-start(bf16[2,2,1024,128]{3,2,1,0:T(8,128)(2,1)S(1)} %get-tuple-element.62.score_grad) | copy-start | bytes 3145732
  85.4 3.2 %copy-start.3 = (bf16[2,2,128,128]{3,2,1,0:T(8,128)(2,1)}, bf16[2,2,128,128]{3,2,1,0:T(8,128)(2,1)S(1)}, u32[]{:S(2)}) copy-start(bf16[2,2,128,128]{3,2,1,0:T(8,128)(2,1)S(1)} %get-tuple-element.63.keys) | copy-start | bytes 393220
  88.6 16.0 %collective-permute-start.11 = (bf16[1,32,7680]{2,1,0:T(8,128)(2,1)S(1)}, bf16[1,32,7680]{2,1,0:T(8,128)(2,1)S(1)}, u32[]{:S(2)}, u32[]{:S(2)}) collective-permute-start(bf16[1,32,7680]{2,1,0:T(8,128)(2,1)S(1)} %get-tuple-element.54), channel_id=1, source_target_pairs={{0,1},{1,2},{2,3},{3,0},{4,5},{5,6},{6,7},{7,4},{8,9},{9,10},{10,1... | collective-permute-start | bytes 1474568 | tf_op jit(solution)/shard_map/ppermute | solution.py:308
  89.6 23.1 %collective-permute-start.12 = (bf16[1,32,7680]{2,1,0:T(8,128)(2,1)S(1)}, bf16[1,32,7680]{2,1,0:T(8,128)(2,1)S(1)}, u32[]{:S(2)}, u32[]{:S(2)}) collective-permute-start(bf16[1,32,7680]{2,1,0:T(8,128)(2,1)S(1)} %get-tuple-element.55), channel_id=1, source_target_pairs={{0,3},{1,0},{2,1},{3,2},{4,7},{5,4},{6,5},{7,6},{8,11},{9,8},{10,9... | collective-permute-start | bytes 1474568 | tf_op jit(solution)/shard_map/ppermute | solution.py:308
  98.8 18.3 %collective-permute-start.10 = (bf16[4,960,512]{2,1,0:T(8,128)(2,1)S(1)}, bf16[4,960,512]{2,1,0:T(8,128)(2,1)S(1)}, u32[]{:S(2)}, u32[]{:S(2)}) collective-permute-start(bf16[4,960,512]{2,1,0:T(8,128)(2,1)S(1)} %dynamic-slice_bitcast_fusion), channel_id=1, source_target_pairs={{0,4},{4,0},{8,12},{12,8},{16,20},{20,16},{24,28},{28,24},{1,5},{5... | collective-permute-start | bytes 11796488 | tf_op jit(solution)/shard_map/ppermute | solution.py:311
  113.1 26.6 %collective-permute-start.13 = (bf16[2,32,7680]{2,1,0:T(8,128)(2,1)S(1)}, bf16[2,32,7680]{2,1,0:T(8,128)(2,1)S(1)}, u32[]{:S(2)}, u32[]{:S(2)}) collective-permute-start(bf16[2,32,7680]{2,1,0:T(8,128)(2,1)S(1)} %pad_maximum_fusion.2), channel_id=1, source_target_pairs={{0,1},{1,2},{2,3},{3,0},{4,5},{5,6},{6,7},{7,4},{8,9},{9,10},{10,1... | collective-permute-start | bytes 2949128 | tf_op jit(solution)/shard_map/ppermute | solution.py:308
  114.7 44.0 %collective-permute-start.14 = (bf16[2,32,7680]{2,1,0:T(8,128)(2,1)S(1)}, bf16[2,32,7680]{2,1,0:T(8,128)(2,1)S(1)}, u32[]{:S(2)}, u32[]{:S(2)}) collective-permute-start(bf16[2,32,7680]{2,1,0:T(8,128)(2,1)S(1)} %pad_maximum_fusion.3), channel_id=1, source_target_pairs={{0,3},{1,0},{2,1},{3,2},{4,7},{5,4},{6,5},{7,6},{8,11},{9,8},{10,9... | collective-permute-start | bytes 2949128 | tf_op jit(solution)/shard_map/ppermute | solution.py:308
  121.4 43.8 %collective-permute-start.15 = (bf16[960,512]{1,0:T(8,128)(2,1)}, bf16[960,512]{1,0:T(8,128)(2,1)}, u32[]{:S(2)}, u32[]{:S(2)}) collective-permute-start(bf16[960,512]{1,0:T(8,128)(2,1)} %bitcast.20), channel_id=1, source_target_pairs={{0,8},{4,12},{8,0},{12,4},{16,24},{20,28},{24,16},{28,20},{1,9},{5... | collective-permute-start | bytes 2949128 | tf_op jit(solution)/shard_map/ppermute | solution.py:311
  122.6 42.5 %collective-permute-start.16 = (bf16[960,512]{1,0:T(8,128)(2,1)}, bf16[960,512]{1,0:T(8,128)(2,1)}, u32[]{:S(2)}, u32[]{:S(2)}) collective-permute-start(bf16[960,512]{1,0:T(8,128)(2,1)} %bitcast.21), channel_id=1, source_target_pairs={{0,16},{4,20},{8,24},{12,28},{16,0},{20,4},{24,8},{28,12},{1,17},{... | collective-permute-start | bytes 2949128 | tf_op jit(solution)/shard_map/ppermute | solution.py:311
  123.5 42.4 %collective-permute-start.17 = (bf16[960,512]{1,0:T(8,128)(2,1)S(1)}, bf16[960,512]{1,0:T(8,128)(2,1)}, u32[]{:S(2)}, u32[]{:S(2)}) collective-permute-start(bf16[960,512]{1,0:T(8,128)(2,1)S(1)} %bitcast.50), channel_id=1, source_target_pairs={{0,24},{4,28},{8,16},{12,20},{16,8},{20,12},{24,0},{28,4},{1,25},{... | collective-permute-start | bytes 2949128 | tf_op jit(solution)/shard_map/ppermute | solution.py:311

commit v9 on v8

--- a/solution.py
+++ b/solution.py
@@ -247,36 +247,73 @@
     )(rows, weight)
 
 
-def merge_kernel(place, held, given, out):
-    out[0] = (held[0, 0].astype(jnp.float32) + given[0].astype(jnp.float32)).astype(out.dtype)
+def pair_sum(held, given):
+    return held[0, 0].astype(jnp.float32) + given[0].astype(jnp.float32)
+
+
+def merge_kernel(place, *refs):
+    count = len(refs) // 3
+    for held, given, out in zip(refs[:count], refs[count : 2 * count], refs[2 * count :]):
+        out[...] = pair_sum(held, given).astype(out.dtype)
+
+
+def finish_kernel(place, held, given, *refs):
+    *sent, key_out, value_out = refs
+    total = pair_sum(held, given)
+    for piece in sent:
+        total = total + piece[...].astype(jnp.float32)
+    cut = key_out.shape[1]
+    key_out[...] = total[:, :cut]
+    value_out[...] = total[:, cut:]
+
+
+def held_specs(own_width, cols, steps, r):
+    rows = own_width // steps
+    return (
+        pl.BlockSpec(
+            (1, 1, rows, cols),
+            lambda i, place: (jnp.bitwise_xor(place[1], r), place[0], i, 0),
+        ),
+        pl.BlockSpec(
+            (1, rows, cols), lambda i, place: (jnp.bitwise_xor(place[1], r), i, 0)
+        ),
+    )
 
 
 def merge(held, given, place):
     pairs, _, own_width, cols = held.shape
-    return [
-        pl.pallas_call(
-            merge_kernel,
-            out_shape=jax.ShapeDtypeStruct((1, own_width, cols), kind),
-            grid_spec=pltpu.PrefetchScalarGridSpec(
-                num_scalar_prefetch=1,
-                grid=(1,),
-                in_specs=[
-                    pl.BlockSpec(
-                        (1, 1, own_width, cols),
-                        lambda i, place, r=r: (jnp.bitwise_xor(place[1], r), place[0], 0, 0),
-                    ),
-                    pl.BlockSpec(
-                        (1, own_width, cols),
-                        lambda i, place, r=r: (jnp.bitwise_xor(place[1], r), 0, 0),
-                    ),
-                ],
-                out_specs=pl.BlockSpec((1, own_width, cols), lambda *_: (0, 0, 0)),
-            ),
-            compiler_params=pltpu.CompilerParams(vmem_limit_bytes=32 * 1024 * 1024),
-            name="merge",
-        )(place, held, given)[0]
-        for r, kind in enumerate([jnp.float32] + [jnp.bfloat16] * (pairs - 1))
-    ]
+    specs = [held_specs(own_width, cols, 2, r) for r in range(1, pairs)]
+    return pl.pallas_call(
+        merge_kernel,
+        out_shape=[jax.ShapeDtypeStruct((own_width, cols), jnp.bfloat16)] * len(specs),
+        grid_spec=pltpu.PrefetchScalarGridSpec(
+            num_scalar_prefetch=1,
+            grid=(2,),
+            in_specs=[spec[0] for spec in specs] + [spec[1] for spec in specs],
+            out_specs=[pl.BlockSpec((own_width // 2, cols), lambda i, _: (i, 0))] * len(specs),
+        ),
+        compiler_params=pltpu.CompilerParams(vmem_limit_bytes=32 * 1024 * 1024),
+        name="merge",
+    )(place, *[held] * len(specs), *[given] * len(specs))
+
+
+def finish(held, given, sent, place):
+    _, _, own_width, cols = held.shape
+    rows = own_width // 2
+    half = jax.ShapeDtypeStruct((own_width, cols // 2), jnp.float32)
+    return pl.pallas_call(
+        finish_kernel,
+        out_shape=(half, half),
+        grid_spec=pltpu.PrefetchScalarGridSpec(
+            num_scalar_prefetch=1,
+            grid=(2,),
+            in_specs=[*held_specs(own_width, cols, 2, 0)]
+            + [pl.BlockSpec((rows, cols), lambda i, _: (i, 0))] * len(sent),
+            out_specs=[pl.BlockSpec((rows, cols // 2), lambda i, _: (i, 0))] * 2,
+        ),
+        compiler_params=pltpu.CompilerParams(vmem_limit_bytes=32 * 1024 * 1024),
+        name="finish",
+    )(place, held, given, *sent)
 
 
 def per_device(
@@ -351,35 +388,42 @@
     wholes = tuple((part, 0, img_count) for part in range(3))
     own, to_left, to_right = terms(rows[:3], weight, wholes, 4)
 
-    right_half, left_half = lax.optimization_barrier(
-        (ring(leaving_right, 1), ring(leaving_left, -1))
-    )
+    right_half, left_half = ring(leaving_right, 1), ring(leaving_left, -1)
+
+    if pairs != 4:
+        all_images = jnp.concatenate((near, far))
+        weight_part = dot(all_images, rows.reshape(-1, cols), 0, 0)
+        weight_grad = lax.psum_scatter(weight_part, "dp", scatter_dimension=0, tiled=True)
+    else:
+        held_rows, leaving_right, leaving_left = lax.optimization_barrier(
+            (rows, leaving_right, leaving_left)
+        )
+        all_images = jnp.concatenate((near, far))
+        weight_part = dot(all_images, held_rows.reshape(-1, cols), 0, 0)
+        weight_part = weight_part.astype(jnp.bfloat16).reshape(pairs, 2, own_width, cols)
+        given = swap(lax.dynamic_index_in_dim(weight_part, 1 - core, 1, keepdims=False), 1)
+        where = jnp.stack((core, pair))
+        sent = merge(weight_part, given, where)
+        right_half, left_half, sent = lax.optimization_barrier((right_half, left_half, sent))
 
     def added(held, half):
         return (held.astype(jnp.float32) + half.astype(jnp.float32)).astype(jnp.bfloat16)
 
     to_right = jnp.concatenate((added(to_right[:first], right_half), to_right[first:]))
     to_left = jnp.concatenate((to_left[:first], added(to_left[first:], left_half)))
-    to_right, to_left = lax.optimization_barrier((to_right, to_left))
+    to_right, to_left, score_grad = lax.optimization_barrier((to_right, to_left, score_grad))
     from_left, from_right = ring(to_right, 1), ring(to_left, -1)
+    query_grad = after(queries, score_grad, seq_keys, query_gain)
+    from_left, from_right, query_grad = lax.optimization_barrier(
+        (from_left, from_right, query_grad)
+    )
     image_grad = (
         own.astype(jnp.float32) + from_left.astype(jnp.float32) + from_right.astype(jnp.float32)
     ).astype(jnp.bfloat16)
-
-    weight_part = dot(jnp.concatenate((near, far)), rows.reshape(-1, cols), 0, 0)
-    if pairs != 4:
-        weight_grad = lax.psum_scatter(weight_part, "dp", scatter_dimension=0, tiled=True)
-    else:
-        weight_part = weight_part.astype(jnp.bfloat16).reshape(pairs, 2, own_width, cols)
-        given = swap(lax.dynamic_index_in_dim(weight_part, 1 - core, 1, keepdims=False), 1)
-        given, to_right, to_left = lax.optimization_barrier((given, to_right, to_left))
-        weight_grad, *sent = merge(weight_part, given, jnp.stack((core, pair)))
-        score_grad, sent = lax.optimization_barrier((score_grad, sent))
+    if pairs == 4:
         sent = [swap(piece, 2 * r) for r, piece in enumerate(sent, 1)]
         image_grad, sent = lax.optimization_barrier((image_grad, sent))
-        for piece in sent:
-            weight_grad = weight_grad + piece.astype(jnp.float32)
-    query_grad = after(queries, score_grad, seq_keys, query_gain)
+        return (query_grad, image_grad, *finish(weight_part, given, sent, where))
     return (query_grad, image_grad, weight_grad[:, :key_cols], weight_grad[:, key_cols:])
 
 

time: 170 us -> 177 us (1.041)
  local copies, waits for them, and re-layouts: 9.23 us -> 14.8 us
    unnamed x29 -> x37, local copies, waits for them, and re-layouts: 0.33 us -> 6.47 us
    add x1 -> x0, other arithmetic: 2.31 us -> none  [per_device(): weight_grad = weight_grad + piece.astype(jnp.float32)]
    convert_element_type x1, other arithmetic: 1.3 us -> 3.09 us  [per_device(): image_grad = (own.astype(jnp.float32) + from_left.astype(jnp.float32) + f...]
    pallas_call x4 -> x2, Pallas kernels: 5.09 us -> 4.84 us  [the longest x1 2.78 us: merge(): pl.pallas_call(merge_kernel, out_shape=[jax.ShapeDtypeStruct((own_width,...]
  transfers between devices with their start and end apart: 18 -> 18, of which waited for: 11 -> 10; matrix products, arithmetic and copies ran while one was open for 9% -> 8% of each run, Pallas kernels for 12% -> 10%
where the time goes in v9:
time: 177 us; the launch traced here: 176 us
  waiting for transfers between devices  95.3 us (54%)
  Pallas kernels  27.7 us (16%)
  starting transfers between devices  24.3 us (14%)
  local copies, waits for them, and re-layouts  14.8 us (8%)
  other arithmetic  7.46 us (4%)
  matrix products  5.62 us (3%)
    ppermute x8, waiting for transfers between devices, ring(): lax.ppermute(value, 'mp', [(i, (i + step) % mp_size) for i in range(mp_si...  92.3 us
    ppermute x8, starting transfers between devices, ring(): lax.ppermute(value, 'mp', [(i, (i + step) % mp_size) for i in range(mp_si...  16.6 us
    ppermute x10, starting transfers between devices, swap(): return lax.ppermute(value, 'dp', [(i, i ^ mask) for i in range(dp_size)])  7.67 us
    pallas_call x2, Pallas kernels, terms(): pl.pallas_call(functools.partial(terms_kernel, splits), out_shape=[jax.Sh...  6.55 us
    unnamed x37, local copies, waits for them, and re-layouts  6.47 us
    dynamic_update_slice x8, local copies, waits for them, and re-layouts, per_device(): lax.dynamic_update_slice_in_dim(weight, source[k:k + 1], 2 * (pair ^ r +...  6.29 us
    dot_general x3, matrix products, dot(): lax.dot_general(left, right, (((left_dim,), (right_dim,)), ((), ())), pre...  5.62 us
    pallas_call x1, Pallas kernels, attend(): pl.pallas_call(functools.partial(attend_kernel, len(pieces)), out_shape=(...  4.99 us
  transfers between devices with their start and end apart: 18, of which 10 were waited for; matrix products, arithmetic and copies ran while one was open for 8% of the time, Pallas kernels for 10%

profile of v9, /device:TPU:0, one launch (start us, length us, event | category | flops | bytes accessed | tf_op | source)
XLA Modules:
  0.0 176.2 jit_solution(9634697167160444440)
XLA Ops:
  0.6 5.1 %collective-permute-start.1 = (bf16[2,32,7680]{2,1,0:T(8,128)(2,1)}, bf16[2,32,7680]{2,1,0:T(8,128)(2,1)S(1)}, u32[]{:S(2)}, u32[]{:S(2)}) collective-permute-start(bf16[2,32,7680]{2,1,0:T(8,128)(2,1)} %param.13), channel_id=1, source_target_pairs={{0,3},{1,0},{2,1},{3,2},{4,7},{5,4},{6,5},{7,6},{8,11},{9,8},{10,9... | collective-permute-start | bytes 2949128 | tf_op jit(solution)/shard_map/ppermute | solution.py:345
  5.7 2.2 %beside.1 = bf16[960,512]{1,0:T(8,128)(2,1)} custom-call(bf16[960,256]{1,0:T(8,128)(2,1)} %left.1, bf16[960,256]{1,0:T(8,128)(2,1)} %right.1), custom_call_target="tpu_custom_call" | custom-call | tf_op jit(solution)/shard_map/beside/pallas_call | solution.py:212
  7.9 1.5 collective-permute-start.2
  9.4 1.5 collective-permute-start.3
  11.0 0.5 collective-permute-start.4
  11.4 4.8 %before.1 = (bf16[2,2,1024,128]{3,2,1,0:T(8,128)(2,1)}, bf16[2,2,1024,128]{3,2,1,0:T(8,128)(2,1)}) custom-call(s32[2]{0:T(128)} %lengths.1, bf16[2,128,2048]{2,1,0:T(8,128)(2,1)} %query.3, bf16[2,128,2048]{2,1,0:T(8,128)(2,1)} %grad.1, f32[1,128]{1,0:T(1,128)} %bitcast.50), custom_call_target="tpu_custom_call" | custom-call | tf_op jit(solution)/shard_map/before/pallas_call | solution.py:58
  16.3 32.7 %collective-permute-done = bf16[2,32,7680]{2,1,0:T(8,128)(2,1)S(1)} collective-permute-done((bf16[2,32,7680]{2,1,0:T(8,128)(2,1)}, bf16[2,32,7680]{2,1,0:T(8,128)(2,1)S(1)}, u32[]{:S(2)}, u32[]{:S(2)}) %collective-permute-start) | collective-permute-done | bytes 983072 | tf_op jit(solution)/shard_map/ppermute | solution.py:345
  49.0 0.9 slice.49
  50.0 1.7 pad_maximum_fusion.1
  51.7 2.0 %collective-permute-done.3 = bf16[960,512]{1,0:T(8,128)(2,1)} collective-permute-done((bf16[960,512]{1,0:T(8,128)(2,1)}, bf16[960,512]{1,0:T(8,128)(2,1)}, u32[]{:S(2)}, u32[]{:S(2)}) %collective-permute-start.3) | collective-permute-done | bytes 983072 | tf_op jit(solution)/shard_map/ppermute | solution.py:348
  53.8 0.5 collective-permute-start.6
  54.4 3.8 %collective-permute-start.9 = (bf16[1,32,7680]{2,1,0:T(8,128)(2,1)}, bf16[1,32,7680]{2,1,0:T(8,128)(2,1)S(1)}, u32[]{:S(2)}, u32[]{:S(2)}) collective-permute-start(bf16[1,32,7680]{2,1,0:T(8,128)(2,1)} %slice.49), channel_id=1, source_target_pairs={{0,3},{1,0},{2,1},{3,2},{4,7},{5,4},{6,5},{7,6},{8,11},{9,8},{10,9... | collective-permute-start | bytes 1474568 | tf_op jit(solution)/shard_map/ppermute | solution.py:345
  58.3 0.7 broadcast_in_dim.16
  59.0 0.3 pad_maximum_fusion
  59.5 2.0 %slice_dynamic-update-slice_fusion.1 = bf16[8,960,512]{2,1,0:T(8,128)(2,1)S(1)} fusion(bf16[8,960,512]{2,1,0:T(8,128)(2,1)S(1)} %slice_dynamic-update-slice_fusion.3, s32[]{:T(128)S(6)} %select_n.49, bf16[2,960,512]{2,1,0:T(8,128)(2,1)} %collective-permute-done.5), kind=kLoop, calls=%fused_computation.10 | loop fusion | bytes 1966084 | tf_op jit(solution)/shard_map/dynamic_update_slice | solution.py:371
  61.7 1.3 slice_dynamic-update-slice_fusion
  63.0 1.3 constant_dynamic-update-slice_fusion.5
  64.4 1.3 constant_dynamic-update-slice_fusion.3
  65.8 1.7 fusion.5
  67.5 2.7 %collective-permute-done.8 = bf16[1,32,7680]{2,1,0:T(8,128)(2,1)S(1)} collective-permute-done((bf16[1,32,7680]{2,1,0:T(8,128)(2,1)S(1)}, bf16[1,32,7680]{2,1,0:T(8,128)(2,1)S(1)}, u32[]{:S(2)}, u32[]{:S(2)}) %collective-permute-start.8) | collective-permute-done | bytes 491552 | tf_op jit(solution)/shard_map/ppermute | solution.py:345
  70.3 8.5 %collective-permute-done.9 = bf16[1,32,7680]{2,1,0:T(8,128)(2,1)S(1)} collective-permute-done((bf16[1,32,7680]{2,1,0:T(8,128)(2,1)}, bf16[1,32,7680]{2,1,0:T(8,128)(2,1)S(1)}, u32[]{:S(2)}, u32[]{:S(2)}) %collective-permute-start.9) | collective-permute-done | bytes 491552 | tf_op jit(solution)/shard_map/ppermute | solution.py:345
  78.8 1.5 convolution_bitcast_fusion.refs_1_.refs_3_
  80.3 5.0 %attend.1 = (bf16[4,2,32,512]{3,2,1,0:T(8,128)(2,1)S(1)}, bf16[2,2,1024,128]{3,2,1,0:T(8,128)(2,1)S(1)}, bf16[2,2,128,128]{3,2,1,0:T(8,128)(2,1)S(1)}) custom-call(s32[2]{0:T(128)S(1)} %copy-done.9, s32[2]{0:T(128)S(1)} %copy-done.10, s32[4]{0:T(128)S(1)} %and_select_fusion.owners, f32[3,2,32,512]{3,2,1,0:T(8,128)S(1)} %bitcast.39, ...), custom_call_target="tpu_custom_call" | custom-call | tf_op jit(solution)/shard_map/attend/pallas_call | solution.py:141
  85.4 3.1 %terms.3 = (bf16[1,32,7680]{2,1,0:T(8,128)(2,1)S(1)}, bf16[1,32,7680]{2,1,0:T(8,128)(2,1)S(1)}) custom-call(bf16[1,2,32,512]{3,2,1,0:T(8,128)(2,1)S(1)} %slice.44.rows, bf16[7680,512]{1,0:T(8,128)(2,1)S(1)} %bitcast.37), custom_call_target="tpu_custom_call" | custom-call | tf_op jit(solution)/shard_map/terms/pallas_call | solution.py:232
  88.5 2.5 %convolution_convert_fusion = bf16[7680,512]{1,0:T(8,128)(2,1)S(1)} fusion(bf16[256,512]{1,0:T(8,128)(2,1)S(1)} %bitcast.41, bf16[64,7680]{1,0:T(8,128)(2,1)S(1)} %bitcast.44, bf16[192,7680]{1,0:T(8,128)(2,1)S(1)} %bitcast.46), kind=kOutput, calls=%fused_computation | convolution fusion | flops 2025062400 | bytes 12058624 | tf_op jit(solution)/shard_map/dot_general | solution.py:29
  91.0 0.3 dynamic-slice_bitcast_fusion
  91.4 2.2 %collective-permute-start.10 = (bf16[1,32,7680]{2,1,0:T(8,128)(2,1)S(1)}, bf16[1,32,7680]{2,1,0:T(8,128)(2,1)S(1)}, u32[]{:S(2)}, u32[]{:S(2)}) collective-permute-start(bf16[1,32,7680]{2,1,0:T(8,128)(2,1)S(1)} %get-tuple-element.61), channel_id=1, source_target_pairs={{0,1},{1,2},{2,3},{3,0},{4,5},{5,6},{6,7},{7,4},{8,9},{9,10},{10,1... | collective-permute-start | bytes 1474568 | tf_op jit(solution)/shard_map/ppermute | solution.py:345
  93.6 1.7 collective-permute-start.11
  95.3 3.5 %terms.2 = (bf16[2,32,7680]{2,1,0:T(8,128)(2,1)S(1)}, bf16[2,32,7680]{2,1,0:T(8,128)(2,1)S(1)}, bf16[2,32,7680]{2,1,0:T(8,128)(2,1)S(1)}) custom-call(bf16[3,2,32,512]{3,2,1,0:T(8,128)(2,1)S(1)} %slice.42.rows, bf16[7680,512]{1,0:T(8,128)(2,1)S(1)} %bitcast.38), custom_call_target="tpu_custom_call" | custom-call | tf_op jit(solution)/shard_map/terms/pallas_call | solution.py:232
  98.9 0.9 copy-done.7
  99.8 2.8 %merge.1 = (bf16[960,512]{1,0:T(8,128)(2,1)}, bf16[960,512]{1,0:T(8,128)(2,1)}, bf16[960,512]{1,0:T(8,128)(2,1)}) custom-call(s32[2]{0:T(128)S(1)} %pad_add_fusion.place, bf16[4,2,960,512]{3,2,1,0:T(8,128)(2,1)S(1)} %bitcast.31, bf16[4,2,960,512]{3,2,1,0:T(8,128)(2,1)S(1)} %bitcast.32, bf16[4,2,960,512]{3,2,1,0:T(8,128)(2,1)S(1)} %bitcast.33, ...), custom_call_target="tpu_custom_call" | custom-call | tf_op jit(solution)/shard_map/merge/pallas_call | solution.py:286
  102.6 4.7 %collective-permute-done.10 = bf16[1,32,7680]{2,1,0:T(8,128)(2,1)S(1)} collective-permute-done((bf16[1,32,7680]{2,1,0:T(8,128)(2,1)S(1)}, bf16[1,32,7680]{2,1,0:T(8,128)(2,1)S(1)}, u32[]{:S(2)}, u32[]{:S(2)}) %collective-permute-start.10) | collective-permute-done | bytes 491552 | tf_op jit(solution)/shard_map/ppermute | solution.py:345
  107.3 10.0 %collective-permute-done.11 = bf16[1,32,7680]{2,1,0:T(8,128)(2,1)S(1)} collective-permute-done((bf16[1,32,7680]{2,1,0:T(8,128)(2,1)S(1)}, bf16[1,32,7680]{2,1,0:T(8,128)(2,1)S(1)}, u32[]{:S(2)}, u32[]{:S(2)}) %collective-permute-start.11) | collective-permute-done | bytes 491552 | tf_op jit(solution)/shard_map/ppermute | solution.py:345
  117.5 1.0 pad_maximum_fusion.2
  118.6 1.0 pad_maximum_fusion.3
  119.6 0.6 collective-permute-start.13
  120.2 3.3 %collective-permute-start.14 = (bf16[2,32,7680]{2,1,0:T(8,128)(2,1)}, bf16[2,32,7680]{2,1,0:T(8,128)(2,1)}, u32[]{:S(2)}, u32[]{:S(2)}) collective-permute-start(bf16[2,32,7680]{2,1,0:T(8,128)(2,1)} %pad_maximum_fusion.3), channel_id=1, source_target_pairs={{0,3},{1,0},{2,1},{3,2},{4,7},{5,4},{6,5},{7,6},{8,11},{9,8},{10,9... | collective-permute-start | bytes 2949128 | tf_op jit(solution)/shard_map/ppermute | solution.py:345
  123.4 1.2 collective-permute-start.15
  124.6 0.9 collective-permute-start.16
  125.6 1.4 collective-permute-start.17
  126.9 4.3 %after.1 = bf16[2,128,2048]{2,1,0:T(8,128)(2,1)} custom-call(bf16[2,128,2048]{2,1,0:T(8,128)(2,1)} %query.3, bf16[2,2,1024,128]{3,2,1,0:T(8,128)(2,1)} %copy-done.4, bf16[2,2,128,128]{3,2,1,0:T(8,128)(2,1)} %copy-done.8, f32[1,128]{1,0:T(1,128)} %bitcast.51), custom_call_target="tpu_custom_call" | custom-call | tf_op jit(solution)/shard_map/after/pallas_call | solution.py:189
  131.2 15.1 %collective-permute-done.13 = bf16[2,32,7680]{2,1,0:T(8,128)(2,1)} collective-permute-done((bf16[2,32,7680]{2,1,0:T(8,128)(2,1)}, bf16[2,32,7680]{2,1,0:T(8,128)(2,1)}, u32[]{:S(2)}, u32[]{:S(2)}) %collective-permute-start.13) | collective-permute-done | bytes 983072 | tf_op jit(solution)/shard_map/ppermute | solution.py:345
  146.4 18.6 %collective-permute-done.14 = bf16[2,32,7680]{2,1,0:T(8,128)(2,1)} collective-permute-done((bf16[2,32,7680]{2,1,0:T(8,128)(2,1)}, bf16[2,32,7680]{2,1,0:T(8,128)(2,1)}, u32[]{:S(2)}, u32[]{:S(2)}) %collective-permute-start.14) | collective-permute-done | bytes 983072 | tf_op jit(solution)/shard_map/ppermute | solution.py:345
  165.0 3.1 %add_convert_fusion = bf16[2,32,7680]{2,1,0:T(8,128)(2,1)} fusion(bf16[2,32,7680]{2,1,0:T(8,128)(2,1)} %collective-permute-done.14, bf16[2,32,7680]{2,1,0:T(8,128)(2,1)} %collective-permute-done.13, bf16[2,32,7680]{2,1,0:T(8,128)(2,1)} %copy-done.7), kind=kLoop, calls=%fused_computation.7 | loop fusion | flops 2949120 | bytes 3932160 | tf_op jit(solution)/shard_map/convert_element_type | solution.py:422
  168.1 0.8 collective-permute-done.17.refs_2_
  168.8 3.2 %copy-done.1 = bf16[7680,512]{1,0:T(8,128)(2,1)S(1)} copy-done((bf16[7680,512]{1,0:T(8,128)(2,1)S(1)}, bf16[7680,512]{1,0:T(8,128)(2,1)}, u32[]{:S(2)}) %copy-start.1) | copy-done | bytes 7864344
  172.1 2.1 %copy-done.3 = bf16[4,960,512]{2,1,0:T(8,128)(2,1)S(1)} copy-done((bf16[4,960,512]{2,1,0:T(8,128)(2,1)S(1)}, bf16[4,960,512]{2,1,0:T(8,128)(2,1)}, u32[]{:S(2)}) %copy-start.3) | copy-done | bytes 3932184
  174.2 2.1 %finish.1 = (f32[960,256]{1,0:T(8,128)}, f32[960,256]{1,0:T(8,128)}) custom-call(s32[2]{0:T(128)S(1)} %pad_add_fusion.place, bf16[4,2,960,512]{3,2,1,0:T(8,128)(2,1)S(1)} %bitcast.34, bf16[4,960,512]{2,1,0:T(8,128)(2,1)S(1)} %copy-done.3, bf16[960,512]{1,0:T(8,128)(2,1)S(1)} %collective-permute-done.15.refs_0_, ...), custom_call_target="tpu_custom_call" | custom-call | tf_op jit(solution)/shard_map/finish/pallas_call | solution.py:304
  (61 shorter events, 1.4 us)
Async XLA Ops:
  0.6 53.1 %copy-start.17 = (s32[4]{0:T(128)S(1)}, s32[4]{0:T(128)}, u32[]{:S(2)}) copy-start(s32[4]{0:T(128)} %constant.61.clone) | copy-start | bytes 52
  0.6 48.3 %collective-permute-start.1 = (bf16[2,32,7680]{2,1,0:T(8,128)(2,1)}, bf16[2,32,7680]{2,1,0:T(8,128)(2,1)S(1)}, u32[]{:S(2)}, u32[]{:S(2)}) collective-permute-start(bf16[2,32,7680]{2,1,0:T(8,128)(2,1)} %param.13), channel_id=1, source_target_pairs={{0,3},{1,0},{2,1},{3,2},{4,7},{5,4},{6,5},{7,6},{8,11},{9,8},{10,9... | collective-permute-start | bytes 2949128 | tf_op jit(solution)/shard_map/ppermute | solution.py:345
  5.7 43.2 %collective-permute-start = (bf16[2,32,7680]{2,1,0:T(8,128)(2,1)}, bf16[2,32,7680]{2,1,0:T(8,128)(2,1)S(1)}, u32[]{:S(2)}, u32[]{:S(2)}) collective-permute-start(bf16[2,32,7680]{2,1,0:T(8,128)(2,1)} %param.13), channel_id=1, source_target_pairs={{0,1},{1,2},{2,3},{3,0},{4,5},{5,6},{6,7},{7,4},{8,9},{9,10},{10,1... | collective-permute-start | bytes 2949128 | tf_op jit(solution)/shard_map/ppermute | solution.py:345
  7.9 42.0 %collective-permute-start.2 = (bf16[960,512]{1,0:T(8,128)(2,1)}, bf16[960,512]{1,0:T(8,128)(2,1)}, u32[]{:S(2)}, u32[]{:S(2)}) collective-permute-start(bf16[960,512]{1,0:T(8,128)(2,1)} %beside.1), channel_id=1, source_target_pairs={{0,8},{4,12},{8,0},{12,4},{16,24},{20,28},{24,16},{28,20},{1,9},{5... | collective-permute-start | bytes 2949128 | tf_op jit(solution)/shard_map/ppermute | solution.py:348
  9.4 44.3 %collective-permute-start.3 = (bf16[960,512]{1,0:T(8,128)(2,1)}, bf16[960,512]{1,0:T(8,128)(2,1)}, u32[]{:S(2)}, u32[]{:S(2)}) collective-permute-start(bf16[960,512]{1,0:T(8,128)(2,1)} %beside.1), channel_id=1, source_target_pairs={{0,16},{4,20},{8,24},{12,28},{16,0},{20,4},{24,8},{28,12},{1,17},{... | collective-permute-start | bytes 2949128 | tf_op jit(solution)/shard_map/ppermute | solution.py:348
  11.0 42.8 %collective-permute-start.4 = (bf16[960,512]{1,0:T(8,128)(2,1)}, bf16[960,512]{1,0:T(8,128)(2,1)}, u32[]{:S(2)}, u32[]{:S(2)}) collective-permute-start(bf16[960,512]{1,0:T(8,128)(2,1)} %beside.1), channel_id=1, source_target_pairs={{0,24},{4,28},{8,16},{12,20},{16,8},{20,12},{24,0},{28,4},{1,25},{... | collective-permute-start | bytes 2949128 | tf_op jit(solution)/shard_map/ppermute | solution.py:348
  48.9 1.1 copy-start.14
  53.8 5.8 %collective-permute-start.5 = (bf16[2,960,512]{2,1,0:T(8,128)(2,1)S(1)}, bf16[2,960,512]{2,1,0:T(8,128)(2,1)}, u32[]{:S(2)}, u32[]{:S(2)}) collective-permute-start(bf16[2,960,512]{2,1,0:T(8,128)(2,1)S(1)} %pad_maximum_fusion.1), channel_id=1, source_target_pairs={{0,4},{4,0},{8,12},{12,8},{16,20},{20,16},{24,28},{28,24},{1,5},{5... | collective-permute-start | bytes 5898248 | tf_op jit(solution)/shard_map/ppermute | solution.py:348
  53.8 5.3 %copy-start.15 = (bf16[2,32,7680]{2,1,0:T(8,128)(2,1)S(1)}, bf16[2,32,7680]{2,1,0:T(8,128)(2,1)}, u32[]{:S(2)}) copy-start(bf16[2,32,7680]{2,1,0:T(8,128)(2,1)} %copy-done.14) | copy-start | bytes 2949124
  53.8 5.3 %copy-start.16 = (bf16[2,32,7680]{2,1,0:T(8,128)(2,1)S(1)}, bf16[2,32,7680]{2,1,0:T(8,128)(2,1)}, u32[]{:S(2)}) copy-start(bf16[2,32,7680]{2,1,0:T(8,128)(2,1)} %param.13) | copy-start | bytes 2949124
  53.8 10.5 %collective-permute-start.6 = (bf16[1,960,512]{2,1,0:T(8,128)(2,1)}, bf16[1,960,512]{2,1,0:T(8,128)(2,1)S(1)}, u32[]{:S(2)}, u32[]{:S(2)}) collective-permute-start(bf16[1,960,512]{2,1,0:T(8,128)(2,1)} %bitcast.7), channel_id=1, source_target_pairs={{0,4},{4,0},{8,12},{12,8},{16,20},{20,16},{24,28},{28,24},{1,5},{5... | collective-permute-start | bytes 2949128 | tf_op jit(solution)/shard_map/ppermute | solution.py:348
  54.4 11.3 %collective-permute-start.7 = (bf16[1,960,512]{2,1,0:T(8,128)(2,1)}, bf16[1,960,512]{2,1,0:T(8,128)(2,1)S(1)}, u32[]{:S(2)}, u32[]{:S(2)}) collective-permute-start(bf16[1,960,512]{2,1,0:T(8,128)(2,1)} %bitcast.8), channel_id=1, source_target_pairs={{0,4},{4,0},{8,12},{12,8},{16,20},{20,16},{24,28},{28,24},{1,5},{5... | collective-permute-start | bytes 2949128 | tf_op jit(solution)/shard_map/ppermute | solution.py:348
  54.4 15.9 %collective-permute-start.8 = (bf16[1,32,7680]{2,1,0:T(8,128)(2,1)S(1)}, bf16[1,32,7680]{2,1,0:T(8,128)(2,1)S(1)}, u32[]{:S(2)}, u32[]{:S(2)}) collective-permute-start(bf16[1,32,7680]{2,1,0:T(8,128)(2,1)S(1)} %slice.48), channel_id=1, source_target_pairs={{0,1},{1,2},{2,3},{3,0},{4,5},{5,6},{6,7},{7,4},{8,9},{9,10},{10,1... | collective-permute-start | bytes 1474568 | tf_op jit(solution)/shard_map/ppermute | solution.py:345
  54.4 24.3 %collective-permute-start.9 = (bf16[1,32,7680]{2,1,0:T(8,128)(2,1)}, bf16[1,32,7680]{2,1,0:T(8,128)(2,1)S(1)}, u32[]{:S(2)}, u32[]{:S(2)}) collective-permute-start(bf16[1,32,7680]{2,1,0:T(8,128)(2,1)} %slice.49), channel_id=1, source_target_pairs={{0,3},{1,0},{2,1},{3,2},{4,7},{5,4},{6,5},{7,6},{8,11},{9,8},{10,9... | collective-permute-start | bytes 1474568 | tf_op jit(solution)/shard_map/ppermute | solution.py:345
  59.4 6.4 %copy-start.12 = (bf16[3,2,32,7680]{3,2,1,0:T(8,128)(2,1)}, bf16[3,2,32,7680]{3,2,1,0:T(8,128)(2,1)S(1)}, u32[]{:S(2)}) copy-start(bf16[3,2,32,7680]{3,2,1,0:T(8,128)(2,1)S(1)} %pad_maximum_fusion) | copy-start | bytes 8847364
  67.5 12.8 %copy-start.5 = (bf16[2,2,1024,128]{3,2,1,0:T(8,128)(2,1)S(1)}, bf16[2,2,1024,128]{3,2,1,0:T(8,128)(2,1)}, u32[]{:S(2)}) copy-start(bf16[2,2,1024,128]{3,2,1,0:T(8,128)(2,1)} %get-tuple-element.57.refs_4_) | copy-start | bytes 3145732
  67.5 12.8 %copy-start.6 = (bf16[2,2,1024,128]{3,2,1,0:T(8,128)(2,1)S(1)}, bf16[2,2,1024,128]{3,2,1,0:T(8,128)(2,1)}, u32[]{:S(2)}) copy-start(bf16[2,2,1024,128]{3,2,1,0:T(8,128)(2,1)} %get-tuple-element.58.refs_5_) | copy-start | bytes 3145732
  67.5 12.8 %copy-start.9 = (s32[2]{0:T(128)S(1)}, s32[2]{0:T(128)}, u32[]{:S(2)}) copy-start(s32[2]{0:T(128)} %assignment.1) | copy-start | bytes 28
  67.5 12.8 %copy-start.10 = (s32[2]{0:T(128)S(1)}, s32[2]{0:T(128)}, u32[]{:S(2)}) copy-start(s32[2]{0:T(128)} %tiles.1) | copy-start | bytes 28
  67.5 12.8 %copy-start.11 = (f32[128]{0:T(128)S(1)}, f32[128]{0:T(128)}, u32[]{:S(2)}) copy-start(f32[128]{0:T(128)} %param.17) | copy-start | bytes 1540
  80.3 8.2 %copy-start.13 = (bf16[3,2,32,7680]{3,2,1,0:T(8,128)(2,1)S(1)}, bf16[3,2,32,7680]{3,2,1,0:T(8,128)(2,1)}, u32[]{:S(2)}) copy-start(bf16[3,2,32,7680]{3,2,1,0:T(8,128)(2,1)} %copy-done.12) | copy-start | bytes 8847364
  85.3 3.1 %copy-start.4 = (bf16[2,2,1024,128]{3,2,1,0:T(8,128)(2,1)}, bf16[2,2,1024,128]{3,2,1,0:T(8,128)(2,1)S(1)}, u32[]{:S(2)}) copy-start(bf16[2,2,1024,128]{3,2,1,0:T(8,128)(2,1)S(1)} %get-tuple-element.73.score_grad) | copy-start | bytes 3145732
  85.4 3.1 %copy-start.8 = (bf16[2,2,128,128]{3,2,1,0:T(8,128)(2,1)}, bf16[2,2,128,128]{3,2,1,0:T(8,128)(2,1)S(1)}, u32[]{:S(2)}) copy-start(bf16[2,2,128,128]{3,2,1,0:T(8,128)(2,1)S(1)} %get-tuple-element.74.keys) | copy-start | bytes 393220
  91.0 8.8 %copy-start = (bf16[7680,512]{1,0:T(8,128)(2,1)}, bf16[7680,512]{1,0:T(8,128)(2,1)S(1)}, u32[]{:S(2)}) copy-start(bf16[7680,512]{1,0:T(8,128)(2,1)S(1)} %convolution_convert_fusion) | copy-start | bytes 23592964
  91.3 8.5 %collective-permute-start.12 = (bf16[4,960,512]{2,1,0:T(8,128)(2,1)S(1)}, bf16[4,960,512]{2,1,0:T(8,128)(2,1)S(1)}, u32[]{:S(2)}, u32[]{:S(2)}) collective-permute-start(bf16[4,960,512]{2,1,0:T(8,128)(2,1)S(1)} %dynamic-slice_bitcast_fusion), channel_id=1, source_target_pairs={{0,4},{4,0},{8,12},{12,8},{16,20},{20,16},{24,28},{28,24},{1,5},{5... | collective-permute-start | bytes 11796488 | tf_op jit(solution)/shard_map/ppermute | solution.py:348
  91.4 15.9 %collective-permute-start.10 = (bf16[1,32,7680]{2,1,0:T(8,128)(2,1)S(1)}, bf16[1,32,7680]{2,1,0:T(8,128)(2,1)S(1)}, u32[]{:S(2)}, u32[]{:S(2)}) collective-permute-start(bf16[1,32,7680]{2,1,0:T(8,128)(2,1)S(1)} %get-tuple-element.61), channel_id=1, source_target_pairs={{0,1},{1,2},{2,3},{3,0},{4,5},{5,6},{6,7},{7,4},{8,9},{9,10},{10,1... | collective-permute-start | bytes 1474568 | tf_op jit(solution)/shard_map/ppermute | solution.py:345
  93.6 23.8 %collective-permute-start.11 = (bf16[1,32,7680]{2,1,0:T(8,128)(2,1)S(1)}, bf16[1,32,7680]{2,1,0:T(8,128)(2,1)S(1)}, u32[]{:S(2)}, u32[]{:S(2)}) collective-permute-start(bf16[1,32,7680]{2,1,0:T(8,128)(2,1)S(1)} %get-tuple-element.62), channel_id=1, source_target_pairs={{0,3},{1,0},{2,1},{3,2},{4,7},{5,4},{6,5},{7,6},{8,11},{9,8},{10,9... | collective-permute-start | bytes 1474568 | tf_op jit(solution)/shard_map/ppermute | solution.py:345
  98.8 0.9 copy-start.7
  99.8 2.8 %copy-start.2 = (bf16[4,960,512]{2,1,0:T(8,128)(2,1)}, bf16[4,960,512]{2,1,0:T(8,128)(2,1)S(1)}, u32[]{:S(2)}) copy-start(bf16[4,960,512]{2,1,0:T(8,128)(2,1)S(1)} %collective-permute-done.12.refs_3_.refs_4_.refs_5_.given) | copy-start | bytes 11796484
  119.6 26.8 %collective-permute-start.13 = (bf16[2,32,7680]{2,1,0:T(8,128)(2,1)}, bf16[2,32,7680]{2,1,0:T(8,128)(2,1)}, u32[]{:S(2)}, u32[]{:S(2)}) collective-permute-start(bf16[2,32,7680]{2,1,0:T(8,128)(2,1)} %pad_maximum_fusion.2), channel_id=1, source_target_pairs={{0,1},{1,2},{2,3},{3,0},{4,5},{5,6},{6,7},{7,4},{8,9},{9,10},{10,1... | collective-permute-start | bytes 2949128 | tf_op jit(solution)/shard_map/ppermute | solution.py:345
  120.2 44.8 %collective-permute-start.14 = (bf16[2,32,7680]{2,1,0:T(8,128)(2,1)}, bf16[2,32,7680]{2,1,0:T(8,128)(2,1)}, u32[]{:S(2)}, u32[]{:S(2)}) collective-permute-start(bf16[2,32,7680]{2,1,0:T(8,128)(2,1)} %pad_maximum_fusion.3), channel_id=1, source_target_pairs={{0,3},{1,0},{2,1},{3,2},{4,7},{5,4},{6,5},{7,6},{8,11},{9,8},{10,9... | collective-permute-start | bytes 2949128 | tf_op jit(solution)/shard_map/ppermute | solution.py:345
  123.4 44.6 %collective-permute-start.15 = (bf16[960,512]{1,0:T(8,128)(2,1)}, bf16[960,512]{1,0:T(8,128)(2,1)S(1)}, u32[]{:S(2)}, u32[]{:S(2)}) collective-permute-start(bf16[960,512]{1,0:T(8,128)(2,1)} %get-tuple-element.79), channel_id=1, source_target_pairs={{0,8},{4,12},{8,0},{12,4},{16,24},{20,28},{24,16},{28,20},{1,9},{5... | collective-permute-start | bytes 2949128 | tf_op jit(solution)/shard_map/ppermute | solution.py:348
  124.6 43.4 %collective-permute-start.16 = (bf16[960,512]{1,0:T(8,128)(2,1)}, bf16[960,512]{1,0:T(8,128)(2,1)S(1)}, u32[]{:S(2)}, u32[]{:S(2)}) collective-permute-start(bf16[960,512]{1,0:T(8,128)(2,1)} %get-tuple-element.80), channel_id=1, source_target_pairs={{0,16},{4,20},{8,24},{12,28},{16,0},{20,4},{24,8},{28,12},{1,17},{... | collective-permute-start | bytes 2949128 | tf_op jit(solution)/shard_map/ppermute | solution.py:348
  125.6 43.3 %collective-permute-start.17 = (bf16[960,512]{1,0:T(8,128)(2,1)}, bf16[960,512]{1,0:T(8,128)(2,1)S(1)}, u32[]{:S(2)}, u32[]{:S(2)}) collective-permute-start(bf16[960,512]{1,0:T(8,128)(2,1)} %get-tuple-element.81), channel_id=1, source_target_pairs={{0,24},{4,28},{8,16},{12,20},{16,8},{20,12},{24,0},{28,4},{1,25},{... | collective-permute-start | bytes 2949128 | tf_op jit(solution)/shard_map/ppermute | solution.py:348
  168.8 3.2 %copy-start.1 = (bf16[7680,512]{1,0:T(8,128)(2,1)S(1)}, bf16[7680,512]{1,0:T(8,128)(2,1)}, u32[]{:S(2)}) copy-start(bf16[7680,512]{1,0:T(8,128)(2,1)} %copy-done) | copy-start | bytes 23592964
  172.0 2.1 %copy-start.3 = (bf16[4,960,512]{2,1,0:T(8,128)(2,1)S(1)}, bf16[4,960,512]{2,1,0:T(8,128)(2,1)}, u32[]{:S(2)}) copy-start(bf16[4,960,512]{2,1,0:T(8,128)(2,1)} %copy-done.2) | copy-start | bytes 11796484

commit v10 on v9

--- a/solution.py
+++ b/solution.py
@@ -247,19 +247,16 @@
     )(rows, weight)
 
 
-def pair_sum(held, given):
-    return held[0, 0].astype(jnp.float32) + given[0].astype(jnp.float32)
-
-
 def merge_kernel(place, *refs):
     count = len(refs) // 3
     for held, given, out in zip(refs[:count], refs[count : 2 * count], refs[2 * count :]):
-        out[...] = pair_sum(held, given).astype(out.dtype)
-
-
-def finish_kernel(place, held, given, *refs):
+        total = held[0, 0].astype(jnp.float32) + given[0].astype(jnp.float32)
+        out[...] = total.astype(out.dtype)
+
+
+def finish_kernel(own, *refs):
     *sent, key_out, value_out = refs
-    total = pair_sum(held, given)
+    total = own[...]
     for piece in sent:
         total = total + piece[...].astype(jnp.float32)
     cut = key_out.shape[1]
@@ -282,10 +279,11 @@
 
 def merge(held, given, place):
     pairs, _, own_width, cols = held.shape
-    specs = [held_specs(own_width, cols, 2, r) for r in range(1, pairs)]
+    specs = [held_specs(own_width, cols, 2, r) for r in range(pairs)]
+    kinds = [jnp.float32] + [jnp.bfloat16] * (pairs - 1)
     return pl.pallas_call(
         merge_kernel,
-        out_shape=[jax.ShapeDtypeStruct((own_width, cols), jnp.bfloat16)] * len(specs),
+        out_shape=[jax.ShapeDtypeStruct((own_width, cols), kind) for kind in kinds],
         grid_spec=pltpu.PrefetchScalarGridSpec(
             num_scalar_prefetch=1,
             grid=(2,),
@@ -297,23 +295,19 @@
     )(place, *[held] * len(specs), *[given] * len(specs))
 
 
-def finish(held, given, sent, place):
-    _, _, own_width, cols = held.shape
+def finish(own, sent):
+    own_width, cols = own.shape
     rows = own_width // 2
     half = jax.ShapeDtypeStruct((own_width, cols // 2), jnp.float32)
     return pl.pallas_call(
         finish_kernel,
         out_shape=(half, half),
-        grid_spec=pltpu.PrefetchScalarGridSpec(
-            num_scalar_prefetch=1,
-            grid=(2,),
-            in_specs=[*held_specs(own_width, cols, 2, 0)]
-            + [pl.BlockSpec((rows, cols), lambda i, _: (i, 0))] * len(sent),
-            out_specs=[pl.BlockSpec((rows, cols // 2), lambda i, _: (i, 0))] * 2,
-        ),
+        grid=(2,),
+        in_specs=[pl.BlockSpec((rows, cols), lambda i: (i, 0))] * (1 + len(sent)),
+        out_specs=[pl.BlockSpec((rows, cols // 2), lambda i: (i, 0))] * 2,
         compiler_params=pltpu.CompilerParams(vmem_limit_bytes=32 * 1024 * 1024),
         name="finish",
-    )(place, held, given, *sent)
+    )(own, *sent)
 
 
 def per_device(
@@ -388,31 +382,32 @@
     wholes = tuple((part, 0, img_count) for part in range(3))
     own, to_left, to_right = terms(rows[:3], weight, wholes, 4)
 
-    right_half, left_half = ring(leaving_right, 1), ring(leaving_left, -1)
+    right_half, left_half = lax.optimization_barrier(
+        (ring(leaving_right, 1), ring(leaving_left, -1))
+    )
+
+    def added(held, half):
+        return (held.astype(jnp.float32) + half.astype(jnp.float32)).astype(jnp.bfloat16)
+
+    to_right = jnp.concatenate((added(to_right[:first], right_half), to_right[first:]))
+    to_left = jnp.concatenate((to_left[:first], added(to_left[first:], left_half)))
+    to_right, to_left = lax.optimization_barrier((to_right, to_left))
+    from_left, from_right = ring(to_right, 1), ring(to_left, -1)
 
     if pairs != 4:
         all_images = jnp.concatenate((near, far))
         weight_part = dot(all_images, rows.reshape(-1, cols), 0, 0)
         weight_grad = lax.psum_scatter(weight_part, "dp", scatter_dimension=0, tiled=True)
     else:
-        held_rows, leaving_right, leaving_left = lax.optimization_barrier(
-            (rows, leaving_right, leaving_left)
-        )
         all_images = jnp.concatenate((near, far))
-        weight_part = dot(all_images, held_rows.reshape(-1, cols), 0, 0)
+        weight_part = dot(all_images, rows.reshape(-1, cols), 0, 0)
         weight_part = weight_part.astype(jnp.bfloat16).reshape(pairs, 2, own_width, cols)
         given = swap(lax.dynamic_index_in_dim(weight_part, 1 - core, 1, keepdims=False), 1)
-        where = jnp.stack((core, pair))
-        sent = merge(weight_part, given, where)
-        right_half, left_half, sent = lax.optimization_barrier((right_half, left_half, sent))
-
-    def added(held, half):
-        return (held.astype(jnp.float32) + half.astype(jnp.float32)).astype(jnp.bfloat16)
-
-    to_right = jnp.concatenate((added(to_right[:first], right_half), to_right[first:]))
-    to_left = jnp.concatenate((to_left[:first], added(to_left[first:], left_half)))
-    to_right, to_left, score_grad = lax.optimization_barrier((to_right, to_left, score_grad))
-    from_left, from_right = ring(to_right, 1), ring(to_left, -1)
+        given, to_right, to_left, score_grad = lax.optimization_barrier(
+            (given, to_right, to_left, score_grad)
+        )
+        own_sum, *sent = merge(weight_part, given, jnp.stack((core, pair)))
+        sent = [swap(piece, 2 * r) for r, piece in enumerate(sent, 1)]
     query_grad = after(queries, score_grad, seq_keys, query_gain)
     from_left, from_right, query_grad = lax.optimization_barrier(
         (from_left, from_right, query_grad)
@@ -421,9 +416,8 @@
         own.astype(jnp.float32) + from_left.astype(jnp.float32) + from_right.astype(jnp.float32)
     ).astype(jnp.bfloat16)
     if pairs == 4:
-        sent = [swap(piece, 2 * r) for r, piece in enumerate(sent, 1)]
         image_grad, sent = lax.optimization_barrier((image_grad, sent))
-        return (query_grad, image_grad, *finish(weight_part, given, sent, where))
+        return (query_grad, image_grad, *finish(own_sum, sent))
     return (query_grad, image_grad, weight_grad[:, :key_cols], weight_grad[:, key_cols:])
 
 

time: 177 us -> 169 us (0.955)
  local copies, waits for them, and re-layouts: 14.8 us -> 9.34 us
  waiting for transfers between devices: 95.3 us -> 92.5 us
    unnamed x37 -> x31, local copies, waits for them, and re-layouts: 6.47 us -> 1.05 us
    ppermute x8, waiting for transfers between devices: 92.3 us -> 88.3 us  [ring(): lax.ppermute(value, 'mp', [(i, (i + step) % mp_size) for i in range(mp_si...]
  transfers between devices with their start and end apart: 18 -> 18, of which waited for: 10 -> 12; matrix products, arithmetic and copies ran while one was open for 8% -> 12% of each run, Pallas kernels for 10% -> 10%
where the time goes in v10:
time: 169 us; the launch traced here: 168 us
  waiting for transfers between devices  92.5 us (55%)
  Pallas kernels  28.1 us (17%)
  starting transfers between devices  24.4 us (14%)
  local copies, waits for them, and re-layouts  9.34 us (6%)
  other arithmetic  7.46 us (4%)
  matrix products  5.62 us (3%)
    ppermute x8, waiting for transfers between devices, ring(): lax.ppermute(value, 'mp', [(i, (i + step) % mp_size) for i in range(mp_si...  88.3 us
    ppermute x8, starting transfers between devices, ring(): lax.ppermute(value, 'mp', [(i, (i + step) % mp_size) for i in range(mp_si...  16.7 us
    ppermute x10, starting transfers between devices, swap(): return lax.ppermute(value, 'dp', [(i, i ^ mask) for i in range(dp_size)])  7.67 us
    pallas_call x2, Pallas kernels, terms(): pl.pallas_call(functools.partial(terms_kernel, splits), out_shape=[jax.Sh...  6.55 us
    dynamic_update_slice x8, local copies, waits for them, and re-layouts, per_device(): lax.dynamic_update_slice_in_dim(weight, source[k:k + 1], 2 * (pair ^ r +...  6.29 us
    dot_general x3, matrix products, dot(): lax.dot_general(left, right, (((left_dim,), (right_dim,)), ((), ())), pre...  5.62 us
    pallas_call x1, Pallas kernels, attend(): pl.pallas_call(functools.partial(attend_kernel, len(pieces)), out_shape=(...  5.01 us
    pallas_call x1, Pallas kernels, before(): pl.pallas_call(before_kernel, out_shape=(shape, shape), grid_spec=pltpu.P...  4.83 us
  transfers between devices with their start and end apart: 18, of which 12 were waited for; matrix products, arithmetic and copies ran while one was open for 12% of the time, Pallas kernels for 10%

profile of v10, /device:TPU:0, one launch (start us, length us, event | category | flops | bytes accessed | tf_op | source)
XLA Modules:
  0.0 168.4 jit_solution(2409821105590093481)
XLA Ops:
  0.6 3.1 %collective-permute-start = (bf16[2,32,7680]{2,1,0:T(8,128)(2,1)}, bf16[2,32,7680]{2,1,0:T(8,128)(2,1)S(1)}, u32[]{:S(2)}, u32[]{:S(2)}) collective-permute-start(bf16[2,32,7680]{2,1,0:T(8,128)(2,1)} %param.13), channel_id=1, source_target_pairs={{0,1},{1,2},{2,3},{3,0},{4,5},{5,6},{6,7},{7,4},{8,9},{9,10},{10,1... | collective-permute-start | bytes 2949128 | tf_op jit(solution)/shard_map/ppermute | solution.py:339
  3.7 2.1 %collective-permute-start.1 = (bf16[2,32,7680]{2,1,0:T(8,128)(2,1)}, bf16[2,32,7680]{2,1,0:T(8,128)(2,1)S(1)}, u32[]{:S(2)}, u32[]{:S(2)}) collective-permute-start(bf16[2,32,7680]{2,1,0:T(8,128)(2,1)} %param.13), channel_id=1, source_target_pairs={{0,3},{1,0},{2,1},{3,2},{4,7},{5,4},{6,5},{7,6},{8,11},{9,8},{10,9... | collective-permute-start | bytes 2949128 | tf_op jit(solution)/shard_map/ppermute | solution.py:339
  5.8 2.2 %beside.1 = bf16[960,512]{1,0:T(8,128)(2,1)} custom-call(bf16[960,256]{1,0:T(8,128)(2,1)} %left.1, bf16[960,256]{1,0:T(8,128)(2,1)} %right.1), custom_call_target="tpu_custom_call" | custom-call | tf_op jit(solution)/shard_map/beside/pallas_call | solution.py:212
  8.0 1.6 collective-permute-start.2
  9.7 1.5 collective-permute-start.3
  11.2 0.3 collective-permute-start.4
  11.5 4.8 %before.1 = (bf16[2,2,1024,128]{3,2,1,0:T(8,128)(2,1)}, bf16[2,2,1024,128]{3,2,1,0:T(8,128)(2,1)}) custom-call(s32[2]{0:T(128)} %lengths.1, bf16[2,128,2048]{2,1,0:T(8,128)(2,1)} %query.3, bf16[2,128,2048]{2,1,0:T(8,128)(2,1)} %grad.1, f32[1,128]{1,0:T(1,128)} %bitcast.51), custom_call_target="tpu_custom_call" | custom-call | tf_op jit(solution)/shard_map/before/pallas_call | solution.py:58
  16.3 12.3 %collective-permute-done = bf16[2,32,7680]{2,1,0:T(8,128)(2,1)S(1)} collective-permute-done((bf16[2,32,7680]{2,1,0:T(8,128)(2,1)}, bf16[2,32,7680]{2,1,0:T(8,128)(2,1)S(1)}, u32[]{:S(2)}, u32[]{:S(2)}) %collective-permute-start) | collective-permute-done | bytes 983072 | tf_op jit(solution)/shard_map/ppermute | solution.py:339
  28.6 19.6 %collective-permute-done.1 = bf16[2,32,7680]{2,1,0:T(8,128)(2,1)S(1)} collective-permute-done((bf16[2,32,7680]{2,1,0:T(8,128)(2,1)}, bf16[2,32,7680]{2,1,0:T(8,128)(2,1)S(1)}, u32[]{:S(2)}, u32[]{:S(2)}) %collective-permute-start.1) | collective-permute-done | bytes 983072 | tf_op jit(solution)/shard_map/ppermute | solution.py:339
  48.2 0.9 slice.49
  49.3 0.8 copy-done.13
  50.1 1.7 pad_maximum_fusion.1
  51.8 2.1 %collective-permute-done.3 = bf16[960,512]{1,0:T(8,128)(2,1)} collective-permute-done((bf16[960,512]{1,0:T(8,128)(2,1)}, bf16[960,512]{1,0:T(8,128)(2,1)}, u32[]{:S(2)}, u32[]{:S(2)}) %collective-permute-start.3) | collective-permute-done | bytes 983072 | tf_op jit(solution)/shard_map/ppermute | solution.py:342
  53.9 0.5 collective-permute-start.6
  54.5 3.8 %collective-permute-start.9 = (bf16[1,32,7680]{2,1,0:T(8,128)(2,1)}, bf16[1,32,7680]{2,1,0:T(8,128)(2,1)S(1)}, u32[]{:S(2)}, u32[]{:S(2)}) collective-permute-start(bf16[1,32,7680]{2,1,0:T(8,128)(2,1)} %slice.49), channel_id=1, source_target_pairs={{0,3},{1,0},{2,1},{3,2},{4,7},{5,4},{6,5},{7,6},{8,11},{9,8},{10,9... | collective-permute-start | bytes 1474568 | tf_op jit(solution)/shard_map/ppermute | solution.py:339
  58.3 0.7 broadcast_in_dim.16
  59.1 0.3 pad_maximum_fusion
  59.6 2.0 %slice_dynamic-update-slice_fusion.1 = bf16[8,960,512]{2,1,0:T(8,128)(2,1)S(1)} fusion(bf16[8,960,512]{2,1,0:T(8,128)(2,1)S(1)} %slice_dynamic-update-slice_fusion.3, s32[]{:T(128)S(6)} %select_n.49, bf16[2,960,512]{2,1,0:T(8,128)(2,1)} %collective-permute-done.5), kind=kLoop, calls=%fused_computation.10 | loop fusion | bytes 1966084 | tf_op jit(solution)/shard_map/dynamic_update_slice | solution.py:365
  61.7 1.3 slice_dynamic-update-slice_fusion
  63.0 1.3 constant_dynamic-update-slice_fusion.5
  64.4 1.3 constant_dynamic-update-slice_fusion.3
  65.9 1.7 fusion.5
  67.6 2.7 %collective-permute-done.8 = bf16[1,32,7680]{2,1,0:T(8,128)(2,1)S(1)} collective-permute-done((bf16[1,32,7680]{2,1,0:T(8,128)(2,1)S(1)}, bf16[1,32,7680]{2,1,0:T(8,128)(2,1)S(1)}, u32[]{:S(2)}, u32[]{:S(2)}) %collective-permute-start.8) | collective-permute-done | bytes 491552 | tf_op jit(solution)/shard_map/ppermute | solution.py:339
  70.4 8.4 %collective-permute-done.9 = bf16[1,32,7680]{2,1,0:T(8,128)(2,1)S(1)} collective-permute-done((bf16[1,32,7680]{2,1,0:T(8,128)(2,1)}, bf16[1,32,7680]{2,1,0:T(8,128)(2,1)S(1)}, u32[]{:S(2)}, u32[]{:S(2)}) %collective-permute-start.9) | collective-permute-done | bytes 491552 | tf_op jit(solution)/shard_map/ppermute | solution.py:339
  78.9 1.5 convolution_bitcast_fusion.refs_1_.refs_3_
  80.4 5.0 %attend.1 = (bf16[4,2,32,512]{3,2,1,0:T(8,128)(2,1)S(1)}, bf16[2,2,1024,128]{3,2,1,0:T(8,128)(2,1)S(1)}, bf16[2,2,128,128]{3,2,1,0:T(8,128)(2,1)S(1)}) custom-call(s32[2]{0:T(128)S(1)} %copy-done.5, s32[2]{0:T(128)S(1)} %copy-done.6, s32[4]{0:T(128)S(1)} %and_select_fusion.owners, f32[3,2,32,512]{3,2,1,0:T(8,128)S(1)} %bitcast.39, ...), custom_call_target="tpu_custom_call" | custom-call | tf_op jit(solution)/shard_map/attend/pallas_call | solution.py:141
  85.5 3.1 %terms.3 = (bf16[1,32,7680]{2,1,0:T(8,128)(2,1)S(1)}, bf16[1,32,7680]{2,1,0:T(8,128)(2,1)S(1)}) custom-call(bf16[1,2,32,512]{3,2,1,0:T(8,128)(2,1)S(1)} %slice.44.rows, bf16[7680,512]{1,0:T(8,128)(2,1)S(1)} %bitcast.37), custom_call_target="tpu_custom_call" | custom-call | tf_op jit(solution)/shard_map/terms/pallas_call | solution.py:232
  88.6 1.0 collective-permute-start.10
  89.6 2.9 %collective-permute-start.11 = (bf16[1,32,7680]{2,1,0:T(8,128)(2,1)S(1)}, bf16[1,32,7680]{2,1,0:T(8,128)(2,1)S(1)}, u32[]{:S(2)}, u32[]{:S(2)}) collective-permute-start(bf16[1,32,7680]{2,1,0:T(8,128)(2,1)S(1)} %get-tuple-element.60), channel_id=1, source_target_pairs={{0,3},{1,0},{2,1},{3,2},{4,7},{5,4},{6,5},{7,6},{8,11},{9,8},{10,9... | collective-permute-start | bytes 1474568 | tf_op jit(solution)/shard_map/ppermute | solution.py:339
  92.5 2.5 %convolution_convert_fusion = bf16[7680,512]{1,0:T(8,128)(2,1)S(1)} fusion(bf16[256,512]{1,0:T(8,128)(2,1)S(1)} %bitcast.41, bf16[64,7680]{1,0:T(8,128)(2,1)S(1)} %bitcast.44, bf16[192,7680]{1,0:T(8,128)(2,1)S(1)} %bitcast.46), kind=kOutput, calls=%fused_computation | convolution fusion | flops 2025062400 | bytes 12058624 | tf_op jit(solution)/shard_map/dot_general | solution.py:29
  95.3 3.5 %terms.2 = (bf16[2,32,7680]{2,1,0:T(8,128)(2,1)S(1)}, bf16[2,32,7680]{2,1,0:T(8,128)(2,1)S(1)}, bf16[2,32,7680]{2,1,0:T(8,128)(2,1)S(1)}) custom-call(bf16[3,2,32,512]{3,2,1,0:T(8,128)(2,1)S(1)} %slice.42.rows, bf16[7680,512]{1,0:T(8,128)(2,1)S(1)} %bitcast.38), custom_call_target="tpu_custom_call" | custom-call | tf_op jit(solution)/shard_map/terms/pallas_call | solution.py:232
  98.9 5.7 %collective-permute-done.10 = bf16[1,32,7680]{2,1,0:T(8,128)(2,1)S(1)} collective-permute-done((bf16[1,32,7680]{2,1,0:T(8,128)(2,1)S(1)}, bf16[1,32,7680]{2,1,0:T(8,128)(2,1)S(1)}, u32[]{:S(2)}, u32[]{:S(2)}) %collective-permute-start.10) | collective-permute-done | bytes 491552 | tf_op jit(solution)/shard_map/ppermute | solution.py:339
  104.6 8.1 %collective-permute-done.11 = bf16[1,32,7680]{2,1,0:T(8,128)(2,1)S(1)} collective-permute-done((bf16[1,32,7680]{2,1,0:T(8,128)(2,1)S(1)}, bf16[1,32,7680]{2,1,0:T(8,128)(2,1)S(1)}, u32[]{:S(2)}, u32[]{:S(2)}) %collective-permute-start.11) | collective-permute-done | bytes 491552 | tf_op jit(solution)/shard_map/ppermute | solution.py:339
  112.9 1.0 pad_maximum_fusion.3
  114.0 1.0 pad_maximum_fusion.2
  115.0 1.6 collective-permute-start.12
  116.6 2.2 %collective-permute-start.13 = (bf16[2,32,7680]{2,1,0:T(8,128)(2,1)}, bf16[2,32,7680]{2,1,0:T(8,128)(2,1)}, u32[]{:S(2)}, u32[]{:S(2)}) collective-permute-start(bf16[2,32,7680]{2,1,0:T(8,128)(2,1)} %pad_maximum_fusion.3), channel_id=1, source_target_pairs={{0,3},{1,0},{2,1},{3,2},{4,7},{5,4},{6,5},{7,6},{8,11},{9,8},{10,9... | collective-permute-start | bytes 2949128 | tf_op jit(solution)/shard_map/ppermute | solution.py:339
  118.9 2.6 %merge.1 = (f32[960,512]{1,0:T(8,128)S(1)}, bf16[960,512]{1,0:T(8,128)(2,1)}, bf16[960,512]{1,0:T(8,128)(2,1)}, bf16[960,512]{1,0:T(8,128)(2,1)}) custom-call(s32[2]{0:T(128)S(1)} %pad_add_fusion.place, bf16[4,2,960,512]{3,2,1,0:T(8,128)(2,1)S(1)} %bitcast.31, bf16[4,2,960,512]{3,2,1,0:T(8,128)(2,1)S(1)} %bitcast.32, bf16[4,2,960,512]{3,2,1,0:T(8,128)(2,1)S(1)} %bitcast.33, ...), custom_call_target="tpu_custom_call" | custom-call | tf_op jit(solution)/shard_map/merge/pallas_call | solution.py:284
  121.5 1.2 collective-permute-start.15
  122.7 0.8 collective-permute-start.16
  123.6 1.4 collective-permute-start.17
  125.0 4.3 %after.1 = bf16[2,128,2048]{2,1,0:T(8,128)(2,1)} custom-call(bf16[2,128,2048]{2,1,0:T(8,128)(2,1)} %query.3, bf16[2,2,1024,128]{3,2,1,0:T(8,128)(2,1)} %copy-done, bf16[2,2,128,128]{3,2,1,0:T(8,128)(2,1)} %copy-done.4, f32[1,128]{1,0:T(1,128)} %bitcast.52), custom_call_target="tpu_custom_call" | custom-call | tf_op jit(solution)/shard_map/after/pallas_call | solution.py:189
  129.3 12.5 %collective-permute-done.12 = bf16[2,32,7680]{2,1,0:T(8,128)(2,1)} collective-permute-done((bf16[2,32,7680]{2,1,0:T(8,128)(2,1)}, bf16[2,32,7680]{2,1,0:T(8,128)(2,1)}, u32[]{:S(2)}, u32[]{:S(2)}) %collective-permute-start.12) | collective-permute-done | bytes 983072 | tf_op jit(solution)/shard_map/ppermute | solution.py:339
  141.8 18.9 %collective-permute-done.13 = bf16[2,32,7680]{2,1,0:T(8,128)(2,1)} collective-permute-done((bf16[2,32,7680]{2,1,0:T(8,128)(2,1)}, bf16[2,32,7680]{2,1,0:T(8,128)(2,1)}, u32[]{:S(2)}, u32[]{:S(2)}) %collective-permute-start.13) | collective-permute-done | bytes 983072 | tf_op jit(solution)/shard_map/ppermute | solution.py:339
  160.8 3.1 %add_convert_fusion = bf16[2,32,7680]{2,1,0:T(8,128)(2,1)} fusion(bf16[2,32,7680]{2,1,0:T(8,128)(2,1)} %collective-permute-done.13, bf16[2,32,7680]{2,1,0:T(8,128)(2,1)} %collective-permute-done.12, bf16[2,32,7680]{2,1,0:T(8,128)(2,1)} %copy-done.3), kind=kLoop, calls=%fused_computation.7 | loop fusion | flops 2949120 | bytes 3932160 | tf_op jit(solution)/shard_map/convert_element_type | solution.py:417
  163.9 0.6 collective-permute-done.16.refs_1_
  164.4 1.4 collective-permute-done.17.refs_2_
  165.8 2.6 %finish.1 = (f32[960,256]{1,0:T(8,128)}, f32[960,256]{1,0:T(8,128)}) custom-call(f32[960,512]{1,0:T(8,128)S(1)} %get-tuple-element.78.own, bf16[960,512]{1,0:T(8,128)(2,1)S(1)} %collective-permute-done.15.refs_0_, bf16[960,512]{1,0:T(8,128)(2,1)} %collective-permute-done.16.refs_1_, bf16[960,512]{1,0:T(8,128)(2,1)} %collective-permute-done.17.refs_2_), custom_call_target="tpu_custom_call" | custom-call | tf_op jit(solution)/shard_map/finish/pallas_call | solution.py:302
  (55 shorter events, 1.7 us)
Async XLA Ops:
  0.6 53.2 %copy-start.14 = (s32[4]{0:T(128)S(1)}, s32[4]{0:T(128)}, u32[]{:S(2)}) copy-start(s32[4]{0:T(128)} %constant.61.clone) | copy-start | bytes 52
  0.6 27.9 %collective-permute-start = (bf16[2,32,7680]{2,1,0:T(8,128)(2,1)}, bf16[2,32,7680]{2,1,0:T(8,128)(2,1)S(1)}, u32[]{:S(2)}, u32[]{:S(2)}) collective-permute-start(bf16[2,32,7680]{2,1,0:T(8,128)(2,1)} %param.13), channel_id=1, source_target_pairs={{0,1},{1,2},{2,3},{3,0},{4,5},{5,6},{6,7},{7,4},{8,9},{9,10},{10,1... | collective-permute-start | bytes 2949128 | tf_op jit(solution)/shard_map/ppermute | solution.py:339
  3.7 44.5 %collective-permute-start.1 = (bf16[2,32,7680]{2,1,0:T(8,128)(2,1)}, bf16[2,32,7680]{2,1,0:T(8,128)(2,1)S(1)}, u32[]{:S(2)}, u32[]{:S(2)}) collective-permute-start(bf16[2,32,7680]{2,1,0:T(8,128)(2,1)} %param.13), channel_id=1, source_target_pairs={{0,3},{1,0},{2,1},{3,2},{4,7},{5,4},{6,5},{7,6},{8,11},{9,8},{10,9... | collective-permute-start | bytes 2949128 | tf_op jit(solution)/shard_map/ppermute | solution.py:339
  8.0 41.1 %collective-permute-start.2 = (bf16[960,512]{1,0:T(8,128)(2,1)}, bf16[960,512]{1,0:T(8,128)(2,1)S(1)}, u32[]{:S(2)}, u32[]{:S(2)}) collective-permute-start(bf16[960,512]{1,0:T(8,128)(2,1)} %beside.1), channel_id=1, source_target_pairs={{0,8},{4,12},{8,0},{12,4},{16,24},{20,28},{24,16},{28,20},{1,9},{5... | collective-permute-start | bytes 2949128 | tf_op jit(solution)/shard_map/ppermute | solution.py:342
  9.7 44.2 %collective-permute-start.3 = (bf16[960,512]{1,0:T(8,128)(2,1)}, bf16[960,512]{1,0:T(8,128)(2,1)}, u32[]{:S(2)}, u32[]{:S(2)}) collective-permute-start(bf16[960,512]{1,0:T(8,128)(2,1)} %beside.1), channel_id=1, source_target_pairs={{0,16},{4,20},{8,24},{12,28},{16,0},{20,4},{24,8},{28,12},{1,17},{... | collective-permute-start | bytes 2949128 | tf_op jit(solution)/shard_map/ppermute | solution.py:342
  11.2 42.6 %collective-permute-start.4 = (bf16[960,512]{1,0:T(8,128)(2,1)}, bf16[960,512]{1,0:T(8,128)(2,1)}, u32[]{:S(2)}, u32[]{:S(2)}) collective-permute-start(bf16[960,512]{1,0:T(8,128)(2,1)} %beside.1), channel_id=1, source_target_pairs={{0,24},{4,28},{8,16},{12,20},{16,8},{20,12},{24,0},{28,4},{1,25},{... | collective-permute-start | bytes 2949128 | tf_op jit(solution)/shard_map/ppermute | solution.py:342
  48.2 1.1 copy-start.10
  49.1 0.9 copy-start.13
  53.8 5.8 %collective-permute-start.5 = (bf16[2,960,512]{2,1,0:T(8,128)(2,1)S(1)}, bf16[2,960,512]{2,1,0:T(8,128)(2,1)}, u32[]{:S(2)}, u32[]{:S(2)}) collective-permute-start(bf16[2,960,512]{2,1,0:T(8,128)(2,1)S(1)} %pad_maximum_fusion.1), channel_id=1, source_target_pairs={{0,4},{4,0},{8,12},{12,8},{16,20},{20,16},{24,28},{28,24},{1,5},{5... | collective-permute-start | bytes 5898248 | tf_op jit(solution)/shard_map/ppermute | solution.py:342
  53.8 5.3 %copy-start.11 = (bf16[2,32,7680]{2,1,0:T(8,128)(2,1)S(1)}, bf16[2,32,7680]{2,1,0:T(8,128)(2,1)}, u32[]{:S(2)}) copy-start(bf16[2,32,7680]{2,1,0:T(8,128)(2,1)} %copy-done.10) | copy-start | bytes 2949124
  53.8 5.3 %copy-start.12 = (bf16[2,32,7680]{2,1,0:T(8,128)(2,1)S(1)}, bf16[2,32,7680]{2,1,0:T(8,128)(2,1)}, u32[]{:S(2)}) copy-start(bf16[2,32,7680]{2,1,0:T(8,128)(2,1)} %param.13) | copy-start | bytes 2949124
  53.9 10.5 %collective-permute-start.6 = (bf16[1,960,512]{2,1,0:T(8,128)(2,1)}, bf16[1,960,512]{2,1,0:T(8,128)(2,1)S(1)}, u32[]{:S(2)}, u32[]{:S(2)}) collective-permute-start(bf16[1,960,512]{2,1,0:T(8,128)(2,1)} %bitcast.7), channel_id=1, source_target_pairs={{0,4},{4,0},{8,12},{12,8},{16,20},{20,16},{24,28},{28,24},{1,5},{5... | collective-permute-start | bytes 2949128 | tf_op jit(solution)/shard_map/ppermute | solution.py:342
  54.4 11.3 %collective-permute-start.7 = (bf16[1,960,512]{2,1,0:T(8,128)(2,1)}, bf16[1,960,512]{2,1,0:T(8,128)(2,1)S(1)}, u32[]{:S(2)}, u32[]{:S(2)}) collective-permute-start(bf16[1,960,512]{2,1,0:T(8,128)(2,1)} %bitcast.8), channel_id=1, source_target_pairs={{0,4},{4,0},{8,12},{12,8},{16,20},{20,16},{24,28},{28,24},{1,5},{5... | collective-permute-start | bytes 2949128 | tf_op jit(solution)/shard_map/ppermute | solution.py:342
  54.5 15.9 %collective-permute-start.8 = (bf16[1,32,7680]{2,1,0:T(8,128)(2,1)S(1)}, bf16[1,32,7680]{2,1,0:T(8,128)(2,1)S(1)}, u32[]{:S(2)}, u32[]{:S(2)}) collective-permute-start(bf16[1,32,7680]{2,1,0:T(8,128)(2,1)S(1)} %slice.48), channel_id=1, source_target_pairs={{0,1},{1,2},{2,3},{3,0},{4,5},{5,6},{6,7},{7,4},{8,9},{9,10},{10,1... | collective-permute-start | bytes 1474568 | tf_op jit(solution)/shard_map/ppermute | solution.py:339
  54.5 24.3 %collective-permute-start.9 = (bf16[1,32,7680]{2,1,0:T(8,128)(2,1)}, bf16[1,32,7680]{2,1,0:T(8,128)(2,1)S(1)}, u32[]{:S(2)}, u32[]{:S(2)}) collective-permute-start(bf16[1,32,7680]{2,1,0:T(8,128)(2,1)} %slice.49), channel_id=1, source_target_pairs={{0,3},{1,0},{2,1},{3,2},{4,7},{5,4},{6,5},{7,6},{8,11},{9,8},{10,9... | collective-permute-start | bytes 1474568 | tf_op jit(solution)/shard_map/ppermute | solution.py:339
  59.4 8.1 %copy-start.8 = (bf16[3,2,32,7680]{3,2,1,0:T(8,128)(2,1)}, bf16[3,2,32,7680]{3,2,1,0:T(8,128)(2,1)S(1)}, u32[]{:S(2)}) copy-start(bf16[3,2,32,7680]{3,2,1,0:T(8,128)(2,1)S(1)} %pad_maximum_fusion) | copy-start | bytes 8847364
  67.6 12.8 %copy-start.1 = (bf16[2,2,1024,128]{3,2,1,0:T(8,128)(2,1)S(1)}, bf16[2,2,1024,128]{3,2,1,0:T(8,128)(2,1)}, u32[]{:S(2)}) copy-start(bf16[2,2,1024,128]{3,2,1,0:T(8,128)(2,1)} %get-tuple-element.55.refs_4_) | copy-start | bytes 3145732
  67.6 12.8 %copy-start.2 = (bf16[2,2,1024,128]{3,2,1,0:T(8,128)(2,1)S(1)}, bf16[2,2,1024,128]{3,2,1,0:T(8,128)(2,1)}, u32[]{:S(2)}) copy-start(bf16[2,2,1024,128]{3,2,1,0:T(8,128)(2,1)} %get-tuple-element.56.refs_5_) | copy-start | bytes 3145732
  67.6 12.8 %copy-start.5 = (s32[2]{0:T(128)S(1)}, s32[2]{0:T(128)}, u32[]{:S(2)}) copy-start(s32[2]{0:T(128)} %assignment.1) | copy-start | bytes 28
  67.6 12.8 %copy-start.6 = (s32[2]{0:T(128)S(1)}, s32[2]{0:T(128)}, u32[]{:S(2)}) copy-start(s32[2]{0:T(128)} %tiles.1) | copy-start | bytes 28
  67.6 12.8 %copy-start.7 = (f32[128]{0:T(128)S(1)}, f32[128]{0:T(128)}, u32[]{:S(2)}) copy-start(f32[128]{0:T(128)} %param.17) | copy-start | bytes 1540
  80.4 12.1 %copy-start.9 = (bf16[3,2,32,7680]{3,2,1,0:T(8,128)(2,1)S(1)}, bf16[3,2,32,7680]{3,2,1,0:T(8,128)(2,1)}, u32[]{:S(2)}) copy-start(bf16[3,2,32,7680]{3,2,1,0:T(8,128)(2,1)} %copy-done.8) | copy-start | bytes 8847364
  85.4 7.0 %copy-start = (bf16[2,2,1024,128]{3,2,1,0:T(8,128)(2,1)}, bf16[2,2,1024,128]{3,2,1,0:T(8,128)(2,1)S(1)}, u32[]{:S(2)}) copy-start(bf16[2,2,1024,128]{3,2,1,0:T(8,128)(2,1)S(1)} %get-tuple-element.67.score_grad) | copy-start | bytes 3145732
  85.5 7.0 %copy-start.4 = (bf16[2,2,128,128]{3,2,1,0:T(8,128)(2,1)}, bf16[2,2,128,128]{3,2,1,0:T(8,128)(2,1)S(1)}, u32[]{:S(2)}) copy-start(bf16[2,2,128,128]{3,2,1,0:T(8,128)(2,1)S(1)} %get-tuple-element.68.keys) | copy-start | bytes 393220
  88.6 16.0 %collective-permute-start.10 = (bf16[1,32,7680]{2,1,0:T(8,128)(2,1)S(1)}, bf16[1,32,7680]{2,1,0:T(8,128)(2,1)S(1)}, u32[]{:S(2)}, u32[]{:S(2)}) collective-permute-start(bf16[1,32,7680]{2,1,0:T(8,128)(2,1)S(1)} %get-tuple-element.59), channel_id=1, source_target_pairs={{0,1},{1,2},{2,3},{3,0},{4,5},{5,6},{6,7},{7,4},{8,9},{9,10},{10,1... | collective-permute-start | bytes 1474568 | tf_op jit(solution)/shard_map/ppermute | solution.py:339
  89.6 23.1 %collective-permute-start.11 = (bf16[1,32,7680]{2,1,0:T(8,128)(2,1)S(1)}, bf16[1,32,7680]{2,1,0:T(8,128)(2,1)S(1)}, u32[]{:S(2)}, u32[]{:S(2)}) collective-permute-start(bf16[1,32,7680]{2,1,0:T(8,128)(2,1)S(1)} %get-tuple-element.60), channel_id=1, source_target_pairs={{0,3},{1,0},{2,1},{3,2},{4,7},{5,4},{6,5},{7,6},{8,11},{9,8},{10,9... | collective-permute-start | bytes 1474568 | tf_op jit(solution)/shard_map/ppermute | solution.py:339
  95.2 23.7 %collective-permute-start.14 = (bf16[4,960,512]{2,1,0:T(8,128)(2,1)S(1)}, bf16[4,960,512]{2,1,0:T(8,128)(2,1)S(1)}, u32[]{:S(2)}, u32[]{:S(2)}) collective-permute-start(bf16[4,960,512]{2,1,0:T(8,128)(2,1)S(1)} %dynamic-slice_bitcast_fusion), channel_id=1, source_target_pairs={{0,4},{4,0},{8,12},{12,8},{16,20},{20,16},{24,28},{28,24},{1,5},{5... | collective-permute-start | bytes 11796488 | tf_op jit(solution)/shard_map/ppermute | solution.py:342
  98.8 22.7 %copy-start.3 = (bf16[2,32,7680]{2,1,0:T(8,128)(2,1)}, bf16[2,32,7680]{2,1,0:T(8,128)(2,1)S(1)}, u32[]{:S(2)}) copy-start(bf16[2,32,7680]{2,1,0:T(8,128)(2,1)S(1)} %get-tuple-element.70) | copy-start | bytes 2949124
  115.0 26.8 %collective-permute-start.12 = (bf16[2,32,7680]{2,1,0:T(8,128)(2,1)}, bf16[2,32,7680]{2,1,0:T(8,128)(2,1)}, u32[]{:S(2)}, u32[]{:S(2)}) collective-permute-start(bf16[2,32,7680]{2,1,0:T(8,128)(2,1)} %pad_maximum_fusion.2), channel_id=1, source_target_pairs={{0,1},{1,2},{2,3},{3,0},{4,5},{5,6},{6,7},{7,4},{8,9},{9,10},{10,1... | collective-permute-start | bytes 2949128 | tf_op jit(solution)/shard_map/ppermute | solution.py:339
  116.6 44.1 %collective-permute-start.13 = (bf16[2,32,7680]{2,1,0:T(8,128)(2,1)}, bf16[2,32,7680]{2,1,0:T(8,128)(2,1)}, u32[]{:S(2)}, u32[]{:S(2)}) collective-permute-start(bf16[2,32,7680]{2,1,0:T(8,128)(2,1)} %pad_maximum_fusion.3), channel_id=1, source_target_pairs={{0,3},{1,0},{2,1},{3,2},{4,7},{5,4},{6,5},{7,6},{8,11},{9,8},{10,9... | collective-permute-start | bytes 2949128 | tf_op jit(solution)/shard_map/ppermute | solution.py:339
  121.5 42.4 %collective-permute-start.15 = (bf16[960,512]{1,0:T(8,128)(2,1)}, bf16[960,512]{1,0:T(8,128)(2,1)S(1)}, u32[]{:S(2)}, u32[]{:S(2)}) collective-permute-start(bf16[960,512]{1,0:T(8,128)(2,1)} %get-tuple-element.74), channel_id=1, source_target_pairs={{0,8},{4,12},{8,0},{12,4},{16,24},{20,28},{24,16},{28,20},{1,9},{5... | collective-permute-start | bytes 2949128 | tf_op jit(solution)/shard_map/ppermute | solution.py:342
  122.7 41.7 %collective-permute-start.16 = (bf16[960,512]{1,0:T(8,128)(2,1)}, bf16[960,512]{1,0:T(8,128)(2,1)}, u32[]{:S(2)}, u32[]{:S(2)}) collective-permute-start(bf16[960,512]{1,0:T(8,128)(2,1)} %get-tuple-element.75), channel_id=1, source_target_pairs={{0,16},{4,20},{8,24},{12,28},{16,0},{20,4},{24,8},{28,12},{1,17},{... | collective-permute-start | bytes 2949128 | tf_op jit(solution)/shard_map/ppermute | solution.py:342
  123.6 42.3 %collective-permute-start.17 = (bf16[960,512]{1,0:T(8,128)(2,1)}, bf16[960,512]{1,0:T(8,128)(2,1)}, u32[]{:S(2)}, u32[]{:S(2)}) collective-permute-start(bf16[960,512]{1,0:T(8,128)(2,1)} %get-tuple-element.76), channel_id=1, source_target_pairs={{0,24},{4,28},{8,16},{12,20},{16,8},{20,12},{24,0},{28,4},{1,25},{... | collective-permute-start | bytes 2949128 | tf_op jit(solution)/shard_map/ppermute | solution.py:342

commit v11 on v10

--- a/solution.py
+++ b/solution.py
@@ -164,7 +164,7 @@
                 pltpu.VMEM((img_count, img_rows, head_dim), jnp.float32),
             ],
         ),
-        compiler_params=pltpu.CompilerParams(vmem_limit_bytes=32 * 1024 * 1024),
+        compiler_params=pltpu.CompilerParams(vmem_limit_bytes=16 * 1024 * 1024),
         name="attend",
     )(assignment, tiles, owners, *pieces, *pieces, normed, masked, gain)
 
@@ -242,7 +242,7 @@
         out_specs=[
             pl.BlockSpec((count, own_rows, width), lambda c: (0, 0, c)) for count in counts
         ],
-        compiler_params=pltpu.CompilerParams(vmem_limit_bytes=32 * 1024 * 1024),
+        compiler_params=pltpu.CompilerParams(vmem_limit_bytes=16 * 1024 * 1024),
         name="terms",
     )(rows, weight)
 
@@ -290,7 +290,7 @@
             in_specs=[spec[0] for spec in specs] + [spec[1] for spec in specs],
             out_specs=[pl.BlockSpec((own_width // 2, cols), lambda i, _: (i, 0))] * len(specs),
         ),
-        compiler_params=pltpu.CompilerParams(vmem_limit_bytes=32 * 1024 * 1024),
+        compiler_params=pltpu.CompilerParams(vmem_limit_bytes=16 * 1024 * 1024),
         name="merge",
     )(place, *[held] * len(specs), *[given] * len(specs))
 
@@ -305,7 +305,7 @@
         grid=(2,),
         in_specs=[pl.BlockSpec((rows, cols), lambda i: (i, 0))] * (1 + len(sent)),
         out_specs=[pl.BlockSpec((rows, cols // 2), lambda i: (i, 0))] * 2,
-        compiler_params=pltpu.CompilerParams(vmem_limit_bytes=32 * 1024 * 1024),
+        compiler_params=pltpu.CompilerParams(vmem_limit_bytes=16 * 1024 * 1024),
         name="finish",
     )(own, *sent)
 
@@ -352,19 +352,19 @@
         opposite = (ring(leaving[0], 1), ring(leaving[1], -1))
     else:
         side, up, across = (swap(own_weight, 2 * r) for r in range(1, pairs))
-        twice = jnp.stack((own_weight, side))
         weight = jnp.zeros((2 * pairs, own_width, cols), jnp.bfloat16)
-        leaving, twice, up, across, normed, masked, weight = lax.optimization_barrier(
-            (leaving, twice, up, across, normed, masked, weight)
+        leaving, side, up, across, normed, masked = lax.optimization_barrier(
+            (leaving, side, up, across, normed, masked)
         )
         opposite = (ring(leaving[0], 1), ring(leaving[1], -1))
-        for r, pieces in ((0, twice), (2, up[None]), (3, across[None])):
-            mates = swap(pieces, 1)
-            for k in range(pieces.shape[0]):
-                for source, half in ((pieces, core), (mates, 1 - core)):
-                    weight = lax.dynamic_update_slice_in_dim(
-                        weight, source[k : k + 1], 2 * (pair ^ (r + k)) + half, axis=0
-                    )
+        mates = [swap(piece, 1) for piece in (side, up, across)]
+        own_weight, mates = lax.optimization_barrier((own_weight, mates))
+        mates = [swap(own_weight, 1), *mates]
+        for r, pieces in enumerate(zip((own_weight, side, up, across), mates)):
+            for source, half in zip(pieces, (core, 1 - core)):
+                weight = lax.dynamic_update_slice_in_dim(
+                    weight, source[None], 2 * (pair ^ r) + half, axis=0
+                )
         weight = weight.reshape(vis_width, cols)
 
     near = jnp.stack((images, from_left, from_right)).reshape(-1, vis_width)

time: 169 us -> 171 us (1.012)
  waiting for transfers between devices: 92.5 us -> 95.4 us
  starting transfers between devices: 24.4 us -> 22.6 us
    ppermute x10 -> x11, waiting for transfers between devices: 4.21 us -> 11.3 us  [swap(): return lax.ppermute(value, 'dp', [(i, i ^ mask) for i in range(dp_size)])]
    ppermute x8, waiting for transfers between devices: 88.3 us -> 84.1 us  [ring(): lax.ppermute(value, 'mp', [(i, (i + step) % mp_size) for i in range(mp_si...]
    ppermute x8, starting transfers between devices: 16.7 us -> 14.9 us  [ring(): lax.ppermute(value, 'mp', [(i, (i + step) % mp_size) for i in range(mp_si...]
    ppermute x10 -> x11, starting transfers between devices: 7.67 us -> 7.7 us  [swap(): return lax.ppermute(value, 'dp', [(i, i ^ mask) for i in range(dp_size)])]
  transfers between devices with their start and end apart: 18 -> 19, of which waited for: 12 -> 13; matrix products, arithmetic and copies ran while one was open for 12% -> 13% of each run, Pallas kernels for 10% -> 10%
where the time goes in v11:
time: 171 us; the launch traced here: 170 us
  waiting for transfers between devices  95.4 us (56%)
  Pallas kernels  28 us (16%)
  starting transfers between devices  22.6 us (13%)
  local copies, waits for them, and re-layouts  9.94 us (6%)
  other arithmetic  7.63 us (4%)
  matrix products  5.61 us (3%)
    ppermute x8, waiting for transfers between devices, ring(): lax.ppermute(value, 'mp', [(i, (i + step) % mp_size) for i in range(mp_si...  84.1 us
    ppermute x8, starting transfers between devices, ring(): lax.ppermute(value, 'mp', [(i, (i + step) % mp_size) for i in range(mp_si...  14.9 us
    ppermute x11, waiting for transfers between devices, swap(): return lax.ppermute(value, 'dp', [(i, i ^ mask) for i in range(dp_size)])  11.3 us
    dynamic_update_slice x8, local copies, waits for them, and re-layouts, per_device(): lax.dynamic_update_slice_in_dim(weight, source[None], 2 * (pair ^ r) + ha...  7.95 us
    ppermute x11, starting transfers between devices, swap(): return lax.ppermute(value, 'dp', [(i, i ^ mask) for i in range(dp_size)])  7.7 us
    pallas_call x2, Pallas kernels, terms(): pl.pallas_call(functools.partial(terms_kernel, splits), out_shape=[jax.Sh...  6.56 us
    dot_general x3, matrix products, dot(): lax.dot_general(left, right, (((left_dim,), (right_dim,)), ((), ())), pre...  5.61 us
    pallas_call x1, Pallas kernels, attend(): pl.pallas_call(functools.partial(attend_kernel, len(pieces)), out_shape=(...  5.01 us
  transfers between devices with their start and end apart: 19, of which 13 were waited for; matrix products, arithmetic and copies ran while one was open for 13% of the time, Pallas kernels for 10%

profile of v11, /device:TPU:0, one launch (start us, length us, event | category | flops | bytes accessed | tf_op | source)
XLA Modules:
  0.0 170.2 jit_solution(7021969951697913389)
XLA Ops:
  0.6 3.1 %collective-permute-start = (bf16[2,32,7680]{2,1,0:T(8,128)(2,1)}, bf16[2,32,7680]{2,1,0:T(8,128)(2,1)S(1)}, u32[]{:S(2)}, u32[]{:S(2)}) collective-permute-start(bf16[2,32,7680]{2,1,0:T(8,128)(2,1)} %param.13), channel_id=1, source_target_pairs={{0,1},{1,2},{2,3},{3,0},{4,5},{5,6},{6,7},{7,4},{8,9},{9,10},{10,1... | collective-permute-start | bytes 2949128 | tf_op jit(solution)/shard_map/ppermute | solution.py:339
  3.7 2.1 %collective-permute-start.1 = (bf16[2,32,7680]{2,1,0:T(8,128)(2,1)}, bf16[2,32,7680]{2,1,0:T(8,128)(2,1)S(1)}, u32[]{:S(2)}, u32[]{:S(2)}) collective-permute-start(bf16[2,32,7680]{2,1,0:T(8,128)(2,1)} %param.13), channel_id=1, source_target_pairs={{0,3},{1,0},{2,1},{3,2},{4,7},{5,4},{6,5},{7,6},{8,11},{9,8},{10,9... | collective-permute-start | bytes 2949128 | tf_op jit(solution)/shard_map/ppermute | solution.py:339
  5.8 2.2 %beside.1 = bf16[960,512]{1,0:T(8,128)(2,1)} custom-call(bf16[960,256]{1,0:T(8,128)(2,1)} %left.1, bf16[960,256]{1,0:T(8,128)(2,1)} %right.1), custom_call_target="tpu_custom_call" | custom-call | tf_op jit(solution)/shard_map/beside/pallas_call | solution.py:212
  8.0 1.6 collective-permute-start.2
  9.6 1.5 collective-permute-start.3
  11.5 4.8 %before.1 = (bf16[2,2,1024,128]{3,2,1,0:T(8,128)(2,1)}, bf16[2,2,1024,128]{3,2,1,0:T(8,128)(2,1)}) custom-call(s32[2]{0:T(128)} %lengths.1, bf16[2,128,2048]{2,1,0:T(8,128)(2,1)} %query.3, bf16[2,128,2048]{2,1,0:T(8,128)(2,1)} %grad.1, f32[1,128]{1,0:T(1,128)} %bitcast.59), custom_call_target="tpu_custom_call" | custom-call | tf_op jit(solution)/shard_map/before/pallas_call | solution.py:58
  16.3 12.3 %collective-permute-done = bf16[2,32,7680]{2,1,0:T(8,128)(2,1)S(1)} collective-permute-done((bf16[2,32,7680]{2,1,0:T(8,128)(2,1)}, bf16[2,32,7680]{2,1,0:T(8,128)(2,1)S(1)}, u32[]{:S(2)}, u32[]{:S(2)}) %collective-permute-start) | collective-permute-done | bytes 983072 | tf_op jit(solution)/shard_map/ppermute | solution.py:339
  28.6 19.6 %collective-permute-done.1 = bf16[2,32,7680]{2,1,0:T(8,128)(2,1)S(1)} collective-permute-done((bf16[2,32,7680]{2,1,0:T(8,128)(2,1)}, bf16[2,32,7680]{2,1,0:T(8,128)(2,1)S(1)}, u32[]{:S(2)}, u32[]{:S(2)}) %collective-permute-start.1) | collective-permute-done | bytes 983072 | tf_op jit(solution)/shard_map/ppermute | solution.py:339
  48.2 0.8 slice.33
  49.0 4.8 %collective-permute-done.3 = bf16[960,512]{1,0:T(8,128)(2,1)} collective-permute-done((bf16[960,512]{1,0:T(8,128)(2,1)}, bf16[960,512]{1,0:T(8,128)(2,1)}, u32[]{:S(2)}, u32[]{:S(2)}) %collective-permute-start.3) | collective-permute-done | bytes 983072 | tf_op jit(solution)/shard_map/ppermute | solution.py:342
  53.8 0.5 collective-permute-start.6
  54.3 0.7 and_select_fusion.owners
  55.0 1.7 collective-permute-start.10
  57.0 1.1 collective-permute-done.6
  58.1 1.4 collective-permute-done.7
  59.7 1.5 pad_maximum_fusion
  61.2 0.7 broadcast_in_dim.33
  62.4 1.3 bitcast_dynamic-update-slice_fusion.5
  63.7 1.3 bitcast_dynamic-update-slice_fusion.4
  65.0 1.3 bitcast_dynamic-update-slice_fusion.3
  66.3 1.3 bitcast_dynamic-update-slice_fusion.2
  67.6 1.3 bitcast_dynamic-update-slice_fusion.1
  68.9 1.3 bitcast_dynamic-update-slice_fusion
  70.2 1.7 fusion.5
  72.0 7.5 %collective-permute-done.9 = bf16[1,32,7680]{2,1,0:T(8,128)(2,1)S(1)} collective-permute-done((bf16[1,32,7680]{2,1,0:T(8,128)(2,1)S(1)}, bf16[1,32,7680]{2,1,0:T(8,128)(2,1)S(1)}, u32[]{:S(2)}, u32[]{:S(2)}) %collective-permute-start.9) | collective-permute-done | bytes 491552 | tf_op jit(solution)/shard_map/ppermute | solution.py:339
  79.5 1.5 convolution_bitcast_fusion.refs_1_.refs_3_
  81.1 5.0 %attend.1 = (bf16[4,2,32,512]{3,2,1,0:T(8,128)(2,1)S(1)}, bf16[2,2,1024,128]{3,2,1,0:T(8,128)(2,1)S(1)}, bf16[2,2,128,128]{3,2,1,0:T(8,128)(2,1)S(1)}) custom-call(s32[2]{0:T(128)S(1)} %copy-done.5, s32[2]{0:T(128)S(1)} %copy-done.6, s32[4]{0:T(128)S(1)} %and_select_fusion.owners, f32[3,2,32,512]{3,2,1,0:T(8,128)S(1)} %bitcast.49, ...), custom_call_target="tpu_custom_call" | custom-call | tf_op jit(solution)/shard_map/attend/pallas_call | solution.py:141
  86.1 3.1 %terms.3 = (bf16[1,32,7680]{2,1,0:T(8,128)(2,1)S(1)}, bf16[1,32,7680]{2,1,0:T(8,128)(2,1)S(1)}) custom-call(bf16[1,2,32,512]{3,2,1,0:T(8,128)(2,1)S(1)} %slice.28.rows, bf16[7680,512]{1,0:T(8,128)(2,1)S(1)} %bitcast.47), custom_call_target="tpu_custom_call" | custom-call | tf_op jit(solution)/shard_map/terms/pallas_call | solution.py:232
  89.2 1.7 collective-permute-start.11
  90.9 2.2 %collective-permute-start.12 = (bf16[1,32,7680]{2,1,0:T(8,128)(2,1)S(1)}, bf16[1,32,7680]{2,1,0:T(8,128)(2,1)S(1)}, u32[]{:S(2)}, u32[]{:S(2)}) collective-permute-start(bf16[1,32,7680]{2,1,0:T(8,128)(2,1)S(1)} %get-tuple-element.66), channel_id=1, source_target_pairs={{0,3},{1,0},{2,1},{3,2},{4,7},{5,4},{6,5},{7,6},{8,11},{9,8},{10,9... | collective-permute-start | bytes 1474568 | tf_op jit(solution)/shard_map/ppermute | solution.py:339
  93.1 2.5 %convolution_convert_fusion = bf16[7680,512]{1,0:T(8,128)(2,1)S(1)} fusion(bf16[256,512]{1,0:T(8,128)(2,1)S(1)} %bitcast.51, bf16[64,7680]{1,0:T(8,128)(2,1)S(1)} %bitcast.53, bf16[192,7680]{1,0:T(8,128)(2,1)S(1)} %bitcast.55), kind=kOutput, calls=%fused_computation | convolution fusion | flops 2025062400 | bytes 12058624 | tf_op jit(solution)/shard_map/dot_general | solution.py:29
  96.0 3.5 %terms.2 = (bf16[2,32,7680]{2,1,0:T(8,128)(2,1)S(1)}, bf16[2,32,7680]{2,1,0:T(8,128)(2,1)S(1)}, bf16[2,32,7680]{2,1,0:T(8,128)(2,1)S(1)}) custom-call(bf16[3,2,32,512]{3,2,1,0:T(8,128)(2,1)S(1)} %slice.26.rows, bf16[7680,512]{1,0:T(8,128)(2,1)S(1)} %bitcast.48), custom_call_target="tpu_custom_call" | custom-call | tf_op jit(solution)/shard_map/terms/pallas_call | solution.py:232
  99.6 5.7 %collective-permute-done.11 = bf16[1,32,7680]{2,1,0:T(8,128)(2,1)S(1)} collective-permute-done((bf16[1,32,7680]{2,1,0:T(8,128)(2,1)S(1)}, bf16[1,32,7680]{2,1,0:T(8,128)(2,1)S(1)}, u32[]{:S(2)}, u32[]{:S(2)}) %collective-permute-start.11) | collective-permute-done | bytes 491552 | tf_op jit(solution)/shard_map/ppermute | solution.py:339
  105.2 8.8 %collective-permute-done.12 = bf16[1,32,7680]{2,1,0:T(8,128)(2,1)S(1)} collective-permute-done((bf16[1,32,7680]{2,1,0:T(8,128)(2,1)S(1)}, bf16[1,32,7680]{2,1,0:T(8,128)(2,1)S(1)}, u32[]{:S(2)}, u32[]{:S(2)}) %collective-permute-start.12) | collective-permute-done | bytes 491552 | tf_op jit(solution)/shard_map/ppermute | solution.py:339
  114.2 1.0 pad_maximum_fusion.2
  115.3 1.0 pad_maximum_fusion.1
  116.7 3.5 %collective-permute-start.14 = (bf16[2,32,7680]{2,1,0:T(8,128)(2,1)}, bf16[2,32,7680]{2,1,0:T(8,128)(2,1)}, u32[]{:S(2)}, u32[]{:S(2)}) collective-permute-start(bf16[2,32,7680]{2,1,0:T(8,128)(2,1)} %pad_maximum_fusion.2), channel_id=1, source_target_pairs={{0,3},{1,0},{2,1},{3,2},{4,7},{5,4},{6,5},{7,6},{8,11},{9,8},{10,9... | collective-permute-start | bytes 2949128 | tf_op jit(solution)/shard_map/ppermute | solution.py:339
  120.2 2.5 %merge.1 = (f32[960,512]{1,0:T(8,128)S(1)}, bf16[960,512]{1,0:T(8,128)(2,1)}, bf16[960,512]{1,0:T(8,128)(2,1)}, bf16[960,512]{1,0:T(8,128)(2,1)}) custom-call(s32[2]{0:T(128)S(1)} %pad_add_fusion.place, bf16[4,2,960,512]{3,2,1,0:T(8,128)(2,1)S(1)} %bitcast.41, bf16[4,2,960,512]{3,2,1,0:T(8,128)(2,1)S(1)} %bitcast.42, bf16[4,2,960,512]{3,2,1,0:T(8,128)(2,1)S(1)} %bitcast.43, ...), custom_call_target="tpu_custom_call" | custom-call | tf_op jit(solution)/shard_map/merge/pallas_call | solution.py:284
  122.7 1.2 collective-permute-start.16
  124.0 0.8 collective-permute-start.17
  124.8 1.4 collective-permute-start.18
  126.2 4.3 %after.1 = bf16[2,128,2048]{2,1,0:T(8,128)(2,1)} custom-call(bf16[2,128,2048]{2,1,0:T(8,128)(2,1)} %query.3, bf16[2,2,1024,128]{3,2,1,0:T(8,128)(2,1)} %copy-done, bf16[2,2,128,128]{3,2,1,0:T(8,128)(2,1)} %copy-done.4, f32[1,128]{1,0:T(1,128)} %bitcast.60), custom_call_target="tpu_custom_call" | custom-call | tf_op jit(solution)/shard_map/after/pallas_call | solution.py:189
  130.5 12.6 %collective-permute-done.13 = bf16[2,32,7680]{2,1,0:T(8,128)(2,1)} collective-permute-done((bf16[2,32,7680]{2,1,0:T(8,128)(2,1)}, bf16[2,32,7680]{2,1,0:T(8,128)(2,1)}, u32[]{:S(2)}, u32[]{:S(2)}) %collective-permute-start.13) | collective-permute-done | bytes 983072 | tf_op jit(solution)/shard_map/ppermute | solution.py:339
  143.1 17.7 %collective-permute-done.14 = bf16[2,32,7680]{2,1,0:T(8,128)(2,1)} collective-permute-done((bf16[2,32,7680]{2,1,0:T(8,128)(2,1)}, bf16[2,32,7680]{2,1,0:T(8,128)(2,1)}, u32[]{:S(2)}, u32[]{:S(2)}) %collective-permute-start.14) | collective-permute-done | bytes 983072 | tf_op jit(solution)/shard_map/ppermute | solution.py:339
  160.8 3.1 %add_convert_fusion = bf16[2,32,7680]{2,1,0:T(8,128)(2,1)} fusion(bf16[2,32,7680]{2,1,0:T(8,128)(2,1)} %collective-permute-done.14, bf16[2,32,7680]{2,1,0:T(8,128)(2,1)} %collective-permute-done.13, bf16[2,32,7680]{2,1,0:T(8,128)(2,1)} %copy-done.3), kind=kLoop, calls=%fused_computation.6 | loop fusion | flops 2949120 | bytes 3932160 | tf_op jit(solution)/shard_map/convert_element_type | solution.py:417
  163.9 2.1 %collective-permute-done.17.refs_1_ = bf16[960,512]{1,0:T(8,128)(2,1)} collective-permute-done((bf16[960,512]{1,0:T(8,128)(2,1)}, bf16[960,512]{1,0:T(8,128)(2,1)}, u32[]{:S(2)}, u32[]{:S(2)}) %collective-permute-start.17) | collective-permute-done | bytes 983072 | tf_op jit(solution)/shard_map/ppermute | solution.py:342
  166.0 1.6 collective-permute-done.18.refs_2_
  167.6 2.6 %finish.1 = (f32[960,256]{1,0:T(8,128)}, f32[960,256]{1,0:T(8,128)}) custom-call(f32[960,512]{1,0:T(8,128)S(1)} %get-tuple-element.84.own, bf16[960,512]{1,0:T(8,128)(2,1)S(1)} %collective-permute-done.16.refs_0_, bf16[960,512]{1,0:T(8,128)(2,1)} %collective-permute-done.17.refs_1_, bf16[960,512]{1,0:T(8,128)(2,1)} %collective-permute-done.18.refs_2_), custom_call_target="tpu_custom_call" | custom-call | tf_op jit(solution)/shard_map/finish/pallas_call | solution.py:302
  (48 shorter events, 2.6 us)
Async XLA Ops:
  0.6 27.9 %collective-permute-start = (bf16[2,32,7680]{2,1,0:T(8,128)(2,1)}, bf16[2,32,7680]{2,1,0:T(8,128)(2,1)S(1)}, u32[]{:S(2)}, u32[]{:S(2)}) collective-permute-start(bf16[2,32,7680]{2,1,0:T(8,128)(2,1)} %param.13), channel_id=1, source_target_pairs={{0,1},{1,2},{2,3},{3,0},{4,5},{5,6},{6,7},{7,4},{8,9},{9,10},{10,1... | collective-permute-start | bytes 2949128 | tf_op jit(solution)/shard_map/ppermute | solution.py:339
  3.7 44.5 %collective-permute-start.1 = (bf16[2,32,7680]{2,1,0:T(8,128)(2,1)}, bf16[2,32,7680]{2,1,0:T(8,128)(2,1)S(1)}, u32[]{:S(2)}, u32[]{:S(2)}) collective-permute-start(bf16[2,32,7680]{2,1,0:T(8,128)(2,1)} %param.13), channel_id=1, source_target_pairs={{0,3},{1,0},{2,1},{3,2},{4,7},{5,4},{6,5},{7,6},{8,11},{9,8},{10,9... | collective-permute-start | bytes 2949128 | tf_op jit(solution)/shard_map/ppermute | solution.py:339
  8.0 41.0 %collective-permute-start.2 = (bf16[960,512]{1,0:T(8,128)(2,1)}, bf16[960,512]{1,0:T(8,128)(2,1)}, u32[]{:S(2)}, u32[]{:S(2)}) collective-permute-start(bf16[960,512]{1,0:T(8,128)(2,1)} %beside.1), channel_id=1, source_target_pairs={{0,8},{4,12},{8,0},{12,4},{16,24},{20,28},{24,16},{28,20},{1,9},{5... | collective-permute-start | bytes 2949128 | tf_op jit(solution)/shard_map/ppermute | solution.py:342
  9.6 44.2 %collective-permute-start.3 = (bf16[960,512]{1,0:T(8,128)(2,1)}, bf16[960,512]{1,0:T(8,128)(2,1)}, u32[]{:S(2)}, u32[]{:S(2)}) collective-permute-start(bf16[960,512]{1,0:T(8,128)(2,1)} %beside.1), channel_id=1, source_target_pairs={{0,16},{4,20},{8,24},{12,28},{16,0},{20,4},{24,8},{28,12},{1,17},{... | collective-permute-start | bytes 2949128 | tf_op jit(solution)/shard_map/ppermute | solution.py:342
  11.2 42.6 %collective-permute-start.4 = (bf16[960,512]{1,0:T(8,128)(2,1)}, bf16[960,512]{1,0:T(8,128)(2,1)}, u32[]{:S(2)}, u32[]{:S(2)}) collective-permute-start(bf16[960,512]{1,0:T(8,128)(2,1)} %beside.1), channel_id=1, source_target_pairs={{0,24},{4,28},{8,16},{12,20},{16,8},{20,12},{24,0},{28,4},{1,25},{... | collective-permute-start | bytes 2949128 | tf_op jit(solution)/shard_map/ppermute | solution.py:342
  16.3 45.6 %copy-start.8 = (bf16[960,512]{1,0:T(8,128)(2,1)S(1)}, bf16[960,512]{1,0:T(8,128)(2,1)}, u32[]{:S(2)}) copy-start(bf16[960,512]{1,0:T(8,128)(2,1)} %beside.1) | copy-start | bytes 2949124
  53.8 3.2 %collective-permute-start.5 = (bf16[960,512]{1,0:T(8,128)(2,1)}, bf16[960,512]{1,0:T(8,128)(2,1)}, u32[]{:S(2)}, u32[]{:S(2)}) collective-permute-start(bf16[960,512]{1,0:T(8,128)(2,1)} %collective-permute-done.2), channel_id=1, source_target_pairs={{0,4},{4,0},{8,12},{12,8},{16,20},{20,16},{24,28},{28,24},{1,5},{5... | collective-permute-start | bytes 2949128 | tf_op jit(solution)/shard_map/ppermute | solution.py:342
  53.8 4.3 %collective-permute-start.6 = (bf16[960,512]{1,0:T(8,128)(2,1)}, bf16[960,512]{1,0:T(8,128)(2,1)}, u32[]{:S(2)}, u32[]{:S(2)}) collective-permute-start(bf16[960,512]{1,0:T(8,128)(2,1)} %collective-permute-done.3), channel_id=1, source_target_pairs={{0,4},{4,0},{8,12},{12,8},{16,20},{20,16},{24,28},{28,24},{1,5},{5... | collective-permute-start | bytes 2949128 | tf_op jit(solution)/shard_map/ppermute | solution.py:342
  54.3 5.2 %collective-permute-start.7 = (bf16[960,512]{1,0:T(8,128)(2,1)}, bf16[960,512]{1,0:T(8,128)(2,1)}, u32[]{:S(2)}, u32[]{:S(2)}) collective-permute-start(bf16[960,512]{1,0:T(8,128)(2,1)} %collective-permute-done.4), channel_id=1, source_target_pairs={{0,4},{4,0},{8,12},{12,8},{16,20},{20,16},{24,28},{28,24},{1,5},{5... | collective-permute-start | bytes 2949128 | tf_op jit(solution)/shard_map/ppermute | solution.py:342
  55.0 17.0 %collective-permute-start.10 = (bf16[1,32,7680]{2,1,0:T(8,128)(2,1)}, bf16[1,32,7680]{2,1,0:T(8,128)(2,1)S(1)}, u32[]{:S(2)}, u32[]{:S(2)}) collective-permute-start(bf16[1,32,7680]{2,1,0:T(8,128)(2,1)} %slice.33), channel_id=1, source_target_pairs={{0,3},{1,0},{2,1},{3,2},{4,7},{5,4},{6,5},{7,6},{8,11},{9,8},{10,9... | collective-permute-start | bytes 1474568 | tf_op jit(solution)/shard_map/ppermute | solution.py:339
  56.7 22.8 %collective-permute-start.9 = (bf16[1,32,7680]{2,1,0:T(8,128)(2,1)S(1)}, bf16[1,32,7680]{2,1,0:T(8,128)(2,1)S(1)}, u32[]{:S(2)}, u32[]{:S(2)}) collective-permute-start(bf16[1,32,7680]{2,1,0:T(8,128)(2,1)S(1)} %slice.32), channel_id=1, source_target_pairs={{0,1},{1,2},{2,3},{3,0},{4,5},{5,6},{6,7},{7,4},{8,9},{9,10},{10,1... | collective-permute-start | bytes 1474568 | tf_op jit(solution)/shard_map/ppermute | solution.py:339
  59.5 2.8 %collective-permute-start.8 = (bf16[960,512]{1,0:T(8,128)(2,1)}, bf16[960,512]{1,0:T(8,128)(2,1)S(1)}, u32[]{:S(2)}, u32[]{:S(2)}) collective-permute-start(bf16[960,512]{1,0:T(8,128)(2,1)} %beside.1), channel_id=1, source_target_pairs={{0,4},{4,0},{8,12},{12,8},{16,20},{20,16},{24,28},{28,24},{1,5},{5... | collective-permute-start | bytes 2949128 | tf_op jit(solution)/shard_map/ppermute | solution.py:342
  61.2 9.0 %copy-start.9 = (bf16[3,2,32,7680]{3,2,1,0:T(8,128)(2,1)}, bf16[3,2,32,7680]{3,2,1,0:T(8,128)(2,1)S(1)}, u32[]{:S(2)}) copy-start(bf16[3,2,32,7680]{3,2,1,0:T(8,128)(2,1)S(1)} %pad_maximum_fusion) | copy-start | bytes 8847364
  71.9 9.1 %copy-start.1 = (bf16[2,2,1024,128]{3,2,1,0:T(8,128)(2,1)S(1)}, bf16[2,2,1024,128]{3,2,1,0:T(8,128)(2,1)}, u32[]{:S(2)}) copy-start(bf16[2,2,1024,128]{3,2,1,0:T(8,128)(2,1)} %get-tuple-element.61.refs_4_) | copy-start | bytes 3145732
  71.9 9.1 %copy-start.2 = (bf16[2,2,1024,128]{3,2,1,0:T(8,128)(2,1)S(1)}, bf16[2,2,1024,128]{3,2,1,0:T(8,128)(2,1)}, u32[]{:S(2)}) copy-start(bf16[2,2,1024,128]{3,2,1,0:T(8,128)(2,1)} %get-tuple-element.62.refs_5_) | copy-start | bytes 3145732
  71.9 9.1 %copy-start.5 = (s32[2]{0:T(128)S(1)}, s32[2]{0:T(128)}, u32[]{:S(2)}) copy-start(s32[2]{0:T(128)} %assignment.1) | copy-start | bytes 28
  71.9 9.1 %copy-start.6 = (s32[2]{0:T(128)S(1)}, s32[2]{0:T(128)}, u32[]{:S(2)}) copy-start(s32[2]{0:T(128)} %tiles.1) | copy-start | bytes 28
  71.9 9.1 %copy-start.7 = (f32[128]{0:T(128)S(1)}, f32[128]{0:T(128)}, u32[]{:S(2)}) copy-start(f32[128]{0:T(128)} %param.17) | copy-start | bytes 1540
  81.0 12.1 %copy-start.10 = (bf16[3,2,32,7680]{3,2,1,0:T(8,128)(2,1)S(1)}, bf16[3,2,32,7680]{3,2,1,0:T(8,128)(2,1)}, u32[]{:S(2)}) copy-start(bf16[3,2,32,7680]{3,2,1,0:T(8,128)(2,1)} %copy-done.9) | copy-start | bytes 8847364
  86.1 7.0 %copy-start = (bf16[2,2,1024,128]{3,2,1,0:T(8,128)(2,1)}, bf16[2,2,1024,128]{3,2,1,0:T(8,128)(2,1)S(1)}, u32[]{:S(2)}) copy-start(bf16[2,2,1024,128]{3,2,1,0:T(8,128)(2,1)S(1)} %get-tuple-element.73.score_grad) | copy-start | bytes 3145732
  86.1 7.0 %copy-start.4 = (bf16[2,2,128,128]{3,2,1,0:T(8,128)(2,1)}, bf16[2,2,128,128]{3,2,1,0:T(8,128)(2,1)S(1)}, u32[]{:S(2)}) copy-start(bf16[2,2,128,128]{3,2,1,0:T(8,128)(2,1)S(1)} %get-tuple-element.74.keys) | copy-start | bytes 393220
  89.2 16.0 %collective-permute-start.11 = (bf16[1,32,7680]{2,1,0:T(8,128)(2,1)S(1)}, bf16[1,32,7680]{2,1,0:T(8,128)(2,1)S(1)}, u32[]{:S(2)}, u32[]{:S(2)}) collective-permute-start(bf16[1,32,7680]{2,1,0:T(8,128)(2,1)S(1)} %get-tuple-element.65), channel_id=1, source_target_pairs={{0,1},{1,2},{2,3},{3,0},{4,5},{5,6},{6,7},{7,4},{8,9},{9,10},{10,1... | collective-permute-start | bytes 1474568 | tf_op jit(solution)/shard_map/ppermute | solution.py:339
  90.9 23.1 %collective-permute-start.12 = (bf16[1,32,7680]{2,1,0:T(8,128)(2,1)S(1)}, bf16[1,32,7680]{2,1,0:T(8,128)(2,1)S(1)}, u32[]{:S(2)}, u32[]{:S(2)}) collective-permute-start(bf16[1,32,7680]{2,1,0:T(8,128)(2,1)S(1)} %get-tuple-element.66), channel_id=1, source_target_pairs={{0,3},{1,0},{2,1},{3,2},{4,7},{5,4},{6,5},{7,6},{8,11},{9,8},{10,9... | collective-permute-start | bytes 1474568 | tf_op jit(solution)/shard_map/ppermute | solution.py:339
  95.9 24.3 %collective-permute-start.15 = (bf16[4,960,512]{2,1,0:T(8,128)(2,1)S(1)}, bf16[4,960,512]{2,1,0:T(8,128)(2,1)S(1)}, u32[]{:S(2)}, u32[]{:S(2)}) collective-permute-start(bf16[4,960,512]{2,1,0:T(8,128)(2,1)S(1)} %dynamic-slice_bitcast_fusion), channel_id=1, source_target_pairs={{0,4},{4,0},{8,12},{12,8},{16,20},{20,16},{24,28},{28,24},{1,5},{5... | collective-permute-start | bytes 11796488 | tf_op jit(solution)/shard_map/ppermute | solution.py:342
  99.5 23.3 %copy-start.3 = (bf16[2,32,7680]{2,1,0:T(8,128)(2,1)}, bf16[2,32,7680]{2,1,0:T(8,128)(2,1)S(1)}, u32[]{:S(2)}) copy-start(bf16[2,32,7680]{2,1,0:T(8,128)(2,1)S(1)} %get-tuple-element.76) | copy-start | bytes 2949124
  116.3 26.8 %collective-permute-start.13 = (bf16[2,32,7680]{2,1,0:T(8,128)(2,1)}, bf16[2,32,7680]{2,1,0:T(8,128)(2,1)}, u32[]{:S(2)}, u32[]{:S(2)}) collective-permute-start(bf16[2,32,7680]{2,1,0:T(8,128)(2,1)} %pad_maximum_fusion.1), channel_id=1, source_target_pairs={{0,1},{1,2},{2,3},{3,0},{4,5},{5,6},{6,7},{7,4},{8,9},{9,10},{10,1... | collective-permute-start | bytes 2949128 | tf_op jit(solution)/shard_map/ppermute | solution.py:339
  116.7 44.1 %collective-permute-start.14 = (bf16[2,32,7680]{2,1,0:T(8,128)(2,1)}, bf16[2,32,7680]{2,1,0:T(8,128)(2,1)}, u32[]{:S(2)}, u32[]{:S(2)}) collective-permute-start(bf16[2,32,7680]{2,1,0:T(8,128)(2,1)} %pad_maximum_fusion.2), channel_id=1, source_target_pairs={{0,3},{1,0},{2,1},{3,2},{4,7},{5,4},{6,5},{7,6},{8,11},{9,8},{10,9... | collective-permute-start | bytes 2949128 | tf_op jit(solution)/shard_map/ppermute | solution.py:339
  122.7 41.2 %collective-permute-start.16 = (bf16[960,512]{1,0:T(8,128)(2,1)}, bf16[960,512]{1,0:T(8,128)(2,1)S(1)}, u32[]{:S(2)}, u32[]{:S(2)}) collective-permute-start(bf16[960,512]{1,0:T(8,128)(2,1)} %get-tuple-element.80), channel_id=1, source_target_pairs={{0,8},{4,12},{8,0},{12,4},{16,24},{20,28},{24,16},{28,20},{1,9},{5... | collective-permute-start | bytes 2949128 | tf_op jit(solution)/shard_map/ppermute | solution.py:342
  124.0 42.0 %collective-permute-start.17 = (bf16[960,512]{1,0:T(8,128)(2,1)}, bf16[960,512]{1,0:T(8,128)(2,1)}, u32[]{:S(2)}, u32[]{:S(2)}) collective-permute-start(bf16[960,512]{1,0:T(8,128)(2,1)} %get-tuple-element.81), channel_id=1, source_target_pairs={{0,16},{4,20},{8,24},{12,28},{16,0},{20,4},{24,8},{28,12},{1,17},{... | collective-permute-start | bytes 2949128 | tf_op jit(solution)/shard_map/ppermute | solution.py:342
  124.8 42.8 %collective-permute-start.18 = (bf16[960,512]{1,0:T(8,128)(2,1)}, bf16[960,512]{1,0:T(8,128)(2,1)}, u32[]{:S(2)}, u32[]{:S(2)}) collective-permute-start(bf16[960,512]{1,0:T(8,128)(2,1)} %get-tuple-element.82), channel_id=1, source_target_pairs={{0,24},{4,28},{8,16},{12,20},{16,8},{20,12},{24,0},{28,4},{1,25},{... | collective-permute-start | bytes 2949128 | tf_op jit(solution)/shard_map/ppermute | solution.py:342

commit v12 on v11

--- a/solution.py
+++ b/solution.py
@@ -212,6 +212,9 @@
     return pl.pallas_call(
         beside_kernel,
         out_shape=jax.ShapeDtypeStruct((rows, 2 * columns), left.dtype),
+        grid=(2,),
+        in_specs=[pl.BlockSpec((rows // 2, columns), lambda i: (i, 0))] * 2,
+        out_specs=pl.BlockSpec((rows // 2, 2 * columns), lambda i: (i, 0)),
         name="beside",
     )(left, right)
 
@@ -245,6 +248,27 @@
         compiler_params=pltpu.CompilerParams(vmem_limit_bytes=16 * 1024 * 1024),
         name="terms",
     )(rows, weight)
+
+
+def total_kernel(own, left, right, out):
+    total = own[...].astype(jnp.float32) + left[...].astype(jnp.float32)
+    out[...] = (total + right[...].astype(jnp.float32)).astype(out.dtype)
+
+
+def total_of(own, left, right):
+    images, own_rows, vis_width = own.shape
+    spec = pl.BlockSpec((images, own_rows, vis_width // 4), lambda i: (0, 0, i))
+    return pl.pallas_call(
+        total_kernel,
+        out_shape=jax.ShapeDtypeStruct(own.shape, own.dtype),
+        grid=(4,),
+        in_specs=[spec] * 3,
+        out_specs=spec,
+        cost_estimate=pl.CostEstimate(
+            flops=2 * own.size, transcendentals=0, bytes_accessed=8 * own.size
+        ),
+        name="total",
+    )(own, left, right)
 
 
 def merge_kernel(place, *refs):
@@ -345,7 +369,10 @@
     query_gain, key_gain = query_gain[None, :], key_gain[None, :]
     normed, masked = before(queries, out_grad, query_gain, lengths, key_heads)
 
-    own_weight = beside(key_weight, value_weight)
+    if pairs != 4:
+        own_weight = jnp.concatenate((key_weight, value_weight), axis=1)
+    else:
+        own_weight = beside(key_weight, value_weight)
     leaving = (from_left[:first], from_right[first:])
     if pairs != 4:
         weight = lax.all_gather(own_weight, "dp", axis=0, tiled=True)
@@ -412,9 +439,7 @@
     from_left, from_right, query_grad = lax.optimization_barrier(
         (from_left, from_right, query_grad)
     )
-    image_grad = (
-        own.astype(jnp.float32) + from_left.astype(jnp.float32) + from_right.astype(jnp.float32)
-    ).astype(jnp.bfloat16)
+    image_grad = total_of(own, from_left, from_right)
     if pairs == 4:
         image_grad, sent = lax.optimization_barrier((image_grad, sent))
         return (query_grad, image_grad, *finish(own_sum, sent))

time: 171 us -> 171 us (level)
  Pallas kernels: 28 us -> 31.8 us
  other arithmetic: 7.63 us -> 4.55 us
    pallas_call x0 -> x1, Pallas kernels: none -> 3.9 us  [total_of(): pl.pallas_call(total_kernel, out_shape=jax.ShapeDtypeStruct(own.shape, ow...]
    convert_element_type x1 -> x0, other arithmetic: 3.09 us -> none  [per_device(): image_grad = (own.astype(jnp.float32) + from_left.astype(jnp.float32) + f...]
  transfers between devices with their start and end apart: 19 -> 19, of which waited for: 13 -> 13; matrix products, arithmetic and copies ran while one was open for 13% -> 11% of each run, Pallas kernels for 10% -> 12%
where the time goes in v12:
time: 171 us; the launch traced here: 170 us
  waiting for transfers between devices  94.5 us (55%)
  Pallas kernels  31.8 us (19%)
  starting transfers between devices  22.6 us (13%)
  local copies, waits for them, and re-layouts  9.94 us (6%)
  matrix products  5.62 us (3%)
  other arithmetic  4.55 us (3%)
    ppermute x8, waiting for transfers between devices, ring(): lax.ppermute(value, 'mp', [(i, (i + step) % mp_size) for i in range(mp_si...  84.1 us
    ppermute x8, starting transfers between devices, ring(): lax.ppermute(value, 'mp', [(i, (i + step) % mp_size) for i in range(mp_si...  14.9 us
    ppermute x11, waiting for transfers between devices, swap(): return lax.ppermute(value, 'dp', [(i, i ^ mask) for i in range(dp_size)])  10.4 us
    dynamic_update_slice x8, local copies, waits for them, and re-layouts, per_device(): lax.dynamic_update_slice_in_dim(weight, source[None], 2 * (pair ^ r) + ha...  7.95 us
    ppermute x11, starting transfers between devices, swap(): return lax.ppermute(value, 'dp', [(i, i ^ mask) for i in range(dp_size)])  7.7 us
    pallas_call x2, Pallas kernels, terms(): pl.pallas_call(functools.partial(terms_kernel, splits), out_shape=[jax.Sh...  6.58 us
    dot_general x3, matrix products, dot(): lax.dot_general(left, right, (((left_dim,), (right_dim,)), ((), ())), pre...  5.62 us
    pallas_call x1, Pallas kernels, attend(): pl.pallas_call(functools.partial(attend_kernel, len(pieces)), out_shape=(...  5.01 us
  transfers between devices with their start and end apart: 19, of which 13 were waited for; matrix products, arithmetic and copies ran while one was open for 11% of the time, Pallas kernels for 12%

profile of v12, /device:TPU:0, one launch (start us, length us, event | category | flops | bytes accessed | tf_op | source)
XLA Modules:
  0.0 170.0 jit_solution(15328822288201827999)
XLA Ops:
  0.6 3.1 %collective-permute-start = (bf16[2,32,7680]{2,1,0:T(8,128)(2,1)}, bf16[2,32,7680]{2,1,0:T(8,128)(2,1)S(1)}, u32[]{:S(2)}, u32[]{:S(2)}) collective-permute-start(bf16[2,32,7680]{2,1,0:T(8,128)(2,1)} %param.13), channel_id=1, source_target_pairs={{0,1},{1,2},{2,3},{3,0},{4,5},{5,6},{6,7},{7,4},{8,9},{9,10},{10,1... | collective-permute-start | bytes 2949128 | tf_op jit(solution)/shard_map/ppermute | solution.py:363
  3.7 2.1 %collective-permute-start.1 = (bf16[2,32,7680]{2,1,0:T(8,128)(2,1)}, bf16[2,32,7680]{2,1,0:T(8,128)(2,1)S(1)}, u32[]{:S(2)}, u32[]{:S(2)}) collective-permute-start(bf16[2,32,7680]{2,1,0:T(8,128)(2,1)} %param.13), channel_id=1, source_target_pairs={{0,3},{1,0},{2,1},{3,2},{4,7},{5,4},{6,5},{7,6},{8,11},{9,8},{10,9... | collective-permute-start | bytes 2949128 | tf_op jit(solution)/shard_map/ppermute | solution.py:363
  5.8 2.1 %beside.1 = bf16[960,512]{1,0:T(8,128)(2,1)} custom-call(bf16[960,256]{1,0:T(8,128)(2,1)} %left.1, bf16[960,256]{1,0:T(8,128)(2,1)} %right.1), custom_call_target="tpu_custom_call" | custom-call | tf_op jit(solution)/shard_map/beside/pallas_call | solution.py:212
  7.9 1.6 collective-permute-start.2
  9.6 1.5 collective-permute-start.3
  11.4 4.8 %before.1 = (bf16[2,2,1024,128]{3,2,1,0:T(8,128)(2,1)}, bf16[2,2,1024,128]{3,2,1,0:T(8,128)(2,1)}) custom-call(s32[2]{0:T(128)} %lengths.1, bf16[2,128,2048]{2,1,0:T(8,128)(2,1)} %query.3, bf16[2,128,2048]{2,1,0:T(8,128)(2,1)} %grad.1, f32[1,128]{1,0:T(1,128)} %bitcast.59), custom_call_target="tpu_custom_call" | custom-call | tf_op jit(solution)/shard_map/before/pallas_call | solution.py:58
  16.3 12.3 %collective-permute-done = bf16[2,32,7680]{2,1,0:T(8,128)(2,1)S(1)} collective-permute-done((bf16[2,32,7680]{2,1,0:T(8,128)(2,1)}, bf16[2,32,7680]{2,1,0:T(8,128)(2,1)S(1)}, u32[]{:S(2)}, u32[]{:S(2)}) %collective-permute-start) | collective-permute-done | bytes 983072 | tf_op jit(solution)/shard_map/ppermute | solution.py:363
  28.6 19.6 %collective-permute-done.1 = bf16[2,32,7680]{2,1,0:T(8,128)(2,1)S(1)} collective-permute-done((bf16[2,32,7680]{2,1,0:T(8,128)(2,1)}, bf16[2,32,7680]{2,1,0:T(8,128)(2,1)S(1)}, u32[]{:S(2)}, u32[]{:S(2)}) %collective-permute-start.1) | collective-permute-done | bytes 983072 | tf_op jit(solution)/shard_map/ppermute | solution.py:363
  48.2 0.8 slice.33
  49.0 4.7 %collective-permute-done.3 = bf16[960,512]{1,0:T(8,128)(2,1)} collective-permute-done((bf16[960,512]{1,0:T(8,128)(2,1)}, bf16[960,512]{1,0:T(8,128)(2,1)}, u32[]{:S(2)}, u32[]{:S(2)}) %collective-permute-start.3) | collective-permute-done | bytes 983072 | tf_op jit(solution)/shard_map/ppermute | solution.py:366
  53.7 0.5 collective-permute-start.6
  54.3 0.7 and_select_fusion.owners
  54.9 1.7 collective-permute-start.10
  57.0 1.1 collective-permute-done.6
  58.1 1.4 collective-permute-done.7
  59.6 1.5 pad_maximum_fusion
  61.1 0.7 broadcast_in_dim.33
  62.3 1.3 bitcast_dynamic-update-slice_fusion.5
  63.6 1.3 bitcast_dynamic-update-slice_fusion.4
  64.9 1.3 bitcast_dynamic-update-slice_fusion.3
  66.2 1.3 bitcast_dynamic-update-slice_fusion.2
  67.5 1.3 bitcast_dynamic-update-slice_fusion.1
  68.8 1.3 bitcast_dynamic-update-slice_fusion
  70.1 1.7 fusion.5
  71.9 7.5 %collective-permute-done.9 = bf16[1,32,7680]{2,1,0:T(8,128)(2,1)S(1)} collective-permute-done((bf16[1,32,7680]{2,1,0:T(8,128)(2,1)S(1)}, bf16[1,32,7680]{2,1,0:T(8,128)(2,1)S(1)}, u32[]{:S(2)}, u32[]{:S(2)}) %collective-permute-start.9) | collective-permute-done | bytes 491552 | tf_op jit(solution)/shard_map/ppermute | solution.py:363
  79.5 1.5 convolution_bitcast_fusion.refs_1_.refs_3_
  81.0 5.0 %attend.1 = (bf16[4,2,32,512]{3,2,1,0:T(8,128)(2,1)S(1)}, bf16[2,2,1024,128]{3,2,1,0:T(8,128)(2,1)S(1)}, bf16[2,2,128,128]{3,2,1,0:T(8,128)(2,1)S(1)}) custom-call(s32[2]{0:T(128)S(1)} %copy-done.5, s32[2]{0:T(128)S(1)} %copy-done.6, s32[4]{0:T(128)S(1)} %and_select_fusion.owners, f32[3,2,32,512]{3,2,1,0:T(8,128)S(1)} %bitcast.49, ...), custom_call_target="tpu_custom_call" | custom-call | tf_op jit(solution)/shard_map/attend/pallas_call | solution.py:141
  86.0 3.1 %terms.3 = (bf16[1,32,7680]{2,1,0:T(8,128)(2,1)S(1)}, bf16[1,32,7680]{2,1,0:T(8,128)(2,1)S(1)}) custom-call(bf16[1,2,32,512]{3,2,1,0:T(8,128)(2,1)S(1)} %slice.28.rows, bf16[7680,512]{1,0:T(8,128)(2,1)S(1)} %bitcast.47), custom_call_target="tpu_custom_call" | custom-call | tf_op jit(solution)/shard_map/terms/pallas_call | solution.py:235
  89.1 1.7 collective-permute-start.11
  90.8 2.2 %collective-permute-start.12 = (bf16[1,32,7680]{2,1,0:T(8,128)(2,1)S(1)}, bf16[1,32,7680]{2,1,0:T(8,128)(2,1)S(1)}, u32[]{:S(2)}, u32[]{:S(2)}) collective-permute-start(bf16[1,32,7680]{2,1,0:T(8,128)(2,1)S(1)} %get-tuple-element.66), channel_id=1, source_target_pairs={{0,3},{1,0},{2,1},{3,2},{4,7},{5,4},{6,5},{7,6},{8,11},{9,8},{10,9... | collective-permute-start | bytes 1474568 | tf_op jit(solution)/shard_map/ppermute | solution.py:363
  93.0 2.5 %convolution_convert_fusion = bf16[7680,512]{1,0:T(8,128)(2,1)S(1)} fusion(bf16[256,512]{1,0:T(8,128)(2,1)S(1)} %bitcast.51, bf16[64,7680]{1,0:T(8,128)(2,1)S(1)} %bitcast.53, bf16[192,7680]{1,0:T(8,128)(2,1)S(1)} %bitcast.55), kind=kOutput, calls=%fused_computation | convolution fusion | flops 2025062400 | bytes 12058624 | tf_op jit(solution)/shard_map/dot_general | solution.py:29
  96.0 3.5 %terms.2 = (bf16[2,32,7680]{2,1,0:T(8,128)(2,1)S(1)}, bf16[2,32,7680]{2,1,0:T(8,128)(2,1)S(1)}, bf16[2,32,7680]{2,1,0:T(8,128)(2,1)S(1)}) custom-call(bf16[3,2,32,512]{3,2,1,0:T(8,128)(2,1)S(1)} %slice.26.rows, bf16[7680,512]{1,0:T(8,128)(2,1)S(1)} %bitcast.48), custom_call_target="tpu_custom_call" | custom-call | tf_op jit(solution)/shard_map/terms/pallas_call | solution.py:235
  99.6 5.6 %collective-permute-done.11 = bf16[1,32,7680]{2,1,0:T(8,128)(2,1)S(1)} collective-permute-done((bf16[1,32,7680]{2,1,0:T(8,128)(2,1)S(1)}, bf16[1,32,7680]{2,1,0:T(8,128)(2,1)S(1)}, u32[]{:S(2)}, u32[]{:S(2)}) %collective-permute-start.11) | collective-permute-done | bytes 491552 | tf_op jit(solution)/shard_map/ppermute | solution.py:363
  105.1 8.8 %collective-permute-done.12 = bf16[1,32,7680]{2,1,0:T(8,128)(2,1)S(1)} collective-permute-done((bf16[1,32,7680]{2,1,0:T(8,128)(2,1)S(1)}, bf16[1,32,7680]{2,1,0:T(8,128)(2,1)S(1)}, u32[]{:S(2)}, u32[]{:S(2)}) %collective-permute-start.12) | collective-permute-done | bytes 491552 | tf_op jit(solution)/shard_map/ppermute | solution.py:363
  114.1 1.0 pad_maximum_fusion.2
  115.2 1.0 pad_maximum_fusion.1
  116.6 3.5 %collective-permute-start.14 = (bf16[2,32,7680]{2,1,0:T(8,128)(2,1)}, bf16[2,32,7680]{2,1,0:T(8,128)(2,1)}, u32[]{:S(2)}, u32[]{:S(2)}) collective-permute-start(bf16[2,32,7680]{2,1,0:T(8,128)(2,1)} %pad_maximum_fusion.2), channel_id=1, source_target_pairs={{0,3},{1,0},{2,1},{3,2},{4,7},{5,4},{6,5},{7,6},{8,11},{9,8},{10,9... | collective-permute-start | bytes 2949128 | tf_op jit(solution)/shard_map/ppermute | solution.py:363
  120.0 2.5 %merge.1 = (f32[960,512]{1,0:T(8,128)S(1)}, bf16[960,512]{1,0:T(8,128)(2,1)}, bf16[960,512]{1,0:T(8,128)(2,1)}, bf16[960,512]{1,0:T(8,128)(2,1)}) custom-call(s32[2]{0:T(128)S(1)} %pad_add_fusion.place, bf16[4,2,960,512]{3,2,1,0:T(8,128)(2,1)S(1)} %bitcast.41, bf16[4,2,960,512]{3,2,1,0:T(8,128)(2,1)S(1)} %bitcast.42, bf16[4,2,960,512]{3,2,1,0:T(8,128)(2,1)S(1)} %bitcast.43, ...), custom_call_target="tpu_custom_call" | custom-call | tf_op jit(solution)/shard_map/merge/pallas_call | solution.py:308
  122.5 1.2 collective-permute-start.16
  123.8 0.8 collective-permute-start.17
  124.6 1.4 collective-permute-start.18
  126.0 4.3 %after.1 = bf16[2,128,2048]{2,1,0:T(8,128)(2,1)} custom-call(bf16[2,128,2048]{2,1,0:T(8,128)(2,1)} %query.3, bf16[2,2,1024,128]{3,2,1,0:T(8,128)(2,1)} %copy-done, bf16[2,2,128,128]{3,2,1,0:T(8,128)(2,1)} %copy-done.4, f32[1,128]{1,0:T(1,128)} %bitcast.60), custom_call_target="tpu_custom_call" | custom-call | tf_op jit(solution)/shard_map/after/pallas_call | solution.py:189
  130.3 12.7 %collective-permute-done.13.left = bf16[2,32,7680]{2,1,0:T(8,128)(2,1)} collective-permute-done((bf16[2,32,7680]{2,1,0:T(8,128)(2,1)}, bf16[2,32,7680]{2,1,0:T(8,128)(2,1)}, u32[]{:S(2)}, u32[]{:S(2)}) %collective-permute-start.13) | collective-permute-done | bytes 983072 | tf_op jit(solution)/shard_map/ppermute | solution.py:363
  143.0 17.7 %collective-permute-done.14.right = bf16[2,32,7680]{2,1,0:T(8,128)(2,1)} collective-permute-done((bf16[2,32,7680]{2,1,0:T(8,128)(2,1)}, bf16[2,32,7680]{2,1,0:T(8,128)(2,1)}, u32[]{:S(2)}, u32[]{:S(2)}) %collective-permute-start.14) | collective-permute-done | bytes 983072 | tf_op jit(solution)/shard_map/ppermute | solution.py:363
  160.7 3.9 %total.1 = bf16[2,32,7680]{2,1,0:T(8,128)(2,1)} custom-call(bf16[2,32,7680]{2,1,0:T(8,128)(2,1)} %copy-done.3, bf16[2,32,7680]{2,1,0:T(8,128)(2,1)} %collective-permute-done.13.left, bf16[2,32,7680]{2,1,0:T(8,128)(2,1)} %collective-permute-done.14.right), custom_call_target="tpu_custom_call" | custom-call | flops 983040 | bytes 3932160 | tf_op jit(solution)/shard_map/total/pallas_call | solution.py:261
  164.6 1.2 collective-permute-done.17.refs_1_
  165.8 1.6 collective-permute-done.18.refs_2_
  167.4 2.6 %finish.1 = (f32[960,256]{1,0:T(8,128)}, f32[960,256]{1,0:T(8,128)}) custom-call(f32[960,512]{1,0:T(8,128)S(1)} %get-tuple-element.84.own, bf16[960,512]{1,0:T(8,128)(2,1)S(1)} %collective-permute-done.16.refs_0_, bf16[960,512]{1,0:T(8,128)(2,1)} %collective-permute-done.17.refs_1_, bf16[960,512]{1,0:T(8,128)(2,1)} %collective-permute-done.18.refs_2_), custom_call_target="tpu_custom_call" | custom-call | tf_op jit(solution)/shard_map/finish/pallas_call | solution.py:326
  (48 shorter events, 2.6 us)
Async XLA Ops:
  0.6 27.9 %collective-permute-start = (bf16[2,32,7680]{2,1,0:T(8,128)(2,1)}, bf16[2,32,7680]{2,1,0:T(8,128)(2,1)S(1)}, u32[]{:S(2)}, u32[]{:S(2)}) collective-permute-start(bf16[2,32,7680]{2,1,0:T(8,128)(2,1)} %param.13), channel_id=1, source_target_pairs={{0,1},{1,2},{2,3},{3,0},{4,5},{5,6},{6,7},{7,4},{8,9},{9,10},{10,1... | collective-permute-start | bytes 2949128 | tf_op jit(solution)/shard_map/ppermute | solution.py:363
  3.7 44.5 %collective-permute-start.1 = (bf16[2,32,7680]{2,1,0:T(8,128)(2,1)}, bf16[2,32,7680]{2,1,0:T(8,128)(2,1)S(1)}, u32[]{:S(2)}, u32[]{:S(2)}) collective-permute-start(bf16[2,32,7680]{2,1,0:T(8,128)(2,1)} %param.13), channel_id=1, source_target_pairs={{0,3},{1,0},{2,1},{3,2},{4,7},{5,4},{6,5},{7,6},{8,11},{9,8},{10,9... | collective-permute-start | bytes 2949128 | tf_op jit(solution)/shard_map/ppermute | solution.py:363
  7.9 41.1 %collective-permute-start.2 = (bf16[960,512]{1,0:T(8,128)(2,1)}, bf16[960,512]{1,0:T(8,128)(2,1)}, u32[]{:S(2)}, u32[]{:S(2)}) collective-permute-start(bf16[960,512]{1,0:T(8,128)(2,1)} %beside.1), channel_id=1, source_target_pairs={{0,8},{4,12},{8,0},{12,4},{16,24},{20,28},{24,16},{28,20},{1,9},{5... | collective-permute-start | bytes 2949128 | tf_op jit(solution)/shard_map/ppermute | solution.py:366
  9.6 44.2 %collective-permute-start.3 = (bf16[960,512]{1,0:T(8,128)(2,1)}, bf16[960,512]{1,0:T(8,128)(2,1)}, u32[]{:S(2)}, u32[]{:S(2)}) collective-permute-start(bf16[960,512]{1,0:T(8,128)(2,1)} %beside.1), channel_id=1, source_target_pairs={{0,16},{4,20},{8,24},{12,28},{16,0},{20,4},{24,8},{28,12},{1,17},{... | collective-permute-start | bytes 2949128 | tf_op jit(solution)/shard_map/ppermute | solution.py:366
  11.1 42.6 %collective-permute-start.4 = (bf16[960,512]{1,0:T(8,128)(2,1)}, bf16[960,512]{1,0:T(8,128)(2,1)}, u32[]{:S(2)}, u32[]{:S(2)}) collective-permute-start(bf16[960,512]{1,0:T(8,128)(2,1)} %beside.1), channel_id=1, source_target_pairs={{0,24},{4,28},{8,16},{12,20},{16,8},{20,12},{24,0},{28,4},{1,25},{... | collective-permute-start | bytes 2949128 | tf_op jit(solution)/shard_map/ppermute | solution.py:366
  16.2 45.6 %copy-start.8 = (bf16[960,512]{1,0:T(8,128)(2,1)S(1)}, bf16[960,512]{1,0:T(8,128)(2,1)}, u32[]{:S(2)}) copy-start(bf16[960,512]{1,0:T(8,128)(2,1)} %beside.1) | copy-start | bytes 2949124
  53.7 3.2 %collective-permute-start.5 = (bf16[960,512]{1,0:T(8,128)(2,1)}, bf16[960,512]{1,0:T(8,128)(2,1)}, u32[]{:S(2)}, u32[]{:S(2)}) collective-permute-start(bf16[960,512]{1,0:T(8,128)(2,1)} %collective-permute-done.2), channel_id=1, source_target_pairs={{0,4},{4,0},{8,12},{12,8},{16,20},{20,16},{24,28},{28,24},{1,5},{5... | collective-permute-start | bytes 2949128 | tf_op jit(solution)/shard_map/ppermute | solution.py:366
  53.7 4.3 %collective-permute-start.6 = (bf16[960,512]{1,0:T(8,128)(2,1)}, bf16[960,512]{1,0:T(8,128)(2,1)}, u32[]{:S(2)}, u32[]{:S(2)}) collective-permute-start(bf16[960,512]{1,0:T(8,128)(2,1)} %collective-permute-done.3), channel_id=1, source_target_pairs={{0,4},{4,0},{8,12},{12,8},{16,20},{20,16},{24,28},{28,24},{1,5},{5... | collective-permute-start | bytes 2949128 | tf_op jit(solution)/shard_map/ppermute | solution.py:366
  54.3 5.2 %collective-permute-start.7 = (bf16[960,512]{1,0:T(8,128)(2,1)}, bf16[960,512]{1,0:T(8,128)(2,1)}, u32[]{:S(2)}, u32[]{:S(2)}) collective-permute-start(bf16[960,512]{1,0:T(8,128)(2,1)} %collective-permute-done.4), channel_id=1, source_target_pairs={{0,4},{4,0},{8,12},{12,8},{16,20},{20,16},{24,28},{28,24},{1,5},{5... | collective-permute-start | bytes 2949128 | tf_op jit(solution)/shard_map/ppermute | solution.py:366
  54.9 17.0 %collective-permute-start.10 = (bf16[1,32,7680]{2,1,0:T(8,128)(2,1)}, bf16[1,32,7680]{2,1,0:T(8,128)(2,1)S(1)}, u32[]{:S(2)}, u32[]{:S(2)}) collective-permute-start(bf16[1,32,7680]{2,1,0:T(8,128)(2,1)} %slice.33), channel_id=1, source_target_pairs={{0,3},{1,0},{2,1},{3,2},{4,7},{5,4},{6,5},{7,6},{8,11},{9,8},{10,9... | collective-permute-start | bytes 1474568 | tf_op jit(solution)/shard_map/ppermute | solution.py:363
  56.6 22.8 %collective-permute-start.9 = (bf16[1,32,7680]{2,1,0:T(8,128)(2,1)S(1)}, bf16[1,32,7680]{2,1,0:T(8,128)(2,1)S(1)}, u32[]{:S(2)}, u32[]{:S(2)}) collective-permute-start(bf16[1,32,7680]{2,1,0:T(8,128)(2,1)S(1)} %slice.32), channel_id=1, source_target_pairs={{0,1},{1,2},{2,3},{3,0},{4,5},{5,6},{6,7},{7,4},{8,9},{9,10},{10,1... | collective-permute-start | bytes 1474568 | tf_op jit(solution)/shard_map/ppermute | solution.py:363
  59.5 2.8 %collective-permute-start.8 = (bf16[960,512]{1,0:T(8,128)(2,1)}, bf16[960,512]{1,0:T(8,128)(2,1)S(1)}, u32[]{:S(2)}, u32[]{:S(2)}) collective-permute-start(bf16[960,512]{1,0:T(8,128)(2,1)} %beside.1), channel_id=1, source_target_pairs={{0,4},{4,0},{8,12},{12,8},{16,20},{20,16},{24,28},{28,24},{1,5},{5... | collective-permute-start | bytes 2949128 | tf_op jit(solution)/shard_map/ppermute | solution.py:366
  61.1 9.0 %copy-start.9 = (bf16[3,2,32,7680]{3,2,1,0:T(8,128)(2,1)}, bf16[3,2,32,7680]{3,2,1,0:T(8,128)(2,1)S(1)}, u32[]{:S(2)}) copy-start(bf16[3,2,32,7680]{3,2,1,0:T(8,128)(2,1)S(1)} %pad_maximum_fusion) | copy-start | bytes 8847364
  71.8 9.1 %copy-start.1 = (bf16[2,2,1024,128]{3,2,1,0:T(8,128)(2,1)S(1)}, bf16[2,2,1024,128]{3,2,1,0:T(8,128)(2,1)}, u32[]{:S(2)}) copy-start(bf16[2,2,1024,128]{3,2,1,0:T(8,128)(2,1)} %get-tuple-element.61.refs_4_) | copy-start | bytes 3145732
  71.8 9.1 %copy-start.2 = (bf16[2,2,1024,128]{3,2,1,0:T(8,128)(2,1)S(1)}, bf16[2,2,1024,128]{3,2,1,0:T(8,128)(2,1)}, u32[]{:S(2)}) copy-start(bf16[2,2,1024,128]{3,2,1,0:T(8,128)(2,1)} %get-tuple-element.62.refs_5_) | copy-start | bytes 3145732
  71.8 9.1 %copy-start.5 = (s32[2]{0:T(128)S(1)}, s32[2]{0:T(128)}, u32[]{:S(2)}) copy-start(s32[2]{0:T(128)} %assignment.1) | copy-start | bytes 28
  71.9 9.1 %copy-start.6 = (s32[2]{0:T(128)S(1)}, s32[2]{0:T(128)}, u32[]{:S(2)}) copy-start(s32[2]{0:T(128)} %tiles.1) | copy-start | bytes 28
  71.9 9.1 %copy-start.7 = (f32[128]{0:T(128)S(1)}, f32[128]{0:T(128)}, u32[]{:S(2)}) copy-start(f32[128]{0:T(128)} %param.17) | copy-start | bytes 1540
  80.9 12.1 %copy-start.10 = (bf16[3,2,32,7680]{3,2,1,0:T(8,128)(2,1)S(1)}, bf16[3,2,32,7680]{3,2,1,0:T(8,128)(2,1)}, u32[]{:S(2)}) copy-start(bf16[3,2,32,7680]{3,2,1,0:T(8,128)(2,1)} %copy-done.9) | copy-start | bytes 8847364
  86.0 7.0 %copy-start = (bf16[2,2,1024,128]{3,2,1,0:T(8,128)(2,1)}, bf16[2,2,1024,128]{3,2,1,0:T(8,128)(2,1)S(1)}, u32[]{:S(2)}) copy-start(bf16[2,2,1024,128]{3,2,1,0:T(8,128)(2,1)S(1)} %get-tuple-element.73.score_grad) | copy-start | bytes 3145732
  86.0 7.0 %copy-start.4 = (bf16[2,2,128,128]{3,2,1,0:T(8,128)(2,1)}, bf16[2,2,128,128]{3,2,1,0:T(8,128)(2,1)S(1)}, u32[]{:S(2)}) copy-start(bf16[2,2,128,128]{3,2,1,0:T(8,128)(2,1)S(1)} %get-tuple-element.74.keys) | copy-start | bytes 393220
  89.1 16.0 %collective-permute-start.11 = (bf16[1,32,7680]{2,1,0:T(8,128)(2,1)S(1)}, bf16[1,32,7680]{2,1,0:T(8,128)(2,1)S(1)}, u32[]{:S(2)}, u32[]{:S(2)}) collective-permute-start(bf16[1,32,7680]{2,1,0:T(8,128)(2,1)S(1)} %get-tuple-element.65), channel_id=1, source_target_pairs={{0,1},{1,2},{2,3},{3,0},{4,5},{5,6},{6,7},{7,4},{8,9},{9,10},{10,1... | collective-permute-start | bytes 1474568 | tf_op jit(solution)/shard_map/ppermute | solution.py:363
  90.8 23.1 %collective-permute-start.12 = (bf16[1,32,7680]{2,1,0:T(8,128)(2,1)S(1)}, bf16[1,32,7680]{2,1,0:T(8,128)(2,1)S(1)}, u32[]{:S(2)}, u32[]{:S(2)}) collective-permute-start(bf16[1,32,7680]{2,1,0:T(8,128)(2,1)S(1)} %get-tuple-element.66), channel_id=1, source_target_pairs={{0,3},{1,0},{2,1},{3,2},{4,7},{5,4},{6,5},{7,6},{8,11},{9,8},{10,9... | collective-permute-start | bytes 1474568 | tf_op jit(solution)/shard_map/ppermute | solution.py:363
  95.8 24.3 %collective-permute-start.15 = (bf16[4,960,512]{2,1,0:T(8,128)(2,1)S(1)}, bf16[4,960,512]{2,1,0:T(8,128)(2,1)S(1)}, u32[]{:S(2)}, u32[]{:S(2)}) collective-permute-start(bf16[4,960,512]{2,1,0:T(8,128)(2,1)S(1)} %dynamic-slice_bitcast_fusion), channel_id=1, source_target_pairs={{0,4},{4,0},{8,12},{12,8},{16,20},{20,16},{24,28},{28,24},{1,5},{5... | collective-permute-start | bytes 11796488 | tf_op jit(solution)/shard_map/ppermute | solution.py:366
  99.5 23.1 %copy-start.3 = (bf16[2,32,7680]{2,1,0:T(8,128)(2,1)}, bf16[2,32,7680]{2,1,0:T(8,128)(2,1)S(1)}, u32[]{:S(2)}) copy-start(bf16[2,32,7680]{2,1,0:T(8,128)(2,1)S(1)} %get-tuple-element.76.own) | copy-start | bytes 2949124
  116.2 26.8 %collective-permute-start.13 = (bf16[2,32,7680]{2,1,0:T(8,128)(2,1)}, bf16[2,32,7680]{2,1,0:T(8,128)(2,1)}, u32[]{:S(2)}, u32[]{:S(2)}) collective-permute-start(bf16[2,32,7680]{2,1,0:T(8,128)(2,1)} %pad_maximum_fusion.1), channel_id=1, source_target_pairs={{0,1},{1,2},{2,3},{3,0},{4,5},{5,6},{6,7},{7,4},{8,9},{9,10},{10,1... | collective-permute-start | bytes 2949128 | tf_op jit(solution)/shard_map/ppermute | solution.py:363
  116.6 44.1 %collective-permute-start.14 = (bf16[2,32,7680]{2,1,0:T(8,128)(2,1)}, bf16[2,32,7680]{2,1,0:T(8,128)(2,1)}, u32[]{:S(2)}, u32[]{:S(2)}) collective-permute-start(bf16[2,32,7680]{2,1,0:T(8,128)(2,1)} %pad_maximum_fusion.2), channel_id=1, source_target_pairs={{0,3},{1,0},{2,1},{3,2},{4,7},{5,4},{6,5},{7,6},{8,11},{9,8},{10,9... | collective-permute-start | bytes 2949128 | tf_op jit(solution)/shard_map/ppermute | solution.py:363
  122.5 42.1 %collective-permute-start.16 = (bf16[960,512]{1,0:T(8,128)(2,1)}, bf16[960,512]{1,0:T(8,128)(2,1)S(1)}, u32[]{:S(2)}, u32[]{:S(2)}) collective-permute-start(bf16[960,512]{1,0:T(8,128)(2,1)} %get-tuple-element.80), channel_id=1, source_target_pairs={{0,8},{4,12},{8,0},{12,4},{16,24},{20,28},{24,16},{28,20},{1,9},{5... | collective-permute-start | bytes 2949128 | tf_op jit(solution)/shard_map/ppermute | solution.py:366
  123.8 42.0 %collective-permute-start.17 = (bf16[960,512]{1,0:T(8,128)(2,1)}, bf16[960,512]{1,0:T(8,128)(2,1)}, u32[]{:S(2)}, u32[]{:S(2)}) collective-permute-start(bf16[960,512]{1,0:T(8,128)(2,1)} %get-tuple-element.81), channel_id=1, source_target_pairs={{0,16},{4,20},{8,24},{12,28},{16,0},{20,4},{24,8},{28,12},{1,17},{... | collective-permute-start | bytes 2949128 | tf_op jit(solution)/shard_map/ppermute | solution.py:366
  124.6 42.8 %collective-permute-start.18 = (bf16[960,512]{1,0:T(8,128)(2,1)}, bf16[960,512]{1,0:T(8,128)(2,1)}, u32[]{:S(2)}, u32[]{:S(2)}) collective-permute-start(bf16[960,512]{1,0:T(8,128)(2,1)} %get-tuple-element.82), channel_id=1, source_target_pairs={{0,24},{4,28},{8,16},{12,20},{16,8},{20,12},{24,0},{28,4},{1,25},{... | collective-permute-start | bytes 2949128 | tf_op jit(solution)/shard_map/ppermute | solution.py:366

commit v13 on v10

--- a/solution.py
+++ b/solution.py
@@ -277,10 +277,10 @@
     )
 
 
-def merge(held, given, place):
-    pairs, _, own_width, cols = held.shape
-    specs = [held_specs(own_width, cols, 2, r) for r in range(pairs)]
-    kinds = [jnp.float32] + [jnp.bfloat16] * (pairs - 1)
+def merge(held, given, place, others, kind):
+    own_width, cols = held.shape[2:]
+    specs = [held_specs(own_width, cols, 2, r) for r in others]
+    kinds = [kind] * len(specs)
     return pl.pallas_call(
         merge_kernel,
         out_shape=[jax.ShapeDtypeStruct((own_width, cols), kind) for kind in kinds],
@@ -378,7 +378,7 @@
         [near_total, far_total], normed, masked, key_gain, assignment, tile_counts, owners
     )
     halves = ((0, 0, first), (0, first, img_count))
-    leaving_right, leaving_left = terms(rows[3:], weight, halves, 4)
+    leaving_right, leaving_left = terms(rows[3:], weight, halves, 2)
     wholes = tuple((part, 0, img_count) for part in range(3))
     own, to_left, to_right = terms(rows[:3], weight, wholes, 4)
 
@@ -406,7 +406,10 @@
         given, to_right, to_left, score_grad = lax.optimization_barrier(
             (given, to_right, to_left, score_grad)
         )
-        own_sum, *sent = merge(weight_part, given, jnp.stack((core, pair)))
+        where = jnp.stack((core, pair))
+        sent = merge(weight_part, given, where, range(1, pairs), jnp.bfloat16)
+        given, score_grad, sent = lax.optimization_barrier((given, score_grad, sent))
+        (own_sum,) = merge(weight_part, given, where, (0,), jnp.float32)
         sent = [swap(piece, 2 * r) for r, piece in enumerate(sent, 1)]
     query_grad = after(queries, score_grad, seq_keys, query_gain)
     from_left, from_right, query_grad = lax.optimization_barrier(

time: 169 us -> 208 us (1.23)
  waiting for transfers between devices: 92.5 us -> 133 us
    ppermute x10, waiting for transfers between devices: 4.21 us -> 41.8 us  [swap(): return lax.ppermute(value, 'dp', [(i, i ^ mask) for i in range(dp_size)])]
    ppermute x8, waiting for transfers between devices: 88.3 us -> 91.4 us  [ring(): lax.ppermute(value, 'mp', [(i, (i + step) % mp_size) for i in range(mp_si...]
  transfers between devices with their start and end apart: 18 -> 18, of which waited for: 12 -> 13; matrix products, arithmetic and copies ran while one was open for 12% -> 9% of each run, Pallas kernels for 10% -> 8%
where the time goes in v13:
time: 208 us
  waiting for transfers between devices  133 us (64%)
  Pallas kernels  26.1 us (13%)
  starting transfers between devices  24.4 us (12%)
  local copies, waits for them, and re-layouts  10.1 us (5%)
  other arithmetic  7.16 us (3%)
  matrix products  5.61 us (3%)
    ppermute x8, waiting for transfers between devices, ring(): lax.ppermute(value, 'mp', [(i, (i + step) % mp_size) for i in range(mp_si...  91.4 us
    ppermute x10, waiting for transfers between devices, swap(): return lax.ppermute(value, 'dp', [(i, i ^ mask) for i in range(dp_size)])  41.8 us
    ppermute x8, starting transfers between devices, ring(): lax.ppermute(value, 'mp', [(i, (i + step) % mp_size) for i in range(mp_si...  16.7 us
    ppermute x10, starting transfers between devices, swap(): return lax.ppermute(value, 'dp', [(i, i ^ mask) for i in range(dp_size)])  7.67 us
    dynamic_update_slice x8, local copies, waits for them, and re-layouts, per_device(): lax.dynamic_update_slice_in_dim(weight, source[k:k + 1], 2 * (pair ^ r +...  6.29 us
    pallas_call x2, Pallas kernels, terms(): pl.pallas_call(functools.partial(terms_kernel, splits), out_shape=[jax.Sh...  6.15 us
    dot_general x3, matrix products, dot(): lax.dot_general(left, right, (((left_dim,), (right_dim,)), ((), ())), pre...  5.61 us
    pallas_call x1, Pallas kernels, attend(): pl.pallas_call(functools.partial(attend_kernel, len(pieces)), out_shape=(...  5 us
  transfers between devices with their start and end apart: 18, of which 13 were waited for; matrix products, arithmetic and copies ran while one was open for 9% of the time, Pallas kernels for 8%

profile of v13, /device:TPU:0, one launch (start us, length us, event | category | flops | bytes accessed | tf_op | source)
XLA Modules:
  0.0 207.6 jit_solution(16914734022057873244)
XLA Ops:
  0.6 3.1 %collective-permute-start = (bf16[2,32,7680]{2,1,0:T(8,128)(2,1)}, bf16[2,32,7680]{2,1,0:T(8,128)(2,1)S(1)}, u32[]{:S(2)}, u32[]{:S(2)}) collective-permute-start(bf16[2,32,7680]{2,1,0:T(8,128)(2,1)} %param.13), channel_id=1, source_target_pairs={{0,1},{1,2},{2,3},{3,0},{4,5},{5,6},{6,7},{7,4},{8,9},{9,10},{10,1... | collective-permute-start | bytes 2949128 | tf_op jit(solution)/shard_map/ppermute | solution.py:339
  3.7 2.1 %collective-permute-start.1 = (bf16[2,32,7680]{2,1,0:T(8,128)(2,1)}, bf16[2,32,7680]{2,1,0:T(8,128)(2,1)S(1)}, u32[]{:S(2)}, u32[]{:S(2)}) collective-permute-start(bf16[2,32,7680]{2,1,0:T(8,128)(2,1)} %param.13), channel_id=1, source_target_pairs={{0,3},{1,0},{2,1},{3,2},{4,7},{5,4},{6,5},{7,6},{8,11},{9,8},{10,9... | collective-permute-start | bytes 2949128 | tf_op jit(solution)/shard_map/ppermute | solution.py:339
  5.8 2.2 %beside.1 = bf16[960,512]{1,0:T(8,128)(2,1)} custom-call(bf16[960,256]{1,0:T(8,128)(2,1)} %left.1, bf16[960,256]{1,0:T(8,128)(2,1)} %right.1), custom_call_target="tpu_custom_call" | custom-call | tf_op jit(solution)/shard_map/beside/pallas_call | solution.py:212
  8.0 1.6 collective-permute-start.2
  9.7 1.5 collective-permute-start.3
  11.5 4.8 %before.1 = (bf16[2,2,1024,128]{3,2,1,0:T(8,128)(2,1)}, bf16[2,2,1024,128]{3,2,1,0:T(8,128)(2,1)}) custom-call(s32[2]{0:T(128)} %lengths.1, bf16[2,128,2048]{2,1,0:T(8,128)(2,1)} %query.3, bf16[2,128,2048]{2,1,0:T(8,128)(2,1)} %grad.1, f32[1,128]{1,0:T(1,128)} %bitcast.51), custom_call_target="tpu_custom_call" | custom-call | tf_op jit(solution)/shard_map/before/pallas_call | solution.py:58
  16.3 12.3 %collective-permute-done = bf16[2,32,7680]{2,1,0:T(8,128)(2,1)S(1)} collective-permute-done((bf16[2,32,7680]{2,1,0:T(8,128)(2,1)}, bf16[2,32,7680]{2,1,0:T(8,128)(2,1)S(1)}, u32[]{:S(2)}, u32[]{:S(2)}) %collective-permute-start) | collective-permute-done | bytes 983072 | tf_op jit(solution)/shard_map/ppermute | solution.py:339
  28.6 19.6 %collective-permute-done.1 = bf16[2,32,7680]{2,1,0:T(8,128)(2,1)S(1)} collective-permute-done((bf16[2,32,7680]{2,1,0:T(8,128)(2,1)}, bf16[2,32,7680]{2,1,0:T(8,128)(2,1)S(1)}, u32[]{:S(2)}, u32[]{:S(2)}) %collective-permute-start.1) | collective-permute-done | bytes 983072 | tf_op jit(solution)/shard_map/ppermute | solution.py:339
  48.2 0.9 slice.49
  49.3 0.8 copy-done.15
  50.1 1.7 pad_maximum_fusion.1
  51.8 2.1 collective-permute-done.3
  53.9 0.5 collective-permute-start.6
  54.5 3.8 %collective-permute-start.9 = (bf16[1,32,7680]{2,1,0:T(8,128)(2,1)}, bf16[1,32,7680]{2,1,0:T(8,128)(2,1)S(1)}, u32[]{:S(2)}, u32[]{:S(2)}) collective-permute-start(bf16[1,32,7680]{2,1,0:T(8,128)(2,1)} %slice.49), channel_id=1, source_target_pairs={{0,3},{1,0},{2,1},{3,2},{4,7},{5,4},{6,5},{7,6},{8,11},{9,8},{10,9... | collective-permute-start | bytes 1474568 | tf_op jit(solution)/shard_map/ppermute | solution.py:339
  58.3 0.7 broadcast_in_dim.16
  59.6 2.0 slice_dynamic-update-slice_fusion.1
  61.7 1.3 slice_dynamic-update-slice_fusion
  63.0 1.3 constant_dynamic-update-slice_fusion.5
  64.4 1.3 constant_dynamic-update-slice_fusion.3
  65.9 1.7 fusion.5
  67.6 2.8 %collective-permute-done.8 = bf16[1,32,7680]{2,1,0:T(8,128)(2,1)S(1)} collective-permute-done((bf16[1,32,7680]{2,1,0:T(8,128)(2,1)S(1)}, bf16[1,32,7680]{2,1,0:T(8,128)(2,1)S(1)}, u32[]{:S(2)}, u32[]{:S(2)}) %collective-permute-start.8) | collective-permute-done | bytes 491552 | tf_op jit(solution)/shard_map/ppermute | solution.py:339
  70.4 8.4 %collective-permute-done.9 = bf16[1,32,7680]{2,1,0:T(8,128)(2,1)S(1)} collective-permute-done((bf16[1,32,7680]{2,1,0:T(8,128)(2,1)}, bf16[1,32,7680]{2,1,0:T(8,128)(2,1)S(1)}, u32[]{:S(2)}, u32[]{:S(2)}) %collective-permute-start.9) | collective-permute-done | bytes 491552 | tf_op jit(solution)/shard_map/ppermute | solution.py:339
  78.9 1.5 convolution_bitcast_fusion.refs_1_.refs_3_
  80.4 5.0 %attend.1 = (bf16[4,2,32,512]{3,2,1,0:T(8,128)(2,1)S(1)}, bf16[2,2,1024,128]{3,2,1,0:T(8,128)(2,1)S(1)}, bf16[2,2,128,128]{3,2,1,0:T(8,128)(2,1)S(1)}) custom-call(s32[2]{0:T(128)S(1)} %copy-done.4, s32[2]{0:T(128)S(1)} %copy-done.5, s32[4]{0:T(128)S(1)} %and_select_fusion.owners, f32[3,2,32,512]{3,2,1,0:T(8,128)S(1)} %bitcast.39, ...), custom_call_target="tpu_custom_call" | custom-call | tf_op jit(solution)/shard_map/attend/pallas_call | solution.py:141
  85.5 2.7 %terms.3 = (bf16[1,32,7680]{2,1,0:T(8,128)(2,1)S(1)}, bf16[1,32,7680]{2,1,0:T(8,128)(2,1)S(1)}) custom-call(bf16[1,2,32,512]{3,2,1,0:T(8,128)(2,1)S(1)} %slice.44.rows, bf16[7680,512]{1,0:T(8,128)(2,1)S(1)} %bitcast.37), custom_call_target="tpu_custom_call" | custom-call | tf_op jit(solution)/shard_map/terms/pallas_call | solution.py:232
  88.2 1.0 collective-permute-start.10
  89.2 2.9 %collective-permute-start.11 = (bf16[1,32,7680]{2,1,0:T(8,128)(2,1)S(1)}, bf16[1,32,7680]{2,1,0:T(8,128)(2,1)S(1)}, u32[]{:S(2)}, u32[]{:S(2)}) collective-permute-start(bf16[1,32,7680]{2,1,0:T(8,128)(2,1)S(1)} %get-tuple-element.64), channel_id=1, source_target_pairs={{0,3},{1,0},{2,1},{3,2},{4,7},{5,4},{6,5},{7,6},{8,11},{9,8},{10,9... | collective-permute-start | bytes 1474568 | tf_op jit(solution)/shard_map/ppermute | solution.py:339
  92.1 2.5 %convolution_convert_fusion = bf16[7680,512]{1,0:T(8,128)(2,1)S(1)} fusion(bf16[256,512]{1,0:T(8,128)(2,1)S(1)} %bitcast.41, bf16[64,7680]{1,0:T(8,128)(2,1)S(1)} %bitcast.44, bf16[192,7680]{1,0:T(8,128)(2,1)S(1)} %bitcast.46), kind=kOutput, calls=%fused_computation | convolution fusion | flops 2025062400 | bytes 12058624 | tf_op jit(solution)/shard_map/dot_general | solution.py:29
  94.9 3.5 %terms.2 = (bf16[2,32,7680]{2,1,0:T(8,128)(2,1)S(1)}, bf16[2,32,7680]{2,1,0:T(8,128)(2,1)S(1)}, bf16[2,32,7680]{2,1,0:T(8,128)(2,1)S(1)}) custom-call(bf16[3,2,32,512]{3,2,1,0:T(8,128)(2,1)S(1)} %slice.42.rows, bf16[7680,512]{1,0:T(8,128)(2,1)S(1)} %bitcast.38), custom_call_target="tpu_custom_call" | custom-call | tf_op jit(solution)/shard_map/terms/pallas_call | solution.py:232
  98.5 5.8 %collective-permute-done.10 = bf16[1,32,7680]{2,1,0:T(8,128)(2,1)S(1)} collective-permute-done((bf16[1,32,7680]{2,1,0:T(8,128)(2,1)S(1)}, bf16[1,32,7680]{2,1,0:T(8,128)(2,1)S(1)}, u32[]{:S(2)}, u32[]{:S(2)}) %collective-permute-start.10) | collective-permute-done | bytes 491552 | tf_op jit(solution)/shard_map/ppermute | solution.py:339
  104.2 8.1 %collective-permute-done.11 = bf16[1,32,7680]{2,1,0:T(8,128)(2,1)S(1)} collective-permute-done((bf16[1,32,7680]{2,1,0:T(8,128)(2,1)S(1)}, bf16[1,32,7680]{2,1,0:T(8,128)(2,1)S(1)}, u32[]{:S(2)}, u32[]{:S(2)}) %collective-permute-start.11) | collective-permute-done | bytes 491552 | tf_op jit(solution)/shard_map/ppermute | solution.py:339
  112.5 1.0 pad_maximum_fusion.3
  113.6 1.0 pad_maximum_fusion.2
  114.6 1.6 collective-permute-start.12
  116.2 2.2 %collective-permute-start.13 = (bf16[2,32,7680]{2,1,0:T(8,128)(2,1)}, bf16[2,32,7680]{2,1,0:T(8,128)(2,1)}, u32[]{:S(2)}, u32[]{:S(2)}) collective-permute-start(bf16[2,32,7680]{2,1,0:T(8,128)(2,1)} %pad_maximum_fusion.3), channel_id=1, source_target_pairs={{0,3},{1,0},{2,1},{3,2},{4,7},{5,4},{6,5},{7,6},{8,11},{9,8},{10,9... | collective-permute-start | bytes 2949128 | tf_op jit(solution)/shard_map/ppermute | solution.py:339
  118.5 1.3 merge.2
  119.9 0.8 merge.3.own
  121.5 4.3 %after.1 = bf16[2,128,2048]{2,1,0:T(8,128)(2,1)} custom-call(bf16[2,128,2048]{2,1,0:T(8,128)(2,1)} %query.3, bf16[2,2,1024,128]{3,2,1,0:T(8,128)(2,1)} %copy-done, bf16[2,2,128,128]{3,2,1,0:T(8,128)(2,1)} %copy-done.3, f32[1,128]{1,0:T(1,128)} %bitcast.52), custom_call_target="tpu_custom_call" | custom-call | tf_op jit(solution)/shard_map/after/pallas_call | solution.py:189
  125.8 15.6 %collective-permute-done.12 = bf16[2,32,7680]{2,1,0:T(8,128)(2,1)} collective-permute-done((bf16[2,32,7680]{2,1,0:T(8,128)(2,1)}, bf16[2,32,7680]{2,1,0:T(8,128)(2,1)}, u32[]{:S(2)}, u32[]{:S(2)}) %collective-permute-start.12) | collective-permute-done | bytes 983072 | tf_op jit(solution)/shard_map/ppermute | solution.py:339
  141.4 18.9 %collective-permute-done.13 = bf16[2,32,7680]{2,1,0:T(8,128)(2,1)} collective-permute-done((bf16[2,32,7680]{2,1,0:T(8,128)(2,1)}, bf16[2,32,7680]{2,1,0:T(8,128)(2,1)}, u32[]{:S(2)}, u32[]{:S(2)}) %collective-permute-start.13) | collective-permute-done | bytes 983072 | tf_op jit(solution)/shard_map/ppermute | solution.py:339
  160.3 1.2 collective-permute-start.15
  161.6 1.2 collective-permute-start.16
  162.7 1.1 collective-permute-start.17
  163.8 2.8 %add_convert_fusion = bf16[2,32,7680]{2,1,0:T(8,128)(2,1)} fusion(bf16[2,32,7680]{2,1,0:T(8,128)(2,1)} %collective-permute-done.13, bf16[2,32,7680]{2,1,0:T(8,128)(2,1)} %collective-permute-done.12, bf16[2,32,7680]{2,1,0:T(8,128)(2,1)S(1)} %get-tuple-element.79), kind=kLoop, calls=%fused_computation.7 | loop fusion | flops 2949120 | bytes 3932160 | tf_op jit(solution)/shard_map/convert_element_type | solution.py:420
  166.6 18.5 %collective-permute-done.15.refs_0_ = bf16[960,512]{1,0:T(8,128)(2,1)S(1)} collective-permute-done((bf16[960,512]{1,0:T(8,128)(2,1)}, bf16[960,512]{1,0:T(8,128)(2,1)S(1)}, u32[]{:S(2)}, u32[]{:S(2)}) %collective-permute-start.15) | collective-permute-done | bytes 983072 | tf_op jit(solution)/shard_map/ppermute | solution.py:342
  185.2 19.9 %collective-permute-done.16.refs_1_ = bf16[960,512]{1,0:T(8,128)(2,1)S(1)} collective-permute-done((bf16[960,512]{1,0:T(8,128)(2,1)}, bf16[960,512]{1,0:T(8,128)(2,1)S(1)}, u32[]{:S(2)}, u32[]{:S(2)}) %collective-permute-start.16) | collective-permute-done | bytes 983072 | tf_op jit(solution)/shard_map/ppermute | solution.py:342
  205.0 1.2 collective-permute-done.17.refs_2_
  206.2 1.4 finish.1
  (60 shorter events, 3.1 us)
Async XLA Ops:
  0.6 53.2 %copy-start.16 = (s32[4]{0:T(128)S(1)}, s32[4]{0:T(128)}, u32[]{:S(2)}) copy-start(s32[4]{0:T(128)} %constant.61.clone) | copy-start | bytes 52
  0.6 27.9 %collective-permute-start = (bf16[2,32,7680]{2,1,0:T(8,128)(2,1)}, bf16[2,32,7680]{2,1,0:T(8,128)(2,1)S(1)}, u32[]{:S(2)}, u32[]{:S(2)}) collective-permute-start(bf16[2,32,7680]{2,1,0:T(8,128)(2,1)} %param.13), channel_id=1, source_target_pairs={{0,1},{1,2},{2,3},{3,0},{4,5},{5,6},{6,7},{7,4},{8,9},{9,10},{10,1... | collective-permute-start | bytes 2949128 | tf_op jit(solution)/shard_map/ppermute | solution.py:339
  3.7 44.5 %collective-permute-start.1 = (bf16[2,32,7680]{2,1,0:T(8,128)(2,1)}, bf16[2,32,7680]{2,1,0:T(8,128)(2,1)S(1)}, u32[]{:S(2)}, u32[]{:S(2)}) collective-permute-start(bf16[2,32,7680]{2,1,0:T(8,128)(2,1)} %param.13), channel_id=1, source_target_pairs={{0,3},{1,0},{2,1},{3,2},{4,7},{5,4},{6,5},{7,6},{8,11},{9,8},{10,9... | collective-permute-start | bytes 2949128 | tf_op jit(solution)/shard_map/ppermute | solution.py:339
  8.0 41.1 %collective-permute-start.2 = (bf16[960,512]{1,0:T(8,128)(2,1)}, bf16[960,512]{1,0:T(8,128)(2,1)S(1)}, u32[]{:S(2)}, u32[]{:S(2)}) collective-permute-start(bf16[960,512]{1,0:T(8,128)(2,1)} %beside.1), channel_id=1, source_target_pairs={{0,8},{4,12},{8,0},{12,4},{16,24},{20,28},{24,16},{28,20},{1,9},{5... | collective-permute-start | bytes 2949128 | tf_op jit(solution)/shard_map/ppermute | solution.py:342
  9.7 44.2 %collective-permute-start.3 = (bf16[960,512]{1,0:T(8,128)(2,1)}, bf16[960,512]{1,0:T(8,128)(2,1)}, u32[]{:S(2)}, u32[]{:S(2)}) collective-permute-start(bf16[960,512]{1,0:T(8,128)(2,1)} %beside.1), channel_id=1, source_target_pairs={{0,16},{4,20},{8,24},{12,28},{16,0},{20,4},{24,8},{28,12},{1,17},{... | collective-permute-start | bytes 2949128 | tf_op jit(solution)/shard_map/ppermute | solution.py:342
  11.2 42.6 %collective-permute-start.4 = (bf16[960,512]{1,0:T(8,128)(2,1)}, bf16[960,512]{1,0:T(8,128)(2,1)}, u32[]{:S(2)}, u32[]{:S(2)}) collective-permute-start(bf16[960,512]{1,0:T(8,128)(2,1)} %beside.1), channel_id=1, source_target_pairs={{0,24},{4,28},{8,16},{12,20},{16,8},{20,12},{24,0},{28,4},{1,25},{... | collective-permute-start | bytes 2949128 | tf_op jit(solution)/shard_map/ppermute | solution.py:342
  48.2 1.1 copy-start.12
  49.1 0.9 copy-start.15
  53.8 5.8 %collective-permute-start.5 = (bf16[2,960,512]{2,1,0:T(8,128)(2,1)S(1)}, bf16[2,960,512]{2,1,0:T(8,128)(2,1)}, u32[]{:S(2)}, u32[]{:S(2)}) collective-permute-start(bf16[2,960,512]{2,1,0:T(8,128)(2,1)S(1)} %pad_maximum_fusion.1), channel_id=1, source_target_pairs={{0,4},{4,0},{8,12},{12,8},{16,20},{20,16},{24,28},{28,24},{1,5},{5... | collective-permute-start | bytes 5898248 | tf_op jit(solution)/shard_map/ppermute | solution.py:342
  53.8 5.3 %copy-start.13 = (bf16[2,32,7680]{2,1,0:T(8,128)(2,1)S(1)}, bf16[2,32,7680]{2,1,0:T(8,128)(2,1)}, u32[]{:S(2)}) copy-start(bf16[2,32,7680]{2,1,0:T(8,128)(2,1)} %copy-done.12) | copy-start | bytes 2949124
  53.8 5.3 %copy-start.14 = (bf16[2,32,7680]{2,1,0:T(8,128)(2,1)S(1)}, bf16[2,32,7680]{2,1,0:T(8,128)(2,1)}, u32[]{:S(2)}) copy-start(bf16[2,32,7680]{2,1,0:T(8,128)(2,1)} %param.13) | copy-start | bytes 2949124
  53.9 10.5 %collective-permute-start.6 = (bf16[1,960,512]{2,1,0:T(8,128)(2,1)}, bf16[1,960,512]{2,1,0:T(8,128)(2,1)S(1)}, u32[]{:S(2)}, u32[]{:S(2)}) collective-permute-start(bf16[1,960,512]{2,1,0:T(8,128)(2,1)} %bitcast.7), channel_id=1, source_target_pairs={{0,4},{4,0},{8,12},{12,8},{16,20},{20,16},{24,28},{28,24},{1,5},{5... | collective-permute-start | bytes 2949128 | tf_op jit(solution)/shard_map/ppermute | solution.py:342
  54.4 11.3 %collective-permute-start.7 = (bf16[1,960,512]{2,1,0:T(8,128)(2,1)}, bf16[1,960,512]{2,1,0:T(8,128)(2,1)S(1)}, u32[]{:S(2)}, u32[]{:S(2)}) collective-permute-start(bf16[1,960,512]{2,1,0:T(8,128)(2,1)} %bitcast.8), channel_id=1, source_target_pairs={{0,4},{4,0},{8,12},{12,8},{16,20},{20,16},{24,28},{28,24},{1,5},{5... | collective-permute-start | bytes 2949128 | tf_op jit(solution)/shard_map/ppermute | solution.py:342
  54.5 15.9 %collective-permute-start.8 = (bf16[1,32,7680]{2,1,0:T(8,128)(2,1)S(1)}, bf16[1,32,7680]{2,1,0:T(8,128)(2,1)S(1)}, u32[]{:S(2)}, u32[]{:S(2)}) collective-permute-start(bf16[1,32,7680]{2,1,0:T(8,128)(2,1)S(1)} %slice.48), channel_id=1, source_target_pairs={{0,1},{1,2},{2,3},{3,0},{4,5},{5,6},{6,7},{7,4},{8,9},{9,10},{10,1... | collective-permute-start | bytes 1474568 | tf_op jit(solution)/shard_map/ppermute | solution.py:339
  54.5 24.3 %collective-permute-start.9 = (bf16[1,32,7680]{2,1,0:T(8,128)(2,1)}, bf16[1,32,7680]{2,1,0:T(8,128)(2,1)S(1)}, u32[]{:S(2)}, u32[]{:S(2)}) collective-permute-start(bf16[1,32,7680]{2,1,0:T(8,128)(2,1)} %slice.49), channel_id=1, source_target_pairs={{0,3},{1,0},{2,1},{3,2},{4,7},{5,4},{6,5},{7,6},{8,11},{9,8},{10,9... | collective-permute-start | bytes 1474568 | tf_op jit(solution)/shard_map/ppermute | solution.py:339
  59.4 8.1 %copy-start.10 = (bf16[3,2,32,7680]{3,2,1,0:T(8,128)(2,1)}, bf16[3,2,32,7680]{3,2,1,0:T(8,128)(2,1)S(1)}, u32[]{:S(2)}) copy-start(bf16[3,2,32,7680]{3,2,1,0:T(8,128)(2,1)S(1)} %pad_maximum_fusion) | copy-start | bytes 8847364
  67.6 12.8 %copy-start.1 = (bf16[2,2,1024,128]{3,2,1,0:T(8,128)(2,1)S(1)}, bf16[2,2,1024,128]{3,2,1,0:T(8,128)(2,1)}, u32[]{:S(2)}) copy-start(bf16[2,2,1024,128]{3,2,1,0:T(8,128)(2,1)} %get-tuple-element.59.refs_4_) | copy-start | bytes 3145732
  67.6 12.8 %copy-start.2 = (bf16[2,2,1024,128]{3,2,1,0:T(8,128)(2,1)S(1)}, bf16[2,2,1024,128]{3,2,1,0:T(8,128)(2,1)}, u32[]{:S(2)}) copy-start(bf16[2,2,1024,128]{3,2,1,0:T(8,128)(2,1)} %get-tuple-element.60.refs_5_) | copy-start | bytes 3145732
  67.6 12.8 %copy-start.4 = (s32[2]{0:T(128)S(1)}, s32[2]{0:T(128)}, u32[]{:S(2)}) copy-start(s32[2]{0:T(128)} %assignment.1) | copy-start | bytes 28
  67.6 12.8 %copy-start.5 = (s32[2]{0:T(128)S(1)}, s32[2]{0:T(128)}, u32[]{:S(2)}) copy-start(s32[2]{0:T(128)} %tiles.1) | copy-start | bytes 28
  67.6 12.8 %copy-start.6 = (f32[128]{0:T(128)S(1)}, f32[128]{0:T(128)}, u32[]{:S(2)}) copy-start(f32[128]{0:T(128)} %param.17) | copy-start | bytes 1540
  80.4 11.7 %copy-start.11 = (bf16[3,2,32,7680]{3,2,1,0:T(8,128)(2,1)S(1)}, bf16[3,2,32,7680]{3,2,1,0:T(8,128)(2,1)}, u32[]{:S(2)}) copy-start(bf16[3,2,32,7680]{3,2,1,0:T(8,128)(2,1)} %copy-done.10) | copy-start | bytes 8847364
  85.4 6.6 %copy-start = (bf16[2,2,1024,128]{3,2,1,0:T(8,128)(2,1)}, bf16[2,2,1024,128]{3,2,1,0:T(8,128)(2,1)S(1)}, u32[]{:S(2)}) copy-start(bf16[2,2,1024,128]{3,2,1,0:T(8,128)(2,1)S(1)} %get-tuple-element.76.score_grad) | copy-start | bytes 3145732
  85.4 6.6 %copy-start.3 = (bf16[2,2,128,128]{3,2,1,0:T(8,128)(2,1)}, bf16[2,2,128,128]{3,2,1,0:T(8,128)(2,1)S(1)}, u32[]{:S(2)}) copy-start(bf16[2,2,128,128]{3,2,1,0:T(8,128)(2,1)S(1)} %get-tuple-element.77.keys) | copy-start | bytes 393220
  88.2 16.0 %collective-permute-start.10 = (bf16[1,32,7680]{2,1,0:T(8,128)(2,1)S(1)}, bf16[1,32,7680]{2,1,0:T(8,128)(2,1)S(1)}, u32[]{:S(2)}, u32[]{:S(2)}) collective-permute-start(bf16[1,32,7680]{2,1,0:T(8,128)(2,1)S(1)} %get-tuple-element.63), channel_id=1, source_target_pairs={{0,1},{1,2},{2,3},{3,0},{4,5},{5,6},{6,7},{7,4},{8,9},{9,10},{10,1... | collective-permute-start | bytes 1474568 | tf_op jit(solution)/shard_map/ppermute | solution.py:339
  89.2 23.1 %collective-permute-start.11 = (bf16[1,32,7680]{2,1,0:T(8,128)(2,1)S(1)}, bf16[1,32,7680]{2,1,0:T(8,128)(2,1)S(1)}, u32[]{:S(2)}, u32[]{:S(2)}) collective-permute-start(bf16[1,32,7680]{2,1,0:T(8,128)(2,1)S(1)} %get-tuple-element.64), channel_id=1, source_target_pairs={{0,3},{1,0},{2,1},{3,2},{4,7},{5,4},{6,5},{7,6},{8,11},{9,8},{10,9... | collective-permute-start | bytes 1474568 | tf_op jit(solution)/shard_map/ppermute | solution.py:339
  94.8 23.7 %collective-permute-start.14 = (bf16[4,960,512]{2,1,0:T(8,128)(2,1)S(1)}, bf16[4,960,512]{2,1,0:T(8,128)(2,1)S(1)}, u32[]{:S(2)}, u32[]{:S(2)}) collective-permute-start(bf16[4,960,512]{2,1,0:T(8,128)(2,1)S(1)} %dynamic-slice_bitcast_fusion), channel_id=1, source_target_pairs={{0,4},{4,0},{8,12},{12,8},{16,20},{20,16},{24,28},{28,24},{1,5},{5... | collective-permute-start | bytes 11796488 | tf_op jit(solution)/shard_map/ppermute | solution.py:342
  114.6 26.8 %collective-permute-start.12 = (bf16[2,32,7680]{2,1,0:T(8,128)(2,1)}, bf16[2,32,7680]{2,1,0:T(8,128)(2,1)}, u32[]{:S(2)}, u32[]{:S(2)}) collective-permute-start(bf16[2,32,7680]{2,1,0:T(8,128)(2,1)} %pad_maximum_fusion.2), channel_id=1, source_target_pairs={{0,1},{1,2},{2,3},{3,0},{4,5},{5,6},{6,7},{7,4},{8,9},{9,10},{10,1... | collective-permute-start | bytes 2949128 | tf_op jit(solution)/shard_map/ppermute | solution.py:339
  116.2 44.1 %collective-permute-start.13 = (bf16[2,32,7680]{2,1,0:T(8,128)(2,1)}, bf16[2,32,7680]{2,1,0:T(8,128)(2,1)}, u32[]{:S(2)}, u32[]{:S(2)}) collective-permute-start(bf16[2,32,7680]{2,1,0:T(8,128)(2,1)} %pad_maximum_fusion.3), channel_id=1, source_target_pairs={{0,3},{1,0},{2,1},{3,2},{4,7},{5,4},{6,5},{7,6},{8,11},{9,8},{10,9... | collective-permute-start | bytes 2949128 | tf_op jit(solution)/shard_map/ppermute | solution.py:339
  119.8 1.0 copy-start.7
  119.9 1.3 copy-start.8
  119.9 1.6 copy-start.9
  160.3 24.8 %collective-permute-start.15 = (bf16[960,512]{1,0:T(8,128)(2,1)}, bf16[960,512]{1,0:T(8,128)(2,1)S(1)}, u32[]{:S(2)}, u32[]{:S(2)}) collective-permute-start(bf16[960,512]{1,0:T(8,128)(2,1)} %copy-done.9), channel_id=1, source_target_pairs={{0,8},{4,12},{8,0},{12,4},{16,24},{20,28},{24,16},{28,20},{1,9},{5... | collective-permute-start | bytes 2949128 | tf_op jit(solution)/shard_map/ppermute | solution.py:342
  161.6 43.5 %collective-permute-start.16 = (bf16[960,512]{1,0:T(8,128)(2,1)}, bf16[960,512]{1,0:T(8,128)(2,1)S(1)}, u32[]{:S(2)}, u32[]{:S(2)}) collective-permute-start(bf16[960,512]{1,0:T(8,128)(2,1)} %copy-done.8), channel_id=1, source_target_pairs={{0,16},{4,20},{8,24},{12,28},{16,0},{20,4},{24,8},{28,12},{1,17},{... | collective-permute-start | bytes 2949128 | tf_op jit(solution)/shard_map/ppermute | solution.py:342
  162.7 43.5 %collective-permute-start.17 = (bf16[960,512]{1,0:T(8,128)(2,1)}, bf16[960,512]{1,0:T(8,128)(2,1)S(1)}, u32[]{:S(2)}, u32[]{:S(2)}) collective-permute-start(bf16[960,512]{1,0:T(8,128)(2,1)} %copy-done.7), channel_id=1, source_target_pairs={{0,24},{4,28},{8,16},{12,20},{16,8},{20,12},{24,0},{28,4},{1,25},{... | collective-permute-start | bytes 2949128 | tf_op jit(solution)/shard_map/ppermute | solution.py:342
